TPU v7x, 32 devices: a whole 2x2x4 slice. The times are simulated.
32 devices in a mesh: row: 4 (over x, core), span: 2 (over y), pitch: 4 (over z).
Axes of the slice: x: 2, y: 2, z: 4, core: 2. Of those that a mesh axis runs over, the one named last changes fastest.
Arguments:
- adjoint_start: float32 [5, 16, 64, 512], P(None, 'row', 'span', 'pitch'), may hold values from -8 to 8
- source: float32 [5, 16, 64, 512], P(None, 'row', 'span', 'pitch'), may hold values from -6 to 6
- couplings: float32 [6, 16, 64, 512], P(None, 'row', 'span', 'pitch'), may hold values from 0.2 to 1
- damping: float32 [16, 64, 512], P('row', 'span', 'pitch'), may hold values from 0.1 to 0.8
- jacobians: float32 [4, 6, 5, 5], P('row')
- giles_real: float32 [3, 64, 5, 5], replicated, may hold values from -6 to 6
- giles_imag: float32 [3, 64, 5, 5], replicated, may hold values from -6 to 6
- blades: int32 [4], replicated, may hold values from 16 to 79
- mode_orders: int32 [3, 64, 2], replicated, may hold values from -2 to 2
- cell_map: int32 [4, 512], P('row'), may hold values from 0 to 511
Outputs:
- adjoint: float32 [5, 16, 64, 512], P(None, 'row', 'span', 'pitch')
All inputs are finite; a program needn't handle non-finite values.
Results may differ from a plain program's by a relative error of at most 0.0001.
Values sent between devices are 32-bit elements; how exact they have to be, the bound alone decides.
No kernel may reach another device: no remote copies, remote signals or barrier semaphores. Data moves between devices by JAX's collectives and lax.ppermute only.
A program may use at most 64 MiB of HBM per device.

v0:
```python
import math

import jax
import jax.numpy as jnp
from jax import lax
from jax.sharding import PartitionSpec as P

ITERS = 5


PRECISE = lax.Precision.HIGHEST


def shifted(x, axis, by):
    size = lax.axis_size(axis)
    pairs = [(i, i + by) for i in range(size) if 0 <= i + by < size]
    return lax.ppermute(x, axis, pairs)


def padded(cells, sides, width, closed):
    for axis, dim in sides:
        count = lax.axis_size(axis)
        ends = count if closed else count - 1
        head = lax.slice_in_dim(cells, 0, width, axis=dim)
        tail = lax.slice_in_dim(cells, cells.shape[dim] - width, cells.shape[dim], axis=dim)
        cells = jnp.concatenate(
            [
                lax.ppermute(tail, axis, [(i, (i + 1) % count) for i in range(ends)]),
                cells,
                lax.ppermute(head, axis, [((i + 1) % count, i) for i in range(ends)]),
            ],
            axis=dim,
        )
    return cells


def phase_table(numbers, positions, length):
    products = positions[:, None] * numbers[None, :]
    return jnp.mod(products, length).astype(jnp.float32) * (2.0 * math.pi / length)


def giles(real_part, imag_part, giles_re, giles_im):
    out_real = jnp.einsum("kjc,jsk->csk", giles_re, real_part, precision=PRECISE) - jnp.einsum(
        "kjc,jsk->csk", giles_im, imag_part, precision=PRECISE
    )
    out_imag = jnp.einsum("kjc,jsk->csk", giles_re, imag_part, precision=PRECISE) + jnp.einsum(
        "kjc,jsk->csk", giles_im, real_part, precision=PRECISE
    )
    return jnp.stack([out_real, out_imag], 2)


def send_upstream(amplitudes):
    return shifted(amplitudes, "row", -1)


def update(adjoint, source, couplings, diag_sum, jacobian_row, boundary):
    axial_cells = adjoint.shape[1]
    span_len = adjoint.shape[2]
    pitch_len = adjoint.shape[3]
    span_edges = jnp.concatenate([adjoint[:, :, :1], adjoint[:, :, -1:]], 2)
    span_got = padded(span_edges, (("span", 2),), 1, False)
    pitch_edges = jnp.concatenate([adjoint[:, :, :, :1], adjoint[:, :, :, -1:]], 3)
    pitch_got = padded(pitch_edges, (("pitch", 3),), 1, True)
    axial_index = lax.broadcasted_iota(jnp.int32, (1, axial_cells, 1, 1), 1)
    span_index = lax.broadcasted_iota(jnp.int32, (1, 1, span_len, 1), 2)
    pitch_index = lax.broadcasted_iota(jnp.int32, (1, 1, 1, pitch_len), 3)
    axial_next = jnp.where(axial_index == axial_cells - 1, 0.0, jnp.roll(adjoint, -1, 1))
    axial_prev = jnp.where(axial_index == 0, 0.0, jnp.roll(adjoint, 1, 1))
    span_next = jnp.where(span_index == span_len - 1, span_got[:, :, 3:4], jnp.roll(adjoint, -1, 2))
    span_prev = jnp.where(span_index == 0, span_got[:, :, 0:1], jnp.roll(adjoint, 1, 2))
    pitch_next = jnp.where(
        pitch_index == pitch_len - 1, pitch_got[:, :, :, 3:4], jnp.roll(adjoint, -1, 3)
    )
    pitch_prev = jnp.where(pitch_index == 0, pitch_got[:, :, :, 0:1], jnp.roll(adjoint, 1, 3))
    neighbours = (axial_next, axial_prev, span_next, span_prev, pitch_next, pitch_prev)
    total = source + jnp.where(axial_index == axial_cells - 1, boundary[:, None], 0.0)
    for direction in range(6):
        mixed = jacobian_row[direction, 0][:, None, None, None] * neighbours[direction][0][None]
        for entry in range(1, 5):
            mixed = (
                mixed
                + jacobian_row[direction, entry][:, None, None, None]
                * neighbours[direction][entry][None]
            )
        total = total + couplings[direction][None] * mixed
    return total / diag_sum[None]


def on_device(
    adjoint_start,
    source,
    couplings,
    damping,
    jacobians,
    giles_real,
    giles_imag,
    blades,
    mode_orders,
    cell_map,
):
    components, axial_cells, span_cells, pitch_cells = adjoint_start.shape
    rows_all = lax.axis_size("row")
    pitch_count = lax.axis_size("pitch")
    length = pitch_cells * pitch_count
    modes_count = mode_orders.shape[1]
    row_id = lax.axis_index("row")
    pitch_id = lax.axis_index("pitch")
    diag_sum = damping + jnp.sum(couplings, 0)
    jacobian_row = jacobians[0]
    sender_face = jnp.maximum(row_id - 1, 0)
    receiver_face = jnp.minimum(row_id, rows_all - 2)

    def mode_numbers(face):
        orders = lax.dynamic_index_in_dim(mode_orders, face, 0, keepdims=False)
        blades_low = lax.dynamic_index_in_dim(blades, face, 0, keepdims=False)
        blades_high = lax.dynamic_index_in_dim(blades, face + 1, 0, keepdims=False)
        return orders[:, 0] * blades_low + orders[:, 1] * blades_high

    send_modes = mode_numbers(sender_face)
    recv_modes = mode_numbers(receiver_face)
    giles_re = lax.dynamic_index_in_dim(giles_real, sender_face, 0, keepdims=False)
    giles_im = lax.dynamic_index_in_dim(giles_imag, sender_face, 0, keepdims=False)
    donor_cells = cell_map[0]
    own_cells = pitch_id * pitch_cells + jnp.arange(pitch_cells, dtype=jnp.int32)
    angles = phase_table(send_modes, own_cells, length)
    local_forward = jnp.concatenate([jnp.cos(angles), -jnp.sin(angles)], 1) * (2.0 / length)
    angles = phase_table(
        recv_modes,
        lax.dynamic_slice_in_dim(donor_cells, pitch_id * pitch_cells, pitch_cells),
        length,
    )
    local_synth = jnp.concatenate([jnp.cos(angles).T, -jnp.sin(angles).T], 0)
    share_count = modes_count // pitch_count
    mode_start = pitch_id * share_count
    giles_re_part = lax.dynamic_slice_in_dim(giles_re, mode_start, share_count, 0)
    giles_im_part = lax.dynamic_slice_in_dim(giles_im, mode_start, share_count, 0)
    adjoint = adjoint_start
    for sweep in range(ITERS):
        inlet_strip = adjoint[:, 0]
        partial_sum = jnp.dot(
            inlet_strip.reshape(components * span_cells, pitch_cells),
            local_forward,
            precision=PRECISE,
        )
        partial_sum = partial_sum.reshape(components, span_cells, 2, modes_count)
        owned = lax.psum_scatter(partial_sum, "pitch", scatter_dimension=3, tiled=True)
        treated = giles(owned[:, :, 0], owned[:, :, 1], giles_re_part, giles_im_part)
        arrived = send_upstream(treated)
        all_modes = lax.all_gather(arrived, "pitch", axis=3, tiled=True)
        boundary_field = jnp.dot(
            all_modes.reshape(components * span_cells, 2 * modes_count),
            local_synth,
            precision=PRECISE,
        )
        boundary = boundary_field.reshape(components, span_cells, pitch_cells)
        adjoint = update(adjoint, source, couplings, diag_sum, jacobian_row, boundary)
    return adjoint


def solution(mesh):
    placed = (
        P(None, "row", "span", "pitch"),
        P(None, "row", "span", "pitch"),
        P(None, "row", "span", "pitch"),
        P("row", "span", "pitch"),
        P("row", None, None, None),
        P(),
        P(),
        P(),
        P(),
        P("row", None),
    )
    return jax.shard_map(
        on_device,
        mesh=mesh,
        in_specs=placed,
        out_specs=P(None, "row", "span", "pitch"),
        check_vma=False,
    )
```

profile of v0, /device:TPU:1, one launch (start us, length us, event | category | flops | bytes accessed | tf_op | source)
XLA Modules:
  0.0 335.0 jit_solution(11793588474378385543)
XLA Ops:
  6.5 1.2 fusion.123
  8.5 2.1 collective-permute-start.4
  11.4 2.0 collective-permute-start.3
  14.1 3.7 %collective-permute-start.2 = (f32[5,4,1,128]{3,2,0,1:T(1,128)}, f32[5,4,1,128]{3,2,0,1:T(1,128)}, u32[]{:S(2)}, u32[]{:S(2)}) collective-permute-start(f32[5,4,1,128]{3,2,0,1:T(1,128)} %copy.232), channel_id=1, source_target_pairs={{0,4},{1,5},{2,6},{3,7},{8,12},{9,13},{10,14},{11,15},{16,20},{17,... | collective-permute-start | bytes 30728 | tf_op jit(solution)/shard_map/ppermute | solution.py:28
  18.4 1.3 collective-permute-start.1
  22.3 2.9 add_bitcast_fusion
  28.8 1.0 slice_reduce_fusion.29
  39.6 1.2 copy.159
  41.7 1.2 copy.155
  45.9 17.7 %all-reduce.3.cloned.1.call-done = f32[5,32,2,64]{1,2,0,3:T(2,128)} async-done(((f32[5,32,2,64]{1,2,0,3:T(2,128)}), f32[5,32,2,64]{1,2,0,3:T(2,128)}) %all-reduce.3.cloned.1.call-update) | async-done | bytes 81936
  63.6 1.0 constant_dynamic-slice_fusion.5
  65.7 4.1 %collective-permute-start = (f32[5,32,2,16]{1,0,3,2:T(8,128)S(1)}, f32[5,32,2,16]{1,0,3,2:T(8,128)S(1)}, u32[]{:S(2)}, u32[]{:S(2)}) collective-permute-start(f32[5,32,2,16]{1,0,3,2:T(8,128)S(1)} %pad_maximum_fusion.4), channel_id=1, source_target_pairs={{8,0},{16,8},{24,16},{9,1},{17,9},{25,17},{10,2},{18,10},{26,18},{... | collective-permute-start | bytes 61448 | tf_op jit(solution)/shard_map/ppermute | solution.py:17
  69.8 3.7 %collective-permute-done = f32[5,32,2,16]{1,0,3,2:T(8,128)S(1)} collective-permute-done((f32[5,32,2,16]{1,0,3,2:T(8,128)S(1)}, f32[5,32,2,16]{1,0,3,2:T(8,128)S(1)}, u32[]{:S(2)}, u32[]{:S(2)}) %collective-permute-start) | collective-permute-done | bytes 20512 | tf_op jit(solution)/shard_map/ppermute | solution.py:17
  73.5 13.2 %all_gather.15 = f32[5,32,2,64]{1,0,3,2:T(8,128)S(1)} all-gather(f32[5,32,2,16]{1,0,3,2:T(8,128)S(1)} %collective-permute-done), channel_id=1, replica_groups=mesh['row'=4,'span'=2,'pitch'=4] {'pitch'}, dimensions={3}, use_global_device_ids=true | all-gather | bytes 102400 | tf_op jit(solution)/shard_map/all_gather | solution.py:149
  88.5 1.2 add_divide_fusion.4
  90.9 3.2 collective-permute-start.8
  94.1 3.7 %collective-permute-start.7 = (f32[5,4,1,128]{3,2,0,1:T(1,128)}, f32[5,4,1,128]{3,2,0,1:T(1,128)}, u32[]{:S(2)}, u32[]{:S(2)}) collective-permute-start(f32[5,4,1,128]{3,2,0,1:T(1,128)} %get-tuple-element.189), channel_id=1, source_target_pairs={{0,4},{1,5},{2,6},{3,7},{8,12},{9,13},{10,14},{11,15},{16,20},{17,... | collective-permute-start | bytes 30728 | tf_op jit(solution)/shard_map/ppermute | solution.py:28
  97.8 1.3 collective-permute-start.6
  100.5 1.2 fusion.26
  102.2 1.7 copy.174
  105.6 1.5 collective-permute-done.8
  107.1 1.2 copy.172
  113.5 8.8 %reduce-scatter.5.cloned.1.call-done = f32[5,32,2,16]{1,3,2,0:T(8,128)} async-done(((f32[5,32,2,64]{1,3,2,0:T(8,128)}), f32[5,32,2,16]{1,3,2,0:T(8,128)}) %reduce-scatter.5.cloned.1.call-update) | async-done | bytes 20496 | tf_op jit(solution)/shard_map/reduce_scatter | solution.py:146
  124.1 4.2 %collective-permute-start.5 = (f32[5,32,2,16]{1,0,3,2:T(8,128)S(1)}, f32[5,32,2,16]{1,0,3,2:T(8,128)S(1)}, u32[]{:S(2)}, u32[]{:S(2)}) collective-permute-start(f32[5,32,2,16]{1,0,3,2:T(8,128)S(1)} %pad_maximum_fusion.5), channel_id=1, source_target_pairs={{8,0},{16,8},{24,16},{9,1},{17,9},{25,17},{10,2},{18,10},{26,18},{... | collective-permute-start | bytes 61448 | tf_op jit(solution)/shard_map/ppermute | solution.py:17
  128.3 3.8 %collective-permute-done.5 = f32[5,32,2,16]{1,0,3,2:T(8,128)S(1)} collective-permute-done((f32[5,32,2,16]{1,0,3,2:T(8,128)S(1)}, f32[5,32,2,16]{1,0,3,2:T(8,128)S(1)}, u32[]{:S(2)}, u32[]{:S(2)}) %collective-permute-start.5) | collective-permute-done | bytes 20512 | tf_op jit(solution)/shard_map/ppermute | solution.py:17
  132.1 13.6 %all_gather.16 = f32[5,32,2,64]{1,0,3,2:T(8,128)S(1)} all-gather(f32[5,32,2,16]{1,0,3,2:T(8,128)S(1)} %collective-permute-done.5), channel_id=1, replica_groups=mesh['row'=4,'span'=2,'pitch'=4] {'pitch'}, dimensions={3}, use_global_device_ids=true | all-gather | bytes 102400 | tf_op jit(solution)/shard_map/all_gather | solution.py:149
  147.3 1.1 add_divide_fusion.3
  150.2 1.2 fusion.24
  151.4 3.3 collective-permute-start.13
  154.7 3.1 collective-permute-start.12
  157.8 1.3 collective-permute-start.11
  159.7 1.0 maximum_select_fusion.9
  162.8 1.2 copy.188
  164.9 3.1 collective-permute-done.13
  168.0 1.2 copy.186
  173.7 8.9 %reduce-scatter.7.cloned.1.call-done = f32[5,32,2,16]{1,3,2,0:T(8,128)} async-done(((f32[5,32,2,64]{1,3,2,0:T(8,128)}), f32[5,32,2,16]{1,3,2,0:T(8,128)}) %reduce-scatter.7.cloned.1.call-update) | async-done | bytes 20496 | tf_op jit(solution)/shard_map/reduce_scatter | solution.py:146
  184.5 4.2 %collective-permute-start.10 = (f32[5,32,2,16]{1,0,3,2:T(8,128)S(1)}, f32[5,32,2,16]{1,0,3,2:T(8,128)S(1)}, u32[]{:S(2)}, u32[]{:S(2)}) collective-permute-start(f32[5,32,2,16]{1,0,3,2:T(8,128)S(1)} %pad_maximum_fusion.6), channel_id=1, source_target_pairs={{8,0},{16,8},{24,16},{9,1},{17,9},{25,17},{10,2},{18,10},{26,18},{... | collective-permute-start | bytes 61448 | tf_op jit(solution)/shard_map/ppermute | solution.py:17
  188.7 3.7 %collective-permute-done.10 = f32[5,32,2,16]{1,0,3,2:T(8,128)S(1)} collective-permute-done((f32[5,32,2,16]{1,0,3,2:T(8,128)S(1)}, f32[5,32,2,16]{1,0,3,2:T(8,128)S(1)}, u32[]{:S(2)}, u32[]{:S(2)}) %collective-permute-start.10) | collective-permute-done | bytes 20512 | tf_op jit(solution)/shard_map/ppermute | solution.py:17
  192.6 13.0 %all_gather.17 = f32[5,32,2,64]{1,0,3,2:T(8,128)S(1)} all-gather(f32[5,32,2,16]{1,0,3,2:T(8,128)S(1)} %collective-permute-done.10), channel_id=1, replica_groups=mesh['row'=4,'span'=2,'pitch'=4] {'pitch'}, dimensions={3}, use_global_device_ids=true | all-gather | bytes 102400 | tf_op jit(solution)/shard_map/all_gather | solution.py:149
  207.0 1.1 add_divide_fusion.2
  209.9 1.2 fusion.22
  211.1 3.3 collective-permute-start.18
  214.4 3.8 %collective-permute-start.17 = (f32[5,4,1,128]{3,2,0,1:T(1,128)S(1)}, f32[5,4,1,128]{3,2,0,1:T(1,128)}, u32[]{:S(2)}, u32[]{:S(2)}) collective-permute-start(f32[5,4,1,128]{3,2,0,1:T(1,128)S(1)} %get-tuple-element.105), channel_id=1, source_target_pairs={{0,4},{1,5},{2,6},{3,7},{8,12},{9,13},{10,14},{11,15},{16,20},{17,... | collective-permute-start | bytes 30728 | tf_op jit(solution)/shard_map/ppermute | solution.py:28
  218.2 1.3 collective-permute-start.16
  222.8 1.2 copy.202
  225.0 2.8 collective-permute-done.18
  227.7 1.2 copy.200
  233.5 9.5 %reduce-scatter.9.cloned.1.call-done = f32[5,32,2,16]{1,3,2,0:T(8,128)} async-done(((f32[5,32,2,64]{1,3,2,0:T(8,128)}), f32[5,32,2,16]{1,3,2,0:T(8,128)}) %reduce-scatter.9.cloned.1.call-update) | async-done | bytes 20496 | tf_op jit(solution)/shard_map/reduce_scatter | solution.py:146
  244.8 4.1 %collective-permute-start.15 = (f32[5,32,2,16]{1,0,3,2:T(8,128)S(1)}, f32[5,32,2,16]{1,0,3,2:T(8,128)S(1)}, u32[]{:S(2)}, u32[]{:S(2)}) collective-permute-start(f32[5,32,2,16]{1,0,3,2:T(8,128)S(1)} %pad_maximum_fusion.7), channel_id=1, source_target_pairs={{8,0},{16,8},{24,16},{9,1},{17,9},{25,17},{10,2},{18,10},{26,18},{... | collective-permute-start | bytes 61448 | tf_op jit(solution)/shard_map/ppermute | solution.py:17
  248.9 3.7 %collective-permute-done.15 = f32[5,32,2,16]{1,0,3,2:T(8,128)S(1)} collective-permute-done((f32[5,32,2,16]{1,0,3,2:T(8,128)S(1)}, f32[5,32,2,16]{1,0,3,2:T(8,128)S(1)}, u32[]{:S(2)}, u32[]{:S(2)}) %collective-permute-start.15) | collective-permute-done | bytes 20512 | tf_op jit(solution)/shard_map/ppermute | solution.py:17
  252.8 13.3 %all_gather.18 = f32[5,32,2,64]{1,0,3,2:T(8,128)S(1)} all-gather(f32[5,32,2,16]{1,0,3,2:T(8,128)S(1)} %collective-permute-done.15), channel_id=1, replica_groups=mesh['row'=4,'span'=2,'pitch'=4] {'pitch'}, dimensions={3}, use_global_device_ids=true | all-gather | bytes 102400 | tf_op jit(solution)/shard_map/all_gather | solution.py:149
  267.5 1.1 add_divide_fusion.1
  270.3 1.2 fusion.20
  271.6 3.3 collective-permute-start.23
  274.8 3.2 collective-permute-start.22
  278.0 1.3 collective-permute-start.21
  283.0 1.2 copy.216
  285.1 3.1 collective-permute-done.23
  288.2 1.2 copy.214
  292.6 9.7 %reduce-scatter.11.cloned.1.call-done = f32[5,32,2,16]{1,3,2,0:T(8,128)} async-done(((f32[5,32,2,64]{1,3,2,0:T(8,128)}), f32[5,32,2,16]{1,3,2,0:T(8,128)}) %reduce-scatter.11.cloned.1.call-update) | async-done | bytes 20496 | tf_op jit(solution)/shard_map/reduce_scatter | solution.py:146
  304.1 4.1 %collective-permute-start.20 = (f32[5,32,2,16]{1,0,3,2:T(8,128)S(1)}, f32[5,32,2,16]{1,0,3,2:T(8,128)S(1)}, u32[]{:S(2)}, u32[]{:S(2)}) collective-permute-start(f32[5,32,2,16]{1,0,3,2:T(8,128)S(1)} %pad_maximum_fusion.8), channel_id=1, source_target_pairs={{8,0},{16,8},{24,16},{9,1},{17,9},{25,17},{10,2},{18,10},{26,18},{... | collective-permute-start | bytes 61448 | tf_op jit(solution)/shard_map/ppermute | solution.py:17
  308.3 3.7 %collective-permute-done.20 = f32[5,32,2,16]{1,0,3,2:T(8,128)S(1)} collective-permute-done((f32[5,32,2,16]{1,0,3,2:T(8,128)S(1)}, f32[5,32,2,16]{1,0,3,2:T(8,128)S(1)}, u32[]{:S(2)}, u32[]{:S(2)}) %collective-permute-start.20) | collective-permute-done | bytes 20512 | tf_op jit(solution)/shard_map/ppermute | solution.py:17
  312.2 13.1 %all_gather.19 = f32[5,32,2,64]{1,0,3,2:T(8,128)S(1)} all-gather(f32[5,32,2,16]{1,0,3,2:T(8,128)S(1)} %collective-permute-done.20), channel_id=1, replica_groups=mesh['row'=4,'span'=2,'pitch'=4] {'pitch'}, dimensions={3}, use_global_device_ids=true | all-gather | bytes 102400 | tf_op jit(solution)/shard_map/all_gather | solution.py:149
  326.7 1.1 add_divide_fusion
  (635 shorter events, 76.6 us)
Async XLA Ops:
  6.5 29.1 %copy-start = (s32[1,512]{1,0:T(1,128)S(1)}, s32[1,512]{1,0:T(1,128)}, u32[]{:S(2)}) copy-start(s32[1,512]{1,0:T(1,128)} %param.19) | copy-start | bytes 6148
  6.5 57.1 %all-reduce.3.cloned.1.call-start = ((), (), s32[]{:S(2)}) async-start(), calls=%async_computation.8 | async-start | bytes 655360
  8.5 31.1 %collective-permute-start.4 = (f32[5,4,32,1]{3,2,0,1:T(8,128)}, f32[5,4,32,1]{3,2,0,1:T(8,128)}, u32[]{:S(2)}, u32[]{:S(2)}) collective-permute-start(f32[5,4,32,1]{3,2,0,1:T(8,128)} %copy.236), channel_id=1, source_target_pairs={{0,1},{1,2},{2,3},{3,0},{4,5},{5,6},{6,7},{7,4},{8,9},{9,10},{10,1... | collective-permute-start | bytes 7688 | tf_op jit(solution)/shard_map/ppermute | solution.py:28
  11.4 30.3 %collective-permute-start.3 = (f32[5,4,32,1]{3,2,0,1:T(8,128)}, f32[5,4,32,1]{3,2,0,1:T(8,128)}, u32[]{:S(2)}, u32[]{:S(2)}) collective-permute-start(f32[5,4,32,1]{3,2,0,1:T(8,128)} %copy.234), channel_id=1, source_target_pairs={{1,0},{2,1},{3,2},{0,3},{5,4},{6,5},{7,6},{4,7},{9,8},{10,9},{11,1... | collective-permute-start | bytes 7688 | tf_op jit(solution)/shard_map/ppermute | solution.py:30
  14.1 29.6 %collective-permute-start.2 = (f32[5,4,1,128]{3,2,0,1:T(1,128)}, f32[5,4,1,128]{3,2,0,1:T(1,128)}, u32[]{:S(2)}, u32[]{:S(2)}) collective-permute-start(f32[5,4,1,128]{3,2,0,1:T(1,128)} %copy.232), channel_id=1, source_target_pairs={{0,4},{1,5},{2,6},{3,7},{8,12},{9,13},{10,14},{11,15},{16,20},{17,... | collective-permute-start | bytes 30728 | tf_op jit(solution)/shard_map/ppermute | solution.py:28
  18.4 26.0 %collective-permute-start.1 = (f32[5,4,1,128]{3,2,0,1:T(1,128)}, f32[5,4,1,128]{3,2,0,1:T(1,128)}, u32[]{:S(2)}, u32[]{:S(2)}) collective-permute-start(f32[5,4,1,128]{3,2,0,1:T(1,128)} %copy.230), channel_id=1, source_target_pairs={{4,0},{5,1},{6,2},{7,3},{12,8},{13,9},{14,10},{15,11},{20,16},{21,... | collective-permute-start | bytes 30728 | tf_op jit(solution)/shard_map/ppermute | solution.py:30
  26.8 95.4 %reduce-scatter.5.cloned.1.call-start = ((), (), s32[]{:S(2)}) async-start(), calls=%async_computation.4 | async-start | bytes 409600 | tf_op jit(solution)/shard_map/reduce_scatter | solution.py:146
  65.7 7.8 %collective-permute-start = (f32[5,32,2,16]{1,0,3,2:T(8,128)S(1)}, f32[5,32,2,16]{1,0,3,2:T(8,128)S(1)}, u32[]{:S(2)}, u32[]{:S(2)}) collective-permute-start(f32[5,32,2,16]{1,0,3,2:T(8,128)S(1)} %pad_maximum_fusion.4), channel_id=1, source_target_pairs={{8,0},{16,8},{24,16},{9,1},{17,9},{25,17},{10,2},{18,10},{26,18},{... | collective-permute-start | bytes 61448 | tf_op jit(solution)/shard_map/ppermute | solution.py:17
  73.5 14.2 %copy-start.15 = (f32[4,32,128]{2,1,0:T(8,128)S(1)}, f32[4,32,128]{2,1,0:T(8,128)}, u32[]{:S(2)}) copy-start(f32[4,32,128]{2,1,0:T(8,128)} %get-tuple-element.215) | copy-start | bytes 196612
  73.5 14.2 %copy-start.16 = (f32[4,32,128]{2,1,0:T(8,128)S(1)}, f32[4,32,128]{2,1,0:T(8,128)}, u32[]{:S(2)}) copy-start(f32[4,32,128]{2,1,0:T(8,128)} %get-tuple-element.216) | copy-start | bytes 196612
  73.5 14.2 %copy-start.17 = (f32[4,32,128]{2,1,0:T(8,128)S(1)}, f32[4,32,128]{2,1,0:T(8,128)}, u32[]{:S(2)}) copy-start(f32[4,32,128]{2,1,0:T(8,128)} %get-tuple-element.217) | copy-start | bytes 196612
  73.5 14.2 %copy-start.18 = (f32[4,32,128]{2,1,0:T(8,128)S(1)}, f32[4,32,128]{2,1,0:T(8,128)}, u32[]{:S(2)}) copy-start(f32[4,32,128]{2,1,0:T(8,128)} %get-tuple-element.218) | copy-start | bytes 196612
  90.8 11.4 %collective-permute-start.9 = (f32[5,4,32,1]{3,2,0,1:T(8,128)S(1)}, f32[5,4,32,1]{3,2,0,1:T(8,128)}, u32[]{:S(2)}, u32[]{:S(2)}) collective-permute-start(f32[5,4,32,1]{3,2,0,1:T(8,128)S(1)} %get-tuple-element.203), channel_id=1, source_target_pairs={{0,1},{1,2},{2,3},{3,0},{4,5},{5,6},{6,7},{7,4},{8,9},{9,10},{10,1... | collective-permute-start | bytes 7688 | tf_op jit(solution)/shard_map/ppermute | solution.py:28
  90.9 16.2 %collective-permute-start.8 = (f32[5,4,32,1]{3,2,0,1:T(8,128)S(1)}, f32[5,4,32,1]{3,2,0,1:T(8,128)}, u32[]{:S(2)}, u32[]{:S(2)}) collective-permute-start(f32[5,4,32,1]{3,2,0,1:T(8,128)S(1)} %get-tuple-element.202), channel_id=1, source_target_pairs={{1,0},{2,1},{3,2},{0,3},{5,4},{6,5},{7,6},{4,7},{9,8},{10,9},{11,1... | collective-permute-start | bytes 7688 | tf_op jit(solution)/shard_map/ppermute | solution.py:30
  94.1 15.1 %collective-permute-start.7 = (f32[5,4,1,128]{3,2,0,1:T(1,128)}, f32[5,4,1,128]{3,2,0,1:T(1,128)}, u32[]{:S(2)}, u32[]{:S(2)}) collective-permute-start(f32[5,4,1,128]{3,2,0,1:T(1,128)} %get-tuple-element.189), channel_id=1, source_target_pairs={{0,4},{1,5},{2,6},{3,7},{8,12},{9,13},{10,14},{11,15},{16,20},{17,... | collective-permute-start | bytes 30728 | tf_op jit(solution)/shard_map/ppermute | solution.py:28
  97.8 13.6 %collective-permute-start.6 = (f32[5,4,1,128]{3,2,0,1:T(1,128)}, f32[5,4,1,128]{3,2,0,1:T(1,128)}, u32[]{:S(2)}, u32[]{:S(2)}) collective-permute-start(f32[5,4,1,128]{3,2,0,1:T(1,128)} %get-tuple-element.188), channel_id=1, source_target_pairs={{4,0},{5,1},{6,2},{7,3},{12,8},{13,9},{14,10},{15,11},{20,16},{21,... | collective-permute-start | bytes 30728 | tf_op jit(solution)/shard_map/ppermute | solution.py:30
  101.9 80.8 %reduce-scatter.7.cloned.1.call-start = ((), (), s32[]{:S(2)}) async-start(), calls=%async_computation.5 | async-start | bytes 409600 | tf_op jit(solution)/shard_map/reduce_scatter | solution.py:146
  124.1 8.0 %collective-permute-start.5 = (f32[5,32,2,16]{1,0,3,2:T(8,128)S(1)}, f32[5,32,2,16]{1,0,3,2:T(8,128)S(1)}, u32[]{:S(2)}, u32[]{:S(2)}) collective-permute-start(f32[5,32,2,16]{1,0,3,2:T(8,128)S(1)} %pad_maximum_fusion.5), channel_id=1, source_target_pairs={{8,0},{16,8},{24,16},{9,1},{17,9},{25,17},{10,2},{18,10},{26,18},{... | collective-permute-start | bytes 61448 | tf_op jit(solution)/shard_map/ppermute | solution.py:17
  151.4 11.4 %collective-permute-start.14 = (f32[5,4,32,1]{3,2,0,1:T(8,128)S(1)}, f32[5,4,32,1]{3,2,0,1:T(8,128)}, u32[]{:S(2)}, u32[]{:S(2)}) collective-permute-start(f32[5,4,32,1]{3,2,0,1:T(8,128)S(1)} %get-tuple-element.161), channel_id=1, source_target_pairs={{0,1},{1,2},{2,3},{3,0},{4,5},{5,6},{6,7},{7,4},{8,9},{9,10},{10,1... | collective-permute-start | bytes 7688 | tf_op jit(solution)/shard_map/ppermute | solution.py:28
  151.4 16.6 %collective-permute-start.13 = (f32[5,4,32,1]{3,2,0,1:T(8,128)S(1)}, f32[5,4,32,1]{3,2,0,1:T(8,128)}, u32[]{:S(2)}, u32[]{:S(2)}) collective-permute-start(f32[5,4,32,1]{3,2,0,1:T(8,128)S(1)} %get-tuple-element.160), channel_id=1, source_target_pairs={{1,0},{2,1},{3,2},{0,3},{5,4},{6,5},{7,6},{4,7},{9,8},{10,9},{11,1... | collective-permute-start | bytes 7688 | tf_op jit(solution)/shard_map/ppermute | solution.py:30
  154.7 15.4 %collective-permute-start.12 = (f32[5,4,1,128]{3,2,0,1:T(1,128)S(1)}, f32[5,4,1,128]{3,2,0,1:T(1,128)}, u32[]{:S(2)}, u32[]{:S(2)}) collective-permute-start(f32[5,4,1,128]{3,2,0,1:T(1,128)S(1)} %get-tuple-element.147), channel_id=1, source_target_pairs={{0,4},{1,5},{2,6},{3,7},{8,12},{9,13},{10,14},{11,15},{16,20},{17,... | collective-permute-start | bytes 30728 | tf_op jit(solution)/shard_map/ppermute | solution.py:28
  157.8 13.8 %collective-permute-start.11 = (f32[5,4,1,128]{3,2,0,1:T(1,128)}, f32[5,4,1,128]{3,2,0,1:T(1,128)}, u32[]{:S(2)}, u32[]{:S(2)}) collective-permute-start(f32[5,4,1,128]{3,2,0,1:T(1,128)} %get-tuple-element.146), channel_id=1, source_target_pairs={{4,0},{5,1},{6,2},{7,3},{12,8},{13,9},{14,10},{15,11},{20,16},{21,... | collective-permute-start | bytes 30728 | tf_op jit(solution)/shard_map/ppermute | solution.py:30
  162.4 80.5 %reduce-scatter.9.cloned.1.call-start = ((), (), s32[]{:S(2)}) async-start(), calls=%async_computation.6 | async-start | bytes 409600 | tf_op jit(solution)/shard_map/reduce_scatter | solution.py:146
  184.5 7.9 %collective-permute-start.10 = (f32[5,32,2,16]{1,0,3,2:T(8,128)S(1)}, f32[5,32,2,16]{1,0,3,2:T(8,128)S(1)}, u32[]{:S(2)}, u32[]{:S(2)}) collective-permute-start(f32[5,32,2,16]{1,0,3,2:T(8,128)S(1)} %pad_maximum_fusion.6), channel_id=1, source_target_pairs={{8,0},{16,8},{24,16},{9,1},{17,9},{25,17},{10,2},{18,10},{26,18},{... | collective-permute-start | bytes 61448 | tf_op jit(solution)/shard_map/ppermute | solution.py:17
  211.1 11.7 %collective-permute-start.19 = (f32[5,4,32,1]{3,2,0,1:T(8,128)S(1)}, f32[5,4,32,1]{3,2,0,1:T(8,128)}, u32[]{:S(2)}, u32[]{:S(2)}) collective-permute-start(f32[5,4,32,1]{3,2,0,1:T(8,128)S(1)} %get-tuple-element.119), channel_id=1, source_target_pairs={{0,1},{1,2},{2,3},{3,0},{4,5},{5,6},{6,7},{7,4},{8,9},{9,10},{10,1... | collective-permute-start | bytes 7688 | tf_op jit(solution)/shard_map/ppermute | solution.py:28
  211.1 16.6 %collective-permute-start.18 = (f32[5,4,32,1]{3,2,0,1:T(8,128)S(1)}, f32[5,4,32,1]{3,2,0,1:T(8,128)}, u32[]{:S(2)}, u32[]{:S(2)}) collective-permute-start(f32[5,4,32,1]{3,2,0,1:T(8,128)S(1)} %get-tuple-element.118), channel_id=1, source_target_pairs={{1,0},{2,1},{3,2},{0,3},{5,4},{6,5},{7,6},{4,7},{9,8},{10,9},{11,1... | collective-permute-start | bytes 7688 | tf_op jit(solution)/shard_map/ppermute | solution.py:30
  214.4 15.4 %collective-permute-start.17 = (f32[5,4,1,128]{3,2,0,1:T(1,128)S(1)}, f32[5,4,1,128]{3,2,0,1:T(1,128)}, u32[]{:S(2)}, u32[]{:S(2)}) collective-permute-start(f32[5,4,1,128]{3,2,0,1:T(1,128)S(1)} %get-tuple-element.105), channel_id=1, source_target_pairs={{0,4},{1,5},{2,6},{3,7},{8,12},{9,13},{10,14},{11,15},{16,20},{17,... | collective-permute-start | bytes 30728 | tf_op jit(solution)/shard_map/ppermute | solution.py:28
  218.2 13.2 %collective-permute-start.16 = (f32[5,4,1,128]{3,2,0,1:T(1,128)}, f32[5,4,1,128]{3,2,0,1:T(1,128)}, u32[]{:S(2)}, u32[]{:S(2)}) collective-permute-start(f32[5,4,1,128]{3,2,0,1:T(1,128)} %get-tuple-element.104), channel_id=1, source_target_pairs={{4,0},{5,1},{6,2},{7,3},{12,8},{13,9},{14,10},{15,11},{20,16},{21,... | collective-permute-start | bytes 30728 | tf_op jit(solution)/shard_map/ppermute | solution.py:30
  222.8 79.5 %reduce-scatter.11.cloned.1.call-start = ((), (), s32[]{:S(2)}) async-start(), calls=%async_computation.7 | async-start | bytes 409600 | tf_op jit(solution)/shard_map/reduce_scatter | solution.py:146
  244.8 7.8 %collective-permute-start.15 = (f32[5,32,2,16]{1,0,3,2:T(8,128)S(1)}, f32[5,32,2,16]{1,0,3,2:T(8,128)S(1)}, u32[]{:S(2)}, u32[]{:S(2)}) collective-permute-start(f32[5,32,2,16]{1,0,3,2:T(8,128)S(1)} %pad_maximum_fusion.7), channel_id=1, source_target_pairs={{8,0},{16,8},{24,16},{9,1},{17,9},{25,17},{10,2},{18,10},{26,18},{... | collective-permute-start | bytes 61448 | tf_op jit(solution)/shard_map/ppermute | solution.py:17
  252.6 14.2 %copy-start.64 = (f32[5]{0:T(128)S(1)}, f32[5]{0:T(128)}, u32[]{:S(2)}) copy-start(f32[5]{0:T(128)} %get-tuple-element.11) | copy-start | bytes 64
  252.6 14.2 %copy-start.69 = (f32[5]{0:T(128)S(1)}, f32[5]{0:T(128)}, u32[]{:S(2)}) copy-start(f32[5]{0:T(128)} %get-tuple-element.12) | copy-start | bytes 64
  252.6 14.2 %copy-start.74 = (f32[5]{0:T(128)S(1)}, f32[5]{0:T(128)}, u32[]{:S(2)}) copy-start(f32[5]{0:T(128)} %get-tuple-element.13) | copy-start | bytes 64
  252.6 14.2 %copy-start.79 = (f32[5]{0:T(128)S(1)}, f32[5]{0:T(128)}, u32[]{:S(2)}) copy-start(f32[5]{0:T(128)} %get-tuple-element.14) | copy-start | bytes 64
  252.6 14.2 %copy-start.84 = (f32[5]{0:T(128)S(1)}, f32[5]{0:T(128)}, u32[]{:S(2)}) copy-start(f32[5]{0:T(128)} %get-tuple-element.15) | copy-start | bytes 64
  252.6 14.2 %copy-start.89 = (f32[5]{0:T(128)S(1)}, f32[5]{0:T(128)}, u32[]{:S(2)}) copy-start(f32[5]{0:T(128)} %get-tuple-element.16) | copy-start | bytes 64
  252.6 14.2 %copy-start.94 = (f32[5]{0:T(128)S(1)}, f32[5]{0:T(128)}, u32[]{:S(2)}) copy-start(f32[5]{0:T(128)} %get-tuple-element.17) | copy-start | bytes 64
  252.7 14.2 %copy-start.99 = (f32[5]{0:T(128)S(1)}, f32[5]{0:T(128)}, u32[]{:S(2)}) copy-start(f32[5]{0:T(128)} %get-tuple-element.18) | copy-start | bytes 64
  252.7 14.2 %copy-start.104 = (f32[5]{0:T(128)S(1)}, f32[5]{0:T(128)}, u32[]{:S(2)}) copy-start(f32[5]{0:T(128)} %get-tuple-element.19) | copy-start | bytes 64
  252.7 14.2 %copy-start.109 = (f32[5]{0:T(128)S(1)}, f32[5]{0:T(128)}, u32[]{:S(2)}) copy-start(f32[5]{0:T(128)} %get-tuple-element.20) | copy-start | bytes 64
  252.7 14.2 %copy-start.114 = (f32[5]{0:T(128)S(1)}, f32[5]{0:T(128)}, u32[]{:S(2)}) copy-start(f32[5]{0:T(128)} %get-tuple-element.21) | copy-start | bytes 64
  252.7 14.2 %copy-start.119 = (f32[5]{0:T(128)S(1)}, f32[5]{0:T(128)}, u32[]{:S(2)}) copy-start(f32[5]{0:T(128)} %get-tuple-element.22) | copy-start | bytes 64
  252.7 14.2 %copy-start.124 = (f32[5]{0:T(128)S(1)}, f32[5]{0:T(128)}, u32[]{:S(2)}) copy-start(f32[5]{0:T(128)} %get-tuple-element.23) | copy-start | bytes 64
  252.7 14.2 %copy-start.129 = (f32[5]{0:T(128)S(1)}, f32[5]{0:T(128)}, u32[]{:S(2)}) copy-start(f32[5]{0:T(128)} %get-tuple-element.24) | copy-start | bytes 64
  252.7 14.2 %copy-start.134 = (f32[5]{0:T(128)S(1)}, f32[5]{0:T(128)}, u32[]{:S(2)}) copy-start(f32[5]{0:T(128)} %get-tuple-element.25) | copy-start | bytes 64
  252.7 14.2 %copy-start.139 = (f32[5]{0:T(128)S(1)}, f32[5]{0:T(128)}, u32[]{:S(2)}) copy-start(f32[5]{0:T(128)} %get-tuple-element.26) | copy-start | bytes 64
  252.7 14.2 %copy-start.144 = (f32[5]{0:T(128)S(1)}, f32[5]{0:T(128)}, u32[]{:S(2)}) copy-start(f32[5]{0:T(128)} %get-tuple-element.27) | copy-start | bytes 64
  252.8 14.2 %copy-start.149 = (f32[5]{0:T(128)S(1)}, f32[5]{0:T(128)}, u32[]{:S(2)}) copy-start(f32[5]{0:T(128)} %get-tuple-element.28) | copy-start | bytes 64
  252.8 14.2 %copy-start.154 = (f32[5]{0:T(128)S(1)}, f32[5]{0:T(128)}, u32[]{:S(2)}) copy-start(f32[5]{0:T(128)} %get-tuple-element.29) | copy-start | bytes 64
  252.8 14.2 %copy-start.159 = (f32[5]{0:T(128)S(1)}, f32[5]{0:T(128)}, u32[]{:S(2)}) copy-start(f32[5]{0:T(128)} %get-tuple-element.30) | copy-start | bytes 64
  252.8 14.2 %copy-start.164 = (f32[5]{0:T(128)S(1)}, f32[5]{0:T(128)}, u32[]{:S(2)}) copy-start(f32[5]{0:T(128)} %get-tuple-element.31) | copy-start | bytes 64
  252.8 14.2 %copy-start.169 = (f32[5]{0:T(128)S(1)}, f32[5]{0:T(128)}, u32[]{:S(2)}) copy-start(f32[5]{0:T(128)} %get-tuple-element.32) | copy-start | bytes 64
  252.8 14.2 %copy-start.174 = (f32[5]{0:T(128)S(1)}, f32[5]{0:T(128)}, u32[]{:S(2)}) copy-start(f32[5]{0:T(128)} %get-tuple-element.33) | copy-start | bytes 64
  252.8 14.2 %copy-start.179 = (f32[5]{0:T(128)S(1)}, f32[5]{0:T(128)}, u32[]{:S(2)}) copy-start(f32[5]{0:T(128)} %get-tuple-element.34) | copy-start | bytes 64
  271.6 11.4 %collective-permute-start.24 = (f32[5,4,32,1]{3,2,0,1:T(8,128)S(1)}, f32[5,4,32,1]{3,2,0,1:T(8,128)}, u32[]{:S(2)}, u32[]{:S(2)}) collective-permute-start(f32[5,4,32,1]{3,2,0,1:T(8,128)S(1)} %get-tuple-element.77), channel_id=1, source_target_pairs={{0,1},{1,2},{2,3},{3,0},{4,5},{5,6},{6,7},{7,4},{8,9},{9,10},{10,1... | collective-permute-start | bytes 7688 | tf_op jit(solution)/shard_map/ppermute | solution.py:28
  271.6 16.6 %collective-permute-start.23 = (f32[5,4,32,1]{3,2,0,1:T(8,128)S(1)}, f32[5,4,32,1]{3,2,0,1:T(8,128)}, u32[]{:S(2)}, u32[]{:S(2)}) collective-permute-start(f32[5,4,32,1]{3,2,0,1:T(8,128)S(1)} %get-tuple-element.76), channel_id=1, source_target_pairs={{1,0},{2,1},{3,2},{0,3},{5,4},{6,5},{7,6},{4,7},{9,8},{10,9},{11,1... | collective-permute-start | bytes 7688 | tf_op jit(solution)/shard_map/ppermute | solution.py:30
  274.8 15.4 %collective-permute-start.22 = (f32[5,4,1,128]{3,2,0,1:T(1,128)S(1)}, f32[5,4,1,128]{3,2,0,1:T(1,128)S(1)}, u32[]{:S(2)}, u32[]{:S(2)}) collective-permute-start(f32[5,4,1,128]{3,2,0,1:T(1,128)S(1)} %get-tuple-element.63), channel_id=1, source_target_pairs={{0,4},{1,5},{2,6},{3,7},{8,12},{9,13},{10,14},{11,15},{16,20},{17,... | collective-permute-start | bytes 30728 | tf_op jit(solution)/shard_map/ppermute | solution.py:28
  278.0 13.1 %collective-permute-start.21 = (f32[5,4,1,128]{3,2,0,1:T(1,128)}, f32[5,4,1,128]{3,2,0,1:T(1,128)S(1)}, u32[]{:S(2)}, u32[]{:S(2)}) collective-permute-start(f32[5,4,1,128]{3,2,0,1:T(1,128)} %get-tuple-element.62), channel_id=1, source_target_pairs={{4,0},{5,1},{6,2},{7,3},{12,8},{13,9},{14,10},{15,11},{20,16},{21,... | collective-permute-start | bytes 30728 | tf_op jit(solution)/shard_map/ppermute | solution.py:30
  304.1 7.9 %collective-permute-start.20 = (f32[5,32,2,16]{1,0,3,2:T(8,128)S(1)}, f32[5,32,2,16]{1,0,3,2:T(8,128)S(1)}, u32[]{:S(2)}, u32[]{:S(2)}) collective-permute-start(f32[5,32,2,16]{1,0,3,2:T(8,128)S(1)} %pad_maximum_fusion.8), channel_id=1, source_target_pairs={{8,0},{16,8},{24,16},{9,1},{17,9},{25,17},{10,2},{18,10},{26,18},{... | collective-permute-start | bytes 61448 | tf_op jit(solution)/shard_map/ppermute | solution.py:17
  312.0 14.0 %copy-start.85 = (f32[5]{0:T(128)S(1)}, f32[5]{0:T(128)}, u32[]{:S(2)}) copy-start(f32[5]{0:T(128)} %get-tuple-element.15) | copy-start | bytes 64
  312.0 14.0 %copy-start.90 = (f32[5]{0:T(128)S(1)}, f32[5]{0:T(128)}, u32[]{:S(2)}) copy-start(f32[5]{0:T(128)} %get-tuple-element.16) | copy-start | bytes 64
  312.0 14.0 %copy-start.95 = (f32[5]{0:T(128)S(1)}, f32[5]{0:T(128)}, u32[]{:S(2)}) copy-start(f32[5]{0:T(128)} %get-tuple-element.17) | copy-start | bytes 64
  312.0 14.0 %copy-start.100 = (f32[5]{0:T(128)S(1)}, f32[5]{0:T(128)}, u32[]{:S(2)}) copy-start(f32[5]{0:T(128)} %get-tuple-element.18) | copy-start | bytes 64
  312.0 14.0 %copy-start.105 = (f32[5]{0:T(128)S(1)}, f32[5]{0:T(128)}, u32[]{:S(2)}) copy-start(f32[5]{0:T(128)} %get-tuple-element.19) | copy-start | bytes 64
  (177 other events, 758.0 us)
Sparse Core Ops, SparseCore 0:
  26.9 36.6 all-reduce.2
  102.0 20.1 reduce-scatter.4
  162.5 20.0 reduce-scatter.6
  222.9 19.9 reduce-scatter.8
  282.8 19.4 reduce-scatter.10
where the time goes:
time: 338 us; the launch traced here: 335 us
  waiting for transfers between devices  84.5 us (25%)
  local copies, waits for them, and re-layouts  69.7 us (21%)
  blocking collectives  66.2 us (20%)
  starting transfers between devices  62 us (18%)
  other arithmetic  21.9 us (6%)
  between operations  17.2 us (5%)
  matrix products  13.5 us (4%)
    all_gather x5, blocking collectives, on_device(): all_modes = lax.all_gather(arrived, 'pitch', axis=3, tiled=True)  66.2 us
    reduce_scatter x4, waiting for transfers between devices, on_device(): lax.psum_scatter(partial_sum, 'pitch', scatter_dimension=3, tiled=True)  36.8 us
    unnamed x428, local copies, waits for them, and re-layouts  25.6 us
    ppermute x10, starting transfers between devices, padded(): lax.ppermute(head, axis, [((i + 1) % count, i) for i in range(ends)])  21.4 us
    ppermute x5, starting transfers between devices, shifted(): return lax.ppermute(x, axis, pairs)  20.7 us
    ppermute x10, starting transfers between devices, padded(): lax.ppermute(tail, axis, [(i, (i + 1) % count) for i in range(ends)])  19.7 us
    ppermute x5, waiting for transfers between devices, shifted(): return lax.ppermute(x, axis, pairs)  18.5 us
    unnamed x6, waiting for transfers between devices  17.8 us
  transfers between devices with their start and end apart: 30, of which 17 were waited for; matrix products, arithmetic and copies ran while one was open for 16% of the time, Pallas kernels for 0%

commit v1 on v0

--- a/solution.py
+++ b/solution.py
@@ -143,10 +143,14 @@
             precision=PRECISE,
         )
         partial_sum = partial_sum.reshape(components, span_cells, 2, modes_count)
-        owned = lax.psum_scatter(partial_sum, "pitch", scatter_dimension=3, tiled=True)
+        pieces = partial_sum.reshape(components, span_cells, 2, pitch_count, share_count)
+        pieces = jnp.moveaxis(pieces, 3, 0)
+        owned = jnp.sum(lax.all_to_all(pieces, "pitch", 0, 0, tiled=True), 0)
         treated = giles(owned[:, :, 0], owned[:, :, 1], giles_re_part, giles_im_part)
         arrived = send_upstream(treated)
-        all_modes = lax.all_gather(arrived, "pitch", axis=3, tiled=True)
+        copies = jnp.broadcast_to(arrived[None], (pitch_count, *arrived.shape))
+        shares = lax.all_to_all(copies, "pitch", 0, 0, tiled=True)
+        all_modes = jnp.moveaxis(shares, 0, 3)
         boundary_field = jnp.dot(
             all_modes.reshape(components * span_cells, 2 * modes_count),
             local_synth,

time: 338 us -> 259 us (0.77)
  blocking collectives: 66.2 us -> 0 us
  waiting for transfers between devices: 84.5 us -> 45.4 us
  starting transfers between devices: 62 us -> 98.9 us
  between operations: 17.2 us -> 4.82 us
  other arithmetic: 21.9 us -> 26.5 us
    all_gather x5 -> x0, blocking collectives: 66.2 us -> none  [on_device(): all_modes = lax.all_gather(arrived, 'pitch', axis=3, tiled=True)]
    all_to_all x0 -> x10, starting transfers between devices: none -> 40.9 us  [the longest x5 23.6 us: on_device(): shares = lax.all_to_all(copies, 'pitch', 0, 0, tiled=True)]
    reduce_scatter x4 -> x0, waiting for transfers between devices: 36.8 us -> none  [on_device(): lax.psum_scatter(partial_sum, 'pitch', scatter_dimension=3, tiled=True)]
    all_to_all x0 -> x10, waiting for transfers between devices: none -> 23.1 us  [the longest x5 23.1 us: on_device(): shares = lax.all_to_all(copies, 'pitch', 0, 0, tiled=True)]
    unnamed x6 -> x0, waiting for transfers between devices: 17.8 us -> none
    ppermute x10, waiting for transfers between devices: 10.4 us -> 0.03 us  [padded(): lax.ppermute(head, axis, [((i + 1) % count, i) for i in range(ends)])]
    ppermute x5, starting transfers between devices: 20.7 us -> 11 us  [shifted(): return lax.ppermute(x, axis, pairs)]
    all_to_all x0 -> x10, other arithmetic: none -> 8.72 us  [the longest x5 4.81 us: on_device(): owned = jnp.sum(lax.all_to_all(pieces, 'pitch', 0, 0, tiled=True), 0)]
  transfers between devices with their start and end apart: 30 -> 35, of which waited for: 17 -> 10; matrix products, arithmetic and copies ran while one was open for 16% -> 20% of each run, Pallas kernels for 0% -> 0%
where the time goes in v1:
time: 259 us; the launch traced here: 256 us
  starting transfers between devices  98.9 us (38%)
  local copies, waits for them, and re-layouts  69.5 us (27%)
  waiting for transfers between devices  45.4 us (18%)
  other arithmetic  26.5 us (10%)
  matrix products  10.7 us (4%)
  between operations  4.82 us (2%)
    unnamed x530, local copies, waits for them, and re-layouts  31.6 us
    ppermute x10, starting transfers between devices, padded(): lax.ppermute(tail, axis, [(i, (i + 1) % count) for i in range(ends)])  28.3 us
    all_to_all x5, starting transfers between devices, on_device(): shares = lax.all_to_all(copies, 'pitch', 0, 0, tiled=True)  23.6 us
    all_to_all x5, waiting for transfers between devices, on_device(): shares = lax.all_to_all(copies, 'pitch', 0, 0, tiled=True)  23.1 us
    ppermute x5, waiting for transfers between devices, shifted(): return lax.ppermute(x, axis, pairs)  22.3 us
    ppermute x10, starting transfers between devices, padded(): lax.ppermute(head, axis, [((i + 1) % count, i) for i in range(ends)])  18.6 us
    all_to_all x5, starting transfers between devices, on_device(): owned = jnp.sum(lax.all_to_all(pieces, 'pitch', 0, 0, tiled=True), 0)  17.3 us
    mul x30, local copies, waits for them, and re-layouts, update(): jacobian_row[direction, 0][:, None, None, None]  12.2 us
  transfers between devices with their start and end apart: 35, of which 10 were waited for; matrix products, arithmetic and copies ran while one was open for 20% of the time, Pallas kernels for 0%

profile of v1, /device:TPU:1, one launch (start us, length us, event | category | flops | bytes accessed | tf_op | source)
XLA Modules:
  0.0 255.9 jit_solution(11236092712355159827)
XLA Ops:
  0.0 1.2 fusion.98
  2.0 2.1 collective-permute-start.4
  4.9 2.0 collective-permute-start.3
  7.6 3.7 %collective-permute-start.2 = (f32[5,4,1,128]{3,2,0,1:T(1,128)}, f32[5,4,1,128]{3,2,0,1:T(1,128)}, u32[]{:S(2)}, u32[]{:S(2)}) collective-permute-start(f32[5,4,1,128]{3,2,0,1:T(1,128)} %copy.317), channel_id=1, source_target_pairs={{0,4},{1,5},{2,6},{3,7},{8,12},{9,13},{10,14},{11,15},{16,20},{17,... | collective-permute-start | bytes 30728 | tf_op jit(solution)/shard_map/ppermute | solution.py:28
  11.9 1.3 collective-permute-start.1
  15.8 3.1 %add_bitcast_fusion = (s32[64]{0:T(128)}, s32[64]{0:T(128)S(1)}) fusion(s32[64,2]{0,1:T(2,128)S(1)} %get-tuple-element.262, s32[]{:T(128)} %bitcast.20, s32[]{:T(128)} %bitcast.19, s32[]{:T(128)} %bitcast.2, s32[64,2]{0,1:T(2,128)S(1)} %get-tuple-element.263, s32[]{:T(128)} %bitcast.1), kind=kLoop, calls=%fused_computation.351 | loop fusion | flops 384 | bytes 1552 | tf_op jit(solution)/shard_map/add | solution.py:117
  20.5 3.9 %all-to-all-start = ((f32[4,1,5120]{2,1,0:T(1,128)}), f32[4,1,5120]{2,1,0:T(1,128)}, u32[]{:S(2)}, u32[]{:S(2)}) async-start(f32[4,1,5120]{2,1,0:T(1,128)} %reshape.205), calls=%async_computation | async-start | bytes 163840 | tf_op jit(solution)/shard_map/all_to_all | solution.py:148
  26.4 1.0 slice_reduce_fusion.29
  27.5 0.9 slice_reduce_fusion.28
  30.7 0.9 copy-done.5
  33.2 0.9 pad_maximum_fusion.2
  35.1 0.9 constant_dynamic-slice_fusion.2
  37.0 1.2 copy.227
  39.0 1.2 copy.223
  43.9 1.7 reduce.60
  46.8 3.4 %collective-permute-start = (f32[5,32,2,16]{1,0,3,2:T(8,128)S(1)}, f32[5,32,2,16]{1,0,3,2:T(8,128)S(1)}, u32[]{:S(2)}, u32[]{:S(2)}) collective-permute-start(f32[5,32,2,16]{1,0,3,2:T(8,128)S(1)} %pad_maximum_fusion.4), channel_id=1, source_target_pairs={{8,0},{16,8},{24,16},{9,1},{17,9},{25,17},{10,2},{18,10},{26,18},{... | collective-permute-start | bytes 61448 | tf_op jit(solution)/shard_map/ppermute | solution.py:17
  50.2 3.7 %collective-permute-done = f32[5,32,2,16]{1,0,3,2:T(8,128)S(1)} collective-permute-done((f32[5,32,2,16]{1,0,3,2:T(8,128)S(1)}, f32[5,32,2,16]{1,0,3,2:T(8,128)S(1)}, u32[]{:S(2)}, u32[]{:S(2)}) %collective-permute-start) | collective-permute-done | bytes 20512 | tf_op jit(solution)/shard_map/ppermute | solution.py:17
  54.8 4.8 %all-to-all-start.1 = ((f32[4,1,5120]{2,1,0:T(1,128)}), f32[4,1,5120]{2,1,0:T(1,128)S(1)}, u32[]{:S(2)}, u32[]{:S(2)}) async-start(f32[4,1,5120]{2,1,0:T(1,128)} %reshape.207), calls=%async_computation.1 | async-start | bytes 163840 | tf_op jit(solution)/shard_map/all_to_all | solution.py:152
  59.6 4.6 %all-to-all-done.1 = f32[4,1,5120]{2,1,0:T(1,128)S(1)} async-done(((f32[4,1,5120]{2,1,0:T(1,128)}), f32[4,1,5120]{2,1,0:T(1,128)S(1)}, u32[]{:S(2)}, u32[]{:S(2)}) %all-to-all-start.1) | async-done | bytes 81952 | tf_op jit(solution)/shard_map/all_to_all | solution.py:152
  67.1 1.9 add_divide_fusion.4
  70.3 2.5 collective-permute-start.8
  72.8 5.4 %collective-permute-start.7 = (f32[5,4,1,128]{3,2,0,1:T(1,128)S(1)}, f32[5,4,1,128]{3,2,0,1:T(1,128)}, u32[]{:S(2)}, u32[]{:S(2)}) collective-permute-start(f32[5,4,1,128]{3,2,0,1:T(1,128)S(1)} %get-tuple-element.189), channel_id=1, source_target_pairs={{0,4},{1,5},{2,6},{3,7},{8,12},{9,13},{10,14},{11,15},{16,20},{17,... | collective-permute-start | bytes 30728 | tf_op jit(solution)/shard_map/ppermute | solution.py:28
  78.2 1.3 collective-permute-start.6
  83.2 3.3 %all-to-all-start.2 = ((f32[4,1,5120]{2,1,0:T(1,128)}), f32[4,1,5120]{2,1,0:T(1,128)S(1)}, u32[]{:S(2)}, u32[]{:S(2)}) async-start(f32[4,1,5120]{2,1,0:T(1,128)} %reshape.209), calls=%async_computation.2 | async-start | bytes 163840 | tf_op jit(solution)/shard_map/all_to_all | solution.py:148
  86.5 1.2 copy.244
  88.7 1.2 copy.242
  95.6 1.9 collective-permute-start.5
  97.7 4.6 %collective-permute-done.5 = f32[5,32,2,16]{1,0,3,2:T(8,128)S(1)} collective-permute-done((f32[5,32,2,16]{1,0,3,2:T(8,128)S(1)}, f32[5,32,2,16]{1,0,3,2:T(8,128)S(1)}, u32[]{:S(2)}, u32[]{:S(2)}) %collective-permute-start.5) | collective-permute-done | bytes 20512 | tf_op jit(solution)/shard_map/ppermute | solution.py:17
  103.2 4.8 %all-to-all-start.3 = ((f32[4,1,5120]{2,1,0:T(1,128)}), f32[4,1,5120]{2,1,0:T(1,128)S(1)}, u32[]{:S(2)}, u32[]{:S(2)}) async-start(f32[4,1,5120]{2,1,0:T(1,128)} %reshape.211), calls=%async_computation.3 | async-start | bytes 163840 | tf_op jit(solution)/shard_map/all_to_all | solution.py:152
  108.0 4.6 %all-to-all-done.3 = f32[4,1,5120]{2,1,0:T(1,128)S(1)} async-done(((f32[4,1,5120]{2,1,0:T(1,128)}), f32[4,1,5120]{2,1,0:T(1,128)S(1)}, u32[]{:S(2)}, u32[]{:S(2)}) %all-to-all-start.3) | async-done | bytes 81952 | tf_op jit(solution)/shard_map/all_to_all | solution.py:152
  115.3 1.1 add_divide_fusion.3
  118.2 2.5 collective-permute-start.13
  120.8 4.8 %collective-permute-start.12 = (f32[5,4,1,128]{3,2,0,1:T(1,128)S(1)}, f32[5,4,1,128]{3,2,0,1:T(1,128)}, u32[]{:S(2)}, u32[]{:S(2)}) collective-permute-start(f32[5,4,1,128]{3,2,0,1:T(1,128)S(1)} %get-tuple-element.147), channel_id=1, source_target_pairs={{0,4},{1,5},{2,6},{3,7},{8,12},{9,13},{10,14},{11,15},{16,20},{17,... | collective-permute-start | bytes 30728 | tf_op jit(solution)/shard_map/ppermute | solution.py:28
  125.6 1.3 collective-permute-start.11
  130.1 3.3 %all-to-all-start.4 = ((f32[4,1,5120]{2,1,0:T(1,128)}), f32[4,1,5120]{2,1,0:T(1,128)S(1)}, u32[]{:S(2)}, u32[]{:S(2)}) async-start(f32[4,1,5120]{2,1,0:T(1,128)} %reshape.213), calls=%async_computation.4 | async-start | bytes 163840 | tf_op jit(solution)/shard_map/all_to_all | solution.py:148
  133.4 1.2 copy.260
  135.5 1.2 copy.258
  142.5 1.9 collective-permute-start.10
  144.5 4.6 %collective-permute-done.10 = f32[5,32,2,16]{1,0,3,2:T(8,128)S(1)} collective-permute-done((f32[5,32,2,16]{1,0,3,2:T(8,128)S(1)}, f32[5,32,2,16]{1,0,3,2:T(8,128)S(1)}, u32[]{:S(2)}, u32[]{:S(2)}) %collective-permute-start.10) | collective-permute-done | bytes 20512 | tf_op jit(solution)/shard_map/ppermute | solution.py:17
  150.0 4.8 %all-to-all-start.5 = ((f32[4,1,5120]{2,1,0:T(1,128)}), f32[4,1,5120]{2,1,0:T(1,128)S(1)}, u32[]{:S(2)}, u32[]{:S(2)}) async-start(f32[4,1,5120]{2,1,0:T(1,128)} %reshape.215), calls=%async_computation.5 | async-start | bytes 163840 | tf_op jit(solution)/shard_map/all_to_all | solution.py:152
  154.8 4.6 %all-to-all-done.5 = f32[4,1,5120]{2,1,0:T(1,128)S(1)} async-done(((f32[4,1,5120]{2,1,0:T(1,128)}), f32[4,1,5120]{2,1,0:T(1,128)S(1)}, u32[]{:S(2)}, u32[]{:S(2)}) %all-to-all-start.5) | async-done | bytes 81952 | tf_op jit(solution)/shard_map/all_to_all | solution.py:152
  162.2 1.1 add_divide_fusion.2
  165.1 2.5 collective-permute-start.18
  167.6 4.8 %collective-permute-start.17 = (f32[5,4,1,128]{3,2,0,1:T(1,128)S(1)}, f32[5,4,1,128]{3,2,0,1:T(1,128)}, u32[]{:S(2)}, u32[]{:S(2)}) collective-permute-start(f32[5,4,1,128]{3,2,0,1:T(1,128)S(1)} %get-tuple-element.105), channel_id=1, source_target_pairs={{0,4},{1,5},{2,6},{3,7},{8,12},{9,13},{10,14},{11,15},{16,20},{17,... | collective-permute-start | bytes 30728 | tf_op jit(solution)/shard_map/ppermute | solution.py:28
  172.5 1.3 collective-permute-start.16
  176.9 3.5 %all-to-all-start.6 = ((f32[4,1,5120]{2,1,0:T(1,128)}), f32[4,1,5120]{2,1,0:T(1,128)S(1)}, u32[]{:S(2)}, u32[]{:S(2)}) async-start(f32[4,1,5120]{2,1,0:T(1,128)} %reshape.217), calls=%async_computation.6 | async-start | bytes 163840 | tf_op jit(solution)/shard_map/all_to_all | solution.py:148
  180.5 1.2 copy.276
  182.6 1.2 copy.274
  189.5 1.9 collective-permute-start.15
  191.6 4.6 %collective-permute-done.15 = f32[5,32,2,16]{1,0,3,2:T(8,128)S(1)} collective-permute-done((f32[5,32,2,16]{1,0,3,2:T(8,128)S(1)}, f32[5,32,2,16]{1,0,3,2:T(8,128)S(1)}, u32[]{:S(2)}, u32[]{:S(2)}) %collective-permute-start.15) | collective-permute-done | bytes 20512 | tf_op jit(solution)/shard_map/ppermute | solution.py:17
  197.1 4.6 %all-to-all-start.7 = ((f32[4,1,5120]{2,1,0:T(1,128)}), f32[4,1,5120]{2,1,0:T(1,128)S(1)}, u32[]{:S(2)}, u32[]{:S(2)}) async-start(f32[4,1,5120]{2,1,0:T(1,128)} %reshape.219), calls=%async_computation.7 | async-start | bytes 163840 | tf_op jit(solution)/shard_map/all_to_all | solution.py:152
  201.7 4.6 %all-to-all-done.7 = f32[4,1,5120]{2,1,0:T(1,128)S(1)} async-done(((f32[4,1,5120]{2,1,0:T(1,128)}), f32[4,1,5120]{2,1,0:T(1,128)S(1)}, u32[]{:S(2)}, u32[]{:S(2)}) %all-to-all-start.7) | async-done | bytes 81952 | tf_op jit(solution)/shard_map/all_to_all | solution.py:152
  209.1 1.1 add_divide_fusion.1
  212.0 2.5 collective-permute-start.23
  214.5 4.3 %collective-permute-start.22 = (f32[5,4,1,128]{3,2,0,1:T(1,128)S(1)}, f32[5,4,1,128]{3,2,0,1:T(1,128)S(1)}, u32[]{:S(2)}, u32[]{:S(2)}) collective-permute-start(f32[5,4,1,128]{3,2,0,1:T(1,128)S(1)} %get-tuple-element.63), channel_id=1, source_target_pairs={{0,4},{1,5},{2,6},{3,7},{8,12},{9,13},{10,14},{11,15},{16,20},{17,... | collective-permute-start | bytes 30728 | tf_op jit(solution)/shard_map/ppermute | solution.py:28
  218.8 1.3 collective-permute-start.21
  223.2 3.3 %all-to-all-start.8 = ((f32[4,1,5120]{2,1,0:T(1,128)}), f32[4,1,5120]{2,1,0:T(1,128)S(1)}, u32[]{:S(2)}, u32[]{:S(2)}) async-start(f32[4,1,5120]{2,1,0:T(1,128)} %reshape.221), calls=%async_computation.8 | async-start | bytes 163840 | tf_op jit(solution)/shard_map/all_to_all | solution.py:148
  226.6 1.2 copy.292
  228.7 1.2 copy.290
  234.3 1.9 collective-permute-start.20
  236.4 4.7 %collective-permute-done.20 = f32[5,32,2,16]{1,0,3,2:T(8,128)S(1)} collective-permute-done((f32[5,32,2,16]{1,0,3,2:T(8,128)S(1)}, f32[5,32,2,16]{1,0,3,2:T(8,128)S(1)}, u32[]{:S(2)}, u32[]{:S(2)}) %collective-permute-start.20) | collective-permute-done | bytes 20512 | tf_op jit(solution)/shard_map/ppermute | solution.py:17
  241.9 4.7 %all-to-all-start.9 = ((f32[4,1,5120]{2,1,0:T(1,128)}), f32[4,1,5120]{2,1,0:T(1,128)S(1)}, u32[]{:S(2)}, u32[]{:S(2)}) async-start(f32[4,1,5120]{2,1,0:T(1,128)} %reshape.223), calls=%async_computation.9 | async-start | bytes 163840 | tf_op jit(solution)/shard_map/all_to_all | solution.py:152
  246.7 4.6 %all-to-all-done.9 = f32[4,1,5120]{2,1,0:T(1,128)S(1)} async-done(((f32[4,1,5120]{2,1,0:T(1,128)}), f32[4,1,5120]{2,1,0:T(1,128)S(1)}, u32[]{:S(2)}, u32[]{:S(2)}) %all-to-all-start.9) | async-done | bytes 81952 | tf_op jit(solution)/shard_map/all_to_all | solution.py:152
  254.0 1.1 add_divide_fusion
  (773 shorter events, 81.5 us)
Async XLA Ops:
  0.0 34.3 %copy-start = (s32[1,512]{1,0:T(1,128)S(1)}, s32[1,512]{1,0:T(1,128)}, u32[]{:S(2)}) copy-start(s32[1,512]{1,0:T(1,128)} %param.19) | copy-start | bytes 6148
  2.0 35.0 %collective-permute-start.4 = (f32[5,4,32,1]{3,2,0,1:T(8,128)}, f32[5,4,32,1]{3,2,0,1:T(8,128)}, u32[]{:S(2)}, u32[]{:S(2)}) collective-permute-start(f32[5,4,32,1]{3,2,0,1:T(8,128)} %copy.321), channel_id=1, source_target_pairs={{0,1},{1,2},{2,3},{3,0},{4,5},{5,6},{6,7},{7,4},{8,9},{9,10},{10,1... | collective-permute-start | bytes 7688 | tf_op jit(solution)/shard_map/ppermute | solution.py:28
  4.1 2.8 %copy-start.1 = (f32[5,4,32,128]{3,2,1,0:T(8,128)S(1)}, f32[5,4,32,128]{3,2,1,0:T(8,128)}, u32[]{:S(2)}) copy-start(f32[5,4,32,128]{3,2,1,0:T(8,128)} %param.10) | copy-start | bytes 983044
  4.9 34.1 %collective-permute-start.3 = (f32[5,4,32,1]{3,2,0,1:T(8,128)}, f32[5,4,32,1]{3,2,0,1:T(8,128)}, u32[]{:S(2)}, u32[]{:S(2)}) collective-permute-start(f32[5,4,32,1]{3,2,0,1:T(8,128)} %copy.319), channel_id=1, source_target_pairs={{1,0},{2,1},{3,2},{0,3},{5,4},{6,5},{7,6},{4,7},{9,8},{10,9},{11,1... | collective-permute-start | bytes 7688 | tf_op jit(solution)/shard_map/ppermute | solution.py:30
  7.6 33.5 %collective-permute-start.2 = (f32[5,4,1,128]{3,2,0,1:T(1,128)}, f32[5,4,1,128]{3,2,0,1:T(1,128)}, u32[]{:S(2)}, u32[]{:S(2)}) collective-permute-start(f32[5,4,1,128]{3,2,0,1:T(1,128)} %copy.317), channel_id=1, source_target_pairs={{0,4},{1,5},{2,6},{3,7},{8,12},{9,13},{10,14},{11,15},{16,20},{17,... | collective-permute-start | bytes 30728 | tf_op jit(solution)/shard_map/ppermute | solution.py:28
  11.9 29.8 %collective-permute-start.1 = (f32[5,4,1,128]{3,2,0,1:T(1,128)}, f32[5,4,1,128]{3,2,0,1:T(1,128)}, u32[]{:S(2)}, u32[]{:S(2)}) collective-permute-start(f32[5,4,1,128]{3,2,0,1:T(1,128)} %copy.315), channel_id=1, source_target_pairs={{4,0},{5,1},{6,2},{7,3},{12,8},{13,9},{14,10},{15,11},{20,16},{21,... | collective-permute-start | bytes 30728 | tf_op jit(solution)/shard_map/ppermute | solution.py:30
  20.5 22.8 %all-to-all-start = ((f32[4,1,5120]{2,1,0:T(1,128)}), f32[4,1,5120]{2,1,0:T(1,128)}, u32[]{:S(2)}, u32[]{:S(2)}) async-start(f32[4,1,5120]{2,1,0:T(1,128)} %reshape.205), calls=%async_computation | async-start | bytes 163840 | tf_op jit(solution)/shard_map/all_to_all | solution.py:148
  36.1 7.1 %copy-start.236 = (pred[32]{0:T(512)(128)(4,1)}, pred[32]{0:T(512)(128)(4,1)S(1)}, u32[]{:S(2)}) copy-start(pred[32]{0:T(512)(128)(4,1)S(1)} %iota_compare_fusion.3) | copy-start | bytes 100
  36.3 1.9 copy-start.4
  46.8 7.1 %collective-permute-start = (f32[5,32,2,16]{1,0,3,2:T(8,128)S(1)}, f32[5,32,2,16]{1,0,3,2:T(8,128)S(1)}, u32[]{:S(2)}, u32[]{:S(2)}) collective-permute-start(f32[5,32,2,16]{1,0,3,2:T(8,128)S(1)} %pad_maximum_fusion.4), channel_id=1, source_target_pairs={{8,0},{16,8},{24,16},{9,1},{17,9},{25,17},{10,2},{18,10},{26,18},{... | collective-permute-start | bytes 61448 | tf_op jit(solution)/shard_map/ppermute | solution.py:17
  54.8 9.4 %all-to-all-start.1 = ((f32[4,1,5120]{2,1,0:T(1,128)}), f32[4,1,5120]{2,1,0:T(1,128)S(1)}, u32[]{:S(2)}, u32[]{:S(2)}) async-start(f32[4,1,5120]{2,1,0:T(1,128)} %reshape.207), calls=%async_computation.1 | async-start | bytes 163840 | tf_op jit(solution)/shard_map/all_to_all | solution.py:152
  69.4 3.4 %copy-start.74 = (f32[5,4,1,128]{3,2,0,1:T(1,128)}, f32[5,4,1,128]{3,2,0,1:T(1,128)S(1)}, u32[]{:S(2)}) copy-start(f32[5,4,1,128]{3,2,0,1:T(1,128)S(1)} %get-tuple-element.189) | copy-start | bytes 30724
  69.4 8.8 %copy-start.66 = (f32[5,4,1,128]{3,2,0,1:T(1,128)}, f32[5,4,1,128]{3,2,0,1:T(1,128)S(1)}, u32[]{:S(2)}) copy-start(f32[5,4,1,128]{3,2,0,1:T(1,128)S(1)} %get-tuple-element.188) | copy-start | bytes 30724
  69.5 17.0 %collective-permute-start.9 = (f32[5,4,32,1]{3,2,0,1:T(8,128)S(1)}, f32[5,4,32,1]{3,2,0,1:T(8,128)}, u32[]{:S(2)}, u32[]{:S(2)}) collective-permute-start(f32[5,4,32,1]{3,2,0,1:T(8,128)S(1)} %get-tuple-element.203), channel_id=1, source_target_pairs={{0,1},{1,2},{2,3},{3,0},{4,5},{5,6},{6,7},{7,4},{8,9},{9,10},{10,1... | collective-permute-start | bytes 7688 | tf_op jit(solution)/shard_map/ppermute | solution.py:28
  70.3 18.4 %collective-permute-start.8 = (f32[5,4,32,1]{3,2,0,1:T(8,128)S(1)}, f32[5,4,32,1]{3,2,0,1:T(8,128)}, u32[]{:S(2)}, u32[]{:S(2)}) collective-permute-start(f32[5,4,32,1]{3,2,0,1:T(8,128)S(1)} %get-tuple-element.202), channel_id=1, source_target_pairs={{1,0},{2,1},{3,2},{0,3},{5,4},{6,5},{7,6},{4,7},{9,8},{10,9},{11,1... | collective-permute-start | bytes 7688 | tf_op jit(solution)/shard_map/ppermute | solution.py:30
  72.8 18.6 %collective-permute-start.7 = (f32[5,4,1,128]{3,2,0,1:T(1,128)S(1)}, f32[5,4,1,128]{3,2,0,1:T(1,128)}, u32[]{:S(2)}, u32[]{:S(2)}) collective-permute-start(f32[5,4,1,128]{3,2,0,1:T(1,128)S(1)} %get-tuple-element.189), channel_id=1, source_target_pairs={{0,4},{1,5},{2,6},{3,7},{8,12},{9,13},{10,14},{11,15},{16,20},{17,... | collective-permute-start | bytes 30728 | tf_op jit(solution)/shard_map/ppermute | solution.py:28
  78.2 13.8 %collective-permute-start.6 = (f32[5,4,1,128]{3,2,0,1:T(1,128)S(1)}, f32[5,4,1,128]{3,2,0,1:T(1,128)S(1)}, u32[]{:S(2)}, u32[]{:S(2)}) collective-permute-start(f32[5,4,1,128]{3,2,0,1:T(1,128)S(1)} %get-tuple-element.188), channel_id=1, source_target_pairs={{4,0},{5,1},{6,2},{7,3},{12,8},{13,9},{14,10},{15,11},{20,16},{21,... | collective-permute-start | bytes 30728 | tf_op jit(solution)/shard_map/ppermute | solution.py:30
  83.2 10.3 %all-to-all-start.2 = ((f32[4,1,5120]{2,1,0:T(1,128)}), f32[4,1,5120]{2,1,0:T(1,128)S(1)}, u32[]{:S(2)}, u32[]{:S(2)}) async-start(f32[4,1,5120]{2,1,0:T(1,128)} %reshape.209), calls=%async_computation.2 | async-start | bytes 163840 | tf_op jit(solution)/shard_map/all_to_all | solution.py:148
  95.6 2.0 copy-start.67
  95.6 2.0 copy-start.237
  95.6 6.7 %collective-permute-start.5 = (f32[5,32,2,16]{1,0,3,2:T(8,128)S(1)}, f32[5,32,2,16]{1,0,3,2:T(8,128)S(1)}, u32[]{:S(2)}, u32[]{:S(2)}) collective-permute-start(f32[5,32,2,16]{1,0,3,2:T(8,128)S(1)} %pad_maximum_fusion.5), channel_id=1, source_target_pairs={{8,0},{16,8},{24,16},{9,1},{17,9},{25,17},{10,2},{18,10},{26,18},{... | collective-permute-start | bytes 61448 | tf_op jit(solution)/shard_map/ppermute | solution.py:17
  103.2 9.4 %all-to-all-start.3 = ((f32[4,1,5120]{2,1,0:T(1,128)}), f32[4,1,5120]{2,1,0:T(1,128)S(1)}, u32[]{:S(2)}, u32[]{:S(2)}) async-start(f32[4,1,5120]{2,1,0:T(1,128)} %reshape.211), calls=%async_computation.3 | async-start | bytes 163840 | tf_op jit(solution)/shard_map/all_to_all | solution.py:152
  116.8 3.9 %copy-start.76 = (f32[5,4,1,128]{3,2,0,1:T(1,128)}, f32[5,4,1,128]{3,2,0,1:T(1,128)S(1)}, u32[]{:S(2)}) copy-start(f32[5,4,1,128]{3,2,0,1:T(1,128)S(1)} %get-tuple-element.147) | copy-start | bytes 30724
  116.8 8.8 %copy-start.68 = (f32[5,4,1,128]{3,2,0,1:T(1,128)}, f32[5,4,1,128]{3,2,0,1:T(1,128)S(1)}, u32[]{:S(2)}) copy-start(f32[5,4,1,128]{3,2,0,1:T(1,128)S(1)} %get-tuple-element.146) | copy-start | bytes 30724
  117.4 15.9 %collective-permute-start.14 = (f32[5,4,32,1]{3,2,0,1:T(8,128)S(1)}, f32[5,4,32,1]{3,2,0,1:T(8,128)}, u32[]{:S(2)}, u32[]{:S(2)}) collective-permute-start(f32[5,4,32,1]{3,2,0,1:T(8,128)S(1)} %get-tuple-element.161), channel_id=1, source_target_pairs={{0,1},{1,2},{2,3},{3,0},{4,5},{5,6},{6,7},{7,4},{8,9},{9,10},{10,1... | collective-permute-start | bytes 7688 | tf_op jit(solution)/shard_map/ppermute | solution.py:28
  118.2 17.3 %collective-permute-start.13 = (f32[5,4,32,1]{3,2,0,1:T(8,128)S(1)}, f32[5,4,32,1]{3,2,0,1:T(8,128)}, u32[]{:S(2)}, u32[]{:S(2)}) collective-permute-start(f32[5,4,32,1]{3,2,0,1:T(8,128)S(1)} %get-tuple-element.160), channel_id=1, source_target_pairs={{1,0},{2,1},{3,2},{0,3},{5,4},{6,5},{7,6},{4,7},{9,8},{10,9},{11,1... | collective-permute-start | bytes 7688 | tf_op jit(solution)/shard_map/ppermute | solution.py:30
  120.8 17.5 %collective-permute-start.12 = (f32[5,4,1,128]{3,2,0,1:T(1,128)S(1)}, f32[5,4,1,128]{3,2,0,1:T(1,128)}, u32[]{:S(2)}, u32[]{:S(2)}) collective-permute-start(f32[5,4,1,128]{3,2,0,1:T(1,128)S(1)} %get-tuple-element.147), channel_id=1, source_target_pairs={{0,4},{1,5},{2,6},{3,7},{8,12},{9,13},{10,14},{11,15},{16,20},{17,... | collective-permute-start | bytes 30728 | tf_op jit(solution)/shard_map/ppermute | solution.py:28
  125.6 13.3 %collective-permute-start.11 = (f32[5,4,1,128]{3,2,0,1:T(1,128)S(1)}, f32[5,4,1,128]{3,2,0,1:T(1,128)S(1)}, u32[]{:S(2)}, u32[]{:S(2)}) collective-permute-start(f32[5,4,1,128]{3,2,0,1:T(1,128)S(1)} %get-tuple-element.146), channel_id=1, source_target_pairs={{4,0},{5,1},{6,2},{7,3},{12,8},{13,9},{14,10},{15,11},{20,16},{21,... | collective-permute-start | bytes 30728 | tf_op jit(solution)/shard_map/ppermute | solution.py:30
  130.1 10.3 %all-to-all-start.4 = ((f32[4,1,5120]{2,1,0:T(1,128)}), f32[4,1,5120]{2,1,0:T(1,128)S(1)}, u32[]{:S(2)}, u32[]{:S(2)}) async-start(f32[4,1,5120]{2,1,0:T(1,128)} %reshape.213), calls=%async_computation.4 | async-start | bytes 163840 | tf_op jit(solution)/shard_map/all_to_all | solution.py:148
  142.4 2.0 copy-start.69
  142.4 2.0 copy-start.238
  142.5 6.7 %collective-permute-start.10 = (f32[5,32,2,16]{1,0,3,2:T(8,128)S(1)}, f32[5,32,2,16]{1,0,3,2:T(8,128)S(1)}, u32[]{:S(2)}, u32[]{:S(2)}) collective-permute-start(f32[5,32,2,16]{1,0,3,2:T(8,128)S(1)} %pad_maximum_fusion.6), channel_id=1, source_target_pairs={{8,0},{16,8},{24,16},{9,1},{17,9},{25,17},{10,2},{18,10},{26,18},{... | collective-permute-start | bytes 61448 | tf_op jit(solution)/shard_map/ppermute | solution.py:17
  150.0 9.4 %all-to-all-start.5 = ((f32[4,1,5120]{2,1,0:T(1,128)}), f32[4,1,5120]{2,1,0:T(1,128)S(1)}, u32[]{:S(2)}, u32[]{:S(2)}) async-start(f32[4,1,5120]{2,1,0:T(1,128)} %reshape.215), calls=%async_computation.5 | async-start | bytes 163840 | tf_op jit(solution)/shard_map/all_to_all | solution.py:152
  163.7 3.9 %copy-start.78 = (f32[5,4,1,128]{3,2,0,1:T(1,128)}, f32[5,4,1,128]{3,2,0,1:T(1,128)S(1)}, u32[]{:S(2)}) copy-start(f32[5,4,1,128]{3,2,0,1:T(1,128)S(1)} %get-tuple-element.105) | copy-start | bytes 30724
  163.7 8.8 %copy-start.70 = (f32[5,4,1,128]{3,2,0,1:T(1,128)}, f32[5,4,1,128]{3,2,0,1:T(1,128)S(1)}, u32[]{:S(2)}) copy-start(f32[5,4,1,128]{3,2,0,1:T(1,128)S(1)} %get-tuple-element.104) | copy-start | bytes 30724
  164.3 16.1 %collective-permute-start.19 = (f32[5,4,32,1]{3,2,0,1:T(8,128)S(1)}, f32[5,4,32,1]{3,2,0,1:T(8,128)}, u32[]{:S(2)}, u32[]{:S(2)}) collective-permute-start(f32[5,4,32,1]{3,2,0,1:T(8,128)S(1)} %get-tuple-element.119), channel_id=1, source_target_pairs={{0,1},{1,2},{2,3},{3,0},{4,5},{5,6},{6,7},{7,4},{8,9},{9,10},{10,1... | collective-permute-start | bytes 7688 | tf_op jit(solution)/shard_map/ppermute | solution.py:28
  165.1 17.5 %collective-permute-start.18 = (f32[5,4,32,1]{3,2,0,1:T(8,128)S(1)}, f32[5,4,32,1]{3,2,0,1:T(8,128)}, u32[]{:S(2)}, u32[]{:S(2)}) collective-permute-start(f32[5,4,32,1]{3,2,0,1:T(8,128)S(1)} %get-tuple-element.118), channel_id=1, source_target_pairs={{1,0},{2,1},{3,2},{0,3},{5,4},{6,5},{7,6},{4,7},{9,8},{10,9},{11,1... | collective-permute-start | bytes 7688 | tf_op jit(solution)/shard_map/ppermute | solution.py:30
  167.6 17.7 %collective-permute-start.17 = (f32[5,4,1,128]{3,2,0,1:T(1,128)S(1)}, f32[5,4,1,128]{3,2,0,1:T(1,128)}, u32[]{:S(2)}, u32[]{:S(2)}) collective-permute-start(f32[5,4,1,128]{3,2,0,1:T(1,128)S(1)} %get-tuple-element.105), channel_id=1, source_target_pairs={{0,4},{1,5},{2,6},{3,7},{8,12},{9,13},{10,14},{11,15},{16,20},{17,... | collective-permute-start | bytes 30728 | tf_op jit(solution)/shard_map/ppermute | solution.py:28
  172.5 13.5 %collective-permute-start.16 = (f32[5,4,1,128]{3,2,0,1:T(1,128)S(1)}, f32[5,4,1,128]{3,2,0,1:T(1,128)S(1)}, u32[]{:S(2)}, u32[]{:S(2)}) collective-permute-start(f32[5,4,1,128]{3,2,0,1:T(1,128)S(1)} %get-tuple-element.104), channel_id=1, source_target_pairs={{4,0},{5,1},{6,2},{7,3},{12,8},{13,9},{14,10},{15,11},{20,16},{21,... | collective-permute-start | bytes 30728 | tf_op jit(solution)/shard_map/ppermute | solution.py:30
  176.9 10.6 %all-to-all-start.6 = ((f32[4,1,5120]{2,1,0:T(1,128)}), f32[4,1,5120]{2,1,0:T(1,128)S(1)}, u32[]{:S(2)}, u32[]{:S(2)}) async-start(f32[4,1,5120]{2,1,0:T(1,128)} %reshape.217), calls=%async_computation.6 | async-start | bytes 163840 | tf_op jit(solution)/shard_map/all_to_all | solution.py:148
  189.5 2.0 copy-start.71
  189.5 2.0 copy-start.239
  189.5 6.7 %collective-permute-start.15 = (f32[5,32,2,16]{1,0,3,2:T(8,128)S(1)}, f32[5,32,2,16]{1,0,3,2:T(8,128)S(1)}, u32[]{:S(2)}, u32[]{:S(2)}) collective-permute-start(f32[5,32,2,16]{1,0,3,2:T(8,128)S(1)} %pad_maximum_fusion.7), channel_id=1, source_target_pairs={{8,0},{16,8},{24,16},{9,1},{17,9},{25,17},{10,2},{18,10},{26,18},{... | collective-permute-start | bytes 61448 | tf_op jit(solution)/shard_map/ppermute | solution.py:17
  197.1 9.2 %all-to-all-start.7 = ((f32[4,1,5120]{2,1,0:T(1,128)}), f32[4,1,5120]{2,1,0:T(1,128)S(1)}, u32[]{:S(2)}, u32[]{:S(2)}) async-start(f32[4,1,5120]{2,1,0:T(1,128)} %reshape.219), calls=%async_computation.7 | async-start | bytes 163840 | tf_op jit(solution)/shard_map/all_to_all | solution.py:152
  210.6 3.9 %copy-start.72 = (f32[5,4,1,128]{3,2,0,1:T(1,128)}, f32[5,4,1,128]{3,2,0,1:T(1,128)S(1)}, u32[]{:S(2)}) copy-start(f32[5,4,1,128]{3,2,0,1:T(1,128)S(1)} %get-tuple-element.63) | copy-start | bytes 30724
  210.6 8.2 %copy-start.64 = (f32[5,4,1,128]{3,2,0,1:T(1,128)}, f32[5,4,1,128]{3,2,0,1:T(1,128)S(1)}, u32[]{:S(2)}) copy-start(f32[5,4,1,128]{3,2,0,1:T(1,128)S(1)} %get-tuple-element.62) | copy-start | bytes 30724
  211.2 15.4 %collective-permute-start.24 = (f32[5,4,32,1]{3,2,0,1:T(8,128)S(1)}, f32[5,4,32,1]{3,2,0,1:T(8,128)}, u32[]{:S(2)}, u32[]{:S(2)}) collective-permute-start(f32[5,4,32,1]{3,2,0,1:T(8,128)S(1)} %get-tuple-element.77), channel_id=1, source_target_pairs={{0,1},{1,2},{2,3},{3,0},{4,5},{5,6},{6,7},{7,4},{8,9},{9,10},{10,1... | collective-permute-start | bytes 7688 | tf_op jit(solution)/shard_map/ppermute | solution.py:28
  212.0 16.7 %collective-permute-start.23 = (f32[5,4,32,1]{3,2,0,1:T(8,128)S(1)}, f32[5,4,32,1]{3,2,0,1:T(8,128)}, u32[]{:S(2)}, u32[]{:S(2)}) collective-permute-start(f32[5,4,32,1]{3,2,0,1:T(8,128)S(1)} %get-tuple-element.76), channel_id=1, source_target_pairs={{1,0},{2,1},{3,2},{0,3},{5,4},{6,5},{7,6},{4,7},{9,8},{10,9},{11,1... | collective-permute-start | bytes 7688 | tf_op jit(solution)/shard_map/ppermute | solution.py:30
  214.5 16.9 %collective-permute-start.22 = (f32[5,4,1,128]{3,2,0,1:T(1,128)S(1)}, f32[5,4,1,128]{3,2,0,1:T(1,128)S(1)}, u32[]{:S(2)}, u32[]{:S(2)}) collective-permute-start(f32[5,4,1,128]{3,2,0,1:T(1,128)S(1)} %get-tuple-element.63), channel_id=1, source_target_pairs={{0,4},{1,5},{2,6},{3,7},{8,12},{9,13},{10,14},{11,15},{16,20},{17,... | collective-permute-start | bytes 30728 | tf_op jit(solution)/shard_map/ppermute | solution.py:28
  218.8 12.6 %collective-permute-start.21 = (f32[5,4,1,128]{3,2,0,1:T(1,128)S(1)}, f32[5,4,1,128]{3,2,0,1:T(1,128)S(1)}, u32[]{:S(2)}, u32[]{:S(2)}) collective-permute-start(f32[5,4,1,128]{3,2,0,1:T(1,128)S(1)} %get-tuple-element.62), channel_id=1, source_target_pairs={{4,0},{5,1},{6,2},{7,3},{12,8},{13,9},{14,10},{15,11},{20,16},{21,... | collective-permute-start | bytes 30728 | tf_op jit(solution)/shard_map/ppermute | solution.py:30
  223.2 9.0 %all-to-all-start.8 = ((f32[4,1,5120]{2,1,0:T(1,128)}), f32[4,1,5120]{2,1,0:T(1,128)S(1)}, u32[]{:S(2)}, u32[]{:S(2)}) async-start(f32[4,1,5120]{2,1,0:T(1,128)} %reshape.221), calls=%async_computation.8 | async-start | bytes 163840 | tf_op jit(solution)/shard_map/all_to_all | solution.py:148
  234.3 2.0 copy-start.65
  234.3 2.0 copy-start.240
  234.3 6.7 %collective-permute-start.20 = (f32[5,32,2,16]{1,0,3,2:T(8,128)S(1)}, f32[5,32,2,16]{1,0,3,2:T(8,128)S(1)}, u32[]{:S(2)}, u32[]{:S(2)}) collective-permute-start(f32[5,32,2,16]{1,0,3,2:T(8,128)S(1)} %pad_maximum_fusion.8), channel_id=1, source_target_pairs={{8,0},{16,8},{24,16},{9,1},{17,9},{25,17},{10,2},{18,10},{26,18},{... | collective-permute-start | bytes 61448 | tf_op jit(solution)/shard_map/ppermute | solution.py:17
  241.9 9.4 %all-to-all-start.9 = ((f32[4,1,5120]{2,1,0:T(1,128)}), f32[4,1,5120]{2,1,0:T(1,128)S(1)}, u32[]{:S(2)}, u32[]{:S(2)}) async-start(f32[4,1,5120]{2,1,0:T(1,128)} %reshape.223), calls=%async_computation.9 | async-start | bytes 163840 | tf_op jit(solution)/shard_map/all_to_all | solution.py:152
  252.2 1.1 copy-start.101
  252.3 1.1 copy-start.106
  252.3 1.1 copy-start.111
  252.3 1.1 copy-start.116
  252.3 1.1 copy-start.121
  252.3 1.1 copy-start.126
  252.3 1.1 copy-start.131
  252.3 1.1 copy-start.136
  252.3 1.1 copy-start.141
  (221 other events, 221.8 us)

commit v2 on v0

v2 whole, which is shorter than its diff:
```python
import functools
import math

import jax
import jax.numpy as jnp
from jax import lax
from jax.experimental import pallas as pl
from jax.experimental.pallas import tpu as pltpu
from jax.sharding import PartitionSpec as P

ITERS = 5
AXES = ("row", "span", "pitch")

ORDER_MAX = 2
BASE = 2 * ORDER_MAX + 1
COSINES = (BASE * BASE + 1) // 2
WAVES = 2 * COSINES - 1
COMPONENTS = 5
EDGE = 8
SEGMENT_LANES = 4 * EDGE
EXACT = lax.Precision.HIGHEST
PARAMS = pltpu.CompilerParams(vmem_limit_bytes=40 * 1024 * 1024)


def lanes(shape):
    return lax.broadcasted_iota(jnp.int32, shape, len(shape) - 1)


def rows(shape):
    return lax.broadcasted_iota(jnp.int32, shape, len(shape) - 2)


def column(j):
    component = (j * 41) >> 10
    wave = j - WAVES * component
    sine = wave >= COSINES
    return component, jnp.where(sine, wave - (COSINES - 1), wave), sine


def mode_number(mode, blades_ref, face):
    high = ((mode + ORDER_MAX) * 13) >> 6
    low = mode - BASE * high
    return high * blades_ref[face] + low * blades_ref[face + 1]


def waves(products, length):
    if length & (length - 1) == 0:
        phase = products & (length - 1)
    else:
        phase = jnp.mod(products, length)
    turn = phase.astype(jnp.float32) * (1.0 / length)
    quarter = jnp.floor(4.0 * turn + 0.5)
    x = (turn - 0.25 * quarter) * (2.0 * math.pi)
    y = x * x
    sine = x * (1.0 + y * (-1.0 / 6 + y * (1.0 / 120 + y * (-1.0 / 5040 + y * (1.0 / 362880)))))
    cosine = 1.0 + y * (-0.5 + y * (1.0 / 24 + y * (-1.0 / 720 + y * (1.0 / 40320 - y * (1.0 / 3628800)))))
    quarter = quarter.astype(jnp.int32) & 3
    odd = (quarter & 1) == 1
    cos_out = jnp.where(odd, sine, cosine)
    sin_out = jnp.where(odd, cosine, sine)
    cos_out = jnp.where((quarter == 1) | (quarter == 2), -cos_out, cos_out)
    sin_out = jnp.where(quarter >= 2, -sin_out, sin_out)
    return cos_out, sin_out


def to_edges(layers, pitch):
    lane = lanes(layers[0].shape)
    block = jnp.zeros_like(layers[0])
    for a, layer in enumerate(layers):
        if layer is None:
            continue
        start = a * SEGMENT_LANES
        first = pltpu.roll(layer, (start + EDGE) % pitch, layer.ndim - 1)
        last = pltpu.roll(layer, (start + 3 * EDGE) % pitch, layer.ndim - 1)
        block = jnp.where((lane >= start + EDGE) & (lane < start + 2 * EDGE), first, block)
        block = jnp.where((lane >= start + 2 * EDGE) & (lane < start + 3 * EDGE), last, block)
    return block


def pack_kernel(
    blades_ref, adjoint_ref, source_ref, couplings_ref, damping_ref,
    coef_ref, inv_ref, edges_ref, span_ref, right_ref, left_ref, dright_ref, dleft_ref,
    table_ref, modes_ref, modes_edge_ref, *, row_count, length,
):
    components, axial, span, pitch = adjoint_ref.shape
    row, side, place = (lax.axis_index(name) for name in AXES)
    tables = 1 + components
    diag = damping_ref[...]
    for d in range(6):
        diag = diag + couplings_ref[d]
    inverse = 1.0 / diag
    for c in range(components):
        coef_ref[c] = source_ref[c] * inverse
    for d in range(6):
        coef_ref[components + d] = couplings_ref[d] * inverse
    inv_ref[...] = inverse[axial - 1]

    fields = 2 * components + 6

    def field_layers(f):
        if f < components:
            return [adjoint_ref[f, a] for a in range(axial)]
        return [coef_ref[f - components, a] for a in range(axial)]

    for f in range(fields):
        edges_ref[f] = to_edges(field_layers(f), pitch)
    last = inv_ref[...]
    edges_ref[fields] = jnp.where(
        lanes(last.shape) >= (axial - 1) * SEGMENT_LANES,
        to_edges([jnp.zeros_like(last)] * (axial - 1) + [last], pitch), 0.0,
    )
    slot = (lanes((span, pitch)) // EDGE) % 4
    edge_row = pl.multiple_of(jnp.where(side == 0, span - EDGE, 0), EDGE)
    for out_ref, corner_ref, at in ((right_ref, dright_ref, 2), (left_ref, dleft_ref, 1)):
        for g in range(right_ref.shape[0]):
            packed = jnp.zeros((span, pitch), jnp.float32)
            for k in range(4):
                if 4 * g + k <= fields:
                    moved_field = pltpu.roll(edges_ref[4 * g + k], ((k - at) * EDGE) % pitch, 1)
                    packed = jnp.where(slot == k, moved_field, packed)
            out_ref[g] = packed
            corner_ref[g] = out_ref[g, pl.ds(edge_row, EDGE), :]
    for f in range(fields):
        ref, at = (adjoint_ref, f) if f < components else (coef_ref, f - components)
        for a in range(axial):
            span_ref[f * axial + a] = ref[at, a, pl.ds(edge_row, EDGE), :]
    span_ref[fields * axial] = inv_ref[pl.ds(edge_row, EDGE), :]

    j = lanes((pitch, pitch))
    component, mode, sine = column(j)
    number = mode_number(mode, blades_ref, jnp.maximum(row - 1, 0))
    cos_table, sin_table = waves(number * (place * pitch + rows((pitch, pitch))), length)
    table = jnp.where(component < components, jnp.where(sine, sin_table, cos_table), 0.0)
    table_ref[...] = table
    total = jnp.zeros((span, pitch), jnp.float32)
    for c in range(components):
        total += jnp.dot(
            adjoint_ref[c, 0], jnp.where(component == c, table, 0.0),
            precision=EXACT, preferred_element_type=jnp.float32,
        )
    modes_ref[...] = total
    modes_edge_ref[...] = modes_ref[pl.ds(edge_row, EDGE), :]


def synth_kernel(
    blades_ref, giles_re_ref, giles_im_ref, orders_ref, cells_ref, synth_ref,
    *, row_count, place_count, components, pitch, length, axial,
):
    row, place = lax.axis_index("row"), lax.axis_index("pitch")
    face = jnp.minimum(row, row_count - 2)
    modes = orders_ref.shape[2]
    orders = orders_ref[face]
    tag = BASE * orders[0:1] + orders[1:2]
    component, mode, _ = column(rows((pitch, modes)))
    same = (jnp.abs(tag) == mode) & (component < components)
    plain = jnp.where(same, 1.0, 0.0)
    signed = jnp.where(tag < 0, -plain, plain)
    dims = (((1,), (1,)), ((), ()))
    sums_re = lax.dot_general(giles_re_ref[...], plain, dims, precision=EXACT, preferred_element_type=jnp.float32)
    sums_im = lax.dot_general(giles_im_ref[...], signed, dims, precision=EXACT, preferred_element_type=jnp.float32)
    component, mode, sine = column(lanes(sums_re.shape))
    scale = 2.0 / length
    with_cos = jnp.where(sine, sums_im, sums_re) * scale
    with_sin = jnp.where(sine, sums_re, -sums_im) * scale
    component = component[0:1]

    def chunk(at):
        start = pl.multiple_of(lax.rem(place + at + place_count, place_count) * pitch, pitch)
        return cells_ref[:, pl.ds(start, pitch)]

    own = chunk(0)
    lane = lanes((1, pitch))
    first = (axial - 1) * SEGMENT_LANES
    edge = jnp.where(lane < first + EDGE, pltpu.roll(chunk(-1), (first + EDGE) % pitch, 1), pltpu.roll(own, (first + EDGE) % pitch, 1))
    edge = jnp.where(lane < first + 2 * EDGE, edge, pltpu.roll(own, (first + 3 * EDGE) % pitch, 1))
    edge = jnp.where(lane < first + 3 * EDGE, edge, pltpu.roll(chunk(1), (first + 3 * EDGE) % pitch, 1))

    def upright(cells):
        wide = jnp.broadcast_to(cells.astype(jnp.float32), (pitch, pitch))
        return jnp.transpose(wide).astype(jnp.int32)

    edge_cells = upright(edge)[first:first + SEGMENT_LANES]
    at_cells = jnp.concatenate([upright(own), edge_cells], 0)
    _, mode, _ = column(lanes(at_cells.shape))
    cos_table, sin_table = waves(mode_number(mode, blades_ref, face) * at_cells, length)
    for c in range(components):
        row_cos = jnp.zeros((1, pitch), jnp.float32)
        row_sin = jnp.zeros((1, pitch), jnp.float32)
        for b in range(components):
            at = b * components + c
            row_cos = jnp.where(component == b, with_cos[at:at + 1], row_cos)
            row_sin = jnp.where(component == b, with_sin[at:at + 1], row_sin)
        part = row_cos * cos_table + row_sin * sin_table
        synth_ref[pl.ds(c * pitch, pitch), :] = part[:pitch]
        synth_ref[pl.ds(components * pitch + c * SEGMENT_LANES, SEGMENT_LANES), :] = part[pitch:]
    used = components * (pitch + SEGMENT_LANES)
    rest = synth_ref.shape[0] - used
    if rest:
        synth_ref[pl.ds(used, rest), :] = jnp.zeros((rest, pitch), jnp.float32)


def mixed(jac_ref, source, couplings, neighbours):
    total = list(source)
    for d, neighbour in enumerate(neighbours):
        for c in range(len(total)):
            term = jac_ref[c, d] * neighbour[0]
            for b in range(1, len(total)):
                term = term + jac_ref[b * len(total) + c, d] * neighbour[b]
            total[c] = total[c] + couplings[d] * term
    return total


def layer_update(jac_ref, state_ref, edge_ref, coef_ref, t, a):
    components, wide, pitch = state_ref.shape[1], state_ref.shape[3], state_ref.shape[4]
    lane = lanes((wide, pitch))
    start = a * SEGMENT_LANES
    own = [state_ref[t, c, a + 1] for c in range(components)]
    above = [state_ref[t, c, a + 2] for c in range(components)]
    below = [state_ref[t, c, a] for c in range(components)]
    edge = [edge_ref[t, c] for c in range(components)]
    span_next = [pltpu.roll(x, wide - 1, 0) for x in own]
    span_prev = [pltpu.roll(x, 1, 0) for x in own]
    to_end = 2 * pitch - 1 - (start + 3 * EDGE)
    to_begin = 2 * pitch - (start + EDGE - 1)
    pitch_next = [
        jnp.where(lane == pitch - 1, pltpu.roll(e, lax.rem(to_end, pitch), 1), pltpu.roll(x, pitch - 1, 1))
        for e, x in zip(edge, own)
    ]
    pitch_prev = [
        jnp.where(lane == 0, pltpu.roll(e, lax.rem(to_begin, pitch), 1), pltpu.roll(x, 1, 1))
        for e, x in zip(edge, own)
    ]
    source = [coef_ref[c, a] for c in range(components)]
    couplings = [coef_ref[components + d, a] for d in range(6)]
    return mixed(jac_ref, source, couplings, (above, below, span_next, span_prev, pitch_next, pitch_prev))


def edge_update(jac_ref, edge_ref, edge_coef_ref, t, axial):
    components, wide, pitch = edge_ref.shape[1:]
    lane = lanes((wide, pitch))
    own = [edge_ref[t, c] for c in range(components)]
    above = [jnp.where(lane < (axial - 1) * SEGMENT_LANES, pltpu.roll(x, pitch - SEGMENT_LANES, 1), 0.0) for x in own]
    below = [jnp.where(lane >= SEGMENT_LANES, pltpu.roll(x, SEGMENT_LANES, 1), 0.0) for x in own]
    span_next = [pltpu.roll(x, wide - 1, 0) for x in own]
    span_prev = [pltpu.roll(x, 1, 0) for x in own]
    pitch_next = [pltpu.roll(x, pitch - 1, 1) for x in own]
    pitch_prev = [pltpu.roll(x, 1, 1) for x in own]
    source = [edge_coef_ref[c] for c in range(components)]
    couplings = [edge_coef_ref[components + d] for d in range(6)]
    return mixed(jac_ref, source, couplings, (above, below, span_next, span_prev, pitch_next, pitch_prev))


def edge_boundary(field, c, components, pitch, axial):
    at = components * pitch + c * SEGMENT_LANES
    tile = field[:, (at // pitch) * pitch:(at // pitch + 1) * pitch]
    return pltpu.roll(tile, ((axial - 1) * SEGMENT_LANES - at % pitch) % pitch, 1)


def first_kernel(
    jac_ref, adjoint_ref, coef_in_ref, inv_in_ref, edges_ref, span_ref,
    from_left_ref, from_right_ref, dleft_ref, dright_ref, table_ref, modes_a_ref, modes_b_ref, synth_ref,
    coef_ref, inv_ref, edge_coef_ref, front_ref, edge_front_ref, modes_ref,
    state_ref, edge_ref, *, fronts,
):
    components, axial, span, pitch = adjoint_ref.shape
    wide = span + EDGE
    side = lax.axis_index("span")
    fields = 2 * components + 6
    ghost_row = rows((EDGE, pitch))
    keep = ghost_row != jnp.where(side == 0, EDGE - 1, 0)

    def ghost(at):
        return jnp.where(keep, span_ref[at], 0.0)

    for f in range(fields):
        for a in range(axial):
            if f < components:
                state_ref[0, f, a + 1, :span] = adjoint_ref[f, a]
                state_ref[0, f, a + 1, span:] = ghost(f * axial + a)
            else:
                coef_ref[f - components, a, :span] = coef_in_ref[f - components, a]
                coef_ref[f - components, a, span:] = ghost(f * axial + a)
    inv_ref[:span] = inv_in_ref[...]
    inv_ref[span:] = ghost(fields * axial)
    for t in range(state_ref.shape[0]):
        for c in range(components):
            state_ref[t, c, 0] = jnp.zeros((wide, pitch), jnp.float32)
            state_ref[t, c, axial + 1] = jnp.zeros((wide, pitch), jnp.float32)

    for f in range(fields + 1):
        g, k = f // 4, f % 4
        target, at = (edge_ref.at[0], f) if f < components else (edge_coef_ref, f - components)
        to_first, to_last = (-k * EDGE) % pitch, ((3 - k) * EDGE) % pitch
        segment = (lanes((span, pitch)) // EDGE) % 4
        value = edges_ref[f]
        value = jnp.where(segment == 0, pltpu.roll(from_left_ref[g], to_first, 1), value)
        value = jnp.where(segment == 3, pltpu.roll(from_right_ref[g], to_last, 1), value)
        segment = (lanes((EDGE, pitch)) // EDGE) % 4
        if f < fields:
            layers = [span_ref[f * axial + a] for a in range(axial)]
        else:
            layers = [None] * (axial - 1) + [span_ref[fields * axial]]
            layers = [jnp.zeros((EDGE, pitch), jnp.float32) if x is None else x for x in layers]
        corner = to_edges(layers, pitch)
        corner = jnp.where(segment == 0, pltpu.roll(dleft_ref[g], to_first, 1), corner)
        corner = jnp.where(segment == 3, pltpu.roll(dright_ref[g], to_last, 1), corner)
        corner = jnp.where(keep, corner, 0.0)
        target[at, :span] = value
        target[at, span:] = corner

    field = lax.dot_general(
        modes_a_ref[...] + modes_b_ref[...], synth_ref[...], (((1,), (1,)), ((), ())),
        precision=EXACT, preferred_element_type=jnp.float32,
    )

    def step(t, count):
        def body(a, carry):
            new = layer_update(jac_ref, state_ref, edge_ref, coef_ref, t, a)
            for c in range(components):
                state_ref[t + 1, c, a + 1] = new[c]
            return carry

        lax.fori_loop(0, count, body, 0)

    def edge_step(t):
        new = edge_update(jac_ref, edge_ref, edge_coef_ref, t, axial)
        for c in range(components):
            edge_ref[t + 1, c] = new[c]

    step(0, axial)
    edge_step(0)
    for c in range(components):
        state_ref[1, c, axial] += inv_ref[...] * field[:, c * pitch:(c + 1) * pitch]
        edge_ref[1, c] += edge_coef_ref[components + 6] * edge_boundary(field, c, components, pitch, axial)

    def later(t, carry):
        step(t, jnp.where(t == 1, axial, axial - t))

        @pl.when(t < axial - 1)
        def _():
            edge_step(t)

        return carry

    lax.fori_loop(1, axial, later, 0)

    component, _, _ = column(lanes((pitch, pitch)))
    total = jnp.zeros((axial * wide, pitch), jnp.float32)
    for c in range(components):
        strips = jnp.concatenate([state_ref[t, c, 1] for t in range(1, axial + 1)], 0)
        total += jnp.dot(
            strips, jnp.where(component == c, table_ref[...], 0.0),
            precision=EXACT, preferred_element_type=jnp.float32,
        )
    modes_ref[...] = total
    for n, (t, a) in enumerate(fronts):
        front_ref[n] = state_ref[t, :, a + 1]
    edge_front_ref[...] = edge_ref[2]


def second_kernel(
    jac_ref, coef_ref, inv_ref, edge_coef_ref, front_ref, edge_front_ref, modes_a_ref, modes_b_ref, synth_ref,
    out_ref, state_ref, edge_ref, bound_ref, edge_bound_ref, *, fronts,
):
    components, axial, span, pitch = out_ref.shape
    wide = span + EDGE
    for t in range(state_ref.shape[0]):
        for c in range(components):
            state_ref[t, c, 0] = jnp.zeros((wide, pitch), jnp.float32)
            state_ref[t, c, axial + 1] = jnp.zeros((wide, pitch), jnp.float32)
    for n, (t, a) in enumerate(fronts):
        state_ref[t, :, a + 1] = front_ref[n]
    field = lax.dot_general(
        modes_a_ref[...] + modes_b_ref[...], synth_ref[...], (((1,), (1,)), ((), ())),
        precision=EXACT, preferred_element_type=jnp.float32,
    )
    for n in range(axial):
        part = field[n * wide:(n + 1) * wide]
        for c in range(components):
            bound_ref[n, c] = inv_ref[...] * part[:, c * pitch:(c + 1) * pitch]
            edge_bound_ref[n, c] = edge_coef_ref[components + 6] * edge_boundary(part, c, components, pitch, axial)
    for c in range(components):
        state_ref[2, c, axial] += bound_ref[0, c]
        edge_ref[2, c] = edge_front_ref[c] + edge_bound_ref[0, c]

    def later(t, carry):
        def body(a, inner):
            new = layer_update(jac_ref, state_ref, edge_ref, coef_ref, t, a)
            for c in range(components):
                state_ref[t + 1, c, a + 1] = new[c]
            return inner

        lax.fori_loop(axial - t, axial, body, 0)
        for c in range(components):
            state_ref[t + 1, c, axial] += bound_ref[t - 1, c]
        new = edge_update(jac_ref, edge_ref, edge_coef_ref, t, axial)
        for c in range(components):
            edge_ref[t + 1, c] = new[c] + edge_bound_ref[t - 1, c]
        return carry

    lax.fori_loop(2, axial, later, 0)

    def final(a, carry):
        new = layer_update(jac_ref, state_ref, edge_ref, coef_ref, axial, a)
        for c in range(components):
            out_ref[c, a] = new[c][:span]
        return carry

    lax.fori_loop(0, axial, final, 0)
    for c in range(components):
        out_ref[c, axial - 1] += bound_ref[axial - 1, c, :span]


def moved(x, to):
    sizes = [lax.axis_size(name) for name in AXES]
    pairs = []
    for r in range(sizes[0]):
        for s in range(sizes[1]):
            for p in range(sizes[2]):
                target = to(r, s, p)
                if all(0 <= at < size for at, size in zip(target, sizes)):
                    number = lambda at: (at[0] * sizes[1] + at[1]) * sizes[2] + at[2]
                    pairs.append((number((r, s, p)), number(target)))
    return lax.ppermute(x, AXES, pairs)


def struct(*shape):
    return jax.ShapeDtypeStruct(shape, jnp.float32)


def on_device(
    adjoint_start, source, couplings, damping, jacobians, giles_real, giles_imag, blades, mode_orders, cell_map,
):
    components, axial, span, pitch = adjoint_start.shape
    row_count, span_count, place_count = (lax.axis_size(name) for name in AXES)
    length = pitch * place_count
    assert components == COMPONENTS and components * WAVES <= pitch
    assert axial == ITERS - 1 and ITERS <= EDGE and axial * SEGMENT_LANES == pitch
    assert span_count == 2 and place_count & (place_count - 1) == 0
    wide = span + EDGE
    fields = 2 * components + 6
    groups = fields // 4 + 1
    smem = pl.BlockSpec(memory_space=pltpu.SMEM)
    vmem = pl.BlockSpec(memory_space=pltpu.VMEM)

    (coef, inv, edges, span_out, right, left, dright, dleft, table, modes, modes_edge) = pl.pallas_call(
        functools.partial(pack_kernel, row_count=row_count, length=length),
        out_shape=(
            struct(components + 6, axial, span, pitch), struct(span, pitch), struct(fields + 1, span, pitch),
            struct(fields * axial + 1, EDGE, pitch), struct(groups, span, pitch), struct(groups, span, pitch),
            struct(groups, EDGE, pitch), struct(groups, EDGE, pitch), struct(pitch, pitch),
            struct(span, pitch), struct(EDGE, pitch),
        ),
        in_specs=[smem] + [vmem] * 4,
        out_specs=[vmem] * 11,
        compiler_params=PARAMS,
        name="pack",
    )(blades, adjoint_start, source, couplings, damping)

    up_own = moved(modes, lambda r, s, p: (r - 1, s, p))
    up_other = moved(modes_edge, lambda r, s, p: (r - 1, 1 - s, p))
    from_span = moved(span_out, lambda r, s, p: (r, 1 - s, p))
    from_left = moved(right, lambda r, s, p: (r, s, (p + 1) % place_count))
    from_right = moved(left, lambda r, s, p: (r, s, (p - 1) % place_count))
    dleft_in = moved(dright, lambda r, s, p: (r, 1 - s, (p + 1) % place_count))
    dright_in = moved(dleft, lambda r, s, p: (r, 1 - s, (p - 1) % place_count))

    face = jnp.minimum(lax.axis_index("row"), row_count - 2)

    def of_face(giles):
        picked = lax.dynamic_index_in_dim(giles, face, 0, keepdims=False)
        return picked.transpose(1, 2, 0).reshape(components * components, -1)

    synth_rows = -(-components * (pitch + SEGMENT_LANES) // pitch) * pitch
    synth = pl.pallas_call(
        functools.partial(
            synth_kernel, row_count=row_count, place_count=place_count, components=components, pitch=pitch,
            length=length, axial=axial,
        ),
        out_shape=struct(synth_rows, pitch),
        in_specs=[smem] + [vmem] * 4,
        out_specs=vmem,
        compiler_params=PARAMS,
        name="synth",
    )(blades, of_face(giles_real), of_face(giles_imag), mode_orders.transpose(0, 2, 1), cell_map)

    def exchanged(x, bit):
        return moved(x, lambda r, s, p: (r, s, p ^ bit))

    total = jnp.concatenate([up_own, up_other], 0)
    other = jnp.zeros_like(total)
    bit = 1
    while bit < place_count:
        total = total + other if bit > 1 else total
        other = exchanged(total, bit)
        bit *= 2

    jac = jacobians[0].transpose(1, 2, 0).reshape(components * components, 6)
    fronts = [(t, a) for t in range(2, axial + 1) for a in range(max(axial - t - 1, 0), max(axial - t + 1, axial if t == 2 else 0))]
    coefx, invx, edge_coef, front, edge_front, modes = pl.pallas_call(
        functools.partial(first_kernel, fronts=fronts),
        out_shape=(
            struct(components + 6, axial, wide, pitch), struct(wide, pitch), struct(components + 7, wide, pitch),
            struct(len(fronts), components, wide, pitch), struct(components, wide, pitch), struct(axial * wide, pitch),
        ),
        in_specs=[smem] + [vmem] * 13,
        out_specs=[vmem] * 6,
        scratch_shapes=[
            pltpu.VMEM((axial + 1, components, axial + 2, wide, pitch), jnp.float32),
            pltpu.VMEM((axial + 1, components, wide, pitch), jnp.float32),
        ],
        compiler_params=PARAMS,
        name="first_sweeps",
    )(
        jac, adjoint_start, coef, inv, edges, from_span, from_left, from_right, dleft_in, dright_in, table,
        total, other, synth,
    )

    bit = 1
    while 2 * bit < place_count:
        modes = modes + exchanged(modes, bit)
        bit *= 2
    modes_a = moved(modes, lambda r, s, p: (r - 1, s, p))
    if bit < place_count:
        modes_b = moved(modes, lambda r, s, p: (r - 1, s, p ^ bit))
    else:
        modes_b = jnp.zeros_like(modes)
    return pl.pallas_call(
        functools.partial(second_kernel, fronts=fronts),
        out_shape=struct(components, axial, span, pitch),
        in_specs=[smem] + [vmem] * 8,
        out_specs=vmem,
        scratch_shapes=[
            pltpu.VMEM((axial + 1, components, axial + 2, wide, pitch), jnp.float32),
            pltpu.VMEM((axial + 1, components, wide, pitch), jnp.float32),
            pltpu.VMEM((axial, components, wide, pitch), jnp.float32),
            pltpu.VMEM((axial, components, wide, pitch), jnp.float32),
        ],
        compiler_params=PARAMS,
        name="second_sweeps",
    )(jac, coefx, invx, edge_coef, front, edge_front, modes_a, modes_b, synth)


def solution(mesh):
    placed = (
        P(None, "row", "span", "pitch"),
        P(None, "row", "span", "pitch"),
        P(None, "row", "span", "pitch"),
        P("row", "span", "pitch"),
        P("row", None, None, None),
        P(),
        P(),
        P(),
        P(),
        P("row", None),
    )
    return jax.shard_map(
        on_device,
        mesh=mesh,
        in_specs=placed,
        out_specs=P(None, "row", "span", "pitch"),
        check_vma=False,
    )
```

time: 338 us -> 54.6 us (0.16)
  waiting for transfers between devices: 84.5 us -> 8.78 us
  blocking collectives: 66.2 us -> 0 us
  local copies, waits for them, and re-layouts: 69.7 us -> 5.94 us
  starting transfers between devices: 62 us -> 25 us
  other arithmetic: 21.9 us -> 0.01 us
  between operations: 17.2 us -> 0.2 us
  Pallas kernels: 0 us -> 14.3 us
  matrix products: 13.5 us -> 0 us
    all_gather x5 -> x0, blocking collectives: 66.2 us -> none  [on_device(): all_modes = lax.all_gather(arrived, 'pitch', axis=3, tiled=True)]
    ppermute x25 -> x12, starting transfers between devices: 61.8 us -> 25 us  [moved(): return lax.ppermute(x, AXES, pairs)]
    reduce_scatter x4 -> x0, waiting for transfers between devices: 36.8 us -> none  [on_device(): lax.psum_scatter(partial_sum, 'pitch', scatter_dimension=3, tiled=True)]
    ppermute x25 -> x12, waiting for transfers between devices: 29.9 us -> 8.78 us  [moved(): return lax.ppermute(x, AXES, pairs)]
    unnamed x428 -> x24, local copies, waits for them, and re-layouts: 25.6 us -> 5.06 us
    unnamed x6 -> x0, waiting for transfers between devices: 17.8 us -> none
    ppermute x20 -> x0, local copies, waits for them, and re-layouts: 17.8 us -> none  [the longest x10 9.18 us: padded(): lax.ppermute(tail, axis, [(i, (i + 1) % count) for i in range(ends)])]
    pallas_call x0 -> x4, Pallas kernels: none -> 14.3 us  [the longest x1 6.61 us: on_device(): pl.pallas_call(functools.partial(first_kernel, fronts=fronts), out_shape=...]
  transfers between devices with their start and end apart: 30 -> 12, of which waited for: 17 -> 5; matrix products, arithmetic and copies ran while one was open for 16% -> 2% of each run, Pallas kernels for 0% -> 2%
where the time goes in v2:
time: 54.6 us; the launch traced here: 54.2 us
  starting transfers between devices  25 us (46%)
  Pallas kernels  14.3 us (26%)
  waiting for transfers between devices  8.78 us (16%)
  local copies, waits for them, and re-layouts  5.94 us (11%)
    ppermute x12, starting transfers between devices, moved(): return lax.ppermute(x, AXES, pairs)  25 us
    ppermute x12, waiting for transfers between devices, moved(): return lax.ppermute(x, AXES, pairs)  8.78 us
    pallas_call x1, Pallas kernels, on_device(): pl.pallas_call(functools.partial(first_kernel, fronts=fronts), out_shape=...  6.61 us
    pallas_call x1, Pallas kernels, on_device(): pl.pallas_call(functools.partial(second_kernel, fronts=fronts), out_shape...  5.37 us
    unnamed x24, local copies, waits for them, and re-layouts  5.06 us
    pallas_call x1, Pallas kernels, on_device(): pl.pallas_call(functools.partial(pack_kernel, row_count=row_count, length...  1.38 us
  transfers between devices with their start and end apart: 12, of which 5 were waited for; matrix products, arithmetic and copies ran while one was open for 2% of the time, Pallas kernels for 2%

profile of v2, /device:TPU:1, one launch (start us, length us, event | category | flops | bytes accessed | tf_op | source)
XLA Modules:
  0.0 54.2 jit_solution(7998105123732804548)
XLA Ops:
  0.0 0.0 copy-start
  0.0 1.0 %copy-done = f32[5,4,32,128]{3,2,1,0:T(8,128)S(1)} copy-done((f32[5,4,32,128]{3,2,1,0:T(8,128)S(1)}, f32[5,4,32,128]{3,2,1,0:T(8,128)}, u32[]{:S(2)}) %copy-start) | copy-done | bytes 327704
  1.0 0.0 copy-start.2
  1.0 1.0 %copy-done.2 = f32[6,4,32,128]{3,2,1,0:T(8,128)S(1)} copy-done((f32[6,4,32,128]{3,2,1,0:T(8,128)S(1)}, f32[6,4,32,128]{3,2,1,0:T(8,128)}, u32[]{:S(2)}) %copy-start.2) | copy-done | bytes 393240
  2.0 0.0 copy-start.3
  2.0 1.0 %copy-done.3 = f32[5,4,32,128]{3,2,1,0:T(8,128)S(1)} copy-done((f32[5,4,32,128]{3,2,1,0:T(8,128)S(1)}, f32[5,4,32,128]{3,2,1,0:T(8,128)}, u32[]{:S(2)}) %copy-start.3) | copy-done | bytes 327704
  2.9 0.0 copy-start.4
  2.9 0.8 %copy-done.4 = f32[4,32,128]{2,1,0:T(8,128)S(1)} copy-done((f32[4,32,128]{2,1,0:T(8,128)S(1)}, f32[4,32,128]{2,1,0:T(8,128)}, u32[]{:S(2)}) %copy-start.4) | copy-done | bytes 65560
  3.8 0.0 copy-start.7
  3.8 0.7 %copy-done.7 = s32[4]{0:T(128)S(1)} copy-done((s32[4]{0:T(128)S(1)}, s32[4]{0:T(128)}, u32[]{:S(2)}) %copy-start.7) | copy-done | bytes 40
  4.4 1.4 %pack.1 = (f32[11,4,32,128]{3,2,1,0:T(8,128)S(1)}, f32[32,128]{1,0:T(8,128)S(1)}, f32[17,32,128]{2,1,0:T(8,128)S(1)}, f32[65,8,128]{2,1,0:T(8,128)S(1)}, f32[5,3...) custom-call(s32[4]{0:T(128)S(1)} %copy-done.7, ...), custom_call_target="tpu_custom_call" | custom-call | tf_op jit(solution)/shard_map/pack/pallas_call | solution.py:446
  5.8 2.0 %collective-permute-start.5 = (f32[32,128]{1,0:T(8,128)S(1)}, f32[32,128]{1,0:T(8,128)S(1)}, u32[]{:S(2)}, u32[]{:S(2)}) collective-permute-start(f32[32,128]{1,0:T(8,128)S(1)} %get-tuple-element.31), channel_id=1, source_target_pairs={{8,0},{9,1},{10,2},{11,3},{12,4},{13,5},{14,6},{15,7},{16,8},{17,9... | collective-permute-start | bytes 49160 | tf_op jit(solution)/shard_map/ppermute | solution.py:424
  7.8 3.9 %collective-permute-start.6 = (f32[8,128]{1,0:T(8,128)S(1)}, f32[8,128]{1,0:T(8,128)S(1)}, u32[]{:S(2)}, u32[]{:S(2)}) collective-permute-start(f32[8,128]{1,0:T(8,128)S(1)} %get-tuple-element.32), channel_id=1, source_target_pairs={{8,4},{9,5},{10,6},{11,7},{12,0},{13,1},{14,2},{15,3},{16,12},{17,... | collective-permute-start | bytes 12296 | tf_op jit(solution)/shard_map/ppermute | solution.py:424
  11.7 0.8 %collective-permute-start = (f32[65,8,128]{2,1,0:T(8,128)S(1)}, f32[65,8,128]{2,1,0:T(8,128)S(1)}, u32[]{:S(2)}, u32[]{:S(2)}) collective-permute-start(f32[65,8,128]{2,1,0:T(8,128)S(1)} %get-tuple-element.25), channel_id=1, source_target_pairs={{0,4},{1,5},{2,6},{3,7},{4,0},{5,1},{6,2},{7,3},{8,12},{9,13},{10,... | collective-permute-start | bytes 798728 | tf_op jit(solution)/shard_map/ppermute | solution.py:424
  12.5 0.0 collective-permute-done.5
  12.5 2.1 %collective-permute-done.6 = f32[8,128]{1,0:T(8,128)S(1)} collective-permute-done((f32[8,128]{1,0:T(8,128)S(1)}, f32[8,128]{1,0:T(8,128)S(1)}, u32[]{:S(2)}, u32[]{:S(2)}) %collective-permute-start.6) | collective-permute-done | bytes 4128 | tf_op jit(solution)/shard_map/ppermute | solution.py:424
  14.6 1.9 %collective-permute-start.7 = (f32[40,128]{1,0:T(8,128)S(1)}, f32[40,128]{1,0:T(8,128)S(1)}, u32[]{:S(2)}, u32[]{:S(2)}) collective-permute-start(f32[40,128]{1,0:T(8,128)S(1)} %constant_dynamic-update-slice_fusion), channel_id=1, source_target_pairs={{0,1},{1,0},{2,3},{3,2},{4,5},{5,4},{6,7},{7,6},{8,9},{9,8},{10,11... | collective-permute-start | bytes 61448 | tf_op jit(solution)/shard_map/ppermute | solution.py:424
  16.5 1.1 %collective-permute-start.3 = (f32[5,8,128]{2,1,0:T(8,128)S(1)}, f32[5,8,128]{2,1,0:T(8,128)S(1)}, u32[]{:S(2)}, u32[]{:S(2)}) collective-permute-start(f32[5,8,128]{2,1,0:T(8,128)S(1)} %get-tuple-element.28), channel_id=1, source_target_pairs={{0,5},{1,6},{2,7},{3,4},{4,1},{5,2},{6,3},{7,0},{8,13},{9,14},{10,... | collective-permute-start | bytes 61448 | tf_op jit(solution)/shard_map/ppermute | solution.py:424
  17.6 3.0 %collective-permute-start.4 = (f32[5,8,128]{2,1,0:T(8,128)S(1)}, f32[5,8,128]{2,1,0:T(8,128)S(1)}, u32[]{:S(2)}, u32[]{:S(2)}) collective-permute-start(f32[5,8,128]{2,1,0:T(8,128)S(1)} %get-tuple-element.29), channel_id=1, source_target_pairs={{0,7},{1,4},{2,5},{3,6},{4,3},{5,0},{6,1},{7,2},{8,15},{9,12},{10,... | collective-permute-start | bytes 61448 | tf_op jit(solution)/shard_map/ppermute | solution.py:424
  20.6 0.0 collective-permute-start.1
  20.6 0.0 collective-permute-done.7
  20.6 3.3 %collective-permute-start.2 = (f32[5,32,128]{2,1,0:T(8,128)S(1)}, f32[5,32,128]{2,1,0:T(8,128)S(1)}, u32[]{:S(2)}, u32[]{:S(2)}) collective-permute-start(f32[5,32,128]{2,1,0:T(8,128)S(1)} %get-tuple-element.27), channel_id=1, source_target_pairs={{0,3},{1,0},{2,1},{3,2},{4,7},{5,4},{6,5},{7,6},{8,11},{9,8},{10,9... | collective-permute-start | bytes 245768 | tf_op jit(solution)/shard_map/ppermute | solution.py:424
  23.9 0.0 copy-start.9
  23.9 0.0 collective-permute-done.3.dleft_ref
  23.9 0.1 collective-permute-start.8
  24.0 0.9 %constant_dynamic-slice_fusion = (f32[1,64,5,5]{1,0,3,2:T(1,128)S(1)}, f32[1,64,5,5]{1,0,3,2:T(1,128)S(1)}) fusion(f32[3,64,5,5]{1,0,3,2:T(4,128)} %param.16, s32[]{:T(128)S(6)} %select_n.5, f32[3,64,5,5]{1,0,3,2:T(4,128)} %param.15), kind=kLoop, calls=%fused_computation.5 | loop fusion | bytes 25604 | tf_op jit(solution)/shard_map/jit(dynamic_index_in_dim)/dynamic_slice | solution.py:471
  24.9 0.0 copy-done.9
  24.9 0.0 copy-start.5
  24.9 0.0 copy-start.6
  24.9 0.0 copy-start.8
  24.9 0.0 copy-start.1
  25.0 0.6 %copy-done.5 = s32[3,64,2]{1,2,0:T(2,128)S(1)} copy-done((s32[3,64,2]{1,2,0:T(2,128)S(1)}, s32[3,64,2]{1,2,0:T(2,128)}, u32[]{:S(2)}) %copy-start.5) | copy-done | bytes 1560
  25.6 0.0 copy-done.6
  25.6 0.0 copy-done.8
  25.6 0.9 %synth.1.synth_ref = f32[896,128]{1,0:T(8,128)S(1)} custom-call(s32[4]{0:T(128)S(1)} %copy-done.8, f32[25,64]{1,0:T(8,128)S(1)} %reshape.10.giles_re_ref, f32[25,64]{1,0:T(8,128)S(1)} %reshape.11.giles_im_ref, s32[3,2,64]{2,1,0:T(2,128)S(1)} %bitcast.16, s32[1,512]{1,0:T(1,128)S(1)} %copy-done.6), custom_call_target="tpu_custom_call" | custom-call | tf_op jit(solution)/shard_map/synth/pallas_call | solution.py:475
  26.5 0.0 collective-permute-done.4.dright_ref
  26.5 1.0 %collective-permute-done.8.modes_b_ref = f32[40,128]{1,0:T(8,128)S(1)} collective-permute-done((f32[40,128]{1,0:T(8,128)S(1)}, f32[40,128]{1,0:T(8,128)S(1)}, u32[]{:S(2)}, u32[]{:S(2)}) %collective-permute-start.8) | collective-permute-done | bytes 20512 | tf_op jit(solution)/shard_map/ppermute | solution.py:424
  27.5 0.0 collective-permute-done.1.from_left_ref
  27.5 0.0 collective-permute-done.2.from_right_ref
  27.5 0.0 collective-permute-done.span_ref
  27.5 0.0 copy-done.1
  27.5 6.6 %first_sweeps.1 = (f32[11,4,40,128]{3,2,1,0:T(8,128)S(1)}, f32[40,128]{1,0:T(8,128)S(1)}, f32[12,40,128]{2,1,0:T(8,128)S(1)}, f32[6,5,40,128]{3,2,1,0:T(8,128)S(...) custom-call(f32[25,6]{1,0:T(8,128)S(1)} %reshape.12.jac_ref, f32[5,4,32,128]{3,2,1,0:T(8,128)S(1)} %copy-done.1, ...), custom_call_target="tpu_custom_call" | custom-call | tf_op jit(solution)/shard_map/first_sweeps/pallas_call | solution.py:500
  34.2 1.8 %collective-permute-start.9 = (f32[160,128]{1,0:T(8,128)S(1)}, f32[160,128]{1,0:T(8,128)S(1)}, u32[]{:S(2)}, u32[]{:S(2)}) collective-permute-start(f32[160,128]{1,0:T(8,128)S(1)} %get-tuple-element.38), channel_id=1, source_target_pairs={{0,1},{1,0},{2,3},{3,2},{4,5},{5,4},{6,7},{7,6},{8,9},{9,8},{10,11... | collective-permute-start | bytes 245768 | tf_op jit(solution)/shard_map/ppermute | solution.py:424
  35.9 1.8 %collective-permute-done.9 = f32[160,128]{1,0:T(8,128)S(1)} collective-permute-done((f32[160,128]{1,0:T(8,128)S(1)}, f32[160,128]{1,0:T(8,128)S(1)}, u32[]{:S(2)}, u32[]{:S(2)}) %collective-permute-start.9) | collective-permute-done | bytes 81952 | tf_op jit(solution)/shard_map/ppermute | solution.py:424
  37.8 5.3 %collective-permute-start.11 = (f32[160,128]{1,0:T(8,128)S(1)}, f32[160,128]{1,0:T(8,128)S(1)}, u32[]{:S(2)}, u32[]{:S(2)}) collective-permute-start(f32[160,128]{1,0:T(8,128)S(1)} %add.13), channel_id=1, source_target_pairs={{8,2},{9,3},{10,0},{11,1},{12,6},{13,7},{14,4},{15,5},{16,10},{17,... | collective-permute-start | bytes 245768 | tf_op jit(solution)/shard_map/ppermute | solution.py:424
  43.1 1.9 %collective-permute-start.10 = (f32[160,128]{1,0:T(8,128)S(1)}, f32[160,128]{1,0:T(8,128)S(1)}, u32[]{:S(2)}, u32[]{:S(2)}) collective-permute-start(f32[160,128]{1,0:T(8,128)S(1)} %add.13), channel_id=1, source_target_pairs={{8,0},{9,1},{10,2},{11,3},{12,4},{13,5},{14,6},{15,7},{16,8},{17,9... | collective-permute-start | bytes 245768 | tf_op jit(solution)/shard_map/ppermute | solution.py:424
  45.0 0.6 %collective-permute-done.11.modes_b_ref = f32[160,128]{1,0:T(8,128)S(1)} collective-permute-done((f32[160,128]{1,0:T(8,128)S(1)}, f32[160,128]{1,0:T(8,128)S(1)}, u32[]{:S(2)}, u32[]{:S(2)}) %collective-permute-start.11) | collective-permute-done | bytes 81952 | tf_op jit(solution)/shard_map/ppermute | solution.py:424
  45.6 3.2 %collective-permute-done.10.modes_a_ref = f32[160,128]{1,0:T(8,128)S(1)} collective-permute-done((f32[160,128]{1,0:T(8,128)S(1)}, f32[160,128]{1,0:T(8,128)S(1)}, u32[]{:S(2)}, u32[]{:S(2)}) %collective-permute-start.10) | collective-permute-done | bytes 81952 | tf_op jit(solution)/shard_map/ppermute | solution.py:424
  48.8 5.4 %second_sweeps.1 = f32[5,4,32,128]{3,2,1,0:T(8,128)} custom-call(f32[25,6]{1,0:T(8,128)S(1)} %reshape.12.jac_ref, f32[11,4,40,128]{3,2,1,0:T(8,128)S(1)} %get-tuple-element.33.coef_ref, f32[40,128]{1,0:T(8,128)S(1)} %get-tuple-element.34.inv_ref, f32[12,40,128]{2,1,0:T(8,128)S(1)} %get-tuple-element.35.edge_coef_ref, ...), custom_call_target="tpu_custom_call" | custom-call | tf_op jit(solution)/shard_map/second_sweeps/pallas_call | solution.py:528
  (10 shorter events, 0.0 us)
Async XLA Ops:
  0.0 1.0 %copy-start = (f32[5,4,32,128]{3,2,1,0:T(8,128)S(1)}, f32[5,4,32,128]{3,2,1,0:T(8,128)}, u32[]{:S(2)}) copy-start(f32[5,4,32,128]{3,2,1,0:T(8,128)} %adjoint_ref.3) | copy-start | bytes 983044
  1.0 1.0 %copy-start.2 = (f32[6,4,32,128]{3,2,1,0:T(8,128)S(1)}, f32[6,4,32,128]{3,2,1,0:T(8,128)}, u32[]{:S(2)}) copy-start(f32[6,4,32,128]{3,2,1,0:T(8,128)} %couplings_ref.1) | copy-start | bytes 1179652
  2.0 1.0 %copy-start.3 = (f32[5,4,32,128]{3,2,1,0:T(8,128)S(1)}, f32[5,4,32,128]{3,2,1,0:T(8,128)}, u32[]{:S(2)}) copy-start(f32[5,4,32,128]{3,2,1,0:T(8,128)} %source_ref.1) | copy-start | bytes 983044
  2.9 0.8 %copy-start.4 = (f32[4,32,128]{2,1,0:T(8,128)S(1)}, f32[4,32,128]{2,1,0:T(8,128)}, u32[]{:S(2)}) copy-start(f32[4,32,128]{2,1,0:T(8,128)} %damping_ref.1) | copy-start | bytes 196612
  3.8 0.7 %copy-start.7 = (s32[4]{0:T(128)S(1)}, s32[4]{0:T(128)}, u32[]{:S(2)}) copy-start(s32[4]{0:T(128)} %blades_ref.3) | copy-start | bytes 52
  5.8 6.7 %collective-permute-start.5 = (f32[32,128]{1,0:T(8,128)S(1)}, f32[32,128]{1,0:T(8,128)S(1)}, u32[]{:S(2)}, u32[]{:S(2)}) collective-permute-start(f32[32,128]{1,0:T(8,128)S(1)} %get-tuple-element.31), channel_id=1, source_target_pairs={{8,0},{9,1},{10,2},{11,3},{12,4},{13,5},{14,6},{15,7},{16,8},{17,9... | collective-permute-start | bytes 49160 | tf_op jit(solution)/shard_map/ppermute | solution.py:424
  7.8 6.8 %collective-permute-start.6 = (f32[8,128]{1,0:T(8,128)S(1)}, f32[8,128]{1,0:T(8,128)S(1)}, u32[]{:S(2)}, u32[]{:S(2)}) collective-permute-start(f32[8,128]{1,0:T(8,128)S(1)} %get-tuple-element.32), channel_id=1, source_target_pairs={{8,4},{9,5},{10,6},{11,7},{12,0},{13,1},{14,2},{15,3},{16,12},{17,... | collective-permute-start | bytes 12296 | tf_op jit(solution)/shard_map/ppermute | solution.py:424
  11.7 15.9 %collective-permute-start = (f32[65,8,128]{2,1,0:T(8,128)S(1)}, f32[65,8,128]{2,1,0:T(8,128)S(1)}, u32[]{:S(2)}, u32[]{:S(2)}) collective-permute-start(f32[65,8,128]{2,1,0:T(8,128)S(1)} %get-tuple-element.25), channel_id=1, source_target_pairs={{0,4},{1,5},{2,6},{3,7},{4,0},{5,1},{6,2},{7,3},{8,12},{9,13},{10,... | collective-permute-start | bytes 798728 | tf_op jit(solution)/shard_map/ppermute | solution.py:424
  14.6 6.0 %collective-permute-start.7 = (f32[40,128]{1,0:T(8,128)S(1)}, f32[40,128]{1,0:T(8,128)S(1)}, u32[]{:S(2)}, u32[]{:S(2)}) collective-permute-start(f32[40,128]{1,0:T(8,128)S(1)} %constant_dynamic-update-slice_fusion), channel_id=1, source_target_pairs={{0,1},{1,0},{2,3},{3,2},{4,5},{5,4},{6,7},{7,6},{8,9},{9,8},{10,11... | collective-permute-start | bytes 61448 | tf_op jit(solution)/shard_map/ppermute | solution.py:424
  16.5 7.4 %collective-permute-start.3 = (f32[5,8,128]{2,1,0:T(8,128)S(1)}, f32[5,8,128]{2,1,0:T(8,128)S(1)}, u32[]{:S(2)}, u32[]{:S(2)}) collective-permute-start(f32[5,8,128]{2,1,0:T(8,128)S(1)} %get-tuple-element.28), channel_id=1, source_target_pairs={{0,5},{1,6},{2,7},{3,4},{4,1},{5,2},{6,3},{7,0},{8,13},{9,14},{10,... | collective-permute-start | bytes 61448 | tf_op jit(solution)/shard_map/ppermute | solution.py:424
  17.6 8.9 %collective-permute-start.4 = (f32[5,8,128]{2,1,0:T(8,128)S(1)}, f32[5,8,128]{2,1,0:T(8,128)S(1)}, u32[]{:S(2)}, u32[]{:S(2)}) collective-permute-start(f32[5,8,128]{2,1,0:T(8,128)S(1)} %get-tuple-element.29), channel_id=1, source_target_pairs={{0,7},{1,4},{2,5},{3,6},{4,3},{5,0},{6,1},{7,2},{8,15},{9,12},{10,... | collective-permute-start | bytes 61448 | tf_op jit(solution)/shard_map/ppermute | solution.py:424
  20.6 6.9 %collective-permute-start.1 = (f32[5,32,128]{2,1,0:T(8,128)S(1)}, f32[5,32,128]{2,1,0:T(8,128)S(1)}, u32[]{:S(2)}, u32[]{:S(2)}) collective-permute-start(f32[5,32,128]{2,1,0:T(8,128)S(1)} %get-tuple-element.26), channel_id=1, source_target_pairs={{0,1},{1,2},{2,3},{3,0},{4,5},{5,6},{6,7},{7,4},{8,9},{9,10},{10,1... | collective-permute-start | bytes 245768 | tf_op jit(solution)/shard_map/ppermute | solution.py:424
  20.6 6.9 %collective-permute-start.2 = (f32[5,32,128]{2,1,0:T(8,128)S(1)}, f32[5,32,128]{2,1,0:T(8,128)S(1)}, u32[]{:S(2)}, u32[]{:S(2)}) collective-permute-start(f32[5,32,128]{2,1,0:T(8,128)S(1)} %get-tuple-element.27), channel_id=1, source_target_pairs={{0,3},{1,0},{2,1},{3,2},{4,7},{5,4},{6,5},{7,6},{8,11},{9,8},{10,9... | collective-permute-start | bytes 245768 | tf_op jit(solution)/shard_map/ppermute | solution.py:424
  23.9 1.0 %copy-start.9 = (f32[1,6,5,5]{1,0,3,2:T(1,128)S(1)}, f32[1,6,5,5]{1,0,3,2:T(1,128)}, u32[]{:S(2)}) copy-start(f32[1,6,5,5]{1,0,3,2:T(1,128)} %param.14) | copy-start | bytes 1804
  23.9 3.6 %collective-permute-start.8 = (f32[40,128]{1,0:T(8,128)S(1)}, f32[40,128]{1,0:T(8,128)S(1)}, u32[]{:S(2)}, u32[]{:S(2)}) collective-permute-start(f32[40,128]{1,0:T(8,128)S(1)} %add.11.modes_a_ref), channel_id=1, source_target_pairs={{0,2},{1,3},{2,0},{3,1},{4,6},{5,7},{6,4},{7,5},{8,10},{9,11},{10,... | collective-permute-start | bytes 61448 | tf_op jit(solution)/shard_map/ppermute | solution.py:424
  24.9 0.7 %copy-start.5 = (s32[3,64,2]{1,2,0:T(2,128)S(1)}, s32[3,64,2]{1,2,0:T(2,128)}, u32[]{:S(2)}) copy-start(s32[3,64,2]{1,2,0:T(2,128)} %param.18) | copy-start | bytes 4612
  24.9 0.7 %copy-start.6 = (s32[1,512]{1,0:T(1,128)S(1)}, s32[1,512]{1,0:T(1,128)}, u32[]{:S(2)}) copy-start(s32[1,512]{1,0:T(1,128)} %cells_ref.1) | copy-start | bytes 6148
  24.9 0.7 %copy-start.8 = (s32[4]{0:T(128)S(1)}, s32[4]{0:T(128)}, u32[]{:S(2)}) copy-start(s32[4]{0:T(128)} %blades_ref.3) | copy-start | bytes 52
  24.9 2.6 %copy-start.1 = (f32[5,4,32,128]{3,2,1,0:T(8,128)S(1)}, f32[5,4,32,128]{3,2,1,0:T(8,128)}, u32[]{:S(2)}) copy-start(f32[5,4,32,128]{3,2,1,0:T(8,128)} %adjoint_ref.3) | copy-start | bytes 983044
  34.2 3.6 %collective-permute-start.9 = (f32[160,128]{1,0:T(8,128)S(1)}, f32[160,128]{1,0:T(8,128)S(1)}, u32[]{:S(2)}, u32[]{:S(2)}) collective-permute-start(f32[160,128]{1,0:T(8,128)S(1)} %get-tuple-element.38), channel_id=1, source_target_pairs={{0,1},{1,0},{2,3},{3,2},{4,5},{5,4},{6,7},{7,6},{8,9},{9,8},{10,11... | collective-permute-start | bytes 245768 | tf_op jit(solution)/shard_map/ppermute | solution.py:424
  37.8 7.8 %collective-permute-start.11 = (f32[160,128]{1,0:T(8,128)S(1)}, f32[160,128]{1,0:T(8,128)S(1)}, u32[]{:S(2)}, u32[]{:S(2)}) collective-permute-start(f32[160,128]{1,0:T(8,128)S(1)} %add.13), channel_id=1, source_target_pairs={{8,2},{9,3},{10,0},{11,1},{12,6},{13,7},{14,4},{15,5},{16,10},{17,... | collective-permute-start | bytes 245768 | tf_op jit(solution)/shard_map/ppermute | solution.py:424
  43.1 5.8 %collective-permute-start.10 = (f32[160,128]{1,0:T(8,128)S(1)}, f32[160,128]{1,0:T(8,128)S(1)}, u32[]{:S(2)}, u32[]{:S(2)}) collective-permute-start(f32[160,128]{1,0:T(8,128)S(1)} %add.13), channel_id=1, source_target_pairs={{8,0},{9,1},{10,2},{11,3},{12,4},{13,5},{14,6},{15,7},{16,8},{17,9... | collective-permute-start | bytes 245768 | tf_op jit(solution)/shard_map/ppermute | solution.py:424

commit v3 on v2

v3 whole, which is shorter than its diff:
```python
import functools
import math

import jax
import jax.numpy as jnp
from jax import lax
from jax.experimental import pallas as pl
from jax.experimental.pallas import tpu as pltpu
from jax.sharding import PartitionSpec as P

ITERS = 5
AXES = ("row", "span", "pitch")

ORDER_MAX = 2
BASE = 2 * ORDER_MAX + 1
COSINES = (BASE * BASE + 1) // 2
WAVES = 2 * COSINES - 1
COMPONENTS = 5
EDGE = 8
HALF = EDGE // 2
SEGMENT_LANES = 4 * EDGE
EXACT = lax.Precision.HIGHEST
PARAMS = pltpu.CompilerParams(vmem_limit_bytes=40 * 1024 * 1024)


def lanes(shape):
    return lax.broadcasted_iota(jnp.int32, shape, len(shape) - 1)


def rows(shape):
    return lax.broadcasted_iota(jnp.int32, shape, len(shape) - 2)


def column(j):
    component = (j * 41) >> 10
    wave = j - WAVES * component
    sine = wave >= COSINES
    return component, jnp.where(sine, wave - (COSINES - 1), wave), sine


def mode_number(mode, blades_ref, face):
    high = ((mode + ORDER_MAX) * 13) >> 6
    low = mode - BASE * high
    return high * blades_ref[face] + low * blades_ref[face + 1]


def waves(products, length):
    if length & (length - 1) == 0:
        phase = products & (length - 1)
    else:
        phase = jnp.mod(products, length)
    turn = phase.astype(jnp.float32) * (1.0 / length)
    quarter = jnp.floor(4.0 * turn + 0.5)
    x = (turn - 0.25 * quarter) * (2.0 * math.pi)
    y = x * x
    sine = x * (1.0 + y * (-1.0 / 6 + y * (1.0 / 120 + y * (-1.0 / 5040 + y * (1.0 / 362880)))))
    cosine = 1.0 + y * (-0.5 + y * (1.0 / 24 + y * (-1.0 / 720 + y * (1.0 / 40320 - y * (1.0 / 3628800)))))
    quarter = quarter.astype(jnp.int32) & 3
    odd = (quarter & 1) == 1
    cos_out = jnp.where(odd, sine, cosine)
    sin_out = jnp.where(odd, cosine, sine)
    cos_out = jnp.where((quarter == 1) | (quarter == 2), -cos_out, cos_out)
    sin_out = jnp.where(quarter >= 2, -sin_out, sin_out)
    return cos_out, sin_out


def to_edges(layers, pitch):
    lane = lanes(layers[0].shape)
    block = jnp.zeros_like(layers[0])
    for a, layer in enumerate(layers):
        if layer is None:
            continue
        start = a * SEGMENT_LANES
        first = pltpu.roll(layer, (start + EDGE) % pitch, layer.ndim - 1)
        last = pltpu.roll(layer, (start + 3 * EDGE) % pitch, layer.ndim - 1)
        block = jnp.where((lane >= start + EDGE) & (lane < start + 2 * EDGE), first, block)
        block = jnp.where((lane >= start + 2 * EDGE) & (lane < start + 3 * EDGE), last, block)
    return block


def half_rows(side):
    return jnp.where(side == 0, EDGE // 2, 0), jnp.where(side == 0, 0, EDGE // 2)


def slots(fields, components):
    per_group = SEGMENT_LANES // HALF
    near = [(f // per_group, f % per_group * HALF) for f in range(fields)]
    group, lane = near[-1]
    far = [(group, lane + HALF + c) for c in range(components)]
    return near, far


def pack_kernel(
    blades_hbm, adjoint_hbm, source_hbm, couplings_hbm, damping_hbm,
    coef_ref, inv_ref, edges_ref, span_ref, corner_ref, right_ref, left_ref, table_ref,
    blades_ref, adjoint_ref, source_ref, couplings_ref, damping_ref, sems, *, length,
):
    components, axial, span, pitch = adjoint_ref.shape
    copies = [
        pltpu.make_async_copy(src, dst, sems.at[n])
        for n, (src, dst) in enumerate((
            (couplings_hbm, couplings_ref), (damping_hbm, damping_ref), (source_hbm, source_ref),
            (adjoint_hbm, adjoint_ref), (blades_hbm, blades_ref),
        ))
    ]
    for copy in copies:
        copy.start()
    row, side, place = (lax.axis_index(name) for name in AXES)
    copies[0].wait()
    copies[1].wait()
    diag = damping_ref[...]
    for d in range(6):
        diag = diag + couplings_ref[d]
    inverse = 1.0 / diag
    for d in range(6):
        coef_ref[components + d] = couplings_ref[d] * inverse
    inv_ref[...] = inverse[axial - 1]
    copies[2].wait()
    for c in range(components):
        coef_ref[c] = source_ref[c] * inverse
    copies[3].wait()

    fields = 2 * components + 6
    for f in range(fields):
        ref, at = (adjoint_ref, f) if f < components else (coef_ref, f - components)
        edges_ref[f] = to_edges([ref[at, a] for a in range(axial)], pitch)
    last = inv_ref[...]
    edges_ref[fields] = jnp.where(
        lanes(last.shape) >= (axial - 1) * SEGMENT_LANES,
        to_edges([jnp.zeros_like(last)] * (axial - 1) + [last], pitch), 0.0,
    )
    edge_row = pl.multiple_of(jnp.where(side == 0, span - EDGE, 0), EDGE)
    near, far = slots(fields + 1, components)
    groups = right_ref.shape[0]
    lane = lanes((span, pitch)) % SEGMENT_LANES
    for n, (out_ref, near_at, far_at) in enumerate((
        (right_ref, 3 * EDGE - HALF, 3 * EDGE - HALF - 1), (left_ref, EDGE, EDGE + HALF),
    )):
        packed = [jnp.zeros((span, pitch), jnp.float32) for _ in range(groups)]
        for f, (g, to) in enumerate(near):
            value = pltpu.roll(edges_ref[f], (to - near_at) % pitch, 1)
            packed[g] = jnp.where((lane >= to) & (lane < to + HALF), value, packed[g])
        for f, (g, to) in enumerate(far):
            packed[g] = jnp.where(lane == to, pltpu.roll(edges_ref[f], (to - far_at) % pitch, 1), packed[g])
        for g in range(groups):
            out_ref[g, :span] = packed[g]
            corner_ref[n * groups + g] = out_ref[g, pl.ds(edge_row, EDGE), :]

    to_low, to_high = half_rows(side)
    line = rows((EDGE, pitch))
    tiles = [(adjoint_ref, c, a) for c in range(components) for a in range(axial)]
    tiles += [(coef_ref, f, a) for f in range(components + 6) for a in range(axial)]
    tiles = [ref[f, a, pl.ds(edge_row, EDGE), :] for ref, f, a in tiles] + [inv_ref[pl.ds(edge_row, EDGE), :]]
    pairs = -(-len(tiles) // 2)
    for n in range(pairs):
        value = pltpu.roll(tiles[2 * n], to_low, 0)
        if 2 * n + 1 < len(tiles):
            value = jnp.where(line < HALF, value, pltpu.roll(tiles[2 * n + 1], to_high, 0))
        span_ref[n] = value
    fifth = jnp.where(side == 0, HALF - 1, HALF)
    for n in range(span_ref.shape[0] - pairs):
        value = jnp.zeros((EDGE, pitch), jnp.float32)
        for k in range(min(EDGE, components * axial - n * EDGE)):
            value = jnp.where(line == k, pltpu.roll(tiles[n * EDGE + k], lax.rem(k + EDGE - fifth, EDGE), 0), value)
        span_ref[pairs + n] = value

    copies[4].wait()
    component, mode, sine = column(lanes((pitch, pitch)))
    number = mode_number(mode, blades_ref, jnp.maximum(row - 1, 0))
    cos_table, sin_table = waves(number * (place * pitch + rows((pitch, pitch))), length)
    table_ref[...] = jnp.where(component < components, jnp.where(sine, sin_table, cos_table), 0.0)


def projected(strips, table):
    component, _, _ = column(lanes(table.shape))
    total = jnp.zeros((strips[0].shape[0], table.shape[1]), jnp.float32)
    for c, strip in enumerate(strips):
        total += jnp.dot(
            strip, jnp.where(component == c, table, 0.0), precision=EXACT, preferred_element_type=jnp.float32,
        )
    return total


def synthesised(modes, synth):
    return lax.dot_general(
        modes, synth, (((1,), (1,)), ((), ())), precision=EXACT, preferred_element_type=jnp.float32,
    )


def synth_kernel(
    blades_ref, giles_re_ref, giles_im_ref, orders_ref, cells_ref, after_ref, synth_ref,
    *, row_count, place_count, components, pitch, length, axial,
):
    row, place = lax.axis_index("row"), lax.axis_index("pitch")
    face = jnp.minimum(row, row_count - 2)
    modes = orders_ref.shape[2]
    orders = orders_ref[face]
    tag = BASE * orders[0:1] + orders[1:2]
    component, mode, _ = column(rows((pitch, modes)))
    same = (jnp.abs(tag) == mode) & (component < components)
    plain = jnp.where(same, 1.0, 0.0)
    signed = jnp.where(tag < 0, -plain, plain)
    dims = (((1,), (1,)), ((), ()))
    sums_re = lax.dot_general(giles_re_ref[...], plain, dims, precision=EXACT, preferred_element_type=jnp.float32)
    sums_im = lax.dot_general(giles_im_ref[...], signed, dims, precision=EXACT, preferred_element_type=jnp.float32)
    component, mode, sine = column(lanes(sums_re.shape))
    scale = 2.0 / length
    with_cos = jnp.where(sine, sums_im, sums_re) * scale
    with_sin = jnp.where(sine, sums_re, -sums_im) * scale
    component = component[0:1]

    def chunk(at):
        start = pl.multiple_of(lax.rem(place + at + place_count, place_count) * pitch, pitch)
        return cells_ref[:, pl.ds(start, pitch)]

    own = chunk(0)
    lane = lanes((1, pitch))
    first = (axial - 1) * SEGMENT_LANES
    edge = jnp.where(lane < first + EDGE, pltpu.roll(chunk(-1), (first + EDGE) % pitch, 1), pltpu.roll(own, (first + EDGE) % pitch, 1))
    edge = jnp.where(lane < first + 2 * EDGE, edge, pltpu.roll(own, (first + 3 * EDGE) % pitch, 1))
    edge = jnp.where(lane < first + 3 * EDGE, edge, pltpu.roll(chunk(1), (first + 3 * EDGE) % pitch, 1))

    def upright(cells):
        wide = jnp.broadcast_to(cells.astype(jnp.float32), (pitch, pitch))
        return jnp.transpose(wide).astype(jnp.int32)

    edge_cells = upright(edge)[first:first + SEGMENT_LANES]
    at_cells = jnp.concatenate([upright(own), edge_cells], 0)
    _, mode, _ = column(lanes(at_cells.shape))
    cos_table, sin_table = waves(mode_number(mode, blades_ref, face) * at_cells, length)
    for c in range(components):
        row_cos = jnp.zeros((1, pitch), jnp.float32)
        row_sin = jnp.zeros((1, pitch), jnp.float32)
        for b in range(components):
            at = b * components + c
            row_cos = jnp.where(component == b, with_cos[at:at + 1], row_cos)
            row_sin = jnp.where(component == b, with_sin[at:at + 1], row_sin)
        part = row_cos * cos_table + row_sin * sin_table
        synth_ref[pl.ds(c * pitch, pitch), :] = part[:pitch]
        synth_ref[pl.ds(components * pitch + c * SEGMENT_LANES, SEGMENT_LANES), :] = part[pitch:]
    used = components * (pitch + SEGMENT_LANES)
    rest = synth_ref.shape[0] - used
    if rest:
        synth_ref[pl.ds(used, rest), :] = jnp.zeros((rest, pitch), jnp.float32)


def mixed(jac_ref, source, couplings, neighbours):
    total = list(source)
    for d, neighbour in enumerate(neighbours):
        for c in range(len(total)):
            term = jac_ref[c, d] * neighbour[0]
            for b in range(1, len(total)):
                term = term + jac_ref[b * len(total) + c, d] * neighbour[b]
            total[c] = total[c] + couplings[d] * term
    return total


def layer_update(jac_ref, state_ref, edge_ref, coef_ref, t, a):
    components, wide, pitch = state_ref.shape[1], state_ref.shape[3], state_ref.shape[4]
    lane = lanes((wide, pitch))
    start = a * SEGMENT_LANES
    own = [state_ref[t, c, a + 1] for c in range(components)]
    above = [state_ref[t, c, a + 2] for c in range(components)]
    below = [state_ref[t, c, a] for c in range(components)]
    edge = [edge_ref[t, c] for c in range(components)]
    span_next = [pltpu.roll(x, wide - 1, 0) for x in own]
    span_prev = [pltpu.roll(x, 1, 0) for x in own]
    to_end = 2 * pitch - 1 - (start + 3 * EDGE)
    to_begin = 2 * pitch - (start + EDGE - 1)
    pitch_next = [
        jnp.where(lane == pitch - 1, pltpu.roll(e, lax.rem(to_end, pitch), 1), pltpu.roll(x, pitch - 1, 1))
        for e, x in zip(edge, own)
    ]
    pitch_prev = [
        jnp.where(lane == 0, pltpu.roll(e, lax.rem(to_begin, pitch), 1), pltpu.roll(x, 1, 1))
        for e, x in zip(edge, own)
    ]
    source = [coef_ref[c, a] for c in range(components)]
    couplings = [coef_ref[components + d, a] for d in range(6)]
    return mixed(jac_ref, source, couplings, (above, below, span_next, span_prev, pitch_next, pitch_prev))


def edge_update(jac_ref, edge_ref, edge_coef_ref, t, axial):
    components, wide, pitch = edge_ref.shape[1:]
    lane = lanes((wide, pitch))
    own = [edge_ref[t, c] for c in range(components)]
    above = [jnp.where(lane < (axial - 1) * SEGMENT_LANES, pltpu.roll(x, pitch - SEGMENT_LANES, 1), 0.0) for x in own]
    below = [jnp.where(lane >= SEGMENT_LANES, pltpu.roll(x, SEGMENT_LANES, 1), 0.0) for x in own]
    span_next = [pltpu.roll(x, wide - 1, 0) for x in own]
    span_prev = [pltpu.roll(x, 1, 0) for x in own]
    pitch_next = [pltpu.roll(x, pitch - 1, 1) for x in own]
    pitch_prev = [pltpu.roll(x, 1, 1) for x in own]
    source = [edge_coef_ref[c] for c in range(components)]
    couplings = [edge_coef_ref[components + d] for d in range(6)]
    return mixed(jac_ref, source, couplings, (above, below, span_next, span_prev, pitch_next, pitch_prev))


def edge_boundary(field, c, components, pitch, axial):
    at = components * pitch + c * SEGMENT_LANES
    tile = field[:, (at // pitch) * pitch:(at // pitch + 1) * pitch]
    return pltpu.roll(tile, ((axial - 1) * SEGMENT_LANES - at % pitch) % pitch, 1)


def advance(refs, t, a):
    state_ref = refs[1]
    for c, value in enumerate(layer_update(*refs, t, a)):
        state_ref[t + 1, c, a + 1] = value


def first_kernel(
    jac_ref, adjoint_ref, coef_in_ref, inv_in_ref, edges_ref, span_ref, from_left_ref, from_right_ref, table_ref,
    coef_ref, inv_ref, edge_coef_ref, state_ref, edge_ref, modes_ref,
):
    components, axial, span, pitch = adjoint_ref.shape
    wide = span + EDGE
    side = lax.axis_index("span")
    fields = 2 * components + 6
    line = rows((EDGE, pitch))
    keep_half = jnp.where(side == 0, line, EDGE - 1 - line) < HALF
    fifth = jnp.where(side == 0, HALF, HALF - 1)
    from_low, from_high = half_rows(1 - side)
    pairs = -(-(fields * axial + 1) // 2)

    def ghost(n):
        value = pltpu.roll(span_ref[n // 2], from_high if n % 2 else from_low, 0)
        value = jnp.where(keep_half, value, 0.0)
        if n < components * axial:
            extra = pltpu.roll(span_ref[pairs + n // EDGE], lax.rem(fifth + EDGE - n % EDGE, EDGE), 0)
            value = jnp.where(line == fifth, extra, value)
        return value

    near, far = slots(fields + 1, components)
    keep_five = keep_half | (line == fifth)
    for f in range(fields + 1):
        if f < fields:
            layers = [ghost(f * axial + a) for a in range(axial)]
        else:
            layers = [jnp.zeros((EDGE, pitch), jnp.float32)] * (axial - 1) + [ghost(fields * axial)]
        if f < components:
            for a in range(axial):
                state_ref[0, f, a + 1, :span] = adjoint_ref[f, a]
                state_ref[0, f, a + 1, span:] = layers[a]
        elif f < fields:
            for a in range(axial):
                coef_ref[f - components, a, :span] = coef_in_ref[f - components, a]
                coef_ref[f - components, a, span:] = layers[a]
        else:
            inv_ref[:span] = inv_in_ref[...]
            inv_ref[span:] = layers[-1]
        g, at = near[f]
        value = jnp.concatenate([edges_ref[f], to_edges(layers, pitch)], 0)
        lane = lanes((wide, pitch)) % SEGMENT_LANES
        value = jnp.where((lane >= HALF) & (lane < EDGE), pltpu.roll(from_left_ref[g], (HALF - at) % pitch, 1), value)
        value = jnp.where(
            (lane >= 3 * EDGE) & (lane < 3 * EDGE + HALF),
            pltpu.roll(from_right_ref[g], (3 * EDGE - at) % pitch, 1), value,
        )
        if f < components:
            g, at = far[f]
            value = jnp.where(lane == HALF - 1, pltpu.roll(from_left_ref[g], (HALF - 1 - at) % pitch, 1), value)
            value = jnp.where(
                lane == 3 * EDGE + HALF, pltpu.roll(from_right_ref[g], (3 * EDGE + HALF - at) % pitch, 1), value,
            )
        target, at = (edge_ref.at[0], f) if f < components else (edge_coef_ref, f - components)
        target[at, :span] = value[:span]
        target[at, span:] = jnp.where(keep_five if f < components else keep_half, value[span:], 0.0)
    for t in range(state_ref.shape[0]):
        for c in range(components):
            state_ref[t, c, 0] = jnp.zeros((wide, pitch), jnp.float32)
            state_ref[t, c, axial + 1] = jnp.zeros((wide, pitch), jnp.float32)

    refs = (jac_ref, state_ref, edge_ref, coef_ref)

    def sweep(t, carry):
        def body(a, inner):
            advance(refs, t, a)
            return inner

        lax.fori_loop(0, axial - 1 - t, body, 0)

        @pl.when(t < axial - 2)
        def _():
            for c, value in enumerate(edge_update(jac_ref, edge_ref, edge_coef_ref, t, axial)):
                edge_ref[t + 1, c] = value

        return carry

    lax.fori_loop(0, axial - 1, sweep, 0)
    strips = [jnp.concatenate([state_ref[t, c, 1] for t in range(axial)], 0) for c in range(components)]
    total = projected(strips, table_ref[...])
    to_low, to_high = half_rows(1 - side)
    for t in range(axial):
        modes_ref[pl.ds(t * span, span), :] = total[t * wide:t * wide + span]
    for n in range(axial // 2):
        low = total[2 * n * wide + span:2 * n * wide + wide]
        high = total[(2 * n + 1) * wide + span:(2 * n + 1) * wide + wide]
        both = jnp.where(line < HALF, pltpu.roll(low, to_low, 0), pltpu.roll(high, to_high, 0))
        modes_ref[pl.ds(axial * span + n * EDGE, EDGE), :] = both


def middle_kernel(
    jac_ref, coef_ref, edge_coef_ref, state_in_ref, edge_in_ref, table_ref, state_ref, edge_ref, modes_ref,
):
    components, axial, span = state_ref.shape[1], state_ref.shape[2] - 2, modes_ref.shape[0]
    refs = (jac_ref, state_ref, edge_ref, coef_ref)
    for c, value in enumerate(edge_update(jac_ref, edge_ref, edge_coef_ref, axial - 2, axial)):
        edge_ref[axial - 1, c] = value

    def body(t, carry):
        advance(refs, t, axial - 1 - t)
        return carry

    lax.fori_loop(0, axial, body, 0)
    modes_ref[...] = projected([state_ref[axial, c, 1, :span] for c in range(components)], table_ref[...])


def along_axis(jac_ref, coef_ref, delta, a, height):
    components = len(delta)
    out = []
    for c in range(components):
        term = jac_ref[c, 0] * delta[0]
        for b in range(1, components):
            term = term + jac_ref[b * components + c, 0] * delta[b]
        out.append(coef_ref[components, a, :height] * term)
    return out


def link_kernel(jac_ref, coef_ref, inv_ref, part_ref, modes_a_ref, modes_b_ref, synth_ref, table_ref, modes_ref):
    span, pitch = modes_ref.shape
    components, axial = coef_ref.shape[0] - 6, coef_ref.shape[1]
    modes = modes_a_ref[:span] + modes_b_ref[:span]
    field = synthesised(modes, synth_ref[:components * pitch])
    delta = [inv_ref[:span] * field[:, c * pitch:(c + 1) * pitch] for c in range(components)]
    for a in range(axial - 2, -1, -1):
        delta = along_axis(jac_ref, coef_ref, delta, a, span)
    modes_ref[...] = part_ref[...] + projected(delta, table_ref[...])


def second_kernel(
    jac_ref, coef_ref, inv_ref, edge_coef_ref, state_in_ref, edge_in_ref, modes_a_ref, modes_b_ref, synth_ref, after_ref,
    state_ref, edge_ref, bound_ref,
):
    components, axial = state_ref.shape[1], state_ref.shape[2] - 2
    wide, pitch = state_ref.shape[3:]
    span = wide - EDGE
    from_low, from_high = half_rows(1 - lax.axis_index("span"))
    packed = modes_a_ref[...] + modes_b_ref[...]
    parts = []
    for t in range(axial):
        ghost = packed[axial * span + t // 2 * EDGE:axial * span + (t // 2 + 1) * EDGE]
        parts += [packed[t * span:(t + 1) * span], pltpu.roll(ghost, from_high if t % 2 else from_low, 0)]
    field = synthesised(jnp.concatenate(parts, 0), synth_ref[...])
    edge_bound = []
    for n in range(axial):
        part = field[n * wide:(n + 1) * wide]
        edge_bound.append([])
        for c in range(components):
            bound_ref[n, c] = inv_ref[...] * part[:, c * pitch:(c + 1) * pitch]
            edge_bound[n].append(edge_coef_ref[components + 6] * edge_boundary(part, c, components, pitch, axial))
    delta = [bound_ref[0, c] for c in range(components)]
    for t in range(1, axial + 1):
        for c in range(components):
            state_ref[t, c, axial + 1 - t] += delta[c]
        if t < axial:
            delta = along_axis(jac_ref, coef_ref, delta, axial - 1 - t, wide)
    for c in range(components):
        edge_ref[1, c] += edge_bound[0][c]
    for t in range(1, axial):
        for c, value in enumerate(edge_update(jac_ref, edge_ref, edge_coef_ref, t, axial)):
            edge_ref[t + 1, c] = value + edge_bound[t][c]
    rest_of_sweeps(jac_ref, coef_ref, state_ref, edge_ref, bound_ref, 1, axial - 1)


def rest_of_sweeps(jac_ref, coef_ref, state_ref, edge_ref, bound_ref, first, last):
    components, axial = state_ref.shape[1], state_ref.shape[2] - 2
    refs = (jac_ref, state_ref, edge_ref, coef_ref)

    def sweep(t, carry):
        def body(a, inner):
            advance(refs, t, a)
            return inner

        lax.fori_loop(axial - t, axial, body, 0)
        for c in range(components):
            state_ref[t + 1, c, axial] += bound_ref[t, c]
        return carry

    lax.fori_loop(first, last, sweep, 0)


def third_kernel(jac_ref, coef_ref, state_in_ref, edge_ref, bound_ref, after_ref, state_ref, out_ref):
    components, axial, span, _ = out_ref.shape
    rest_of_sweeps(jac_ref, coef_ref, state_ref, edge_ref, bound_ref, axial - 1, axial)

    def final(a, carry):
        for c, value in enumerate(layer_update(jac_ref, state_ref, edge_ref, coef_ref, axial, a)):
            out_ref[c, a] = value[:span]
        return carry

    lax.fori_loop(0, axial, final, 0)


def last_kernel(inv_ref, modes_a_ref, modes_b_ref, synth_ref, swept_ref, out_ref):
    components, axial, span, pitch = out_ref.shape
    field = synthesised(modes_a_ref[...] + modes_b_ref[...], synth_ref[:components * pitch])
    for c in range(components):
        for a in range(axial - 1):
            out_ref[c, a] = swept_ref[c, a]
        out_ref[c, axial - 1] = swept_ref[c, axial - 1] + inv_ref[:span] * field[:, c * pitch:(c + 1) * pitch]


def moved(x, to):
    sizes = [lax.axis_size(name) for name in AXES]
    pairs = []
    for r in range(sizes[0]):
        for s in range(sizes[1]):
            for p in range(sizes[2]):
                target = to(r, s, p)
                if all(0 <= at < size for at, size in zip(target, sizes)):
                    number = lambda at: (at[0] * sizes[1] + at[1]) * sizes[2] + at[2]
                    pairs.append((number((r, s, p)), number(target)))
    return lax.ppermute(x, AXES, pairs)


def struct(*shape):
    return jax.ShapeDtypeStruct(shape, jnp.float32)


def on_device(
    adjoint_start, source, couplings, damping, jacobians, giles_real, giles_imag, blades, mode_orders, cell_map,
):
    components, axial, span, pitch = adjoint_start.shape
    row_count, span_count, place_count = (lax.axis_size(name) for name in AXES)
    length = pitch * place_count
    assert components == COMPONENTS and components * WAVES <= pitch
    assert axial == ITERS - 1 and ITERS <= EDGE and axial * SEGMENT_LANES == pitch
    assert span_count == 2 and place_count & (place_count - 1) == 0
    wide = span + EDGE
    fields = 2 * components + 6
    groups = slots(fields + 1, components)[1][-1][0] + 1
    pairs = -(-(fields * axial + 1) // 2)
    span_tiles = pairs + -(-components * axial // EDGE)
    smem = pl.BlockSpec(memory_space=pltpu.SMEM)
    vmem = pl.BlockSpec(memory_space=pltpu.VMEM)
    hbm = pl.BlockSpec(memory_space=pltpu.HBM)
    anywhere = pl.BlockSpec(memory_space=pl.ANY)

    def call(kernel, name, outs, ins, aliases=None, scratch=(), **fixed):
        specs = [spec for spec, _ in ins]
        return pl.pallas_call(
            functools.partial(kernel, **fixed),
            out_shape=outs,
            in_specs=specs,
            out_specs=jax.tree.map(lambda _: vmem, outs),
            scratch_shapes=scratch,
            input_output_aliases=aliases or {},
            compiler_params=PARAMS,
            name=name,
        )(*[value for _, value in ins])

    coef, inv, edges, span_out, corner, right, left, table = call(
        pack_kernel, "pack",
        (
            struct(components + 6, axial, span, pitch), struct(span, pitch), struct(fields + 1, span, pitch),
            struct(span_tiles, EDGE, pitch), struct(2 * groups, EDGE, pitch), struct(groups, wide, pitch),
            struct(groups, wide, pitch), struct(pitch, pitch),
        ),
        [(hbm, blades), (hbm, adjoint_start), (hbm, source), (hbm, couplings), (hbm, damping)],
        scratch=[
            pltpu.SMEM(blades.shape, jnp.int32), pltpu.VMEM(adjoint_start.shape, jnp.float32),
            pltpu.VMEM(source.shape, jnp.float32), pltpu.VMEM(couplings.shape, jnp.float32),
            pltpu.VMEM(damping.shape, jnp.float32), pltpu.SemaphoreType.DMA((5,)),
        ],
        length=length,
    )
    corner = moved(corner, lambda r, s, p: (r, 1 - s, p))
    from_span = moved(span_out, lambda r, s, p: (r, 1 - s, p))
    right = lax.dynamic_update_slice(right, corner[:groups], (0, span, 0))
    left = lax.dynamic_update_slice(left, corner[groups:], (0, span, 0))
    from_left = moved(right, lambda r, s, p: (r, s, (p + 1) % place_count))
    from_right = moved(left, lambda r, s, p: (r, s, (p - 1) % place_count))

    jac = jacobians[0].transpose(1, 2, 0).reshape(components * components, 6)
    state_shape = struct(axial + 1, components, axial + 2, wide, pitch)
    edge_shape = struct(axial + 1, components, wide, pitch)
    coef, inv, edge_coef, state, edge, modes = call(
        first_kernel, "first_sweeps",
        (
            struct(components + 6, axial, wide, pitch), struct(wide, pitch), struct(components + 7, wide, pitch),
            state_shape, edge_shape, struct(axial * span + axial // 2 * EDGE, pitch),
        ),
        [(smem, jac)] + [(vmem, x) for x in (adjoint_start, coef, inv, edges, from_span, from_left, from_right, table)],
    )

    def summed(x):
        bit = 1
        while 2 * bit < place_count:
            x = x + moved(x, lambda r, s, p: (r, s, p ^ bit))
            bit *= 2
        if bit < place_count:
            far = moved(x, lambda r, s, p: (r - 1, s, p ^ bit))
        else:
            far = jnp.zeros_like(x)
        return x, moved(x, lambda r, s, p: (r - 1, s, p)), far

    state, edge, part = call(
        middle_kernel, "middle_sweeps", (state_shape, edge_shape, struct(span, pitch)),
        [(smem, jac)] + [(vmem, x) for x in (coef, edge_coef, state, edge, table)],
        aliases={3: 0, 4: 1},
    )
    halfway, modes_a, modes_b = summed(modes)

    giles_real, giles_imag, halfway = lax.optimization_barrier((giles_real, giles_imag, halfway))
    face = jnp.minimum(lax.axis_index("row"), row_count - 2)

    def of_face(giles):
        picked = lax.dynamic_index_in_dim(giles, face, 0, keepdims=False)
        return picked.transpose(1, 2, 0).reshape(components * components, -1)

    synth = call(
        synth_kernel, "synth", struct(-(-components * (pitch + SEGMENT_LANES) // pitch) * pitch, pitch),
        [(smem, blades), (vmem, of_face(giles_real)), (vmem, of_face(giles_imag))]
        + [(vmem, mode_orders.transpose(0, 2, 1)), (vmem, cell_map), (anywhere, halfway)],
        row_count=row_count, place_count=place_count, components=components, pitch=pitch, length=length, axial=axial,
    )
    late = call(
        link_kernel, "late_modes", struct(span, pitch),
        [(smem, jac)] + [(vmem, x) for x in (coef, inv, part, modes_a, modes_b, synth, table)],
    )
    halfway, late_a, late_b = summed(late)
    state, edge, bound = call(
        second_kernel, "second_sweeps", (state_shape, edge_shape, struct(axial, components, wide, pitch)),
        [(smem, jac)] + [(vmem, x) for x in (coef, inv, edge_coef, state, edge, modes_a, modes_b, synth)]
        + [(anywhere, late)],
        aliases={4: 0, 5: 1},
    )
    state, swept = call(
        third_kernel, "third_sweeps", (state_shape, struct(components, axial, span, pitch)),
        [(smem, jac)] + [(vmem, x) for x in (coef, state, edge, bound)] + [(anywhere, halfway)],
        aliases={2: 0},
    )
    return call(
        last_kernel, "last_boundary", struct(components, axial, span, pitch),
        [(vmem, x) for x in (inv, late_a, late_b, synth, swept)],
    )


def solution(mesh):
    placed = (
        P(None, "row", "span", "pitch"),
        P(None, "row", "span", "pitch"),
        P(None, "row", "span", "pitch"),
        P("row", "span", "pitch"),
        P("row", None, None, None),
        P(),
        P(),
        P(),
        P(),
        P("row", None),
    )
    return jax.shard_map(
        on_device,
        mesh=mesh,
        in_specs=placed,
        out_specs=P(None, "row", "span", "pitch"),
        check_vma=False,
    )
```

time: 54.6 us -> 80.1 us (1.47)
  the two profiles are of different devices: /device:TPU:1 before, /device:TPU:15 now
where the time goes in v3:
time: 80.1 us; the launch traced here: 78.6 us
  local copies, waits for them, and re-layouts  31.3 us (39%)
  starting transfers between devices  19.9 us (25%)
  Pallas kernels  19.2 us (24%)
  waiting for transfers between devices  7.12 us (9%)
  other arithmetic  0.9 us (1%)
    unnamed x69, local copies, waits for them, and re-layouts  26.4 us
    ppermute x10, starting transfers between devices, moved(): return lax.ppermute(x, AXES, pairs)  19.9 us
    pallas_call x8, Pallas kernels, call(): pl.pallas_call(functools.partial(kernel, **fixed), out_shape=outs, in_spe...  19.2 us
    ppermute x10, waiting for transfers between devices, moved(): return lax.ppermute(x, AXES, pairs)  7.12 us
    reshape x2, local copies, waits for them, and re-layouts, of_face(): return picked.transpose(1, 2, 0).reshape(components * components, -1)  2.66 us
    optimization_barrier x2, local copies, waits for them, and re-layouts, on_device(): lax.optimization_barrier((giles_real, giles_imag, halfway))  1.62 us
  transfers between devices with their start and end apart: 10, of which 4 were waited for; matrix products, arithmetic and copies ran while one was open for 7% of the time, Pallas kernels for 12%

profile of v3, /device:TPU:15, one launch (start us, length us, event | category | flops | bytes accessed | tf_op | source)
XLA Modules:
  0.0 78.6 jit_solution(17347514315395020349)
XLA Ops:
  0.0 1.0 %copy-done.8 = f32[5,4,32,128]{3,2,1,0:T(8,128)S(1)} copy-done((f32[5,4,32,128]{3,2,1,0:T(8,128)S(1)}, f32[5,4,32,128]{3,2,1,0:T(8,128)}, u32[]{:S(2)}) %copy-start.8) | copy-done | bytes 327704
  1.0 1.0 %copy-done.12 = f32[6,4,32,128]{3,2,1,0:T(8,128)S(1)} copy-done((f32[6,4,32,128]{3,2,1,0:T(8,128)S(1)}, f32[6,4,32,128]{3,2,1,0:T(8,128)}, u32[]{:S(2)}) %copy-start.12) | copy-done | bytes 393240
  2.0 1.0 %copy-done.13 = f32[5,4,32,128]{3,2,1,0:T(8,128)S(1)} copy-done((f32[5,4,32,128]{3,2,1,0:T(8,128)S(1)}, f32[5,4,32,128]{3,2,1,0:T(8,128)}, u32[]{:S(2)}) %copy-start.13) | copy-done | bytes 327704
  2.9 0.8 %copy-done.19 = f32[4,32,128]{2,1,0:T(8,128)S(1)} copy-done((f32[4,32,128]{2,1,0:T(8,128)S(1)}, f32[4,32,128]{2,1,0:T(8,128)}, u32[]{:S(2)}) %copy-start.19) | copy-done | bytes 65560
  3.8 0.7 copy-done.32
  4.4 1.5 %pack.1 = (f32[11,4,32,128]{3,2,1,0:T(8,128)S(1)}, f32[32,128]{1,0:T(8,128)S(1)}, f32[17,32,128]{2,1,0:T(8,128)S(1)}, f32[36,8,128]{2,1,0:T(8,128)S(1)}, f32[6,8...) custom-call(s32[4]{0:T(128)S(1)} %copy-done.32, ...), custom_call_target="tpu_custom_call" | custom-call | tf_op jit(solution)/shard_map/pack/pallas_call | solution.py:550
  6.0 0.9 %copy-done.10 = f32[11,4,32,128]{3,2,1,0:T(8,128)} copy-done((f32[11,4,32,128]{3,2,1,0:T(8,128)}, f32[11,4,32,128]{3,2,1,0:T(8,128)S(1)}, u32[]{:S(2)}) %copy-start.10) | copy-done | bytes 720920
  6.8 0.7 copy-done.14
  7.6 0.2 collective-permute-start.1
  7.8 1.2 %collective-permute-start = (f32[36,8,128]{2,1,0:T(8,128)S(1)}, f32[36,8,128]{2,1,0:T(8,128)S(1)}, u32[]{:S(2)}, u32[]{:S(2)}) collective-permute-start(f32[36,8,128]{2,1,0:T(8,128)S(1)} %get-tuple-element.32), channel_id=1, source_target_pairs={{0,4},{1,5},{2,6},{3,7},{4,0},{5,1},{6,2},{7,3},{8,12},{9,13},{10,... | collective-permute-start | bytes 442376 | tf_op jit(solution)/shard_map/ppermute | solution.py:522
  9.0 1.2 %collective-permute-done.1 = f32[6,8,128]{2,1,0:T(8,128)S(1)} collective-permute-done((f32[6,8,128]{2,1,0:T(8,128)S(1)}, f32[6,8,128]{2,1,0:T(8,128)S(1)}, u32[]{:S(2)}, u32[]{:S(2)}) %collective-permute-start.1) | collective-permute-done | bytes 24608 | tf_op jit(solution)/shard_map/ppermute | solution.py:522
  10.2 0.2 collective-permute-start.3
  10.4 1.3 %collective-permute-start.2 = (f32[3,40,128]{2,1,0:T(8,128)S(1)}, f32[3,40,128]{2,1,0:T(8,128)S(1)}, u32[]{:S(2)}, u32[]{:S(2)}) collective-permute-start(f32[3,40,128]{2,1,0:T(8,128)S(1)} %get-tuple-element.54), channel_id=1, source_target_pairs={{0,1},{1,2},{2,3},{3,0},{4,5},{5,6},{6,7},{7,4},{8,9},{9,10},{10,1... | collective-permute-start | bytes 184328 | tf_op jit(solution)/shard_map/ppermute | solution.py:522
  11.7 0.7 copy.27
  12.4 1.2 %collective-permute-done.3.from_right_ref = f32[3,40,128]{2,1,0:T(8,128)S(1)} collective-permute-done((f32[3,40,128]{2,1,0:T(8,128)S(1)}, f32[3,40,128]{2,1,0:T(8,128)S(1)}, u32[]{:S(2)}, u32[]{:S(2)}) %collective-permute-start.3) | collective-permute-done | bytes 61472 | tf_op jit(solution)/shard_map/ppermute | solution.py:522
  13.6 0.6 copy-done.22
  14.2 1.9 %collective-permute-done.2.from_left_ref = f32[3,40,128]{2,1,0:T(8,128)S(1)} collective-permute-done((f32[3,40,128]{2,1,0:T(8,128)S(1)}, f32[3,40,128]{2,1,0:T(8,128)S(1)}, u32[]{:S(2)}, u32[]{:S(2)}) %collective-permute-start.2) | collective-permute-done | bytes 61472 | tf_op jit(solution)/shard_map/ppermute | solution.py:522
  16.2 0.6 copy-done.24
  16.8 0.0 collective-permute-done.span_ref
  16.8 1.0 %copy-done.9 = f32[5,4,32,128]{3,2,1,0:T(8,128)S(1)} copy-done((f32[5,4,32,128]{3,2,1,0:T(8,128)S(1)}, f32[5,4,32,128]{3,2,1,0:T(8,128)}, u32[]{:S(2)}) %copy-start.9) | copy-done | bytes 327704
  17.8 1.1 %copy-done.11 = f32[11,4,32,128]{3,2,1,0:T(8,128)S(1)} copy-done((f32[11,4,32,128]{3,2,1,0:T(8,128)S(1)}, f32[11,4,32,128]{3,2,1,0:T(8,128)}, u32[]{:S(2)}) %copy-start.11) | copy-done | bytes 720920
  18.9 1.0 %copy-done.15 = f32[17,32,128]{2,1,0:T(8,128)S(1)} copy-done((f32[17,32,128]{2,1,0:T(8,128)S(1)}, f32[17,32,128]{2,1,0:T(8,128)}, u32[]{:S(2)}) %copy-start.15) | copy-done | bytes 278552
  19.8 0.8 %copy-done.23 = f32[3,40,128]{2,1,0:T(8,128)S(1)} copy-done((f32[3,40,128]{2,1,0:T(8,128)S(1)}, f32[3,40,128]{2,1,0:T(8,128)}, u32[]{:S(2)}) %copy-start.23) | copy-done | bytes 61464
  20.7 0.8 %copy-done.25 = f32[3,40,128]{2,1,0:T(8,128)S(1)} copy-done((f32[3,40,128]{2,1,0:T(8,128)S(1)}, f32[3,40,128]{2,1,0:T(8,128)}, u32[]{:S(2)}) %copy-start.25) | copy-done | bytes 61464
  21.5 0.7 copy-done.27
  22.2 4.7 %first_sweeps.1 = (f32[11,4,40,128]{3,2,1,0:T(8,128)S(1)}, f32[40,128]{1,0:T(8,128)S(1)}, f32[12,40,128]{2,1,0:T(8,128)S(1)}, f32[5,5,6,40,128]{4,3,2,1,0:T(8,12...) custom-call(f32[25,6]{1,0:T(8,128)S(1)} %reshape.12.jac_ref, f32[5,4,32,128]{3,2,1,0:T(8,128)S(1)} %copy-done.9, ...), custom_call_target="tpu_custom_call" | custom-call | tf_op jit(solution)/shard_map/first_sweeps/pallas_call | solution.py:550
  27.0 0.9 %copy-done = f32[11,4,40,128]{3,2,1,0:T(8,128)} copy-done((f32[11,4,40,128]{3,2,1,0:T(8,128)}, f32[11,4,40,128]{3,2,1,0:T(8,128)S(1)}, u32[]{:S(2)}) %copy-start) | copy-done | bytes 901144
  27.9 0.8 copy-done.4
  28.7 0.6 copy-done.16
  29.3 2.6 %collective-permute-start.4 = (f32[144,128]{1,0:T(8,128)}, f32[144,128]{1,0:T(8,128)S(1)}, u32[]{:S(2)}, u32[]{:S(2)}) collective-permute-start(f32[144,128]{1,0:T(8,128)} %get-tuple-element.43), channel_id=1, source_target_pairs={{0,1},{1,0},{2,3},{3,2},{4,5},{5,4},{6,7},{7,6},{8,9},{9,8},{10,11... | collective-permute-start | bytes 221192 | tf_op jit(solution)/shard_map/ppermute | solution.py:522
  31.9 1.2 %copy-done.1 = f32[11,4,40,128]{3,2,1,0:T(8,128)S(1)} copy-done((f32[11,4,40,128]{3,2,1,0:T(8,128)S(1)}, f32[11,4,40,128]{3,2,1,0:T(8,128)}, u32[]{:S(2)}) %copy-start.1) | copy-done | bytes 901144
  33.0 1.0 %copy-done.5 = f32[5,5,40,128]{3,2,1,0:T(8,128)S(1)} copy-done((f32[5,5,40,128]{3,2,1,0:T(8,128)S(1)}, f32[5,5,40,128]{3,2,1,0:T(8,128)}, u32[]{:S(2)}) %copy-start.5) | copy-done | bytes 512024
  34.1 2.6 %middle_sweeps.1 = (f32[5,5,6,40,128]{4,3,2,1,0:T(8,128)S(1)}, f32[5,5,40,128]{3,2,1,0:T(8,128)S(1)}, f32[32,128]{1,0:T(8,128)S(1)}) custom-call(f32[25,6]{1,0:T(8,128)S(1)} %reshape.12.jac_ref, f32[11,4,40,128]{3,2,1,0:T(8,128)S(1)} %copy-done.1, f32[12,40,128]{2,1,0:T(8,128)S(1)} %get-tuple-element.39.edge_coef_ref, ...), custom_call_target="tpu_custom_call", output_to_operand_aliasing={{0}: (3, {}), {1}: (4, {})} | custom-call | tf_op jit(solution)/shard_map/middle_sweeps/pallas_call | solution.py:550
  36.7 0.8 %copy-done.6 = f32[5,5,40,128]{3,2,1,0:T(8,128)} copy-done((f32[5,5,40,128]{3,2,1,0:T(8,128)}, f32[5,5,40,128]{3,2,1,0:T(8,128)S(1)}, u32[]{:S(2)}) %copy-start.6) | copy-done | bytes 512024
  37.5 0.0 collective-permute-done.4
  37.5 0.9 %add.11.after_ref = f32[144,128]{1,0:T(8,128)S(1)} add(f32[144,128]{1,0:T(8,128)} %get-tuple-element.43, f32[144,128]{1,0:T(8,128)S(1)} %collective-permute-done.4) | non-fusion elementwise | flops 18432 | bytes 221184 | tf_op jit(solution)/shard_map/add | solution.py:598
  38.4 4.4 %collective-permute-start.6 = (f32[144,128]{1,0:T(8,128)S(1)}, f32[144,128]{1,0:T(8,128)S(1)}, u32[]{:S(2)}, u32[]{:S(2)}) collective-permute-start(f32[144,128]{1,0:T(8,128)S(1)} %add.11.after_ref), channel_id=1, source_target_pairs={{8,2},{9,3},{10,0},{11,1},{12,6},{13,7},{14,4},{15,5},{16,10},{17,... | collective-permute-start | bytes 221192 | tf_op jit(solution)/shard_map/ppermute | solution.py:522
  42.8 3.8 %collective-permute-start.5 = (f32[144,128]{1,0:T(8,128)S(1)}, f32[144,128]{1,0:T(8,128)}, u32[]{:S(2)}, u32[]{:S(2)}) collective-permute-start(f32[144,128]{1,0:T(8,128)S(1)} %add.11.after_ref), channel_id=1, source_target_pairs={{8,0},{9,1},{10,2},{11,3},{12,4},{13,5},{14,6},{15,7},{16,8},{17,9... | collective-permute-start | bytes 221192 | tf_op jit(solution)/shard_map/ppermute | solution.py:522
  46.5 0.8 %copy.19 = f32[3,64,5,5]{1,3,2,0:T(8,128)S(1)} copy(f32[3,64,5,5]{1,0,3,2:T(4,128)} %param.15) | data formatting | bytes 38400 | tf_op jit(solution)/shard_map/optimization_barrier | solution.py:613
  47.4 0.8 %copy.20 = f32[3,64,5,5]{1,3,2,0:T(8,128)S(1)} copy(f32[3,64,5,5]{1,0,3,2:T(4,128)} %param.16) | data formatting | bytes 38400 | tf_op jit(solution)/shard_map/optimization_barrier | solution.py:613
  48.2 0.6 dynamic-slice_bitcast_fusion
  48.8 1.3 %reshape.11.giles_im_ref = f32[25,64]{1,0:T(8,128)} reshape(f32[5,5,64]{2,1,0:T(8,128)} %get-tuple-element.55) | data formatting | bytes 12800 | tf_op jit(solution)/shard_map/reshape | solution.py:618
  50.1 1.3 %reshape.10.giles_re_ref = f32[25,64]{1,0:T(8,128)} reshape(f32[5,5,64]{2,1,0:T(8,128)} %get-tuple-element.56) | data formatting | bytes 12800 | tf_op jit(solution)/shard_map/reshape | solution.py:618
  51.5 0.7 copy-done.20
  52.2 0.7 copy-done.21
  52.9 0.7 copy-done.33
  53.5 0.9 %synth.1.synth_ref = f32[896,128]{1,0:T(8,128)S(1)} custom-call(s32[4]{0:T(128)S(1)} %copy-done.33, f32[25,64]{1,0:T(8,128)S(1)} %copy-done.21, f32[25,64]{1,0:T(8,128)S(1)} %copy-done.20, s32[3,2,64]{2,1,0:T(2,128)S(1)} %bitcast.14, s32[1,512]{1,0:T(1,128)S(1)} %copy-done.31, f32[144,128]{1,0:T(8,128)S(1)} %add.11.after_ref), custom_call_target="tpu_custom_call" | custom-call | tf_op jit(solution)/shard_map/synth/pallas_call | solution.py:550
  54.5 0.0 collective-permute-done.6.modes_b_ref
  54.5 0.0 collective-permute-done.5.modes_a_ref
  54.5 1.2 %copy-done.2 = f32[11,4,40,128]{3,2,1,0:T(8,128)S(1)} copy-done((f32[11,4,40,128]{3,2,1,0:T(8,128)S(1)}, f32[11,4,40,128]{3,2,1,0:T(8,128)}, u32[]{:S(2)}) %copy-start.2) | copy-done | bytes 901144
  55.7 0.7 copy-done.17
  56.4 0.7 copy-done.29
  57.1 2.2 %late_modes.1.after_ref = f32[32,128]{1,0:T(8,128)S(1)} custom-call(f32[25,6]{1,0:T(8,128)S(1)} %reshape.12.jac_ref, f32[11,4,40,128]{3,2,1,0:T(8,128)S(1)} %copy-done.2, f32[40,128]{1,0:T(8,128)S(1)} %copy-done.17, f32[32,128]{1,0:T(8,128)S(1)} %copy-done.29, f32[144,128]{1,0:T(8,128)} %collective-permute-done.5.modes_a_ref, ...), custom_call_target="tpu_custom_call" | custom-call | tf_op jit(solution)/shard_map/late_modes/pallas_call | solution.py:550
  59.3 0.0 collective-permute-start.7
  59.3 2.8 %collective-permute-done.7 = f32[32,128]{1,0:T(8,128)S(1)} collective-permute-done((f32[32,128]{1,0:T(8,128)S(1)}, f32[32,128]{1,0:T(8,128)S(1)}, u32[]{:S(2)}, u32[]{:S(2)}) %collective-permute-start.7) | collective-permute-done | bytes 16416 | tf_op jit(solution)/shard_map/ppermute | solution.py:522
  62.1 5.0 %collective-permute-start.9 = (f32[32,128]{1,0:T(8,128)S(1)}, f32[32,128]{1,0:T(8,128)S(1)}, u32[]{:S(2)}, u32[]{:S(2)}) collective-permute-start(f32[32,128]{1,0:T(8,128)S(1)} %add.13.after_ref), channel_id=1, source_target_pairs={{8,2},{9,3},{10,0},{11,1},{12,6},{13,7},{14,4},{15,5},{16,10},{17,... | collective-permute-start | bytes 49160 | tf_op jit(solution)/shard_map/ppermute | solution.py:522
  67.1 1.3 %collective-permute-start.8 = (f32[32,128]{1,0:T(8,128)S(1)}, f32[32,128]{1,0:T(8,128)S(1)}, u32[]{:S(2)}, u32[]{:S(2)}) collective-permute-start(f32[32,128]{1,0:T(8,128)S(1)} %add.13.after_ref), channel_id=1, source_target_pairs={{8,0},{9,1},{10,2},{11,3},{12,4},{13,5},{14,6},{15,7},{16,8},{17,9... | collective-permute-start | bytes 49160 | tf_op jit(solution)/shard_map/ppermute | solution.py:522
  68.4 1.2 %copy-done.3 = f32[11,4,40,128]{3,2,1,0:T(8,128)S(1)} copy-done((f32[11,4,40,128]{3,2,1,0:T(8,128)S(1)}, f32[11,4,40,128]{3,2,1,0:T(8,128)}, u32[]{:S(2)}) %copy-start.3) | copy-done | bytes 901144
  69.6 1.0 %copy-done.7 = f32[5,5,40,128]{3,2,1,0:T(8,128)S(1)} copy-done((f32[5,5,40,128]{3,2,1,0:T(8,128)S(1)}, f32[5,5,40,128]{3,2,1,0:T(8,128)}, u32[]{:S(2)}) %copy-start.7) | copy-done | bytes 512024
  70.6 0.7 copy-done.18
  71.4 3.4 %second_sweeps.1 = (f32[5,5,6,40,128]{4,3,2,1,0:T(8,128)S(1)}, f32[5,5,40,128]{3,2,1,0:T(8,128)S(1)}, f32[4,5,40,128]{3,2,1,0:T(8,128)S(1)}) custom-call(f32[25,6]{1,0:T(8,128)S(1)} %reshape.12.jac_ref, f32[11,4,40,128]{3,2,1,0:T(8,128)S(1)} %copy-done.3, f32[40,128]{1,0:T(8,128)S(1)} %copy-done.18, ...), custom_call_target="tpu_custom_call", output_to_operand_aliasing={{0}: (4, {}), {1}: (5, {})} | custom-call | tf_op jit(solution)/shard_map/second_sweeps/pallas_call | solution.py:550
  74.8 2.6 %third_sweeps.1 = (f32[5,5,6,40,128]{4,3,2,1,0:T(8,128)S(1)}, f32[5,4,32,128]{3,2,1,0:T(8,128)S(1)}) custom-call(f32[25,6]{1,0:T(8,128)S(1)} %reshape.12.jac_ref, f32[11,4,40,128]{3,2,1,0:T(8,128)S(1)} %copy-done.3, f32[5,5,6,40,128]{4,3,2,1,0:T(8,128)S(1)} %get-tuple-element.49.state_in_ref, ...), custom_call_target="tpu_custom_call", output_to_operand_aliasing={{0}: (2, {})} | custom-call | tf_op jit(solution)/shard_map/third_sweeps/pallas_call | solution.py:550
  77.4 0.0 collective-permute-done.9.modes_b_ref
  77.4 1.2 %last_boundary.1 = f32[5,4,32,128]{3,2,1,0:T(8,128)} custom-call(f32[40,128]{1,0:T(8,128)S(1)} %copy-done.18, f32[32,128]{1,0:T(8,128)S(1)} %collective-permute-done.8.modes_a_ref, f32[32,128]{1,0:T(8,128)S(1)} %collective-permute-done.9.modes_b_ref, f32[896,128]{1,0:T(8,128)S(1)} %synth.1.synth_ref, f32[5,4,32,128]{3,2,1,0:T(8,128)S(1)} %get-tuple-element.52.swept_ref), custom_call_target="tpu_custom_call" | custom-call | tf_op jit(solution)/shard_map/last_boundary/pallas_call | solution.py:550
  (42 shorter events, 0.1 us)
Async XLA Ops:
  0.0 1.0 %copy-start.8 = (f32[5,4,32,128]{3,2,1,0:T(8,128)S(1)}, f32[5,4,32,128]{3,2,1,0:T(8,128)}, u32[]{:S(2)}) copy-start(f32[5,4,32,128]{3,2,1,0:T(8,128)} %adjoint_ref.1) | copy-start | bytes 983044
  1.0 1.0 %copy-start.12 = (f32[6,4,32,128]{3,2,1,0:T(8,128)S(1)}, f32[6,4,32,128]{3,2,1,0:T(8,128)}, u32[]{:S(2)}) copy-start(f32[6,4,32,128]{3,2,1,0:T(8,128)} %couplings_hbm.1) | copy-start | bytes 1179652
  2.0 1.0 %copy-start.13 = (f32[5,4,32,128]{3,2,1,0:T(8,128)S(1)}, f32[5,4,32,128]{3,2,1,0:T(8,128)}, u32[]{:S(2)}) copy-start(f32[5,4,32,128]{3,2,1,0:T(8,128)} %source_hbm.1) | copy-start | bytes 983044
  2.9 0.8 %copy-start.19 = (f32[4,32,128]{2,1,0:T(8,128)S(1)}, f32[4,32,128]{2,1,0:T(8,128)}, u32[]{:S(2)}) copy-start(f32[4,32,128]{2,1,0:T(8,128)} %damping_hbm.1) | copy-start | bytes 196612
  3.8 0.7 copy-start.32
  6.0 0.9 %copy-start.10 = (f32[11,4,32,128]{3,2,1,0:T(8,128)}, f32[11,4,32,128]{3,2,1,0:T(8,128)S(1)}, u32[]{:S(2)}) copy-start(f32[11,4,32,128]{3,2,1,0:T(8,128)S(1)} %get-tuple-element.29.coef_in_ref) | copy-start | bytes 2162692
  6.8 0.7 copy-start.14
  7.6 4.9 %copy-start.26 = (f32[32,128]{1,0:T(8,128)}, f32[32,128]{1,0:T(8,128)S(1)}, u32[]{:S(2)}) copy-start(f32[32,128]{1,0:T(8,128)S(1)} %get-tuple-element.30.inv_in_ref) | copy-start | bytes 49156
  7.6 2.7 %collective-permute-start.1 = (f32[6,8,128]{2,1,0:T(8,128)S(1)}, f32[6,8,128]{2,1,0:T(8,128)S(1)}, u32[]{:S(2)}, u32[]{:S(2)}) collective-permute-start(f32[6,8,128]{2,1,0:T(8,128)S(1)} %get-tuple-element.34), channel_id=1, source_target_pairs={{0,4},{1,5},{2,6},{3,7},{4,0},{5,1},{6,2},{7,3},{8,12},{9,13},{10,... | collective-permute-start | bytes 73736 | tf_op jit(solution)/shard_map/ppermute | solution.py:522
  7.8 9.0 %collective-permute-start = (f32[36,8,128]{2,1,0:T(8,128)S(1)}, f32[36,8,128]{2,1,0:T(8,128)S(1)}, u32[]{:S(2)}, u32[]{:S(2)}) collective-permute-start(f32[36,8,128]{2,1,0:T(8,128)S(1)} %get-tuple-element.32), channel_id=1, source_target_pairs={{0,4},{1,5},{2,6},{3,7},{4,0},{5,1},{6,2},{7,3},{8,12},{9,13},{10,... | collective-permute-start | bytes 442376 | tf_op jit(solution)/shard_map/ppermute | solution.py:522
  10.2 3.4 %collective-permute-start.3 = (f32[3,40,128]{2,1,0:T(8,128)S(1)}, f32[3,40,128]{2,1,0:T(8,128)S(1)}, u32[]{:S(2)}, u32[]{:S(2)}) collective-permute-start(f32[3,40,128]{2,1,0:T(8,128)S(1)} %get-tuple-element.53), channel_id=1, source_target_pairs={{0,3},{1,0},{2,1},{3,2},{4,7},{5,4},{6,5},{7,6},{8,11},{9,8},{10,9... | collective-permute-start | bytes 184328 | tf_op jit(solution)/shard_map/ppermute | solution.py:522
  10.4 5.8 %collective-permute-start.2 = (f32[3,40,128]{2,1,0:T(8,128)S(1)}, f32[3,40,128]{2,1,0:T(8,128)S(1)}, u32[]{:S(2)}, u32[]{:S(2)}) collective-permute-start(f32[3,40,128]{2,1,0:T(8,128)S(1)} %get-tuple-element.54), channel_id=1, source_target_pairs={{0,1},{1,2},{2,3},{3,0},{4,5},{5,6},{6,7},{7,4},{8,9},{9,10},{10,1... | collective-permute-start | bytes 184328 | tf_op jit(solution)/shard_map/ppermute | solution.py:522
  13.6 0.6 copy-start.22
  16.2 0.6 copy-start.24
  16.8 1.0 %copy-start.9 = (f32[5,4,32,128]{3,2,1,0:T(8,128)S(1)}, f32[5,4,32,128]{3,2,1,0:T(8,128)}, u32[]{:S(2)}) copy-start(f32[5,4,32,128]{3,2,1,0:T(8,128)} %adjoint_ref.1) | copy-start | bytes 983044
  17.8 1.1 %copy-start.11 = (f32[11,4,32,128]{3,2,1,0:T(8,128)S(1)}, f32[11,4,32,128]{3,2,1,0:T(8,128)}, u32[]{:S(2)}) copy-start(f32[11,4,32,128]{3,2,1,0:T(8,128)} %copy-done.10) | copy-start | bytes 2162692
  18.9 1.0 %copy-start.15 = (f32[17,32,128]{2,1,0:T(8,128)S(1)}, f32[17,32,128]{2,1,0:T(8,128)}, u32[]{:S(2)}) copy-start(f32[17,32,128]{2,1,0:T(8,128)} %copy-done.14) | copy-start | bytes 835588
  19.8 0.8 %copy-start.23 = (f32[3,40,128]{2,1,0:T(8,128)S(1)}, f32[3,40,128]{2,1,0:T(8,128)}, u32[]{:S(2)}) copy-start(f32[3,40,128]{2,1,0:T(8,128)} %copy-done.22) | copy-start | bytes 184324
  20.7 0.8 %copy-start.25 = (f32[3,40,128]{2,1,0:T(8,128)S(1)}, f32[3,40,128]{2,1,0:T(8,128)}, u32[]{:S(2)}) copy-start(f32[3,40,128]{2,1,0:T(8,128)} %copy-done.24) | copy-start | bytes 184324
  21.5 0.7 copy-start.27
  27.0 0.9 %copy-start = (f32[11,4,40,128]{3,2,1,0:T(8,128)}, f32[11,4,40,128]{3,2,1,0:T(8,128)S(1)}, u32[]{:S(2)}) copy-start(f32[11,4,40,128]{3,2,1,0:T(8,128)S(1)} %get-tuple-element.38.coef_ref) | copy-start | bytes 2703364
  27.9 0.8 copy-start.4
  28.7 0.6 copy-start.16
  29.3 22.2 %copy-start.30 = (s32[3,64,2]{1,2,0:T(2,128)S(1)}, s32[3,64,2]{1,2,0:T(2,128)}, u32[]{:S(2)}) copy-start(s32[3,64,2]{1,2,0:T(2,128)} %param.18) | copy-start | bytes 4612
  29.3 22.2 %copy-start.31 = (s32[1,512]{1,0:T(1,128)S(1)}, s32[1,512]{1,0:T(1,128)}, u32[]{:S(2)}) copy-start(s32[1,512]{1,0:T(1,128)} %cells_ref.1) | copy-start | bytes 6148
  29.3 8.2 %collective-permute-start.4 = (f32[144,128]{1,0:T(8,128)}, f32[144,128]{1,0:T(8,128)S(1)}, u32[]{:S(2)}, u32[]{:S(2)}) collective-permute-start(f32[144,128]{1,0:T(8,128)} %get-tuple-element.43), channel_id=1, source_target_pairs={{0,1},{1,0},{2,3},{3,2},{4,5},{5,4},{6,7},{7,6},{8,9},{9,8},{10,11... | collective-permute-start | bytes 221192 | tf_op jit(solution)/shard_map/ppermute | solution.py:522
  31.9 1.2 %copy-start.1 = (f32[11,4,40,128]{3,2,1,0:T(8,128)S(1)}, f32[11,4,40,128]{3,2,1,0:T(8,128)}, u32[]{:S(2)}) copy-start(f32[11,4,40,128]{3,2,1,0:T(8,128)} %copy-done) | copy-start | bytes 2703364
  33.0 1.0 %copy-start.5 = (f32[5,5,40,128]{3,2,1,0:T(8,128)S(1)}, f32[5,5,40,128]{3,2,1,0:T(8,128)}, u32[]{:S(2)}) copy-start(f32[5,5,40,128]{3,2,1,0:T(8,128)} %copy-done.4) | copy-start | bytes 1536004
  36.7 0.8 %copy-start.6 = (f32[5,5,40,128]{3,2,1,0:T(8,128)}, f32[5,5,40,128]{3,2,1,0:T(8,128)S(1)}, u32[]{:S(2)}) copy-start(f32[5,5,40,128]{3,2,1,0:T(8,128)S(1)} %get-tuple-element.48.edge_in_ref) | copy-start | bytes 1536004
  37.5 0.9 %copy-start.28 = (f32[32,128]{1,0:T(8,128)}, f32[32,128]{1,0:T(8,128)S(1)}, u32[]{:S(2)}) copy-start(f32[32,128]{1,0:T(8,128)S(1)} %get-tuple-element.42.part_ref) | copy-start | bytes 49156
  38.4 16.1 %collective-permute-start.6 = (f32[144,128]{1,0:T(8,128)S(1)}, f32[144,128]{1,0:T(8,128)S(1)}, u32[]{:S(2)}, u32[]{:S(2)}) collective-permute-start(f32[144,128]{1,0:T(8,128)S(1)} %add.11.after_ref), channel_id=1, source_target_pairs={{8,2},{9,3},{10,0},{11,1},{12,6},{13,7},{14,4},{15,5},{16,10},{17,... | collective-permute-start | bytes 221192 | tf_op jit(solution)/shard_map/ppermute | solution.py:522
  42.8 11.7 %collective-permute-start.5 = (f32[144,128]{1,0:T(8,128)S(1)}, f32[144,128]{1,0:T(8,128)}, u32[]{:S(2)}, u32[]{:S(2)}) collective-permute-start(f32[144,128]{1,0:T(8,128)S(1)} %add.11.after_ref), channel_id=1, source_target_pairs={{8,0},{9,1},{10,2},{11,3},{12,4},{13,5},{14,6},{15,7},{16,8},{17,9... | collective-permute-start | bytes 221192 | tf_op jit(solution)/shard_map/ppermute | solution.py:522
  51.5 0.7 copy-start.20
  52.2 0.7 copy-start.21
  52.9 0.7 copy-start.33
  54.5 1.2 %copy-start.2 = (f32[11,4,40,128]{3,2,1,0:T(8,128)S(1)}, f32[11,4,40,128]{3,2,1,0:T(8,128)}, u32[]{:S(2)}) copy-start(f32[11,4,40,128]{3,2,1,0:T(8,128)} %copy-done) | copy-start | bytes 2703364
  55.7 0.7 copy-start.17
  56.4 0.7 copy-start.29
  59.3 2.8 %collective-permute-start.7 = (f32[32,128]{1,0:T(8,128)S(1)}, f32[32,128]{1,0:T(8,128)S(1)}, u32[]{:S(2)}, u32[]{:S(2)}) collective-permute-start(f32[32,128]{1,0:T(8,128)S(1)} %late_modes.1.after_ref), channel_id=1, source_target_pairs={{0,1},{1,0},{2,3},{3,2},{4,5},{5,4},{6,7},{7,6},{8,9},{9,8},{10,11... | collective-permute-start | bytes 49160 | tf_op jit(solution)/shard_map/ppermute | solution.py:522
  62.1 15.3 %collective-permute-start.9 = (f32[32,128]{1,0:T(8,128)S(1)}, f32[32,128]{1,0:T(8,128)S(1)}, u32[]{:S(2)}, u32[]{:S(2)}) collective-permute-start(f32[32,128]{1,0:T(8,128)S(1)} %add.13.after_ref), channel_id=1, source_target_pairs={{8,2},{9,3},{10,0},{11,1},{12,6},{13,7},{14,4},{15,5},{16,10},{17,... | collective-permute-start | bytes 49160 | tf_op jit(solution)/shard_map/ppermute | solution.py:522
  67.1 10.3 %collective-permute-start.8 = (f32[32,128]{1,0:T(8,128)S(1)}, f32[32,128]{1,0:T(8,128)S(1)}, u32[]{:S(2)}, u32[]{:S(2)}) collective-permute-start(f32[32,128]{1,0:T(8,128)S(1)} %add.13.after_ref), channel_id=1, source_target_pairs={{8,0},{9,1},{10,2},{11,3},{12,4},{13,5},{14,6},{15,7},{16,8},{17,9... | collective-permute-start | bytes 49160 | tf_op jit(solution)/shard_map/ppermute | solution.py:522
  68.4 1.2 %copy-start.3 = (f32[11,4,40,128]{3,2,1,0:T(8,128)S(1)}, f32[11,4,40,128]{3,2,1,0:T(8,128)}, u32[]{:S(2)}) copy-start(f32[11,4,40,128]{3,2,1,0:T(8,128)} %copy-done) | copy-start | bytes 2703364
  69.6 1.0 %copy-start.7 = (f32[5,5,40,128]{3,2,1,0:T(8,128)S(1)}, f32[5,5,40,128]{3,2,1,0:T(8,128)}, u32[]{:S(2)}) copy-start(f32[5,5,40,128]{3,2,1,0:T(8,128)} %copy-done.6) | copy-start | bytes 1536004
  70.6 0.7 copy-start.18

commit v4 on v3

--- a/solution.py
+++ b/solution.py
@@ -20,7 +20,11 @@
 HALF = EDGE // 2
 SEGMENT_LANES = 4 * EDGE
 EXACT = lax.Precision.HIGHEST
-PARAMS = pltpu.CompilerParams(vmem_limit_bytes=40 * 1024 * 1024)
+MIB = 1024 * 1024
+
+
+def params(limit):
+    return pltpu.CompilerParams(vmem_limit_bytes=limit)
 
 
 def lanes(shape):
@@ -38,10 +42,10 @@
     return component, jnp.where(sine, wave - (COSINES - 1), wave), sine
 
 
-def mode_number(mode, blades_ref, face):
+def mode_number(mode, blades):
     high = ((mode + ORDER_MAX) * 13) >> 6
     low = mode - BASE * high
-    return high * blades_ref[face] + low * blades_ref[face + 1]
+    return high * blades[0] + low * blades[1]
 
 
 def waves(products, length):
@@ -91,16 +95,16 @@
 
 
 def pack_kernel(
-    blades_hbm, adjoint_hbm, source_hbm, couplings_hbm, damping_hbm,
-    coef_ref, inv_ref, edges_ref, span_ref, corner_ref, right_ref, left_ref, table_ref,
-    blades_ref, adjoint_ref, source_ref, couplings_ref, damping_ref, sems, *, length,
+    blades_hbm, jacobians_hbm, adjoint_hbm, source_hbm, couplings_hbm, damping_hbm,
+    adjoint_ref, coef_ref, inv_ref, edges_ref, span_ref, corner_ref, right_ref, left_ref, table_ref, rows_ref,
+    blades_ref, jacobians_ref, source_ref, couplings_ref, damping_ref, sems, *, row_count, length,
 ):
     components, axial, span, pitch = adjoint_ref.shape
     copies = [
         pltpu.make_async_copy(src, dst, sems.at[n])
         for n, (src, dst) in enumerate((
             (couplings_hbm, couplings_ref), (damping_hbm, damping_ref), (source_hbm, source_ref),
-            (adjoint_hbm, adjoint_ref), (blades_hbm, blades_ref),
+            (adjoint_hbm, adjoint_ref), (blades_hbm, blades_ref), (jacobians_hbm, jacobians_ref),
         ))
     ]
     for copy in copies:
@@ -166,9 +170,20 @@
 
     copies[4].wait()
     component, mode, sine = column(lanes((pitch, pitch)))
-    number = mode_number(mode, blades_ref, jnp.maximum(row - 1, 0))
+    face = jnp.maximum(row - 1, 0)
+    number = mode_number(mode, (blades_ref[face], blades_ref[face + 1]))
     cos_table, sin_table = waves(number * (place * pitch + rows((pitch, pitch))), length)
     table_ref[...] = jnp.where(component < components, jnp.where(sine, sin_table, cos_table), 0.0)
+    copies[5].wait()
+    entries = 6 * components * components
+    for b in range(components):
+        for c in range(components):
+            for d in range(6):
+                entry = jnp.full((1, pitch), jacobians_ref[b, c, 0, d], jnp.float32)
+                rows_ref[pl.ds((b * components + c) * 6 + d, 1), :] = entry
+    face = jnp.minimum(row, row_count - 2)
+    for n in range(2):
+        rows_ref[pl.ds(entries + n, 1), :] = jnp.full((1, pitch), blades_ref[face + n].astype(jnp.float32), jnp.float32)
 
 
 def projected(strips, table):
@@ -188,7 +203,7 @@
 
 
 def synth_kernel(
-    blades_ref, giles_re_ref, giles_im_ref, orders_ref, cells_ref, after_ref, synth_ref,
+    rows_ref, giles_re_ref, giles_im_ref, orders_ref, cells_ref, after_ref, synth_ref, sums_ref,
     *, row_count, place_count, components, pitch, length, axial,
 ):
     row, place = lax.axis_index("row"), lax.axis_index("pitch")
@@ -201,8 +216,12 @@
     plain = jnp.where(same, 1.0, 0.0)
     signed = jnp.where(tag < 0, -plain, plain)
     dims = (((1,), (1,)), ((), ()))
-    sums_re = lax.dot_general(giles_re_ref[...], plain, dims, precision=EXACT, preferred_element_type=jnp.float32)
-    sums_im = lax.dot_general(giles_im_ref[...], signed, dims, precision=EXACT, preferred_element_type=jnp.float32)
+    for n, ref in enumerate((giles_re_ref, giles_im_ref)):
+        for b in range(components):
+            for c in range(components):
+                sums_ref[n, pl.ds(b * components + c, 1), :] = ref[b, c, pl.ds(face, 1), :]
+    sums_re = lax.dot_general(sums_ref[0], plain, dims, precision=EXACT, preferred_element_type=jnp.float32)
+    sums_im = lax.dot_general(sums_ref[1], signed, dims, precision=EXACT, preferred_element_type=jnp.float32)
     component, mode, sine = column(lanes(sums_re.shape))
     scale = 2.0 / length
     with_cos = jnp.where(sine, sums_im, sums_re) * scale
@@ -227,7 +246,9 @@
     edge_cells = upright(edge)[first:first + SEGMENT_LANES]
     at_cells = jnp.concatenate([upright(own), edge_cells], 0)
     _, mode, _ = column(lanes(at_cells.shape))
-    cos_table, sin_table = waves(mode_number(mode, blades_ref, face) * at_cells, length)
+    entries = 6 * components * components
+    blades = [rows_ref[pl.ds(entries + n, 1), :].astype(jnp.int32) for n in range(2)]
+    cos_table, sin_table = waves(mode_number(mode, blades) * at_cells, length)
     for c in range(components):
         row_cos = jnp.zeros((1, pitch), jnp.float32)
         row_sin = jnp.zeros((1, pitch), jnp.float32)
@@ -244,13 +265,18 @@
         synth_ref[pl.ds(used, rest), :] = jnp.zeros((rest, pitch), jnp.float32)
 
 
+def jacobian(jac_ref, components, b, c, d):
+    return jac_ref[pl.ds((b * components + c) * 6 + d, 1), :]
+
+
 def mixed(jac_ref, source, couplings, neighbours):
     total = list(source)
+    jac = functools.partial(jacobian, jac_ref, len(total))
     for d, neighbour in enumerate(neighbours):
         for c in range(len(total)):
-            term = jac_ref[c, d] * neighbour[0]
+            term = jac(0, c, d) * neighbour[0]
             for b in range(1, len(total)):
-                term = term + jac_ref[b * len(total) + c, d] * neighbour[b]
+                term = term + jac(b, c, d) * neighbour[b]
             total[c] = total[c] + couplings[d] * term
     return total
 
@@ -418,9 +444,9 @@
     components = len(delta)
     out = []
     for c in range(components):
-        term = jac_ref[c, 0] * delta[0]
+        term = jacobian(jac_ref, components, 0, c, 0) * delta[0]
         for b in range(1, components):
-            term = term + jac_ref[b * components + c, 0] * delta[b]
+            term = term + jacobian(jac_ref, components, b, c, 0) * delta[b]
         out.append(coef_ref[components, a, :height] * term)
     return out
 
@@ -540,12 +566,11 @@
     groups = slots(fields + 1, components)[1][-1][0] + 1
     pairs = -(-(fields * axial + 1) // 2)
     span_tiles = pairs + -(-components * axial // EDGE)
-    smem = pl.BlockSpec(memory_space=pltpu.SMEM)
     vmem = pl.BlockSpec(memory_space=pltpu.VMEM)
     hbm = pl.BlockSpec(memory_space=pltpu.HBM)
     anywhere = pl.BlockSpec(memory_space=pl.ANY)
 
-    def call(kernel, name, outs, ins, aliases=None, scratch=(), **fixed):
+    def call(kernel, name, outs, ins, aliases=None, scratch=(), limit=40 * MIB, **fixed):
         specs = [spec for spec, _ in ins]
         return pl.pallas_call(
             functools.partial(kernel, **fixed),
@@ -554,24 +579,28 @@
             out_specs=jax.tree.map(lambda _: vmem, outs),
             scratch_shapes=scratch,
             input_output_aliases=aliases or {},
-            compiler_params=PARAMS,
+            compiler_params=params(limit),
             name=name,
         )(*[value for _, value in ins])
 
-    coef, inv, edges, span_out, corner, right, left, table = call(
+    adjoint, coef, inv, edges, span_out, corner, right, left, table, jac = call(
         pack_kernel, "pack",
         (
+            struct(components, axial, span, pitch),
             struct(components + 6, axial, span, pitch), struct(span, pitch), struct(fields + 1, span, pitch),
             struct(span_tiles, EDGE, pitch), struct(2 * groups, EDGE, pitch), struct(groups, wide, pitch),
             struct(groups, wide, pitch), struct(pitch, pitch),
+            struct(6 * components * components + 2, pitch),
         ),
-        [(hbm, blades), (hbm, adjoint_start), (hbm, source), (hbm, couplings), (hbm, damping)],
+        [(hbm, pltpu.with_memory_space_constraint(x, pltpu.HBM)) for x in (
+            blades, jacobians.transpose(2, 3, 0, 1), adjoint_start, source, couplings, damping,
+        )],
         scratch=[
-            pltpu.SMEM(blades.shape, jnp.int32), pltpu.VMEM(adjoint_start.shape, jnp.float32),
+            pltpu.SMEM(blades.shape, jnp.int32), pltpu.SMEM((components, components, 1, 6), jnp.float32),
             pltpu.VMEM(source.shape, jnp.float32), pltpu.VMEM(couplings.shape, jnp.float32),
-            pltpu.VMEM(damping.shape, jnp.float32), pltpu.SemaphoreType.DMA((5,)),
+            pltpu.VMEM(damping.shape, jnp.float32), pltpu.SemaphoreType.DMA((6,)),
         ],
-        length=length,
+        row_count=row_count, length=length,
     )
     corner = moved(corner, lambda r, s, p: (r, 1 - s, p))
     from_span = moved(span_out, lambda r, s, p: (r, 1 - s, p))
@@ -580,7 +609,6 @@
     from_left = moved(right, lambda r, s, p: (r, s, (p + 1) % place_count))
     from_right = moved(left, lambda r, s, p: (r, s, (p - 1) % place_count))
 
-    jac = jacobians[0].transpose(1, 2, 0).reshape(components * components, 6)
     state_shape = struct(axial + 1, components, axial + 2, wide, pitch)
     edge_shape = struct(axial + 1, components, wide, pitch)
     coef, inv, edge_coef, state, edge, modes = call(
@@ -589,7 +617,7 @@
             struct(components + 6, axial, wide, pitch), struct(wide, pitch), struct(components + 7, wide, pitch),
             state_shape, edge_shape, struct(axial * span + axial // 2 * EDGE, pitch),
         ),
-        [(smem, jac)] + [(vmem, x) for x in (adjoint_start, coef, inv, edges, from_span, from_left, from_right, table)],
+        [(vmem, jac)] + [(vmem, x) for x in (adjoint, coef, inv, edges, from_span, from_left, from_right, table)],
     )
 
     def summed(x):
@@ -605,38 +633,32 @@
 
     state, edge, part = call(
         middle_kernel, "middle_sweeps", (state_shape, edge_shape, struct(span, pitch)),
-        [(smem, jac)] + [(vmem, x) for x in (coef, edge_coef, state, edge, table)],
+        [(vmem, jac)] + [(vmem, x) for x in (coef, edge_coef, state, edge, table)],
         aliases={3: 0, 4: 1},
     )
     halfway, modes_a, modes_b = summed(modes)
-
-    giles_real, giles_imag, halfway = lax.optimization_barrier((giles_real, giles_imag, halfway))
-    face = jnp.minimum(lax.axis_index("row"), row_count - 2)
-
-    def of_face(giles):
-        picked = lax.dynamic_index_in_dim(giles, face, 0, keepdims=False)
-        return picked.transpose(1, 2, 0).reshape(components * components, -1)
 
     synth = call(
         synth_kernel, "synth", struct(-(-components * (pitch + SEGMENT_LANES) // pitch) * pitch, pitch),
-        [(smem, blades), (vmem, of_face(giles_real)), (vmem, of_face(giles_imag))]
+        [(vmem, jac), (vmem, giles_real.transpose(2, 3, 0, 1)), (vmem, giles_imag.transpose(2, 3, 0, 1))]
         + [(vmem, mode_orders.transpose(0, 2, 1)), (vmem, cell_map), (anywhere, halfway)],
+        scratch=[pltpu.VMEM((2, components * components, mode_orders.shape[1]), jnp.float32)],
         row_count=row_count, place_count=place_count, components=components, pitch=pitch, length=length, axial=axial,
     )
     late = call(
         link_kernel, "late_modes", struct(span, pitch),
-        [(smem, jac)] + [(vmem, x) for x in (coef, inv, part, modes_a, modes_b, synth, table)],
+        [(vmem, jac)] + [(vmem, x) for x in (coef, inv, part, modes_a, modes_b, synth, table)],
     )
     halfway, late_a, late_b = summed(late)
     state, edge, bound = call(
         second_kernel, "second_sweeps", (state_shape, edge_shape, struct(axial, components, wide, pitch)),
-        [(smem, jac)] + [(vmem, x) for x in (coef, inv, edge_coef, state, edge, modes_a, modes_b, synth)]
+        [(vmem, jac)] + [(vmem, x) for x in (coef, inv, edge_coef, state, edge, modes_a, modes_b, synth)]
         + [(anywhere, late)],
         aliases={4: 0, 5: 1},
     )
     state, swept = call(
         third_kernel, "third_sweeps", (state_shape, struct(components, axial, span, pitch)),
-        [(smem, jac)] + [(vmem, x) for x in (coef, state, edge, bound)] + [(anywhere, halfway)],
+        [(vmem, jac)] + [(vmem, x) for x in (coef, state, edge, bound)] + [(anywhere, halfway)],
         aliases={2: 0},
     )
     return call(

time: 80.1 us -> 48.3 us (0.60)
  the two profiles are of different devices: /device:TPU:15 before, /device:TPU:7 now
where the time goes in v4:
time: 48.3 us; the launch traced here: 48.1 us
  starting transfers between devices  21.2 us (44%)
  Pallas kernels  14.7 us (30%)
  waiting for transfers between devices  12 us (25%)
    ppermute x10, starting transfers between devices, moved(): return lax.ppermute(x, AXES, pairs)  21.2 us
    pallas_call x8, Pallas kernels, call(): pl.pallas_call(functools.partial(kernel, **fixed), out_shape=outs, in_spe...  14.7 us
    ppermute x10, waiting for transfers between devices, moved(): return lax.ppermute(x, AXES, pairs)  12 us
  transfers between devices with their start and end apart: 10, of which 5 were waited for; matrix products, arithmetic and copies ran while one was open for 0% of the time, Pallas kernels for 14%

profile of v4, /device:TPU:7, one launch (start us, length us, event | category | flops | bytes accessed | tf_op | source)
XLA Modules:
  0.0 48.1 jit_solution(10897529297902743177)
XLA Ops:
  0.0 2.3 %pack.1 = (f32[5,4,32,128]{3,2,1,0:T(8,128)S(1)}, f32[11,4,32,128]{3,2,1,0:T(8,128)S(1)}, f32[32,128]{1,0:T(8,128)S(1)}, f32[17,32,128]{2,1,0:T(8,128)S(1)}, f32...) custom-call(s32[4]{0:T(128)} %blades_hbm.1, ...), custom_call_target="tpu_custom_call" | custom-call | tf_op jit(solution)/shard_map/pack/pallas_call | solution.py:575
  2.3 0.3 collective-permute-start.1
  2.6 1.2 %collective-permute-start = (f32[36,8,128]{2,1,0:T(8,128)S(1)}, f32[36,8,128]{2,1,0:T(8,128)S(1)}, u32[]{:S(2)}, u32[]{:S(2)}) collective-permute-start(f32[36,8,128]{2,1,0:T(8,128)S(1)} %get-tuple-element.33), channel_id=1, source_target_pairs={{0,4},{1,5},{2,6},{3,7},{4,0},{5,1},{6,2},{7,3},{8,12},{9,13},{10,... | collective-permute-start | bytes 442376 | tf_op jit(solution)/shard_map/ppermute | solution.py:548
  3.8 1.2 %collective-permute-done.1 = f32[6,8,128]{2,1,0:T(8,128)S(1)} collective-permute-done((f32[6,8,128]{2,1,0:T(8,128)S(1)}, f32[6,8,128]{2,1,0:T(8,128)S(1)}, u32[]{:S(2)}, u32[]{:S(2)}) %collective-permute-start.1) | collective-permute-done | bytes 24608 | tf_op jit(solution)/shard_map/ppermute | solution.py:548
  5.0 3.3 %collective-permute-start.3 = (f32[3,40,128]{2,1,0:T(8,128)S(1)}, f32[3,40,128]{2,1,0:T(8,128)S(1)}, u32[]{:S(2)}, u32[]{:S(2)}) collective-permute-start(f32[3,40,128]{2,1,0:T(8,128)S(1)} %get-tuple-element.51), channel_id=1, source_target_pairs={{0,3},{1,0},{2,1},{3,2},{4,7},{5,4},{6,5},{7,6},{8,11},{9,8},{10,9... | collective-permute-start | bytes 184328 | tf_op jit(solution)/shard_map/ppermute | solution.py:548
  8.3 0.0 collective-permute-start.2
  8.3 1.3 %collective-permute-done.3.from_right_ref = f32[3,40,128]{2,1,0:T(8,128)S(1)} collective-permute-done((f32[3,40,128]{2,1,0:T(8,128)S(1)}, f32[3,40,128]{2,1,0:T(8,128)S(1)}, u32[]{:S(2)}, u32[]{:S(2)}) %collective-permute-start.3) | collective-permute-done | bytes 61472 | tf_op jit(solution)/shard_map/ppermute | solution.py:548
  9.6 3.7 %collective-permute-done.2.from_left_ref = f32[3,40,128]{2,1,0:T(8,128)S(1)} collective-permute-done((f32[3,40,128]{2,1,0:T(8,128)S(1)}, f32[3,40,128]{2,1,0:T(8,128)S(1)}, u32[]{:S(2)}, u32[]{:S(2)}) %collective-permute-start.2) | collective-permute-done | bytes 61472 | tf_op jit(solution)/shard_map/ppermute | solution.py:548
  13.3 0.0 collective-permute-done.span_ref
  13.3 0.0 copy-start
  13.3 0.0 copy-start.1
  13.3 0.0 copy-start.2
  13.3 0.0 copy-start.3
  13.4 3.4 %first_sweeps.1 = (f32[11,4,40,128]{3,2,1,0:T(8,128)S(1)}, f32[40,128]{1,0:T(8,128)S(1)}, f32[12,40,128]{2,1,0:T(8,128)S(1)}, f32[5,5,6,40,128]{4,3,2,1,0:T(8,12...) custom-call(f32[152,128]{1,0:T(8,128)S(1)} %get-tuple-element.28.jac_ref.rows_ref, ...), custom_call_target="tpu_custom_call" | custom-call | tf_op jit(solution)/shard_map/first_sweeps/pallas_call | solution.py:575
  16.7 0.1 collective-permute-start.4
  16.8 3.2 %collective-permute-done.4 = f32[144,128]{1,0:T(8,128)S(1)} collective-permute-done((f32[144,128]{1,0:T(8,128)S(1)}, f32[144,128]{1,0:T(8,128)S(1)}, u32[]{:S(2)}, u32[]{:S(2)}) %collective-permute-start.4) | collective-permute-done | bytes 73760 | tf_op jit(solution)/shard_map/ppermute | solution.py:548
  20.0 4.6 %collective-permute-start.6 = (f32[144,128]{1,0:T(8,128)S(1)}, f32[144,128]{1,0:T(8,128)S(1)}, u32[]{:S(2)}, u32[]{:S(2)}) collective-permute-start(f32[144,128]{1,0:T(8,128)S(1)} %add.6.after_ref), channel_id=1, source_target_pairs={{8,2},{9,3},{10,0},{11,1},{12,6},{13,7},{14,4},{15,5},{16,10},{17,... | collective-permute-start | bytes 221192 | tf_op jit(solution)/shard_map/ppermute | solution.py:548
  24.6 3.8 %collective-permute-start.5 = (f32[144,128]{1,0:T(8,128)S(1)}, f32[144,128]{1,0:T(8,128)S(1)}, u32[]{:S(2)}, u32[]{:S(2)}) collective-permute-start(f32[144,128]{1,0:T(8,128)S(1)} %add.6.after_ref), channel_id=1, source_target_pairs={{8,0},{9,1},{10,2},{11,3},{12,4},{13,5},{14,6},{15,7},{16,8},{17,9... | collective-permute-start | bytes 221192 | tf_op jit(solution)/shard_map/ppermute | solution.py:548
  28.4 1.8 %middle_sweeps.1 = (f32[5,5,6,40,128]{4,3,2,1,0:T(8,128)S(1)}, f32[5,5,40,128]{3,2,1,0:T(8,128)S(1)}, f32[32,128]{1,0:T(8,128)S(1)}) custom-call(f32[152,128]{1,0:T(8,128)S(1)} %get-tuple-element.28.jac_ref.rows_ref, f32[11,4,40,128]{3,2,1,0:T(8,128)S(1)} %get-tuple-element.39.coef_ref, ...), custom_call_target="tpu_custom_call", output_to_operand_aliasing={{0}: (3, {}), {1}: (4, {})} | custom-call | tf_op jit(solution)/shard_map/middle_sweeps/pallas_call | solution.py:575
  30.2 0.0 copy-done
  30.2 0.0 copy-done.1
  30.3 0.0 copy-done.2
  30.3 0.0 copy-done.3
  30.3 0.4 synth.1.synth_ref
  30.7 0.0 collective-permute-done.6.modes_b_ref
  30.7 0.0 collective-permute-done.5.modes_a_ref
  30.7 1.3 %late_modes.1.after_ref = f32[32,128]{1,0:T(8,128)S(1)} custom-call(f32[152,128]{1,0:T(8,128)S(1)} %get-tuple-element.28.jac_ref.rows_ref, f32[11,4,40,128]{3,2,1,0:T(8,128)S(1)} %get-tuple-element.39.coef_ref, f32[40,128]{1,0:T(8,128)S(1)} %get-tuple-element.38.inv_ref, f32[32,128]{1,0:T(8,128)S(1)} %get-tuple-element.43.part_ref, ...), custom_call_target="tpu_custom_call" | custom-call | tf_op jit(solution)/shard_map/late_modes/pallas_call | solution.py:575
  32.0 0.0 collective-permute-start.7
  32.0 2.6 %collective-permute-done.7 = f32[32,128]{1,0:T(8,128)S(1)} collective-permute-done((f32[32,128]{1,0:T(8,128)S(1)}, f32[32,128]{1,0:T(8,128)S(1)}, u32[]{:S(2)}, u32[]{:S(2)}) %collective-permute-start.7) | collective-permute-done | bytes 16416 | tf_op jit(solution)/shard_map/ppermute | solution.py:548
  34.6 5.8 %collective-permute-start.9 = (f32[32,128]{1,0:T(8,128)S(1)}, f32[32,128]{1,0:T(8,128)S(1)}, u32[]{:S(2)}, u32[]{:S(2)}) collective-permute-start(f32[32,128]{1,0:T(8,128)S(1)} %add.7.after_ref), channel_id=1, source_target_pairs={{8,2},{9,3},{10,0},{11,1},{12,6},{13,7},{14,4},{15,5},{16,10},{17,... | collective-permute-start | bytes 49160 | tf_op jit(solution)/shard_map/ppermute | solution.py:548
  40.4 2.0 %collective-permute-start.8 = (f32[32,128]{1,0:T(8,128)S(1)}, f32[32,128]{1,0:T(8,128)S(1)}, u32[]{:S(2)}, u32[]{:S(2)}) collective-permute-start(f32[32,128]{1,0:T(8,128)S(1)} %add.7.after_ref), channel_id=1, source_target_pairs={{8,0},{9,1},{10,2},{11,3},{12,4},{13,5},{14,6},{15,7},{16,8},{17,9... | collective-permute-start | bytes 49160 | tf_op jit(solution)/shard_map/ppermute | solution.py:548
  42.5 2.6 %second_sweeps.1 = (f32[5,5,6,40,128]{4,3,2,1,0:T(8,128)S(1)}, f32[5,5,40,128]{3,2,1,0:T(8,128)S(1)}, f32[4,5,40,128]{3,2,1,0:T(8,128)S(1)}) custom-call(f32[152,128]{1,0:T(8,128)S(1)} %get-tuple-element.28.jac_ref.rows_ref, f32[11,4,40,128]{3,2,1,0:T(8,128)S(1)} %get-tuple-element.39.coef_ref, ...), custom_call_target="tpu_custom_call", output_to_operand_aliasing={{0}: (4, {}), {1}: (5, {})} | custom-call | tf_op jit(solution)/shard_map/second_sweeps/pallas_call | solution.py:575
  45.1 1.8 %third_sweeps.1 = (f32[5,5,6,40,128]{4,3,2,1,0:T(8,128)S(1)}, f32[5,4,32,128]{3,2,1,0:T(8,128)S(1)}) custom-call(f32[152,128]{1,0:T(8,128)S(1)} %get-tuple-element.28.jac_ref.rows_ref, f32[11,4,40,128]{3,2,1,0:T(8,128)S(1)} %get-tuple-element.39.coef_ref, f32[5,5,6,40,128]{4,3,2,1,0:T(8,128)S(1)} %get-tuple-element.47.state_in_ref, ...), custom_call_target="tpu_custom_call", output_to_operand_aliasing={{0}: (2, {})} | custom-call | tf_op jit(solution)/shard_map/third_sweeps/pallas_call | solution.py:575
  46.9 0.0 collective-permute-done.9.modes_b_ref
  46.9 0.0 collective-permute-done.8.modes_a_ref
  46.9 1.2 %last_boundary.1 = f32[5,4,32,128]{3,2,1,0:T(8,128)} custom-call(f32[40,128]{1,0:T(8,128)S(1)} %get-tuple-element.38.inv_ref, f32[32,128]{1,0:T(8,128)S(1)} %collective-permute-done.8.modes_a_ref, f32[32,128]{1,0:T(8,128)S(1)} %collective-permute-done.9.modes_b_ref, f32[896,128]{1,0:T(8,128)S(1)} %synth.1.synth_ref, ...), custom_call_target="tpu_custom_call" | custom-call | tf_op jit(solution)/shard_map/last_boundary/pallas_call | solution.py:575
  (3 shorter events, 0.0 us)
Async XLA Ops:
  2.3 2.7 %collective-permute-start.1 = (f32[6,8,128]{2,1,0:T(8,128)S(1)}, f32[6,8,128]{2,1,0:T(8,128)S(1)}, u32[]{:S(2)}, u32[]{:S(2)}) collective-permute-start(f32[6,8,128]{2,1,0:T(8,128)S(1)} %get-tuple-element.35), channel_id=1, source_target_pairs={{0,4},{1,5},{2,6},{3,7},{4,0},{5,1},{6,2},{7,3},{8,12},{9,13},{10,... | collective-permute-start | bytes 73736 | tf_op jit(solution)/shard_map/ppermute | solution.py:548
  2.6 10.8 %collective-permute-start = (f32[36,8,128]{2,1,0:T(8,128)S(1)}, f32[36,8,128]{2,1,0:T(8,128)S(1)}, u32[]{:S(2)}, u32[]{:S(2)}) collective-permute-start(f32[36,8,128]{2,1,0:T(8,128)S(1)} %get-tuple-element.33), channel_id=1, source_target_pairs={{0,4},{1,5},{2,6},{3,7},{4,0},{5,1},{6,2},{7,3},{8,12},{9,13},{10,... | collective-permute-start | bytes 442376 | tf_op jit(solution)/shard_map/ppermute | solution.py:548
  5.0 4.6 %collective-permute-start.3 = (f32[3,40,128]{2,1,0:T(8,128)S(1)}, f32[3,40,128]{2,1,0:T(8,128)S(1)}, u32[]{:S(2)}, u32[]{:S(2)}) collective-permute-start(f32[3,40,128]{2,1,0:T(8,128)S(1)} %get-tuple-element.51), channel_id=1, source_target_pairs={{0,3},{1,0},{2,1},{3,2},{4,7},{5,4},{6,5},{7,6},{8,11},{9,8},{10,9... | collective-permute-start | bytes 184328 | tf_op jit(solution)/shard_map/ppermute | solution.py:548
  8.3 5.0 %collective-permute-start.2 = (f32[3,40,128]{2,1,0:T(8,128)S(1)}, f32[3,40,128]{2,1,0:T(8,128)S(1)}, u32[]{:S(2)}, u32[]{:S(2)}) collective-permute-start(f32[3,40,128]{2,1,0:T(8,128)S(1)} %get-tuple-element.52), channel_id=1, source_target_pairs={{0,1},{1,2},{2,3},{3,0},{4,5},{5,6},{6,7},{7,4},{8,9},{9,10},{10,1... | collective-permute-start | bytes 184328 | tf_op jit(solution)/shard_map/ppermute | solution.py:548
  13.3 16.9 %copy-start = (f32[3,64,5,5]{1,0,3,2:T(4,128)S(1)}, f32[3,64,5,5]{1,0,3,2:T(4,128)}, u32[]{:S(2)}) copy-start(f32[3,64,5,5]{1,0,3,2:T(4,128)} %param.15) | copy-start | bytes 57604
  13.3 16.9 %copy-start.1 = (f32[3,64,5,5]{1,0,3,2:T(4,128)S(1)}, f32[3,64,5,5]{1,0,3,2:T(4,128)}, u32[]{:S(2)}) copy-start(f32[3,64,5,5]{1,0,3,2:T(4,128)} %param.16) | copy-start | bytes 57604
  13.3 16.9 %copy-start.2 = (s32[3,64,2]{1,2,0:T(2,128)S(1)}, s32[3,64,2]{1,2,0:T(2,128)}, u32[]{:S(2)}) copy-start(s32[3,64,2]{1,2,0:T(2,128)} %param.18) | copy-start | bytes 4612
  13.3 16.9 %copy-start.3 = (s32[1,512]{1,0:T(1,128)S(1)}, s32[1,512]{1,0:T(1,128)}, u32[]{:S(2)}) copy-start(s32[1,512]{1,0:T(1,128)} %cells_ref.1) | copy-start | bytes 6148
  16.7 3.3 %collective-permute-start.4 = (f32[144,128]{1,0:T(8,128)S(1)}, f32[144,128]{1,0:T(8,128)S(1)}, u32[]{:S(2)}, u32[]{:S(2)}) collective-permute-start(f32[144,128]{1,0:T(8,128)S(1)} %get-tuple-element.44), channel_id=1, source_target_pairs={{0,1},{1,0},{2,3},{3,2},{4,5},{5,4},{6,7},{7,6},{8,9},{9,8},{10,11... | collective-permute-start | bytes 221192 | tf_op jit(solution)/shard_map/ppermute | solution.py:548
  20.0 10.7 %collective-permute-start.6 = (f32[144,128]{1,0:T(8,128)S(1)}, f32[144,128]{1,0:T(8,128)S(1)}, u32[]{:S(2)}, u32[]{:S(2)}) collective-permute-start(f32[144,128]{1,0:T(8,128)S(1)} %add.6.after_ref), channel_id=1, source_target_pairs={{8,2},{9,3},{10,0},{11,1},{12,6},{13,7},{14,4},{15,5},{16,10},{17,... | collective-permute-start | bytes 221192 | tf_op jit(solution)/shard_map/ppermute | solution.py:548
  24.6 6.1 %collective-permute-start.5 = (f32[144,128]{1,0:T(8,128)S(1)}, f32[144,128]{1,0:T(8,128)S(1)}, u32[]{:S(2)}, u32[]{:S(2)}) collective-permute-start(f32[144,128]{1,0:T(8,128)S(1)} %add.6.after_ref), channel_id=1, source_target_pairs={{8,0},{9,1},{10,2},{11,3},{12,4},{13,5},{14,6},{15,7},{16,8},{17,9... | collective-permute-start | bytes 221192 | tf_op jit(solution)/shard_map/ppermute | solution.py:548
  32.0 2.6 %collective-permute-start.7 = (f32[32,128]{1,0:T(8,128)S(1)}, f32[32,128]{1,0:T(8,128)S(1)}, u32[]{:S(2)}, u32[]{:S(2)}) collective-permute-start(f32[32,128]{1,0:T(8,128)S(1)} %late_modes.1.after_ref), channel_id=1, source_target_pairs={{0,1},{1,0},{2,3},{3,2},{4,5},{5,4},{6,7},{7,6},{8,9},{9,8},{10,11... | collective-permute-start | bytes 49160 | tf_op jit(solution)/shard_map/ppermute | solution.py:548
  34.6 12.3 %collective-permute-start.9 = (f32[32,128]{1,0:T(8,128)S(1)}, f32[32,128]{1,0:T(8,128)S(1)}, u32[]{:S(2)}, u32[]{:S(2)}) collective-permute-start(f32[32,128]{1,0:T(8,128)S(1)} %add.7.after_ref), channel_id=1, source_target_pairs={{8,2},{9,3},{10,0},{11,1},{12,6},{13,7},{14,4},{15,5},{16,10},{17,... | collective-permute-start | bytes 49160 | tf_op jit(solution)/shard_map/ppermute | solution.py:548
  40.4 6.5 %collective-permute-start.8 = (f32[32,128]{1,0:T(8,128)S(1)}, f32[32,128]{1,0:T(8,128)S(1)}, u32[]{:S(2)}, u32[]{:S(2)}) collective-permute-start(f32[32,128]{1,0:T(8,128)S(1)} %add.7.after_ref), channel_id=1, source_target_pairs={{8,0},{9,1},{10,2},{11,3},{12,4},{13,5},{14,6},{15,7},{16,8},{17,9... | collective-permute-start | bytes 49160 | tf_op jit(solution)/shard_map/ppermute | solution.py:548

commit v5 on v4

--- a/solution.py
+++ b/solution.py
@@ -95,21 +95,21 @@
 
 
 def pack_kernel(
-    blades_hbm, jacobians_hbm, adjoint_hbm, source_hbm, couplings_hbm, damping_hbm,
-    adjoint_ref, coef_ref, inv_ref, edges_ref, span_ref, corner_ref, right_ref, left_ref, table_ref, rows_ref,
-    blades_ref, jacobians_ref, source_ref, couplings_ref, damping_ref, sems, *, row_count, length,
+    adjoint_hbm, source_hbm, couplings_hbm, damping_hbm,
+    adjoint_ref, coef_ref, inv_ref, edges_ref, span_ref, corner_ref, inner_ref, outer_ref,
+    source_ref, couplings_ref, damping_ref, sems,
 ):
     components, axial, span, pitch = adjoint_ref.shape
     copies = [
         pltpu.make_async_copy(src, dst, sems.at[n])
         for n, (src, dst) in enumerate((
             (couplings_hbm, couplings_ref), (damping_hbm, damping_ref), (source_hbm, source_ref),
-            (adjoint_hbm, adjoint_ref), (blades_hbm, blades_ref), (jacobians_hbm, jacobians_ref),
+            (adjoint_hbm, adjoint_ref),
         ))
     ]
     for copy in copies:
         copy.start()
-    row, side, place = (lax.axis_index(name) for name in AXES)
+    side, place = lax.axis_index("span"), lax.axis_index("pitch")
     copies[0].wait()
     copies[1].wait()
     diag = damping_ref[...]
@@ -135,20 +135,23 @@
     )
     edge_row = pl.multiple_of(jnp.where(side == 0, span - EDGE, 0), EDGE)
     near, far = slots(fields + 1, components)
-    groups = right_ref.shape[0]
+    groups = inner_ref.shape[0]
     lane = lanes((span, pitch)) % SEGMENT_LANES
-    for n, (out_ref, near_at, far_at) in enumerate((
-        (right_ref, 3 * EDGE - HALF, 3 * EDGE - HALF - 1), (left_ref, EDGE, EDGE + HALF),
-    )):
+    sides = []
+    for near_at, far_at in ((3 * EDGE - HALF, 3 * EDGE - HALF - 1), (EDGE, EDGE + HALF)):
         packed = [jnp.zeros((span, pitch), jnp.float32) for _ in range(groups)]
         for f, (g, to) in enumerate(near):
             value = pltpu.roll(edges_ref[f], (to - near_at) % pitch, 1)
             packed[g] = jnp.where((lane >= to) & (lane < to + HALF), value, packed[g])
         for f, (g, to) in enumerate(far):
             packed[g] = jnp.where(lane == to, pltpu.roll(edges_ref[f], (to - far_at) % pitch, 1), packed[g])
-        for g in range(groups):
-            out_ref[g, :span] = packed[g]
-            corner_ref[n * groups + g] = out_ref[g, pl.ds(edge_row, EDGE), :]
+        sides.append(packed)
+    even = lax.rem(place, 2) == 0
+    for g in range(groups):
+        inner_ref[g, :span] = jnp.where(even, sides[0][g], sides[1][g])
+        outer_ref[g, :span] = jnp.where(even, sides[1][g], sides[0][g])
+        corner_ref[g] = inner_ref[g, pl.ds(edge_row, EDGE), :]
+        corner_ref[groups + g] = outer_ref[g, pl.ds(edge_row, EDGE), :]
 
     to_low, to_high = half_rows(side)
     line = rows((EDGE, pitch))
@@ -168,13 +171,28 @@
             value = jnp.where(line == k, pltpu.roll(tiles[n * EDGE + k], lax.rem(k + EDGE - fifth, EDGE), 0), value)
         span_ref[pairs + n] = value
 
-    copies[4].wait()
+
+def prepare_kernel(
+    blades_hbm, jacobians_hbm, adjoint_ref, table_ref, rows_ref, modes_ref, blades_ref, jacobians_ref, sems,
+    *, row_count, length,
+):
+    components, _, span, pitch = adjoint_ref.shape
+    copies = [
+        pltpu.make_async_copy(blades_hbm, blades_ref, sems.at[0]),
+        pltpu.make_async_copy(jacobians_hbm, jacobians_ref, sems.at[1]),
+    ]
+    for copy in copies:
+        copy.start()
+    row, place = lax.axis_index("row"), lax.axis_index("pitch")
+    copies[0].wait()
     component, mode, sine = column(lanes((pitch, pitch)))
     face = jnp.maximum(row - 1, 0)
     number = mode_number(mode, (blades_ref[face], blades_ref[face + 1]))
     cos_table, sin_table = waves(number * (place * pitch + rows((pitch, pitch))), length)
-    table_ref[...] = jnp.where(component < components, jnp.where(sine, sin_table, cos_table), 0.0)
-    copies[5].wait()
+    table = jnp.where(component < components, jnp.where(sine, sin_table, cos_table), 0.0)
+    table_ref[...] = table
+    modes_ref[...] = projected([adjoint_ref[c, 0] for c in range(components)], table)
+    copies[1].wait()
     entries = 6 * components * components
     for b in range(components):
         for c in range(components):
@@ -203,11 +221,22 @@
 
 
 def synth_kernel(
-    rows_ref, giles_re_ref, giles_im_ref, orders_ref, cells_ref, after_ref, synth_ref, sums_ref,
+    rows_ref, giles_re_hbm, giles_im_hbm, orders_hbm, cells_hbm, synth_ref,
+    giles_re_ref, giles_im_ref, orders_ref, cells_ref, sums_ref, sems,
     *, row_count, place_count, components, pitch, length, axial,
 ):
+    copies = [
+        pltpu.make_async_copy(src, dst, sems.at[n])
+        for n, (src, dst) in enumerate((
+            (orders_hbm, orders_ref), (giles_re_hbm, giles_re_ref), (giles_im_hbm, giles_im_ref), (cells_hbm, cells_ref),
+        ))
+    ]
+    for copy in copies:
+        copy.start()
     row, place = lax.axis_index("row"), lax.axis_index("pitch")
     face = jnp.minimum(row, row_count - 2)
+    for copy in copies:
+        copy.wait()
     modes = orders_ref.shape[2]
     orders = orders_ref[face]
     tag = BASE * orders[0:1] + orders[1:2]
@@ -334,8 +363,8 @@
 
 
 def first_kernel(
-    jac_ref, adjoint_ref, coef_in_ref, inv_in_ref, edges_ref, span_ref, from_left_ref, from_right_ref, table_ref,
-    coef_ref, inv_ref, edge_coef_ref, state_ref, edge_ref, modes_ref,
+    jac_ref, adjoint_ref, coef_in_ref, inv_in_ref, edges_ref, span_ref, inner_ref, outer_ref, table_ref,
+    coef_ref, inv_ref, edge_coef_ref, state_ref, edge_ref, modes_ref, part_ref,
 ):
     components, axial, span, pitch = adjoint_ref.shape
     wide = span + EDGE
@@ -355,6 +384,9 @@
             value = jnp.where(line == fifth, extra, value)
         return value
 
+    even = lax.rem(lax.axis_index("pitch"), 2) == 0
+    from_left = [jnp.where(even, outer_ref[g], inner_ref[g]) for g in range(inner_ref.shape[0])]
+    from_right = [jnp.where(even, inner_ref[g], outer_ref[g]) for g in range(inner_ref.shape[0])]
     near, far = slots(fields + 1, components)
     keep_five = keep_half | (line == fifth)
     for f in range(fields + 1):
@@ -376,16 +408,16 @@
         g, at = near[f]
         value = jnp.concatenate([edges_ref[f], to_edges(layers, pitch)], 0)
         lane = lanes((wide, pitch)) % SEGMENT_LANES
-        value = jnp.where((lane >= HALF) & (lane < EDGE), pltpu.roll(from_left_ref[g], (HALF - at) % pitch, 1), value)
+        value = jnp.where((lane >= HALF) & (lane < EDGE), pltpu.roll(from_left[g], (HALF - at) % pitch, 1), value)
         value = jnp.where(
             (lane >= 3 * EDGE) & (lane < 3 * EDGE + HALF),
-            pltpu.roll(from_right_ref[g], (3 * EDGE - at) % pitch, 1), value,
+            pltpu.roll(from_right[g], (3 * EDGE - at) % pitch, 1), value,
         )
         if f < components:
             g, at = far[f]
-            value = jnp.where(lane == HALF - 1, pltpu.roll(from_left_ref[g], (HALF - 1 - at) % pitch, 1), value)
+            value = jnp.where(lane == HALF - 1, pltpu.roll(from_left[g], (HALF - 1 - at) % pitch, 1), value)
             value = jnp.where(
-                lane == 3 * EDGE + HALF, pltpu.roll(from_right_ref[g], (3 * EDGE + HALF - at) % pitch, 1), value,
+                lane == 3 * EDGE + HALF, pltpu.roll(from_right[g], (3 * EDGE + HALF - at) % pitch, 1), value,
             )
         target, at = (edge_ref.at[0], f) if f < components else (edge_coef_ref, f - components)
         target[at, :span] = value[:span]
@@ -402,42 +434,32 @@
             advance(refs, t, a)
             return inner
 
-        lax.fori_loop(0, axial - 1 - t, body, 0)
-
-        @pl.when(t < axial - 2)
+        lax.fori_loop(0, axial - t, body, 0)
+
+        @pl.when(t < axial - 1)
         def _():
             for c, value in enumerate(edge_update(jac_ref, edge_ref, edge_coef_ref, t, axial)):
                 edge_ref[t + 1, c] = value
 
         return carry
 
-    lax.fori_loop(0, axial - 1, sweep, 0)
-    strips = [jnp.concatenate([state_ref[t, c, 1] for t in range(axial)], 0) for c in range(components)]
+    lax.fori_loop(0, axial, sweep, 0)
+    strips = [
+        jnp.concatenate(
+            [state_ref[t, c, 1] for t in range(1, axial)] + [state_ref[axial, c, 1, :span], state_ref[0, c, 1, span:]], 0,
+        )
+        for c in range(components)
+    ]
     total = projected(strips, table_ref[...])
     to_low, to_high = half_rows(1 - side)
-    for t in range(axial):
-        modes_ref[pl.ds(t * span, span), :] = total[t * wide:t * wide + span]
+    for t in range(1, axial):
+        modes_ref[pl.ds((t - 1) * span, span), :] = total[(t - 1) * wide:(t - 1) * wide + span]
+    last = (axial - 1) * wide
+    part_ref[...] = total[last:last + span]
+    ghosts = [total[last + span:]] + [total[t * wide + span:(t + 1) * wide] for t in range(axial - 1)]
     for n in range(axial // 2):
-        low = total[2 * n * wide + span:2 * n * wide + wide]
-        high = total[(2 * n + 1) * wide + span:(2 * n + 1) * wide + wide]
-        both = jnp.where(line < HALF, pltpu.roll(low, to_low, 0), pltpu.roll(high, to_high, 0))
-        modes_ref[pl.ds(axial * span + n * EDGE, EDGE), :] = both
-
-
-def middle_kernel(
-    jac_ref, coef_ref, edge_coef_ref, state_in_ref, edge_in_ref, table_ref, state_ref, edge_ref, modes_ref,
-):
-    components, axial, span = state_ref.shape[1], state_ref.shape[2] - 2, modes_ref.shape[0]
-    refs = (jac_ref, state_ref, edge_ref, coef_ref)
-    for c, value in enumerate(edge_update(jac_ref, edge_ref, edge_coef_ref, axial - 2, axial)):
-        edge_ref[axial - 1, c] = value
-
-    def body(t, carry):
-        advance(refs, t, axial - 1 - t)
-        return carry
-
-    lax.fori_loop(0, axial, body, 0)
-    modes_ref[...] = projected([state_ref[axial, c, 1, :span] for c in range(components)], table_ref[...])
+        both = jnp.where(line < HALF, pltpu.roll(ghosts[2 * n], to_low, 0), pltpu.roll(ghosts[2 * n + 1], to_high, 0))
+        modes_ref[pl.ds((axial - 1) * span + n * EDGE, EDGE), :] = both
 
 
 def along_axis(jac_ref, coef_ref, delta, a, height):
@@ -451,31 +473,35 @@
     return out
 
 
-def link_kernel(jac_ref, coef_ref, inv_ref, part_ref, modes_a_ref, modes_b_ref, synth_ref, table_ref, modes_ref):
-    span, pitch = modes_ref.shape
+def late_kernel(
+    jac_ref, coef_ref, inv_ref, part_ref, more_ref, modes_a_ref, modes_b_ref, synth_ref, table_ref, modes_ref,
+):
+    span, pitch = part_ref.shape
     components, axial = coef_ref.shape[0] - 6, coef_ref.shape[1]
-    modes = modes_a_ref[:span] + modes_b_ref[:span]
-    field = synthesised(modes, synth_ref[:components * pitch])
+    field = synthesised(modes_a_ref[...] + modes_b_ref[...], synth_ref[:components * pitch])
     delta = [inv_ref[:span] * field[:, c * pitch:(c + 1) * pitch] for c in range(components)]
     for a in range(axial - 2, -1, -1):
         delta = along_axis(jac_ref, coef_ref, delta, a, span)
-    modes_ref[...] = part_ref[...] + projected(delta, table_ref[...])
+    before = more_ref.shape[0]
+    modes_ref[:before] = more_ref[...]
+    modes_ref[before:] = part_ref[...] + projected(delta, table_ref[...])
 
 
 def second_kernel(
-    jac_ref, coef_ref, inv_ref, edge_coef_ref, state_in_ref, edge_in_ref, modes_a_ref, modes_b_ref, synth_ref, after_ref,
-    state_ref, edge_ref, bound_ref,
+    jac_ref, coef_ref, inv_ref, edge_coef_ref, state_in_ref, edge_in_ref, modes_a_ref, modes_b_ref, more_a_ref, more_b_ref,
+    synth_ref, state_ref, edge_ref, out_ref, bound_ref,
 ):
-    components, axial = state_ref.shape[1], state_ref.shape[2] - 2
-    wide, pitch = state_ref.shape[3:]
-    span = wide - EDGE
+    components, axial, span, pitch = out_ref.shape
+    wide = span + EDGE
     from_low, from_high = half_rows(1 - lax.axis_index("span"))
-    packed = modes_a_ref[...] + modes_b_ref[...]
+    more = more_a_ref[...] + more_b_ref[...]
+    own = [modes_a_ref[...] + modes_b_ref[...]] + [more[t * span:(t + 1) * span] for t in range(axial - 1)]
+    start = (axial - 1) * span
     parts = []
     for t in range(axial):
-        ghost = packed[axial * span + t // 2 * EDGE:axial * span + (t // 2 + 1) * EDGE]
-        parts += [packed[t * span:(t + 1) * span], pltpu.roll(ghost, from_high if t % 2 else from_low, 0)]
-    field = synthesised(jnp.concatenate(parts, 0), synth_ref[...])
+        ghost = more[start + t // 2 * EDGE:start + (t // 2 + 1) * EDGE]
+        parts += [own[t], pltpu.roll(ghost, from_high if t % 2 else from_low, 0)]
+    field = synthesised(jnp.concatenate(parts + [more[start + axial // 2 * EDGE:]], 0), synth_ref[...])
     edge_bound = []
     for n in range(axial):
         part = field[n * wide:(n + 1) * wide]
@@ -483,6 +509,8 @@
         for c in range(components):
             bound_ref[n, c] = inv_ref[...] * part[:, c * pitch:(c + 1) * pitch]
             edge_bound[n].append(edge_coef_ref[components + 6] * edge_boundary(part, c, components, pitch, axial))
+    for c in range(components):
+        bound_ref[axial, c, :span] = inv_ref[:span] * field[axial * wide:, c * pitch:(c + 1) * pitch]
     delta = [bound_ref[0, c] for c in range(components)]
     for t in range(1, axial + 1):
         for c in range(components):
@@ -494,11 +522,6 @@
     for t in range(1, axial):
         for c, value in enumerate(edge_update(jac_ref, edge_ref, edge_coef_ref, t, axial)):
             edge_ref[t + 1, c] = value + edge_bound[t][c]
-    rest_of_sweeps(jac_ref, coef_ref, state_ref, edge_ref, bound_ref, 1, axial - 1)
-
-
-def rest_of_sweeps(jac_ref, coef_ref, state_ref, edge_ref, bound_ref, first, last):
-    components, axial = state_ref.shape[1], state_ref.shape[2] - 2
     refs = (jac_ref, state_ref, edge_ref, coef_ref)
 
     def sweep(t, carry):
@@ -511,28 +534,16 @@
             state_ref[t + 1, c, axial] += bound_ref[t, c]
         return carry
 
-    lax.fori_loop(first, last, sweep, 0)
-
-
-def third_kernel(jac_ref, coef_ref, state_in_ref, edge_ref, bound_ref, after_ref, state_ref, out_ref):
-    components, axial, span, _ = out_ref.shape
-    rest_of_sweeps(jac_ref, coef_ref, state_ref, edge_ref, bound_ref, axial - 1, axial)
+    lax.fori_loop(1, axial, sweep, 0)
 
     def final(a, carry):
-        for c, value in enumerate(layer_update(jac_ref, state_ref, edge_ref, coef_ref, axial, a)):
+        for c, value in enumerate(layer_update(*refs, axial, a)):
             out_ref[c, a] = value[:span]
         return carry
 
     lax.fori_loop(0, axial, final, 0)
-
-
-def last_kernel(inv_ref, modes_a_ref, modes_b_ref, synth_ref, swept_ref, out_ref):
-    components, axial, span, pitch = out_ref.shape
-    field = synthesised(modes_a_ref[...] + modes_b_ref[...], synth_ref[:components * pitch])
     for c in range(components):
-        for a in range(axial - 1):
-            out_ref[c, a] = swept_ref[c, a]
-        out_ref[c, axial - 1] = swept_ref[c, axial - 1] + inv_ref[:span] * field[:, c * pitch:(c + 1) * pitch]
+        out_ref[c, axial - 1] += bound_ref[axial, c, :span]
 
 
 def moved(x, to):
@@ -560,7 +571,7 @@
     length = pitch * place_count
     assert components == COMPONENTS and components * WAVES <= pitch
     assert axial == ITERS - 1 and ITERS <= EDGE and axial * SEGMENT_LANES == pitch
-    assert span_count == 2 and place_count & (place_count - 1) == 0
+    assert span_count == 2 and place_count > 1 and place_count & (place_count - 1) == 0
     wide = span + EDGE
     fields = 2 * components + 6
     groups = slots(fields + 1, components)[1][-1][0] + 1
@@ -568,7 +579,9 @@
     span_tiles = pairs + -(-components * axial // EDGE)
     vmem = pl.BlockSpec(memory_space=pltpu.VMEM)
     hbm = pl.BlockSpec(memory_space=pltpu.HBM)
-    anywhere = pl.BlockSpec(memory_space=pl.ANY)
+
+    def in_hbm(x):
+        return pltpu.with_memory_space_constraint(x, pltpu.HBM)
 
     def call(kernel, name, outs, ins, aliases=None, scratch=(), limit=40 * MIB, **fixed):
         specs = [spec for spec, _ in ins]
@@ -583,88 +596,90 @@
             name=name,
         )(*[value for _, value in ins])
 
-    adjoint, coef, inv, edges, span_out, corner, right, left, table, jac = call(
+    adjoint, coef, inv, edges, span_out, corner, inner, outer = call(
         pack_kernel, "pack",
         (
             struct(components, axial, span, pitch),
             struct(components + 6, axial, span, pitch), struct(span, pitch), struct(fields + 1, span, pitch),
             struct(span_tiles, EDGE, pitch), struct(2 * groups, EDGE, pitch), struct(groups, wide, pitch),
-            struct(groups, wide, pitch), struct(pitch, pitch),
-            struct(6 * components * components + 2, pitch),
+            struct(groups, wide, pitch),
         ),
-        [(hbm, pltpu.with_memory_space_constraint(x, pltpu.HBM)) for x in (
-            blades, jacobians.transpose(2, 3, 0, 1), adjoint_start, source, couplings, damping,
-        )],
+        [(hbm, in_hbm(x)) for x in (adjoint_start, source, couplings, damping)],
+        scratch=[
+            pltpu.VMEM(source.shape, jnp.float32), pltpu.VMEM(couplings.shape, jnp.float32),
+            pltpu.VMEM(damping.shape, jnp.float32), pltpu.SemaphoreType.DMA((4,)),
+        ],
+    )
+    table, jac, modes = call(
+        prepare_kernel, "prepare",
+        (struct(pitch, pitch), struct(6 * components * components + 2, pitch), struct(span, pitch)),
+        [(hbm, in_hbm(blades)), (hbm, in_hbm(jacobians.transpose(2, 3, 0, 1))), (vmem, adjoint)],
         scratch=[
             pltpu.SMEM(blades.shape, jnp.int32), pltpu.SMEM((components, components, 1, 6), jnp.float32),
-            pltpu.VMEM(source.shape, jnp.float32), pltpu.VMEM(couplings.shape, jnp.float32),
-            pltpu.VMEM(damping.shape, jnp.float32), pltpu.SemaphoreType.DMA((6,)),
+            pltpu.SemaphoreType.DMA((2,)),
         ],
         row_count=row_count, length=length,
     )
+    steps = [1 << n for n in range(place_count.bit_length() - 2)]
+    last_step = place_count // 2
+
+    def near(x):
+        return moved(x, lambda r, s, p: (r - 1, s, p))
+
+    def far(x):
+        return moved(x, lambda r, s, p: (r - 1, s, p ^ last_step))
+
     corner = moved(corner, lambda r, s, p: (r, 1 - s, p))
     from_span = moved(span_out, lambda r, s, p: (r, 1 - s, p))
-    right = lax.dynamic_update_slice(right, corner[:groups], (0, span, 0))
-    left = lax.dynamic_update_slice(left, corner[groups:], (0, span, 0))
-    from_left = moved(right, lambda r, s, p: (r, s, (p + 1) % place_count))
-    from_right = moved(left, lambda r, s, p: (r, s, (p - 1) % place_count))
+    inner = lax.dynamic_update_slice(inner, corner[:groups], (0, span, 0))
+    outer = lax.dynamic_update_slice(outer, corner[groups:], (0, span, 0))
+    outer = moved(outer, lambda r, s, p: (r, s, (p - 1 + 2 * (p % 2)) % place_count))
+    inner = moved(inner, lambda r, s, p: (r, s, p ^ 1))
+
+    for step in steps:
+        modes = modes + moved(modes, lambda r, s, p: (r, s, p ^ step))
+    modes_b = far(modes)
+    modes_a = near(modes)
 
     state_shape = struct(axial + 1, components, axial + 2, wide, pitch)
     edge_shape = struct(axial + 1, components, wide, pitch)
-    coef, inv, edge_coef, state, edge, modes = call(
+    coef, inv, edge_coef, state, edge, more, part = call(
         first_kernel, "first_sweeps",
         (
             struct(components + 6, axial, wide, pitch), struct(wide, pitch), struct(components + 7, wide, pitch),
-            state_shape, edge_shape, struct(axial * span + axial // 2 * EDGE, pitch),
+            state_shape, edge_shape,
+            struct((axial - 1) * span + axial // 2 * EDGE, pitch), struct(span, pitch),
         ),
-        [(vmem, jac)] + [(vmem, x) for x in (adjoint, coef, inv, edges, from_span, from_left, from_right, table)],
-    )
-
-    def summed(x):
-        bit = 1
-        while 2 * bit < place_count:
-            x = x + moved(x, lambda r, s, p: (r, s, p ^ bit))
-            bit *= 2
-        if bit < place_count:
-            far = moved(x, lambda r, s, p: (r - 1, s, p ^ bit))
-        else:
-            far = jnp.zeros_like(x)
-        return x, moved(x, lambda r, s, p: (r - 1, s, p)), far
-
-    state, edge, part = call(
-        middle_kernel, "middle_sweeps", (state_shape, edge_shape, struct(span, pitch)),
-        [(vmem, jac)] + [(vmem, x) for x in (coef, edge_coef, state, edge, table)],
-        aliases={3: 0, 4: 1},
-    )
-    halfway, modes_a, modes_b = summed(modes)
-
+        [(vmem, jac)] + [(vmem, x) for x in (adjoint, coef, inv, edges, from_span, inner, outer, table)],
+    )
+
+    tables = (
+        giles_real.transpose(2, 3, 0, 1), giles_imag.transpose(2, 3, 0, 1), mode_orders.transpose(0, 2, 1), cell_map,
+    )
     synth = call(
         synth_kernel, "synth", struct(-(-components * (pitch + SEGMENT_LANES) // pitch) * pitch, pitch),
-        [(vmem, jac), (vmem, giles_real.transpose(2, 3, 0, 1)), (vmem, giles_imag.transpose(2, 3, 0, 1))]
-        + [(vmem, mode_orders.transpose(0, 2, 1)), (vmem, cell_map), (anywhere, halfway)],
-        scratch=[pltpu.VMEM((2, components * components, mode_orders.shape[1]), jnp.float32)],
+        [(vmem, jac)] + [(hbm, in_hbm(x)) for x in tables],
+        scratch=[pltpu.VMEM(x.shape, x.dtype) for x in tables] + [
+            pltpu.VMEM((2, components * components, mode_orders.shape[1]), jnp.float32), pltpu.SemaphoreType.DMA((4,)),
+        ],
         row_count=row_count, place_count=place_count, components=components, pitch=pitch, length=length, axial=axial,
     )
-    late = call(
-        link_kernel, "late_modes", struct(span, pitch),
-        [(vmem, jac)] + [(vmem, x) for x in (coef, inv, part, modes_a, modes_b, synth, table)],
-    )
-    halfway, late_a, late_b = summed(late)
-    state, edge, bound = call(
-        second_kernel, "second_sweeps", (state_shape, edge_shape, struct(axial, components, wide, pitch)),
-        [(vmem, jac)] + [(vmem, x) for x in (coef, inv, edge_coef, state, edge, modes_a, modes_b, synth)]
-        + [(anywhere, late)],
+    more = call(
+        late_kernel, "late_modes", struct(axial * span + axial // 2 * EDGE, pitch),
+        [(vmem, x) for x in (jac, coef, inv, part, more, modes_a, modes_b, synth, table)],
+    )
+    for step in steps:
+        more = more + moved(more, lambda r, s, p: (r, s, p ^ step))
+    more_b = far(more)
+    more_a = near(more)
+    return call(
+        second_kernel, "second_sweeps", (state_shape, edge_shape, struct(components, axial, span, pitch)),
+        [(vmem, x) for x in (
+            jac, coef, inv, edge_coef, state, edge, modes_a, modes_b, more_a, more_b, synth,
+        )],
         aliases={4: 0, 5: 1},
-    )
-    state, swept = call(
-        third_kernel, "third_sweeps", (state_shape, struct(components, axial, span, pitch)),
-        [(vmem, jac)] + [(vmem, x) for x in (coef, state, edge, bound)] + [(anywhere, halfway)],
-        aliases={2: 0},
-    )
-    return call(
-        last_kernel, "last_boundary", struct(components, axial, span, pitch),
-        [(vmem, x) for x in (inv, late_a, late_b, synth, swept)],
-    )
+        scratch=[pltpu.VMEM((axial + 1, components, wide, pitch), jnp.float32)],
+    )[2]
 
 
 def solution(mesh):

time: 48.3 us -> 47.4 us (0.981)
  the two profiles are of different devices: /device:TPU:7 before, /device:TPU:1 now
where the time goes in v5:
time: 47.4 us; the launch traced here: 47.1 us
  starting transfers between devices  19.2 us (41%)
  Pallas kernels  15.8 us (33%)
  waiting for transfers between devices  11.9 us (25%)
    ppermute x10, starting transfers between devices, moved(): return lax.ppermute(x, AXES, pairs)  19.2 us
    pallas_call x6, Pallas kernels, call(): pl.pallas_call(functools.partial(kernel, **fixed), out_shape=outs, in_spe...  15.8 us
    ppermute x10, waiting for transfers between devices, moved(): return lax.ppermute(x, AXES, pairs)  11.9 us
  transfers between devices with their start and end apart: 10, of which 4 were waited for; matrix products, arithmetic and copies ran while one was open for 0% of the time, Pallas kernels for 15%

profile of v5, /device:TPU:1, one launch (start us, length us, event | category | flops | bytes accessed | tf_op | source)
XLA Modules:
  0.0 47.1 jit_solution(14534317774939001884)
XLA Ops:
  0.0 2.1 %pack.1 = (f32[5,4,32,128]{3,2,1,0:T(8,128)S(1)}, f32[11,4,32,128]{3,2,1,0:T(8,128)S(1)}, f32[32,128]{1,0:T(8,128)S(1)}, f32[17,32,128]{2,1,0:T(8,128)S(1)}, f32...) custom-call(f32[5,4,32,128]{3,2,1,0:T(8,128)} %adjoint_hbm.1, ...), custom_call_target="tpu_custom_call" | custom-call | tf_op jit(solution)/shard_map/pack/pallas_call | solution.py:588
  2.1 2.1 %collective-permute-start.1 = (f32[6,8,128]{2,1,0:T(8,128)S(1)}, f32[6,8,128]{2,1,0:T(8,128)S(1)}, u32[]{:S(2)}, u32[]{:S(2)}) collective-permute-start(f32[6,8,128]{2,1,0:T(8,128)S(1)} %get-tuple-element.31), channel_id=1, source_target_pairs={{0,4},{1,5},{2,6},{3,7},{4,0},{5,1},{6,2},{7,3},{8,12},{9,13},{10,... | collective-permute-start | bytes 73736 | tf_op jit(solution)/shard_map/ppermute | solution.py:559
  4.2 0.1 collective-permute-start
  4.3 1.1 %collective-permute-done.1 = f32[6,8,128]{2,1,0:T(8,128)S(1)} collective-permute-done((f32[6,8,128]{2,1,0:T(8,128)S(1)}, f32[6,8,128]{2,1,0:T(8,128)S(1)}, u32[]{:S(2)}, u32[]{:S(2)}) %collective-permute-start.1) | collective-permute-done | bytes 24608 | tf_op jit(solution)/shard_map/ppermute | solution.py:559
  5.4 3.5 %collective-permute-start.3 = (f32[3,40,128]{2,1,0:T(8,128)S(1)}, f32[3,40,128]{2,1,0:T(8,128)S(1)}, u32[]{:S(2)}, u32[]{:S(2)}) collective-permute-start(f32[3,40,128]{2,1,0:T(8,128)S(1)} %get-tuple-element.43), channel_id=1, source_target_pairs={{0,3},{1,2},{2,1},{3,0},{4,7},{5,6},{6,5},{7,4},{8,11},{9,10},{10,... | collective-permute-start | bytes 184328 | tf_op jit(solution)/shard_map/ppermute | solution.py:559
  9.0 0.0 collective-permute-start.2
  9.0 1.2 %prepare.1 = (f32[128,128]{1,0:T(8,128)S(1)}, f32[152,128]{1,0:T(8,128)S(1)}, f32[32,128]{1,0:T(8,128)S(1)}) custom-call(s32[4]{0:T(128)} %blades_hbm.1, f32[5,5,1,6]{3,2,1,0:T(1,128)} %bitcast.6, f32[5,4,32,128]{3,2,1,0:T(8,128)S(1)} %get-tuple-element.24.adjoint_ref), custom_call_target="tpu_custom_call" | custom-call | tf_op jit(solution)/shard_map/prepare/pallas_call | solution.py:588
  10.2 1.5 %collective-permute-start.4 = (f32[32,128]{1,0:T(8,128)S(1)}, f32[32,128]{1,0:T(8,128)S(1)}, u32[]{:S(2)}, u32[]{:S(2)}) collective-permute-start(f32[32,128]{1,0:T(8,128)S(1)} %get-tuple-element.39), channel_id=1, source_target_pairs={{0,1},{1,0},{2,3},{3,2},{4,5},{5,4},{6,7},{7,6},{8,9},{9,8},{10,11... | collective-permute-start | bytes 49160 | tf_op jit(solution)/shard_map/ppermute | solution.py:559
  11.7 1.4 %collective-permute-done.4 = f32[32,128]{1,0:T(8,128)S(1)} collective-permute-done((f32[32,128]{1,0:T(8,128)S(1)}, f32[32,128]{1,0:T(8,128)S(1)}, u32[]{:S(2)}, u32[]{:S(2)}) %collective-permute-start.4) | collective-permute-done | bytes 16416 | tf_op jit(solution)/shard_map/ppermute | solution.py:559
  13.1 5.2 %collective-permute-start.6 = (f32[32,128]{1,0:T(8,128)S(1)}, f32[32,128]{1,0:T(8,128)S(1)}, u32[]{:S(2)}, u32[]{:S(2)}) collective-permute-start(f32[32,128]{1,0:T(8,128)S(1)} %add.6), channel_id=1, source_target_pairs={{8,2},{9,3},{10,0},{11,1},{12,6},{13,7},{14,4},{15,5},{16,10},{17,... | collective-permute-start | bytes 49160 | tf_op jit(solution)/shard_map/ppermute | solution.py:559
  18.3 1.9 %collective-permute-start.5 = (f32[32,128]{1,0:T(8,128)S(1)}, f32[32,128]{1,0:T(8,128)S(1)}, u32[]{:S(2)}, u32[]{:S(2)}) collective-permute-start(f32[32,128]{1,0:T(8,128)S(1)} %add.6), channel_id=1, source_target_pairs={{8,0},{9,1},{10,2},{11,3},{12,4},{13,5},{14,6},{15,7},{16,8},{17,9... | collective-permute-start | bytes 49160 | tf_op jit(solution)/shard_map/ppermute | solution.py:559
  20.3 1.2 %synth.1.synth_ref = f32[896,128]{1,0:T(8,128)S(1)} custom-call(f32[152,128]{1,0:T(8,128)S(1)} %get-tuple-element.25.jac_ref.rows_ref, f32[5,5,3,64]{3,2,1,0:T(4,128)} %bitcast.4, f32[5,5,3,64]{3,2,1,0:T(4,128)} %bitcast.5, s32[3,2,64]{2,1,0:T(2,128)} %bitcast.7, s32[1,512]{1,0:T(1,128)} %cells_hbm.1), custom_call_target="tpu_custom_call" | custom-call | tf_op jit(solution)/shard_map/synth/pallas_call | solution.py:588
  21.5 0.0 collective-permute-done.3.outer_ref
  21.5 0.0 collective-permute-done.2.inner_ref
  21.5 0.0 collective-permute-done.span_ref
  21.6 4.8 %first_sweeps.1 = (f32[11,4,40,128]{3,2,1,0:T(8,128)S(1)}, f32[40,128]{1,0:T(8,128)S(1)}, f32[12,40,128]{2,1,0:T(8,128)S(1)}, f32[5,5,6,40,128]{4,3,2,1,0:T(8,12...) custom-call(f32[152,128]{1,0:T(8,128)S(1)} %get-tuple-element.25.jac_ref.rows_ref, ...), custom_call_target="tpu_custom_call" | custom-call | tf_op jit(solution)/shard_map/first_sweeps/pallas_call | solution.py:588
  26.4 0.0 collective-permute-done.6.modes_b_ref
  26.4 0.0 collective-permute-done.5.modes_a_ref
  26.4 1.3 %late_modes.1 = f32[144,128]{1,0:T(8,128)S(1)} custom-call(f32[152,128]{1,0:T(8,128)S(1)} %get-tuple-element.25.jac_ref.rows_ref, f32[11,4,40,128]{3,2,1,0:T(8,128)S(1)} %get-tuple-element.34.coef_ref, f32[40,128]{1,0:T(8,128)S(1)} %get-tuple-element.35.inv_ref, f32[32,128]{1,0:T(8,128)S(1)} %get-tuple-element.40.part_ref, ...), custom_call_target="tpu_custom_call" | custom-call | tf_op jit(solution)/shard_map/late_modes/pallas_call | solution.py:588
  27.7 1.0 %collective-permute-start.7 = (f32[144,128]{1,0:T(8,128)S(1)}, f32[144,128]{1,0:T(8,128)S(1)}, u32[]{:S(2)}, u32[]{:S(2)}) collective-permute-start(f32[144,128]{1,0:T(8,128)S(1)} %late_modes.1), channel_id=1, source_target_pairs={{0,1},{1,0},{2,3},{3,2},{4,5},{5,4},{6,7},{7,6},{8,9},{9,8},{10,11... | collective-permute-start | bytes 221192 | tf_op jit(solution)/shard_map/ppermute | solution.py:559
  28.7 2.3 %collective-permute-done.7 = f32[144,128]{1,0:T(8,128)S(1)} collective-permute-done((f32[144,128]{1,0:T(8,128)S(1)}, f32[144,128]{1,0:T(8,128)S(1)}, u32[]{:S(2)}, u32[]{:S(2)}) %collective-permute-start.7) | collective-permute-done | bytes 73760 | tf_op jit(solution)/shard_map/ppermute | solution.py:559
  30.9 1.9 %collective-permute-start.9 = (f32[144,128]{1,0:T(8,128)S(1)}, f32[144,128]{1,0:T(8,128)S(1)}, u32[]{:S(2)}, u32[]{:S(2)}) collective-permute-start(f32[144,128]{1,0:T(8,128)S(1)} %add.7), channel_id=1, source_target_pairs={{8,2},{9,3},{10,0},{11,1},{12,6},{13,7},{14,4},{15,5},{16,10},{17,... | collective-permute-start | bytes 221192 | tf_op jit(solution)/shard_map/ppermute | solution.py:559
  32.9 1.9 %collective-permute-start.8 = (f32[144,128]{1,0:T(8,128)S(1)}, f32[144,128]{1,0:T(8,128)S(1)}, u32[]{:S(2)}, u32[]{:S(2)}) collective-permute-start(f32[144,128]{1,0:T(8,128)S(1)} %add.7), channel_id=1, source_target_pairs={{8,0},{9,1},{10,2},{11,3},{12,4},{13,5},{14,6},{15,7},{16,8},{17,9... | collective-permute-start | bytes 221192 | tf_op jit(solution)/shard_map/ppermute | solution.py:559
  34.8 7.1 %collective-permute-done.9.more_b_ref = f32[144,128]{1,0:T(8,128)S(1)} collective-permute-done((f32[144,128]{1,0:T(8,128)S(1)}, f32[144,128]{1,0:T(8,128)S(1)}, u32[]{:S(2)}, u32[]{:S(2)}) %collective-permute-start.9) | collective-permute-done | bytes 73760 | tf_op jit(solution)/shard_map/ppermute | solution.py:559
  41.9 0.0 collective-permute-done.8.more_a_ref
  41.9 5.2 %second_sweeps.1 = (f32[5,5,6,40,128]{4,3,2,1,0:T(8,128)S(1)}, f32[5,5,40,128]{3,2,1,0:T(8,128)S(1)}, f32[5,4,32,128]{3,2,1,0:T(8,128)}) custom-call(f32[152,128]{1,0:T(8,128)S(1)} %get-tuple-element.25.jac_ref.rows_ref, f32[11,4,40,128]{3,2,1,0:T(8,128)S(1)} %get-tuple-element.34.coef_ref, ...), custom_call_target="tpu_custom_call", output_to_operand_aliasing={{0}: (4, {}), {1}: (5, {})} | custom-call | tf_op jit(solution)/shard_map/second_sweeps/pallas_call | solution.py:588
  (3 shorter events, 0.0 us)
Async XLA Ops:
  2.1 3.4 %collective-permute-start.1 = (f32[6,8,128]{2,1,0:T(8,128)S(1)}, f32[6,8,128]{2,1,0:T(8,128)S(1)}, u32[]{:S(2)}, u32[]{:S(2)}) collective-permute-start(f32[6,8,128]{2,1,0:T(8,128)S(1)} %get-tuple-element.31), channel_id=1, source_target_pairs={{0,4},{1,5},{2,6},{3,7},{4,0},{5,1},{6,2},{7,3},{8,12},{9,13},{10,... | collective-permute-start | bytes 73736 | tf_op jit(solution)/shard_map/ppermute | solution.py:559
  4.2 17.3 %collective-permute-start = (f32[36,8,128]{2,1,0:T(8,128)S(1)}, f32[36,8,128]{2,1,0:T(8,128)S(1)}, u32[]{:S(2)}, u32[]{:S(2)}) collective-permute-start(f32[36,8,128]{2,1,0:T(8,128)S(1)} %get-tuple-element.29), channel_id=1, source_target_pairs={{0,4},{1,5},{2,6},{3,7},{4,0},{5,1},{6,2},{7,3},{8,12},{9,13},{10,... | collective-permute-start | bytes 442376 | tf_op jit(solution)/shard_map/ppermute | solution.py:559
  5.4 16.1 %collective-permute-start.3 = (f32[3,40,128]{2,1,0:T(8,128)S(1)}, f32[3,40,128]{2,1,0:T(8,128)S(1)}, u32[]{:S(2)}, u32[]{:S(2)}) collective-permute-start(f32[3,40,128]{2,1,0:T(8,128)S(1)} %get-tuple-element.43), channel_id=1, source_target_pairs={{0,3},{1,2},{2,1},{3,0},{4,7},{5,6},{6,5},{7,4},{8,11},{9,10},{10,... | collective-permute-start | bytes 184328 | tf_op jit(solution)/shard_map/ppermute | solution.py:559
  9.0 12.6 %collective-permute-start.2 = (f32[3,40,128]{2,1,0:T(8,128)S(1)}, f32[3,40,128]{2,1,0:T(8,128)S(1)}, u32[]{:S(2)}, u32[]{:S(2)}) collective-permute-start(f32[3,40,128]{2,1,0:T(8,128)S(1)} %get-tuple-element.44), channel_id=1, source_target_pairs={{0,1},{1,0},{2,3},{3,2},{4,5},{5,4},{6,7},{7,6},{8,9},{9,8},{10,11... | collective-permute-start | bytes 184328 | tf_op jit(solution)/shard_map/ppermute | solution.py:559
  10.2 2.9 %collective-permute-start.4 = (f32[32,128]{1,0:T(8,128)S(1)}, f32[32,128]{1,0:T(8,128)S(1)}, u32[]{:S(2)}, u32[]{:S(2)}) collective-permute-start(f32[32,128]{1,0:T(8,128)S(1)} %get-tuple-element.39), channel_id=1, source_target_pairs={{0,1},{1,0},{2,3},{3,2},{4,5},{5,4},{6,7},{7,6},{8,9},{9,8},{10,11... | collective-permute-start | bytes 49160 | tf_op jit(solution)/shard_map/ppermute | solution.py:559
  13.1 13.3 %collective-permute-start.6 = (f32[32,128]{1,0:T(8,128)S(1)}, f32[32,128]{1,0:T(8,128)S(1)}, u32[]{:S(2)}, u32[]{:S(2)}) collective-permute-start(f32[32,128]{1,0:T(8,128)S(1)} %add.6), channel_id=1, source_target_pairs={{8,2},{9,3},{10,0},{11,1},{12,6},{13,7},{14,4},{15,5},{16,10},{17,... | collective-permute-start | bytes 49160 | tf_op jit(solution)/shard_map/ppermute | solution.py:559
  18.3 8.1 %collective-permute-start.5 = (f32[32,128]{1,0:T(8,128)S(1)}, f32[32,128]{1,0:T(8,128)S(1)}, u32[]{:S(2)}, u32[]{:S(2)}) collective-permute-start(f32[32,128]{1,0:T(8,128)S(1)} %add.6), channel_id=1, source_target_pairs={{8,0},{9,1},{10,2},{11,3},{12,4},{13,5},{14,6},{15,7},{16,8},{17,9... | collective-permute-start | bytes 49160 | tf_op jit(solution)/shard_map/ppermute | solution.py:559
  27.7 3.2 %collective-permute-start.7 = (f32[144,128]{1,0:T(8,128)S(1)}, f32[144,128]{1,0:T(8,128)S(1)}, u32[]{:S(2)}, u32[]{:S(2)}) collective-permute-start(f32[144,128]{1,0:T(8,128)S(1)} %late_modes.1), channel_id=1, source_target_pairs={{0,1},{1,0},{2,3},{3,2},{4,5},{5,4},{6,7},{7,6},{8,9},{9,8},{10,11... | collective-permute-start | bytes 221192 | tf_op jit(solution)/shard_map/ppermute | solution.py:559
  30.9 11.0 %collective-permute-start.9 = (f32[144,128]{1,0:T(8,128)S(1)}, f32[144,128]{1,0:T(8,128)S(1)}, u32[]{:S(2)}, u32[]{:S(2)}) collective-permute-start(f32[144,128]{1,0:T(8,128)S(1)} %add.7), channel_id=1, source_target_pairs={{8,2},{9,3},{10,0},{11,1},{12,6},{13,7},{14,4},{15,5},{16,10},{17,... | collective-permute-start | bytes 221192 | tf_op jit(solution)/shard_map/ppermute | solution.py:559
  32.9 9.0 %collective-permute-start.8 = (f32[144,128]{1,0:T(8,128)S(1)}, f32[144,128]{1,0:T(8,128)S(1)}, u32[]{:S(2)}, u32[]{:S(2)}) collective-permute-start(f32[144,128]{1,0:T(8,128)S(1)} %add.7), channel_id=1, source_target_pairs={{8,0},{9,1},{10,2},{11,3},{12,4},{13,5},{14,6},{15,7},{16,8},{17,9... | collective-permute-start | bytes 221192 | tf_op jit(solution)/shard_map/ppermute | solution.py:559

commit v6 on v5

--- a/solution.py
+++ b/solution.py
@@ -95,21 +95,21 @@
 
 
 def pack_kernel(
-    adjoint_hbm, source_hbm, couplings_hbm, damping_hbm,
-    adjoint_ref, coef_ref, inv_ref, edges_ref, span_ref, corner_ref, inner_ref, outer_ref,
-    source_ref, couplings_ref, damping_ref, sems,
+    adjoint_hbm, source_hbm, couplings_hbm, damping_hbm, blades_hbm, *refs, groups, length,
 ):
+    (adjoint_ref, coef_ref, inv_ref, edges_ref, span_ref, small_ref, inner_ref, outer_ref, table_ref, blades_ref) = refs[5:15]
+    source_ref, couplings_ref, damping_ref, sems = refs[20:]
     components, axial, span, pitch = adjoint_ref.shape
     copies = [
         pltpu.make_async_copy(src, dst, sems.at[n])
         for n, (src, dst) in enumerate((
             (couplings_hbm, couplings_ref), (damping_hbm, damping_ref), (source_hbm, source_ref),
-            (adjoint_hbm, adjoint_ref),
+            (adjoint_hbm, adjoint_ref), (blades_hbm, blades_ref), *zip(refs[:5], refs[15:20]),
         ))
     ]
     for copy in copies:
         copy.start()
-    side, place = lax.axis_index("span"), lax.axis_index("pitch")
+    row, side, place = (lax.axis_index(name) for name in AXES)
     copies[0].wait()
     copies[1].wait()
     diag = damping_ref[...]
@@ -135,7 +135,6 @@
     )
     edge_row = pl.multiple_of(jnp.where(side == 0, span - EDGE, 0), EDGE)
     near, far = slots(fields + 1, components)
-    groups = inner_ref.shape[0]
     lane = lanes((span, pitch)) % SEGMENT_LANES
     sides = []
     for near_at, far_at in ((3 * EDGE - HALF, 3 * EDGE - HALF - 1), (EDGE, EDGE + HALF)):
@@ -148,10 +147,21 @@
         sides.append(packed)
     even = lax.rem(place, 2) == 0
     for g in range(groups):
-        inner_ref[g, :span] = jnp.where(even, sides[0][g], sides[1][g])
-        outer_ref[g, :span] = jnp.where(even, sides[1][g], sides[0][g])
-        corner_ref[g] = inner_ref[g, pl.ds(edge_row, EDGE), :]
-        corner_ref[groups + g] = outer_ref[g, pl.ds(edge_row, EDGE), :]
+        for n, (out_ref, value) in enumerate((
+            (inner_ref, jnp.where(even, sides[0][g], sides[1][g])), (outer_ref, jnp.where(even, sides[1][g], sides[0][g])),
+        )):
+            out_ref[pl.ds(g * span, span), :] = value
+            small_ref[pl.ds((n * (groups + 1) + g) * EDGE, EDGE), :] = out_ref[pl.ds(g * span + edge_row, EDGE), :]
+    copies[4].wait()
+    face = jnp.maximum(row - 1, 0)
+    component, mode, sine = column(lanes((pitch, pitch)))
+    number = mode_number(mode, [picked(blades_ref[...], face + n) for n in range(2)])
+    cos_table, sin_table = waves(number * (place * pitch + rows((pitch, pitch))), length)
+    table = jnp.where(component < components, jnp.where(sine, sin_table, cos_table), 0.0)
+    table_ref[...] = table
+    start = groups * span + (groups + 1) * EDGE
+    inner_ref[pl.ds(start, span), :] = projected([adjoint_ref[c, 0] for c in range(components)], table)
+    small_ref[pl.ds(groups * EDGE, EDGE), :] = inner_ref[pl.ds(start + edge_row, EDGE), :]
 
     to_low, to_high = half_rows(side)
     line = rows((EDGE, pitch))
@@ -170,38 +180,13 @@
         for k in range(min(EDGE, components * axial - n * EDGE)):
             value = jnp.where(line == k, pltpu.roll(tiles[n * EDGE + k], lax.rem(k + EDGE - fifth, EDGE), 0), value)
         span_ref[pairs + n] = value
-
-
-def prepare_kernel(
-    blades_hbm, jacobians_hbm, adjoint_ref, table_ref, rows_ref, modes_ref, blades_ref, jacobians_ref, sems,
-    *, row_count, length,
-):
-    components, _, span, pitch = adjoint_ref.shape
-    copies = [
-        pltpu.make_async_copy(blades_hbm, blades_ref, sems.at[0]),
-        pltpu.make_async_copy(jacobians_hbm, jacobians_ref, sems.at[1]),
-    ]
-    for copy in copies:
-        copy.start()
-    row, place = lax.axis_index("row"), lax.axis_index("pitch")
-    copies[0].wait()
-    component, mode, sine = column(lanes((pitch, pitch)))
-    face = jnp.maximum(row - 1, 0)
-    number = mode_number(mode, (blades_ref[face], blades_ref[face + 1]))
-    cos_table, sin_table = waves(number * (place * pitch + rows((pitch, pitch))), length)
-    table = jnp.where(component < components, jnp.where(sine, sin_table, cos_table), 0.0)
-    table_ref[...] = table
-    modes_ref[...] = projected([adjoint_ref[c, 0] for c in range(components)], table)
-    copies[1].wait()
-    entries = 6 * components * components
-    for b in range(components):
-        for c in range(components):
-            for d in range(6):
-                entry = jnp.full((1, pitch), jacobians_ref[b, c, 0, d], jnp.float32)
-                rows_ref[pl.ds((b * components + c) * 6 + d, 1), :] = entry
-    face = jnp.minimum(row, row_count - 2)
-    for n in range(2):
-        rows_ref[pl.ds(entries + n, 1), :] = jnp.full((1, pitch), blades_ref[face + n].astype(jnp.float32), jnp.float32)
+    for copy in copies[5:]:
+        copy.wait()
+
+
+def picked(values, at):
+    chosen = jnp.where(lanes(values.shape) == at, values.astype(jnp.float32), 0.0)
+    return jnp.sum(chosen, axis=1, keepdims=True).astype(jnp.int32)
 
 
 def projected(strips, table):
@@ -221,22 +206,17 @@
 
 
 def synth_kernel(
-    rows_ref, giles_re_hbm, giles_im_hbm, orders_hbm, cells_hbm, synth_ref,
-    giles_re_ref, giles_im_ref, orders_ref, cells_ref, sums_ref, sems,
+    blades_ref, jacobians_ref, giles_re_ref, giles_im_ref, orders_ref, cells_ref, synth_ref, rows_ref, sums_ref,
     *, row_count, place_count, components, pitch, length, axial,
 ):
-    copies = [
-        pltpu.make_async_copy(src, dst, sems.at[n])
-        for n, (src, dst) in enumerate((
-            (orders_hbm, orders_ref), (giles_re_hbm, giles_re_ref), (giles_im_hbm, giles_im_ref), (cells_hbm, cells_ref),
-        ))
-    ]
-    for copy in copies:
-        copy.start()
     row, place = lax.axis_index("row"), lax.axis_index("pitch")
     face = jnp.minimum(row, row_count - 2)
-    for copy in copies:
-        copy.wait()
+    for b in range(components):
+        for c in range(components):
+            entries = jacobians_ref[b, c]
+            for d in range(6):
+                at = (b * components + c) * 6 + d
+                rows_ref[pl.ds(at, 1), :] = jnp.broadcast_to(entries[:, d:d + 1], (1, pitch))
     modes = orders_ref.shape[2]
     orders = orders_ref[face]
     tag = BASE * orders[0:1] + orders[1:2]
@@ -275,8 +255,7 @@
     edge_cells = upright(edge)[first:first + SEGMENT_LANES]
     at_cells = jnp.concatenate([upright(own), edge_cells], 0)
     _, mode, _ = column(lanes(at_cells.shape))
-    entries = 6 * components * components
-    blades = [rows_ref[pl.ds(entries + n, 1), :].astype(jnp.int32) for n in range(2)]
+    blades = [picked(blades_ref[...], face + n) for n in range(2)]
     cos_table, sin_table = waves(mode_number(mode, blades) * at_cells, length)
     for c in range(components):
         row_cos = jnp.zeros((1, pitch), jnp.float32)
@@ -364,7 +343,7 @@
 
 def first_kernel(
     jac_ref, adjoint_ref, coef_in_ref, inv_in_ref, edges_ref, span_ref, inner_ref, outer_ref, table_ref,
-    coef_ref, inv_ref, edge_coef_ref, state_ref, edge_ref, modes_ref, part_ref,
+    coef_ref, inv_ref, edge_coef_ref, state_ref, edge_ref, modes_ref, part_ref, *, groups,
 ):
     components, axial, span, pitch = adjoint_ref.shape
     wide = span + EDGE
@@ -385,8 +364,14 @@
         return value
 
     even = lax.rem(lax.axis_index("pitch"), 2) == 0
-    from_left = [jnp.where(even, outer_ref[g], inner_ref[g]) for g in range(inner_ref.shape[0])]
-    from_right = [jnp.where(even, inner_ref[g], outer_ref[g]) for g in range(inner_ref.shape[0])]
+
+    def group(ref, g):
+        corner = ref[pl.ds(groups * span + g * EDGE, EDGE), :]
+        return jnp.concatenate([ref[pl.ds(g * span, span), :], corner], 0)
+
+    halves = [(group(inner_ref, g), group(outer_ref, g)) for g in range(groups)]
+    from_left = [jnp.where(even, outer, inner) for inner, outer in halves]
+    from_right = [jnp.where(even, inner, outer) for inner, outer in halves]
     near, far = slots(fields + 1, components)
     keep_five = keep_half | (line == fifth)
     for f in range(fields + 1):
@@ -445,21 +430,27 @@
 
     lax.fori_loop(0, axial, sweep, 0)
     strips = [
-        jnp.concatenate(
-            [state_ref[t, c, 1] for t in range(1, axial)] + [state_ref[axial, c, 1, :span], state_ref[0, c, 1, span:]], 0,
-        )
+        jnp.concatenate([state_ref[t, c, 1] for t in range(1, axial)] + [state_ref[axial, c, 1, :span]], 0)
         for c in range(components)
     ]
     total = projected(strips, table_ref[...])
-    to_low, to_high = half_rows(1 - side)
+    ghosts = jnp.zeros((EDGE, pitch), jnp.float32)
     for t in range(1, axial):
-        modes_ref[pl.ds((t - 1) * span, span), :] = total[(t - 1) * wide:(t - 1) * wide + span]
-    last = (axial - 1) * wide
-    part_ref[...] = total[last:last + span]
-    ghosts = [total[last + span:]] + [total[t * wide + span:(t + 1) * wide] for t in range(axial - 1)]
-    for n in range(axial // 2):
-        both = jnp.where(line < HALF, pltpu.roll(ghosts[2 * n], to_low, 0), pltpu.roll(ghosts[2 * n + 1], to_high, 0))
-        modes_ref[pl.ds((axial - 1) * span + n * EDGE, EDGE), :] = both
+        part = total[(t - 1) * wide:t * wide]
+        modes_ref[pl.ds((t - 1) * span, span), :] = part[:span]
+        keep, to_packed, _ = ghost_rows(side, t, axial)
+        ghosts = jnp.where(keep, pltpu.roll(part[span:], to_packed, 0), ghosts)
+    modes_ref[pl.ds((axial - 1) * span, EDGE), :] = ghosts
+    part_ref[...] = total[(axial - 1) * wide:]
+
+
+def ghost_rows(side, t, axial):
+    line = rows((EDGE, 1))
+    distance = jnp.where(side == 0, line, EDGE - 1 - line)
+    start = sum(axial - n for n in range(1, t))
+    to_packed = jnp.where(side == 0, start, (EDGE - start) % EDGE)
+    from_packed = jnp.where(side == 0, (EDGE - start) % EDGE, start)
+    return (distance >= start) & (distance < start + axial - t), to_packed, from_packed
 
 
 def along_axis(jac_ref, coef_ref, delta, a, height):
@@ -478,7 +469,7 @@
 ):
     span, pitch = part_ref.shape
     components, axial = coef_ref.shape[0] - 6, coef_ref.shape[1]
-    field = synthesised(modes_a_ref[...] + modes_b_ref[...], synth_ref[:components * pitch])
+    field = synthesised(modes_a_ref[EDGE:] + modes_b_ref[EDGE:], synth_ref[:components * pitch])
     delta = [inv_ref[:span] * field[:, c * pitch:(c + 1) * pitch] for c in range(components)]
     for a in range(axial - 2, -1, -1):
         delta = along_axis(jac_ref, coef_ref, delta, a, span)
@@ -487,41 +478,71 @@
     modes_ref[before:] = part_ref[...] + projected(delta, table_ref[...])
 
 
-def second_kernel(
-    jac_ref, coef_ref, inv_ref, edge_coef_ref, state_in_ref, edge_in_ref, modes_a_ref, modes_b_ref, more_a_ref, more_b_ref,
-    synth_ref, state_ref, edge_ref, out_ref, bound_ref,
+def between_kernel(
+    jac_ref, coef_ref, inv_ref, edge_coef_ref, state_in_ref, edge_in_ref, modes_a_ref, modes_b_ref, synth_ref, more_ref,
+    state_ref, edge_ref, sent_ref,
 ):
-    components, axial, span, pitch = out_ref.shape
-    wide = span + EDGE
-    from_low, from_high = half_rows(1 - lax.axis_index("span"))
-    more = more_a_ref[...] + more_b_ref[...]
-    own = [modes_a_ref[...] + modes_b_ref[...]] + [more[t * span:(t + 1) * span] for t in range(axial - 1)]
-    start = (axial - 1) * span
-    parts = []
-    for t in range(axial):
-        ghost = more[start + t // 2 * EDGE:start + (t // 2 + 1) * EDGE]
-        parts += [own[t], pltpu.roll(ghost, from_high if t % 2 else from_low, 0)]
-    field = synthesised(jnp.concatenate(parts + [more[start + axial // 2 * EDGE:]], 0), synth_ref[...])
-    edge_bound = []
-    for n in range(axial):
-        part = field[n * wide:(n + 1) * wide]
-        edge_bound.append([])
-        for c in range(components):
-            bound_ref[n, c] = inv_ref[...] * part[:, c * pitch:(c + 1) * pitch]
-            edge_bound[n].append(edge_coef_ref[components + 6] * edge_boundary(part, c, components, pitch, axial))
-    for c in range(components):
-        bound_ref[axial, c, :span] = inv_ref[:span] * field[axial * wide:, c * pitch:(c + 1) * pitch]
-    delta = [bound_ref[0, c] for c in range(components)]
+    sent_ref[...] = more_ref[...]
+    components, axial = state_ref.shape[1], state_ref.shape[2] - 2
+    wide, pitch = state_ref.shape[3:]
+    modes = modes_a_ref[...] + modes_b_ref[...]
+    field = synthesised(jnp.concatenate([modes[EDGE:], modes[:EDGE]], 0), synth_ref[...])
+    delta = [inv_ref[...] * field[:, c * pitch:(c + 1) * pitch] for c in range(components)]
     for t in range(1, axial + 1):
         for c in range(components):
             state_ref[t, c, axial + 1 - t] += delta[c]
         if t < axial:
             delta = along_axis(jac_ref, coef_ref, delta, axial - 1 - t, wide)
     for c in range(components):
-        edge_ref[1, c] += edge_bound[0][c]
+        edge_ref[1, c] += edge_coef_ref[components + 6] * edge_boundary(field, c, components, pitch, axial)
+    refs = (jac_ref, state_ref, edge_ref, coef_ref)
+
+    def sweep(t, carry):
+        advance(refs, t, axial - t)
+
+        @pl.when(t < axial)
+        def _():
+            for c, value in enumerate(edge_update(jac_ref, edge_ref, edge_coef_ref, t, axial)):
+                edge_ref[t + 1, c] = value
+
+        return carry
+
+    lax.fori_loop(1, axial + 1, sweep, 0)
+
+
+def second_kernel(
+    jac_ref, coef_ref, inv_ref, edge_coef_ref, state_in_ref, edge_in_ref, more_a_ref, more_b_ref, synth_ref,
+    state_ref, edge_ref, out_ref, bound_ref,
+):
+    components, axial, span, pitch = out_ref.shape
+    wide = span + EDGE
+    side = lax.axis_index("span")
+    more = more_a_ref[...] + more_b_ref[...]
+    start = (axial - 1) * span
+    parts = []
     for t in range(1, axial):
-        for c, value in enumerate(edge_update(jac_ref, edge_ref, edge_coef_ref, t, axial)):
-            edge_ref[t + 1, c] = value + edge_bound[t][c]
+        _, _, from_packed = ghost_rows(side, t, axial)
+        parts += [more[(t - 1) * span:t * span], pltpu.roll(more[start:start + EDGE], from_packed, 0)]
+    field = synthesised(jnp.concatenate(parts + [more[start + EDGE:]], 0), synth_ref[...])
+    for t in range(1, axial):
+        part = field[(t - 1) * wide:t * wide]
+        for c in range(components):
+            bound_ref[t, c] = inv_ref[...] * part[:, c * pitch:(c + 1) * pitch]
+    for c in range(components):
+        bound_ref[axial, c, :span] = inv_ref[:span] * field[(axial - 1) * wide:, c * pitch:(c + 1) * pitch]
+    delta = [bound_ref[1, c] for c in range(components)]
+    for t in range(2, axial + 2):
+        for c in range(components):
+            state_ref[t, c, axial + 2 - t] += delta[c]
+        if t < axial + 1:
+            delta = along_axis(jac_ref, coef_ref, delta, axial - t, wide)
+    for t in range(1, axial):
+        if t > 1:
+            for c, value in enumerate(edge_update(jac_ref, edge_ref, edge_coef_ref, t, axial)):
+                edge_ref[t + 1, c] = value
+        part = field[(t - 1) * wide:t * wide]
+        for c in range(components):
+            edge_ref[t + 1, c] += edge_coef_ref[components + 6] * edge_boundary(part, c, components, pitch, axial)
     refs = (jac_ref, state_ref, edge_ref, coef_ref)
 
     def sweep(t, carry):
@@ -529,20 +550,21 @@
             advance(refs, t, a)
             return inner
 
-        lax.fori_loop(axial - t, axial, body, 0)
+        lax.fori_loop(axial + 1 - t, axial, body, 0)
         for c in range(components):
             state_ref[t + 1, c, axial] += bound_ref[t, c]
         return carry
 
-    lax.fori_loop(1, axial, sweep, 0)
+    lax.fori_loop(2, axial, sweep, 0)
 
     def final(a, carry):
         for c, value in enumerate(layer_update(*refs, axial, a)):
             out_ref[c, a] = value[:span]
         return carry
 
-    lax.fori_loop(0, axial, final, 0)
+    lax.fori_loop(1, axial, final, 0)
     for c in range(components):
+        out_ref[c, 0] = state_ref[axial + 1, c, 1, :span]
         out_ref[c, axial - 1] += bound_ref[axial, c, :span]
 
 
@@ -569,6 +591,7 @@
     components, axial, span, pitch = adjoint_start.shape
     row_count, span_count, place_count = (lax.axis_size(name) for name in AXES)
     length = pitch * place_count
+    assert sum(axial - t for t in range(1, axial)) <= EDGE
     assert components == COMPONENTS and components * WAVES <= pitch
     assert axial == ITERS - 1 and ITERS <= EDGE and axial * SEGMENT_LANES == pitch
     assert span_count == 2 and place_count > 1 and place_count & (place_count - 1) == 0
@@ -596,29 +619,26 @@
             name=name,
         )(*[value for _, value in ins])
 
-    adjoint, coef, inv, edges, span_out, corner, inner, outer = call(
+    tables = (
+        jacobians.transpose(2, 3, 0, 1), giles_real.transpose(2, 3, 0, 1), giles_imag.transpose(2, 3, 0, 1),
+        mode_orders.transpose(0, 2, 1), cell_map,
+    )
+    blades = blades.reshape(1, -1)
+    corner_rows = groups * EDGE
+    adjoint, coef, inv, edges, span_out, small, inner, outer, table, blades, *tables = call(
         pack_kernel, "pack",
         (
-            struct(components, axial, span, pitch),
-            struct(components + 6, axial, span, pitch), struct(span, pitch), struct(fields + 1, span, pitch),
-            struct(span_tiles, EDGE, pitch), struct(2 * groups, EDGE, pitch), struct(groups, wide, pitch),
-            struct(groups, wide, pitch),
+            struct(components, axial, span, pitch), struct(components + 6, axial, span, pitch), struct(span, pitch),
+            struct(fields + 1, span, pitch), struct(span_tiles, EDGE, pitch), struct(2 * corner_rows + EDGE, pitch),
+            struct(groups * span + corner_rows + EDGE + span, pitch), struct(groups * span + corner_rows, pitch),
+            struct(pitch, pitch), *(jax.ShapeDtypeStruct(x.shape, x.dtype) for x in (blades, *tables)),
         ),
-        [(hbm, in_hbm(x)) for x in (adjoint_start, source, couplings, damping)],
+        [(hbm, in_hbm(x)) for x in (adjoint_start, source, couplings, damping, blades, *tables)],
         scratch=[
             pltpu.VMEM(source.shape, jnp.float32), pltpu.VMEM(couplings.shape, jnp.float32),
-            pltpu.VMEM(damping.shape, jnp.float32), pltpu.SemaphoreType.DMA((4,)),
+            pltpu.VMEM(damping.shape, jnp.float32), pltpu.SemaphoreType.DMA((5 + len(tables),)),
         ],
-    )
-    table, jac, modes = call(
-        prepare_kernel, "prepare",
-        (struct(pitch, pitch), struct(6 * components * components + 2, pitch), struct(span, pitch)),
-        [(hbm, in_hbm(blades)), (hbm, in_hbm(jacobians.transpose(2, 3, 0, 1))), (vmem, adjoint)],
-        scratch=[
-            pltpu.SMEM(blades.shape, jnp.int32), pltpu.SMEM((components, components, 1, 6), jnp.float32),
-            pltpu.SemaphoreType.DMA((2,)),
-        ],
-        row_count=row_count, length=length,
+        groups=groups, length=length,
     )
     steps = [1 << n for n in range(place_count.bit_length() - 2)]
     last_step = place_count // 2
@@ -629,54 +649,61 @@
     def far(x):
         return moved(x, lambda r, s, p: (r - 1, s, p ^ last_step))
 
-    corner = moved(corner, lambda r, s, p: (r, 1 - s, p))
+    small = moved(small, lambda r, s, p: (r, 1 - s, p))
     from_span = moved(span_out, lambda r, s, p: (r, 1 - s, p))
-    inner = lax.dynamic_update_slice(inner, corner[:groups], (0, span, 0))
-    outer = lax.dynamic_update_slice(outer, corner[groups:], (0, span, 0))
+    inner = lax.dynamic_update_slice(inner, small[:corner_rows + EDGE], (groups * span, 0))
+    outer = lax.dynamic_update_slice(outer, small[corner_rows + EDGE:], (groups * span, 0))
+    modes = inner[groups * span + corner_rows:]
     outer = moved(outer, lambda r, s, p: (r, s, (p - 1 + 2 * (p % 2)) % place_count))
     inner = moved(inner, lambda r, s, p: (r, s, p ^ 1))
 
-    for step in steps:
+    modes = modes + inner[groups * span + corner_rows:] if steps else modes
+    for step in steps[1:]:
         modes = modes + moved(modes, lambda r, s, p: (r, s, p ^ step))
     modes_b = far(modes)
     modes_a = near(modes)
 
-    state_shape = struct(axial + 1, components, axial + 2, wide, pitch)
+    synth, jac = call(
+        synth_kernel, "synth",
+        (
+            struct(-(-components * (pitch + SEGMENT_LANES) // pitch) * pitch, pitch),
+            struct(-(-6 * components * components // EDGE) * EDGE, pitch),
+        ),
+        [(vmem, x) for x in (blades, *tables)],
+        scratch=[pltpu.VMEM((2, components * components, mode_orders.shape[1]), jnp.float32)],
+        row_count=row_count, place_count=place_count, components=components, pitch=pitch, length=length, axial=axial,
+    )
+    state_shape = struct(axial + 2, components, axial + 2, wide, pitch)
     edge_shape = struct(axial + 1, components, wide, pitch)
     coef, inv, edge_coef, state, edge, more, part = call(
         first_kernel, "first_sweeps",
         (
             struct(components + 6, axial, wide, pitch), struct(wide, pitch), struct(components + 7, wide, pitch),
             state_shape, edge_shape,
-            struct((axial - 1) * span + axial // 2 * EDGE, pitch), struct(span, pitch),
+            struct((axial - 1) * span + EDGE, pitch), struct(span, pitch),
         ),
         [(vmem, jac)] + [(vmem, x) for x in (adjoint, coef, inv, edges, from_span, inner, outer, table)],
-    )
-
-    tables = (
-        giles_real.transpose(2, 3, 0, 1), giles_imag.transpose(2, 3, 0, 1), mode_orders.transpose(0, 2, 1), cell_map,
-    )
-    synth = call(
-        synth_kernel, "synth", struct(-(-components * (pitch + SEGMENT_LANES) // pitch) * pitch, pitch),
-        [(vmem, jac)] + [(hbm, in_hbm(x)) for x in tables],
-        scratch=[pltpu.VMEM(x.shape, x.dtype) for x in tables] + [
-            pltpu.VMEM((2, components * components, mode_orders.shape[1]), jnp.float32), pltpu.SemaphoreType.DMA((4,)),
-        ],
-        row_count=row_count, place_count=place_count, components=components, pitch=pitch, length=length, axial=axial,
-    )
+        groups=groups,
+    )
+
+    more_shape = struct(axial * span + EDGE, pitch)
     more = call(
-        late_kernel, "late_modes", struct(axial * span + axial // 2 * EDGE, pitch),
+        late_kernel, "late_modes", more_shape,
         [(vmem, x) for x in (jac, coef, inv, part, more, modes_a, modes_b, synth, table)],
     )
+    state, edge, sent = call(
+        between_kernel, "between_sweeps", (state_shape, edge_shape, more_shape),
+        [(vmem, x) for x in (jac, coef, inv, edge_coef, state, edge, modes_a, modes_b, synth, more)],
+        aliases={4: 0, 5: 1},
+    )
     for step in steps:
-        more = more + moved(more, lambda r, s, p: (r, s, p ^ step))
+        got = moved(more, lambda r, s, p: (r, s, p ^ step))
+        more, sent = sent + got, sent + got
     more_b = far(more)
     more_a = near(more)
     return call(
         second_kernel, "second_sweeps", (state_shape, edge_shape, struct(components, axial, span, pitch)),
-        [(vmem, x) for x in (
-            jac, coef, inv, edge_coef, state, edge, modes_a, modes_b, more_a, more_b, synth,
-        )],
+        [(vmem, x) for x in (jac, coef, inv, edge_coef, state, edge, more_a, more_b, synth)],
         aliases={4: 0, 5: 1},
         scratch=[pltpu.VMEM((axial + 1, components, wide, pitch), jnp.float32)],
     )[2]

time: 47.4 us -> 43.6 us (0.920)
  waiting for transfers between devices: 11.9 us -> 6.84 us
  starting transfers between devices: 19.2 us -> 20.3 us
    ppermute x10 -> x9, waiting for transfers between devices: 11.9 us -> 6.84 us  [moved(): return lax.ppermute(x, AXES, pairs)]
    ppermute x10 -> x9, starting transfers between devices: 19.2 us -> 20.3 us  [moved(): return lax.ppermute(x, AXES, pairs)]
  transfers between devices with their start and end apart: 10 -> 9, of which waited for: 4 -> 2; matrix products, arithmetic and copies ran while one was open for 0% -> 0% of each run, Pallas kernels for 15% -> 19%
where the time goes in v6:
time: 43.6 us; the launch traced here: 43.4 us
  starting transfers between devices  20.3 us (47%)
  Pallas kernels  16.1 us (37%)
  waiting for transfers between devices  6.84 us (16%)
    ppermute x9, starting transfers between devices, moved(): return lax.ppermute(x, AXES, pairs)  20.3 us
    pallas_call x6, Pallas kernels, call(): pl.pallas_call(functools.partial(kernel, **fixed), out_shape=outs, in_spe...  16.1 us
    ppermute x9, waiting for transfers between devices, moved(): return lax.ppermute(x, AXES, pairs)  6.84 us
  transfers between devices with their start and end apart: 9, of which 2 were waited for; matrix products, arithmetic and copies ran while one was open for 0% of the time, Pallas kernels for 19%

profile of v6, /device:TPU:1, one launch (start us, length us, event | category | flops | bytes accessed | tf_op | source)
XLA Modules:
  0.0 43.4 jit_solution(14954040256954632131)
XLA Ops:
  0.0 2.7 %pack.1 = (f32[5,4,32,128]{3,2,1,0:T(8,128)S(1)}, f32[11,4,32,128]{3,2,1,0:T(8,128)S(1)}, f32[32,128]{1,0:T(8,128)S(1)}, f32[17,32,128]{2,1,0:T(8,128)S(1)}, f32...) custom-call(f32[5,4,32,128]{3,2,1,0:T(8,128)} %adjoint_hbm.1, ...), custom_call_target="tpu_custom_call" | custom-call | tf_op jit(solution)/shard_map/pack/pallas_call | solution.py:611
  2.7 2.1 %collective-permute-start.1 = (f32[56,128]{1,0:T(8,128)S(1)}, f32[56,128]{1,0:T(8,128)S(1)}, u32[]{:S(2)}, u32[]{:S(2)}) collective-permute-start(f32[56,128]{1,0:T(8,128)S(1)} %get-tuple-element.46), channel_id=1, source_target_pairs={{0,4},{1,5},{2,6},{3,7},{4,0},{5,1},{6,2},{7,3},{8,12},{9,13},{10,... | collective-permute-start | bytes 86024 | tf_op jit(solution)/shard_map/ppermute | solution.py:581
  4.8 0.1 collective-permute-start
  4.9 1.2 %collective-permute-done.1 = f32[56,128]{1,0:T(8,128)S(1)} collective-permute-done((f32[56,128]{1,0:T(8,128)S(1)}, f32[56,128]{1,0:T(8,128)S(1)}, u32[]{:S(2)}, u32[]{:S(2)}) %collective-permute-start.1) | collective-permute-done | bytes 28704 | tf_op jit(solution)/shard_map/ppermute | solution.py:581
  6.1 1.5 %collective-permute-start.2 = (f32[160,128]{1,0:T(8,128)S(1)}, f32[160,128]{1,0:T(8,128)S(1)}, u32[]{:S(2)}, u32[]{:S(2)}) collective-permute-start(f32[160,128]{1,0:T(8,128)S(1)} %slice_dynamic-update-slice_fusion), channel_id=1, source_target_pairs={{0,1},{1,0},{2,3},{3,2},{4,5},{5,4},{6,7},{7,6},{8,9},{9,8},{10,11... | collective-permute-start | bytes 245768 | tf_op jit(solution)/shard_map/ppermute | solution.py:581
  7.6 2.2 %collective-permute-start.3 = (f32[120,128]{1,0:T(8,128)S(1)}, f32[120,128]{1,0:T(8,128)S(1)}, u32[]{:S(2)}, u32[]{:S(2)}) collective-permute-start(f32[120,128]{1,0:T(8,128)S(1)} %slice_dynamic-update-slice_fusion.1), channel_id=1, source_target_pairs={{0,3},{1,2},{2,1},{3,0},{4,7},{5,6},{6,5},{7,4},{8,11},{9,10},{10,... | collective-permute-start | bytes 184328 | tf_op jit(solution)/shard_map/ppermute | solution.py:581
  9.8 0.0 collective-permute-done.2.inner_ref
  9.8 7.1 %collective-permute-start.5 = (f32[40,128]{1,0:T(8,128)S(1)}, f32[40,128]{1,0:T(8,128)S(1)}, u32[]{:S(2)}, u32[]{:S(2)}) collective-permute-start(f32[40,128]{1,0:T(8,128)S(1)} %slice_add_fusion), channel_id=1, source_target_pairs={{8,2},{9,3},{10,0},{11,1},{12,6},{13,7},{14,4},{15,5},{16,10},{17,... | collective-permute-start | bytes 61448 | tf_op jit(solution)/shard_map/ppermute | solution.py:581
  16.9 1.9 %collective-permute-start.4 = (f32[40,128]{1,0:T(8,128)S(1)}, f32[40,128]{1,0:T(8,128)S(1)}, u32[]{:S(2)}, u32[]{:S(2)}) collective-permute-start(f32[40,128]{1,0:T(8,128)S(1)} %slice_add_fusion), channel_id=1, source_target_pairs={{8,0},{9,1},{10,2},{11,3},{12,4},{13,5},{14,6},{15,7},{16,8},{17,9... | collective-permute-start | bytes 61448 | tf_op jit(solution)/shard_map/ppermute | solution.py:581
  18.8 0.6 %synth.1 = (f32[896,128]{1,0:T(8,128)S(1)}, f32[152,128]{1,0:T(8,128)S(1)}) custom-call(s32[1,4]{1,0:T(1,128)S(1)} %get-tuple-element.33.blades_ref, f32[5,5,1,6]{3,2,1,0:T(1,128)S(1)} %get-tuple-element.34.jacobians_ref, f32[5,5,3,64]{3,2,1,0:T(4,128)S(1)} %get-tuple-element.35.giles_re_ref, f32[5,5,3,64]{3,2,1,0:T(4,128)S(1)} %get-tuple-element.36.giles_im_ref, ...), custom_call_target="tpu_custom_call" | custom-call | tf_op jit(solution)/shard_map/synth/pallas_call | solution.py:611
  19.4 0.0 collective-permute-done.3.outer_ref
  19.4 0.0 collective-permute-done.span_ref
  19.4 5.1 %first_sweeps.1 = (f32[11,4,40,128]{3,2,1,0:T(8,128)S(1)}, f32[40,128]{1,0:T(8,128)S(1)}, f32[12,40,128]{2,1,0:T(8,128)S(1)}, f32[6,5,6,40,128]{4,3,2,1,0:T(8,12...) custom-call(f32[152,128]{1,0:T(8,128)S(1)} %get-tuple-element.39.jac_ref, ...), custom_call_target="tpu_custom_call" | custom-call | tf_op jit(solution)/shard_map/first_sweeps/pallas_call | solution.py:611
  24.5 0.0 collective-permute-done.5.modes_b_ref
  24.5 0.0 collective-permute-done.4.modes_a_ref
  24.5 1.3 %late_modes.1.more_ref = f32[136,128]{1,0:T(8,128)S(1)} custom-call(f32[152,128]{1,0:T(8,128)S(1)} %get-tuple-element.39.jac_ref, f32[11,4,40,128]{3,2,1,0:T(8,128)S(1)} %get-tuple-element.49.coef_ref, f32[40,128]{1,0:T(8,128)S(1)} %get-tuple-element.50.inv_ref, f32[32,128]{1,0:T(8,128)S(1)} %get-tuple-element.55.part_ref, ...), custom_call_target="tpu_custom_call" | custom-call | tf_op jit(solution)/shard_map/late_modes/pallas_call | solution.py:611
  25.8 1.6 %collective-permute-start.6 = (f32[136,128]{1,0:T(8,128)S(1)}, f32[136,128]{1,0:T(8,128)S(1)}, u32[]{:S(2)}, u32[]{:S(2)}) collective-permute-start(f32[136,128]{1,0:T(8,128)S(1)} %late_modes.1.more_ref), channel_id=1, source_target_pairs={{0,1},{1,0},{2,3},{3,2},{4,5},{5,4},{6,7},{7,6},{8,9},{9,8},{10,11... | collective-permute-start | bytes 208904 | tf_op jit(solution)/shard_map/ppermute | solution.py:581
  27.4 2.8 %between_sweeps.1 = (f32[6,5,6,40,128]{4,3,2,1,0:T(8,128)S(1)}, f32[5,5,40,128]{3,2,1,0:T(8,128)S(1)}, f32[136,128]{1,0:T(8,128)S(1)}) custom-call(f32[152,128]{1,0:T(8,128)S(1)} %get-tuple-element.39.jac_ref, f32[11,4,40,128]{3,2,1,0:T(8,128)S(1)} %get-tuple-element.49.coef_ref, ...), custom_call_target="tpu_custom_call", output_to_operand_aliasing={{0}: (4, {}), {1}: (5, {})} | custom-call | tf_op jit(solution)/shard_map/between_sweeps/pallas_call | solution.py:611
  30.2 0.0 collective-permute-done.6
  30.2 1.9 %collective-permute-start.8 = (f32[136,128]{1,0:T(8,128)S(1)}, f32[136,128]{1,0:T(8,128)S(1)}, u32[]{:S(2)}, u32[]{:S(2)}) collective-permute-start(f32[136,128]{1,0:T(8,128)S(1)} %add.7), channel_id=1, source_target_pairs={{8,2},{9,3},{10,0},{11,1},{12,6},{13,7},{14,4},{15,5},{16,10},{17,... | collective-permute-start | bytes 208904 | tf_op jit(solution)/shard_map/ppermute | solution.py:581
  32.2 1.9 %collective-permute-start.7 = (f32[136,128]{1,0:T(8,128)S(1)}, f32[136,128]{1,0:T(8,128)S(1)}, u32[]{:S(2)}, u32[]{:S(2)}) collective-permute-start(f32[136,128]{1,0:T(8,128)S(1)} %add.7), channel_id=1, source_target_pairs={{8,0},{9,1},{10,2},{11,3},{12,4},{13,5},{14,6},{15,7},{16,8},{17,9... | collective-permute-start | bytes 208904 | tf_op jit(solution)/shard_map/ppermute | solution.py:581
  34.1 5.6 %collective-permute-done.8.more_b_ref = f32[136,128]{1,0:T(8,128)S(1)} collective-permute-done((f32[136,128]{1,0:T(8,128)S(1)}, f32[136,128]{1,0:T(8,128)S(1)}, u32[]{:S(2)}, u32[]{:S(2)}) %collective-permute-start.8) | collective-permute-done | bytes 69664 | tf_op jit(solution)/shard_map/ppermute | solution.py:581
  39.7 0.0 collective-permute-done.7.more_a_ref
  39.7 3.7 %second_sweeps.1 = (f32[6,5,6,40,128]{4,3,2,1,0:T(8,128)S(1)}, f32[5,5,40,128]{3,2,1,0:T(8,128)S(1)}, f32[5,4,32,128]{3,2,1,0:T(8,128)}) custom-call(f32[152,128]{1,0:T(8,128)S(1)} %get-tuple-element.39.jac_ref, f32[11,4,40,128]{3,2,1,0:T(8,128)S(1)} %get-tuple-element.49.coef_ref, ...), custom_call_target="tpu_custom_call", output_to_operand_aliasing={{0}: (4, {}), {1}: (5, {})} | custom-call | tf_op jit(solution)/shard_map/second_sweeps/pallas_call | solution.py:611
  (4 shorter events, 0.0 us)
Async XLA Ops:
  2.7 3.4 %collective-permute-start.1 = (f32[56,128]{1,0:T(8,128)S(1)}, f32[56,128]{1,0:T(8,128)S(1)}, u32[]{:S(2)}, u32[]{:S(2)}) collective-permute-start(f32[56,128]{1,0:T(8,128)S(1)} %get-tuple-element.46), channel_id=1, source_target_pairs={{0,4},{1,5},{2,6},{3,7},{4,0},{5,1},{6,2},{7,3},{8,12},{9,13},{10,... | collective-permute-start | bytes 86024 | tf_op jit(solution)/shard_map/ppermute | solution.py:581
  4.8 14.6 %collective-permute-start = (f32[36,8,128]{2,1,0:T(8,128)S(1)}, f32[36,8,128]{2,1,0:T(8,128)S(1)}, u32[]{:S(2)}, u32[]{:S(2)}) collective-permute-start(f32[36,8,128]{2,1,0:T(8,128)S(1)} %get-tuple-element.44), channel_id=1, source_target_pairs={{0,4},{1,5},{2,6},{3,7},{4,0},{5,1},{6,2},{7,3},{8,12},{9,13},{10,... | collective-permute-start | bytes 442376 | tf_op jit(solution)/shard_map/ppermute | solution.py:581
  6.1 3.7 %collective-permute-start.2 = (f32[160,128]{1,0:T(8,128)S(1)}, f32[160,128]{1,0:T(8,128)S(1)}, u32[]{:S(2)}, u32[]{:S(2)}) collective-permute-start(f32[160,128]{1,0:T(8,128)S(1)} %slice_dynamic-update-slice_fusion), channel_id=1, source_target_pairs={{0,1},{1,0},{2,3},{3,2},{4,5},{5,4},{6,7},{7,6},{8,9},{9,8},{10,11... | collective-permute-start | bytes 245768 | tf_op jit(solution)/shard_map/ppermute | solution.py:581
  7.6 11.8 %collective-permute-start.3 = (f32[120,128]{1,0:T(8,128)S(1)}, f32[120,128]{1,0:T(8,128)S(1)}, u32[]{:S(2)}, u32[]{:S(2)}) collective-permute-start(f32[120,128]{1,0:T(8,128)S(1)} %slice_dynamic-update-slice_fusion.1), channel_id=1, source_target_pairs={{0,3},{1,2},{2,1},{3,0},{4,7},{5,6},{6,5},{7,4},{8,11},{9,10},{10,... | collective-permute-start | bytes 184328 | tf_op jit(solution)/shard_map/ppermute | solution.py:581
  9.8 14.7 %collective-permute-start.5 = (f32[40,128]{1,0:T(8,128)S(1)}, f32[40,128]{1,0:T(8,128)S(1)}, u32[]{:S(2)}, u32[]{:S(2)}) collective-permute-start(f32[40,128]{1,0:T(8,128)S(1)} %slice_add_fusion), channel_id=1, source_target_pairs={{8,2},{9,3},{10,0},{11,1},{12,6},{13,7},{14,4},{15,5},{16,10},{17,... | collective-permute-start | bytes 61448 | tf_op jit(solution)/shard_map/ppermute | solution.py:581
  16.9 7.7 %collective-permute-start.4 = (f32[40,128]{1,0:T(8,128)S(1)}, f32[40,128]{1,0:T(8,128)S(1)}, u32[]{:S(2)}, u32[]{:S(2)}) collective-permute-start(f32[40,128]{1,0:T(8,128)S(1)} %slice_add_fusion), channel_id=1, source_target_pairs={{8,0},{9,1},{10,2},{11,3},{12,4},{13,5},{14,6},{15,7},{16,8},{17,9... | collective-permute-start | bytes 61448 | tf_op jit(solution)/shard_map/ppermute | solution.py:581
  25.8 4.4 %collective-permute-start.6 = (f32[136,128]{1,0:T(8,128)S(1)}, f32[136,128]{1,0:T(8,128)S(1)}, u32[]{:S(2)}, u32[]{:S(2)}) collective-permute-start(f32[136,128]{1,0:T(8,128)S(1)} %late_modes.1.more_ref), channel_id=1, source_target_pairs={{0,1},{1,0},{2,3},{3,2},{4,5},{5,4},{6,7},{7,6},{8,9},{9,8},{10,11... | collective-permute-start | bytes 208904 | tf_op jit(solution)/shard_map/ppermute | solution.py:581
  30.2 9.5 %collective-permute-start.8 = (f32[136,128]{1,0:T(8,128)S(1)}, f32[136,128]{1,0:T(8,128)S(1)}, u32[]{:S(2)}, u32[]{:S(2)}) collective-permute-start(f32[136,128]{1,0:T(8,128)S(1)} %add.7), channel_id=1, source_target_pairs={{8,2},{9,3},{10,0},{11,1},{12,6},{13,7},{14,4},{15,5},{16,10},{17,... | collective-permute-start | bytes 208904 | tf_op jit(solution)/shard_map/ppermute | solution.py:581
  32.2 7.6 %collective-permute-start.7 = (f32[136,128]{1,0:T(8,128)S(1)}, f32[136,128]{1,0:T(8,128)S(1)}, u32[]{:S(2)}, u32[]{:S(2)}) collective-permute-start(f32[136,128]{1,0:T(8,128)S(1)} %add.7), channel_id=1, source_target_pairs={{8,0},{9,1},{10,2},{11,3},{12,4},{13,5},{14,6},{15,7},{16,8},{17,9... | collective-permute-start | bytes 208904 | tf_op jit(solution)/shard_map/ppermute | solution.py:581

commit v7 on v6

--- a/solution.py
+++ b/solution.py
@@ -97,14 +97,14 @@
 def pack_kernel(
     adjoint_hbm, source_hbm, couplings_hbm, damping_hbm, blades_hbm, *refs, groups, length,
 ):
-    (adjoint_ref, coef_ref, inv_ref, edges_ref, span_ref, small_ref, inner_ref, outer_ref, table_ref, blades_ref) = refs[5:15]
-    source_ref, couplings_ref, damping_ref, sems = refs[20:]
+    (adjoint_ref, coef_ref, inv_ref, edges_ref, span_ref, small_ref, inner_ref, outer_ref, table_ref, modes_ref, blades_ref) = refs[5:16]
+    source_ref, couplings_ref, damping_ref, sems = refs[21:]
     components, axial, span, pitch = adjoint_ref.shape
     copies = [
         pltpu.make_async_copy(src, dst, sems.at[n])
         for n, (src, dst) in enumerate((
             (couplings_hbm, couplings_ref), (damping_hbm, damping_ref), (source_hbm, source_ref),
-            (adjoint_hbm, adjoint_ref), (blades_hbm, blades_ref), *zip(refs[:5], refs[15:20]),
+            (adjoint_hbm, adjoint_ref), (blades_hbm, blades_ref), *zip(refs[:5], refs[16:21]),
         ))
     ]
     for copy in copies:
@@ -151,7 +151,7 @@
             (inner_ref, jnp.where(even, sides[0][g], sides[1][g])), (outer_ref, jnp.where(even, sides[1][g], sides[0][g])),
         )):
             out_ref[pl.ds(g * span, span), :] = value
-            small_ref[pl.ds((n * (groups + 1) + g) * EDGE, EDGE), :] = out_ref[pl.ds(g * span + edge_row, EDGE), :]
+            small_ref[pl.ds((n * groups + g) * EDGE, EDGE), :] = out_ref[pl.ds(g * span + edge_row, EDGE), :]
     copies[4].wait()
     face = jnp.maximum(row - 1, 0)
     component, mode, sine = column(lanes((pitch, pitch)))
@@ -159,9 +159,8 @@
     cos_table, sin_table = waves(number * (place * pitch + rows((pitch, pitch))), length)
     table = jnp.where(component < components, jnp.where(sine, sin_table, cos_table), 0.0)
     table_ref[...] = table
-    start = groups * span + (groups + 1) * EDGE
-    inner_ref[pl.ds(start, span), :] = projected([adjoint_ref[c, 0] for c in range(components)], table)
-    small_ref[pl.ds(groups * EDGE, EDGE), :] = inner_ref[pl.ds(start + edge_row, EDGE), :]
+    modes_ref[:span] = projected([adjoint_ref[c, 0] for c in range(components)], table)
+    small_ref[pl.ds(2 * groups * EDGE, EDGE), :] = modes_ref[pl.ds(edge_row, EDGE), :]
 
     to_low, to_high = half_rows(side)
     line = rows((EDGE, pitch))
@@ -342,8 +341,8 @@
 
 
 def first_kernel(
-    jac_ref, adjoint_ref, coef_in_ref, inv_in_ref, edges_ref, span_ref, inner_ref, outer_ref, table_ref,
-    coef_ref, inv_ref, edge_coef_ref, state_ref, edge_ref, modes_ref, part_ref, *, groups,
+    jac_ref, adjoint_ref, coef_in_ref, inv_in_ref, edges_ref, inner_ref, outer_ref, span_ref,
+    coef_ref, inv_ref, edge_coef_ref, state_ref, edge_ref, *, groups,
 ):
     components, axial, span, pitch = adjoint_ref.shape
     wide = span + EDGE
@@ -412,6 +411,11 @@
             state_ref[t, c, 0] = jnp.zeros((wide, pitch), jnp.float32)
             state_ref[t, c, axial + 1] = jnp.zeros((wide, pitch), jnp.float32)
 
+    sweeps_without_boundaries(jac_ref, state_ref, edge_ref, coef_ref, edge_coef_ref, 0, 1)
+
+
+def sweeps_without_boundaries(jac_ref, state_ref, edge_ref, coef_ref, edge_coef_ref, first, last):
+    axial = state_ref.shape[2] - 2
     refs = (jac_ref, state_ref, edge_ref, coef_ref)
 
     def sweep(t, carry):
@@ -428,7 +432,17 @@
 
         return carry
 
-    lax.fori_loop(0, axial, sweep, 0)
+    lax.fori_loop(first, last, sweep, 0)
+
+
+def more_kernel(
+    jac_ref, coef_ref, edge_coef_ref, state_in_ref, edge_in_ref, table_ref, state_ref, edge_ref, modes_ref, part_ref,
+):
+    components, axial = state_ref.shape[1], state_ref.shape[2] - 2
+    wide, pitch = state_ref.shape[3:]
+    span = wide - EDGE
+    side = lax.axis_index("span")
+    sweeps_without_boundaries(jac_ref, state_ref, edge_ref, coef_ref, edge_coef_ref, 1, axial)
     strips = [
         jnp.concatenate([state_ref[t, c, 1] for t in range(1, axial)] + [state_ref[axial, c, 1, :span]], 0)
         for c in range(components)
@@ -469,7 +483,7 @@
 ):
     span, pitch = part_ref.shape
     components, axial = coef_ref.shape[0] - 6, coef_ref.shape[1]
-    field = synthesised(modes_a_ref[EDGE:] + modes_b_ref[EDGE:], synth_ref[:components * pitch])
+    field = synthesised(modes_a_ref[:span] + modes_b_ref[:span], synth_ref[:components * pitch])
     delta = [inv_ref[:span] * field[:, c * pitch:(c + 1) * pitch] for c in range(components)]
     for a in range(axial - 2, -1, -1):
         delta = along_axis(jac_ref, coef_ref, delta, a, span)
@@ -485,8 +499,7 @@
     sent_ref[...] = more_ref[...]
     components, axial = state_ref.shape[1], state_ref.shape[2] - 2
     wide, pitch = state_ref.shape[3:]
-    modes = modes_a_ref[...] + modes_b_ref[...]
-    field = synthesised(jnp.concatenate([modes[EDGE:], modes[:EDGE]], 0), synth_ref[...])
+    field = synthesised(modes_a_ref[...] + modes_b_ref[...], synth_ref[...])
     delta = [inv_ref[...] * field[:, c * pitch:(c + 1) * pitch] for c in range(components)]
     for t in range(1, axial + 1):
         for c in range(components):
@@ -625,13 +638,13 @@
     )
     blades = blades.reshape(1, -1)
     corner_rows = groups * EDGE
-    adjoint, coef, inv, edges, span_out, small, inner, outer, table, blades, *tables = call(
+    adjoint, coef, inv, edges, span_out, small, inner, outer, table, modes, blades, *tables = call(
         pack_kernel, "pack",
         (
             struct(components, axial, span, pitch), struct(components + 6, axial, span, pitch), struct(span, pitch),
             struct(fields + 1, span, pitch), struct(span_tiles, EDGE, pitch), struct(2 * corner_rows + EDGE, pitch),
-            struct(groups * span + corner_rows + EDGE + span, pitch), struct(groups * span + corner_rows, pitch),
-            struct(pitch, pitch), *(jax.ShapeDtypeStruct(x.shape, x.dtype) for x in (blades, *tables)),
+            struct(groups * wide, pitch), struct(groups * wide, pitch),
+            struct(pitch, pitch), struct(wide, pitch), *(jax.ShapeDtypeStruct(x.shape, x.dtype) for x in (blades, *tables)),
         ),
         [(hbm, in_hbm(x)) for x in (adjoint_start, source, couplings, damping, blades, *tables)],
         scratch=[
@@ -650,18 +663,15 @@
         return moved(x, lambda r, s, p: (r - 1, s, p ^ last_step))
 
     small = moved(small, lambda r, s, p: (r, 1 - s, p))
+    small, span_out = lax.optimization_barrier((small, span_out))
     from_span = moved(span_out, lambda r, s, p: (r, 1 - s, p))
-    inner = lax.dynamic_update_slice(inner, small[:corner_rows + EDGE], (groups * span, 0))
-    outer = lax.dynamic_update_slice(outer, small[corner_rows + EDGE:], (groups * span, 0))
-    modes = inner[groups * span + corner_rows:]
+    inner = lax.dynamic_update_slice(inner, small[:corner_rows], (groups * span, 0))
+    outer = lax.dynamic_update_slice(outer, small[corner_rows:2 * corner_rows], (groups * span, 0))
+    modes = lax.dynamic_update_slice(modes, small[2 * corner_rows:], (span, 0))
     outer = moved(outer, lambda r, s, p: (r, s, (p - 1 + 2 * (p % 2)) % place_count))
     inner = moved(inner, lambda r, s, p: (r, s, p ^ 1))
-
-    modes = modes + inner[groups * span + corner_rows:] if steps else modes
-    for step in steps[1:]:
+    for step in steps:
         modes = modes + moved(modes, lambda r, s, p: (r, s, p ^ step))
-    modes_b = far(modes)
-    modes_a = near(modes)
 
     synth, jac = call(
         synth_kernel, "synth",
@@ -675,17 +685,24 @@
     )
     state_shape = struct(axial + 2, components, axial + 2, wide, pitch)
     edge_shape = struct(axial + 1, components, wide, pitch)
-    coef, inv, edge_coef, state, edge, more, part = call(
-        first_kernel, "first_sweeps",
+    coef, inv, edge_coef, state, edge = call(
+        first_kernel, "first_sweep",
         (
             struct(components + 6, axial, wide, pitch), struct(wide, pitch), struct(components + 7, wide, pitch),
             state_shape, edge_shape,
-            struct((axial - 1) * span + EDGE, pitch), struct(span, pitch),
         ),
-        [(vmem, jac)] + [(vmem, x) for x in (adjoint, coef, inv, edges, from_span, inner, outer, table)],
+        [(vmem, x) for x in (jac, adjoint, coef, inv, edges, inner, outer, from_span)],
         groups=groups,
     )
-
+    inv, modes = lax.optimization_barrier((inv, modes))
+    modes_b = far(modes)
+    modes_a = near(modes)
+    state, edge, more, part = call(
+        more_kernel, "more_sweeps",
+        (state_shape, edge_shape, struct((axial - 1) * span + EDGE, pitch), struct(span, pitch)),
+        [(vmem, x) for x in (jac, coef, edge_coef, state, edge, table)],
+        aliases={3: 0, 4: 1},
+    )
     more_shape = struct(axial * span + EDGE, pitch)
     more = call(
         late_kernel, "late_modes", more_shape,

time: 43.6 us -> 45.6 us (1.046)
  starting transfers between devices: 20.3 us -> 21.6 us
  waiting for transfers between devices: 6.84 us -> 7.77 us
    ppermute x9 -> x10, starting transfers between devices: 20.3 us -> 21.6 us  [moved(): return lax.ppermute(x, AXES, pairs)]
    ppermute x9 -> x10, waiting for transfers between devices: 6.84 us -> 7.77 us  [moved(): return lax.ppermute(x, AXES, pairs)]
    pallas_call x6 -> x7, Pallas kernels: 16.1 us -> 15.8 us  [call(): pl.pallas_call(functools.partial(kernel, **fixed), out_shape=outs, in_spe...]
  transfers between devices with their start and end apart: 9 -> 10, of which waited for: 2 -> 5; matrix products, arithmetic and copies ran while one was open for 0% -> 0% of each run, Pallas kernels for 19% -> 14%
where the time goes in v7:
time: 45.6 us; the launch traced here: 45.4 us
  starting transfers between devices  21.6 us (47%)
  Pallas kernels  15.8 us (35%)
  waiting for transfers between devices  7.77 us (17%)
    ppermute x10, starting transfers between devices, moved(): return lax.ppermute(x, AXES, pairs)  21.6 us
    pallas_call x7, Pallas kernels, call(): pl.pallas_call(functools.partial(kernel, **fixed), out_shape=outs, in_spe...  15.8 us
    ppermute x10, waiting for transfers between devices, moved(): return lax.ppermute(x, AXES, pairs)  7.77 us
  transfers between devices with their start and end apart: 10, of which 5 were waited for; matrix products, arithmetic and copies ran while one was open for 0% of the time, Pallas kernels for 14%

profile of v7, /device:TPU:1, one launch (start us, length us, event | category | flops | bytes accessed | tf_op | source)
XLA Modules:
  0.0 45.4 jit_solution(16968154035875941637)
XLA Ops:
  0.0 2.7 %pack.1 = (f32[5,4,32,128]{3,2,1,0:T(8,128)S(1)}, f32[11,4,32,128]{3,2,1,0:T(8,128)S(1)}, f32[32,128]{1,0:T(8,128)S(1)}, f32[17,32,128]{2,1,0:T(8,128)S(1)}, f32...) custom-call(f32[5,4,32,128]{3,2,1,0:T(8,128)} %adjoint_hbm.1, ...), custom_call_target="tpu_custom_call" | custom-call | tf_op jit(solution)/shard_map/pack/pallas_call | solution.py:624
  2.7 2.1 %collective-permute-start = (f32[56,128]{1,0:T(8,128)S(1)}, f32[56,128]{1,0:T(8,128)S(1)}, u32[]{:S(2)}, u32[]{:S(2)}) collective-permute-start(f32[56,128]{1,0:T(8,128)S(1)} %get-tuple-element.52), channel_id=1, source_target_pairs={{0,4},{1,5},{2,6},{3,7},{4,0},{5,1},{6,2},{7,3},{8,12},{9,13},{10,... | collective-permute-start | bytes 86024 | tf_op jit(solution)/shard_map/ppermute | solution.py:594
  4.8 1.3 %collective-permute-done = f32[56,128]{1,0:T(8,128)S(1)} collective-permute-done((f32[56,128]{1,0:T(8,128)S(1)}, f32[56,128]{1,0:T(8,128)S(1)}, u32[]{:S(2)}, u32[]{:S(2)}) %collective-permute-start) | collective-permute-done | bytes 28704 | tf_op jit(solution)/shard_map/ppermute | solution.py:594
  6.1 3.5 %collective-permute-start.2 = (f32[120,128]{1,0:T(8,128)S(1)}, f32[120,128]{1,0:T(8,128)S(1)}, u32[]{:S(2)}, u32[]{:S(2)}) collective-permute-start(f32[120,128]{1,0:T(8,128)S(1)} %get-tuple-element.75), channel_id=1, source_target_pairs={{0,3},{1,2},{2,1},{3,0},{4,7},{5,6},{6,5},{7,4},{8,11},{9,10},{10,... | collective-permute-start | bytes 184328 | tf_op jit(solution)/shard_map/ppermute | solution.py:594
  9.6 0.0 collective-permute-start.1
  9.6 1.2 %collective-permute-start.3 = (f32[36,8,128]{2,1,0:T(8,128)S(1)}, f32[36,8,128]{2,1,0:T(8,128)S(1)}, u32[]{:S(2)}, u32[]{:S(2)}) collective-permute-start(f32[36,8,128]{2,1,0:T(8,128)S(1)} %get-tuple-element.56), channel_id=1, source_target_pairs={{0,4},{1,5},{2,6},{3,7},{4,0},{5,1},{6,2},{7,3},{8,12},{9,13},{10,... | collective-permute-start | bytes 442376 | tf_op jit(solution)/shard_map/ppermute | solution.py:594
  10.9 1.5 %collective-permute-start.4 = (f32[40,128]{1,0:T(8,128)S(1)}, f32[40,128]{1,0:T(8,128)S(1)}, u32[]{:S(2)}, u32[]{:S(2)}) collective-permute-start(f32[40,128]{1,0:T(8,128)S(1)} %slice_dynamic-update-slice_fusion.2), channel_id=1, source_target_pairs={{0,1},{1,0},{2,3},{3,2},{4,5},{5,4},{6,7},{7,6},{8,9},{9,8},{10,11... | collective-permute-start | bytes 61448 | tf_op jit(solution)/shard_map/ppermute | solution.py:594
  12.3 0.6 %synth.1 = (f32[896,128]{1,0:T(8,128)S(1)}, f32[152,128]{1,0:T(8,128)S(1)}) custom-call(s32[1,4]{1,0:T(1,128)S(1)} %get-tuple-element.40.blades_ref, f32[5,5,1,6]{3,2,1,0:T(1,128)S(1)} %get-tuple-element.41.jacobians_ref, f32[5,5,3,64]{3,2,1,0:T(4,128)S(1)} %get-tuple-element.42.giles_re_ref, f32[5,5,3,64]{3,2,1,0:T(4,128)S(1)} %get-tuple-element.43.giles_im_ref, ...), custom_call_target="tpu_custom_call" | custom-call | tf_op jit(solution)/shard_map/synth/pallas_call | solution.py:624
  12.9 0.7 %collective-permute-done.4 = f32[40,128]{1,0:T(8,128)S(1)} collective-permute-done((f32[40,128]{1,0:T(8,128)S(1)}, f32[40,128]{1,0:T(8,128)S(1)}, u32[]{:S(2)}, u32[]{:S(2)}) %collective-permute-start.4) | collective-permute-done | bytes 20512 | tf_op jit(solution)/shard_map/ppermute | solution.py:594
  13.6 0.0 collective-permute-done.2.outer_ref
  13.6 0.0 collective-permute-done.1.inner_ref
  13.6 0.0 collective-permute-done.3.span_ref
  13.6 1.9 %first_sweep.1 = (f32[11,4,40,128]{3,2,1,0:T(8,128)S(1)}, f32[40,128]{1,0:T(8,128)S(1)}, f32[12,40,128]{2,1,0:T(8,128)S(1)}, f32[6,5,6,40,128]{4,3,2,1,0:T(8,128)S(1)}, f32[5,5,40,128]{3,2,1,0:T(8,128)S(1)}) custom-call(f32[152,128]{1,0:T(8,128)S(1)} %get-tuple-element.46.jac_ref, f32[5,4,32,128]{3,2,1,0:T(8,128)S(1)} %get-tuple-element.47.adjoint_ref, ...), custom_call_target="tpu_custom_call" | custom-call | tf_op jit(solution)/shard_map/first_sweep/pallas_call | solution.py:624
  15.5 5.7 %collective-permute-start.6 = (f32[40,128]{1,0:T(8,128)S(1)}, f32[40,128]{1,0:T(8,128)S(1)}, u32[]{:S(2)}, u32[]{:S(2)}) collective-permute-start(f32[40,128]{1,0:T(8,128)S(1)} %add.6), channel_id=1, source_target_pairs={{8,2},{9,3},{10,0},{11,1},{12,6},{13,7},{14,4},{15,5},{16,10},{17,... | collective-permute-start | bytes 61448 | tf_op jit(solution)/shard_map/ppermute | solution.py:594
  21.3 1.9 %collective-permute-start.5 = (f32[40,128]{1,0:T(8,128)S(1)}, f32[40,128]{1,0:T(8,128)S(1)}, u32[]{:S(2)}, u32[]{:S(2)}) collective-permute-start(f32[40,128]{1,0:T(8,128)S(1)} %add.6), channel_id=1, source_target_pairs={{8,0},{9,1},{10,2},{11,3},{12,4},{13,5},{14,6},{15,7},{16,8},{17,9... | collective-permute-start | bytes 61448 | tf_op jit(solution)/shard_map/ppermute | solution.py:594
  23.2 3.1 %more_sweeps.1 = (f32[6,5,6,40,128]{4,3,2,1,0:T(8,128)S(1)}, f32[5,5,40,128]{3,2,1,0:T(8,128)S(1)}, f32[104,128]{1,0:T(8,128)S(1)}, f32[32,128]{1,0:T(8,128)S(1)}) custom-call(f32[152,128]{1,0:T(8,128)S(1)} %get-tuple-element.46.jac_ref, f32[11,4,40,128]{3,2,1,0:T(8,128)S(1)} %get-tuple-element.57.coef_ref, ...), custom_call_target="tpu_custom_call", output_to_operand_aliasing={{0}: (3, {}), {1}: (4, {})} | custom-call | tf_op jit(solution)/shard_map/more_sweeps/pallas_call | solution.py:624
  26.3 0.0 collective-permute-done.6.modes_b_ref
  26.3 0.1 collective-permute-done.5.modes_a_ref
  26.4 1.3 %late_modes.1.more_ref = f32[136,128]{1,0:T(8,128)S(1)} custom-call(f32[152,128]{1,0:T(8,128)S(1)} %get-tuple-element.46.jac_ref, f32[11,4,40,128]{3,2,1,0:T(8,128)S(1)} %get-tuple-element.57.coef_ref, f32[40,128]{1,0:T(8,128)S(1)} %get-tuple-element.60.inv_ref, f32[32,128]{1,0:T(8,128)S(1)} %get-tuple-element.69.part_ref, ...), custom_call_target="tpu_custom_call" | custom-call | tf_op jit(solution)/shard_map/late_modes/pallas_call | solution.py:624
  27.7 0.7 %collective-permute-start.7 = (f32[136,128]{1,0:T(8,128)S(1)}, f32[136,128]{1,0:T(8,128)S(1)}, u32[]{:S(2)}, u32[]{:S(2)}) collective-permute-start(f32[136,128]{1,0:T(8,128)S(1)} %late_modes.1.more_ref), channel_id=1, source_target_pairs={{0,1},{1,0},{2,3},{3,2},{4,5},{5,4},{6,7},{7,6},{8,9},{9,8},{10,11... | collective-permute-start | bytes 208904 | tf_op jit(solution)/shard_map/ppermute | solution.py:594
  28.4 2.7 %between_sweeps.1 = (f32[6,5,6,40,128]{4,3,2,1,0:T(8,128)S(1)}, f32[5,5,40,128]{3,2,1,0:T(8,128)S(1)}, f32[136,128]{1,0:T(8,128)S(1)}) custom-call(f32[152,128]{1,0:T(8,128)S(1)} %get-tuple-element.46.jac_ref, f32[11,4,40,128]{3,2,1,0:T(8,128)S(1)} %get-tuple-element.57.coef_ref, ...), custom_call_target="tpu_custom_call", output_to_operand_aliasing={{0}: (4, {}), {1}: (5, {})} | custom-call | tf_op jit(solution)/shard_map/between_sweeps/pallas_call | solution.py:624
  31.1 0.0 collective-permute-done.7
  31.2 2.9 %collective-permute-start.9 = (f32[136,128]{1,0:T(8,128)S(1)}, f32[136,128]{1,0:T(8,128)S(1)}, u32[]{:S(2)}, u32[]{:S(2)}) collective-permute-start(f32[136,128]{1,0:T(8,128)S(1)} %add.7), channel_id=1, source_target_pairs={{8,2},{9,3},{10,0},{11,1},{12,6},{13,7},{14,4},{15,5},{16,10},{17,... | collective-permute-start | bytes 208904 | tf_op jit(solution)/shard_map/ppermute | solution.py:594
  34.1 1.9 %collective-permute-start.8 = (f32[136,128]{1,0:T(8,128)S(1)}, f32[136,128]{1,0:T(8,128)S(1)}, u32[]{:S(2)}, u32[]{:S(2)}) collective-permute-start(f32[136,128]{1,0:T(8,128)S(1)} %add.7), channel_id=1, source_target_pairs={{8,0},{9,1},{10,2},{11,3},{12,4},{13,5},{14,6},{15,7},{16,8},{17,9... | collective-permute-start | bytes 208904 | tf_op jit(solution)/shard_map/ppermute | solution.py:594
  36.0 5.7 %collective-permute-done.9.more_b_ref = f32[136,128]{1,0:T(8,128)S(1)} collective-permute-done((f32[136,128]{1,0:T(8,128)S(1)}, f32[136,128]{1,0:T(8,128)S(1)}, u32[]{:S(2)}, u32[]{:S(2)}) %collective-permute-start.9) | collective-permute-done | bytes 69664 | tf_op jit(solution)/shard_map/ppermute | solution.py:594
  41.7 0.1 collective-permute-done.8.more_a_ref
  41.8 3.6 %second_sweeps.1 = (f32[6,5,6,40,128]{4,3,2,1,0:T(8,128)S(1)}, f32[5,5,40,128]{3,2,1,0:T(8,128)S(1)}, f32[5,4,32,128]{3,2,1,0:T(8,128)}) custom-call(f32[152,128]{1,0:T(8,128)S(1)} %get-tuple-element.46.jac_ref, f32[11,4,40,128]{3,2,1,0:T(8,128)S(1)} %get-tuple-element.57.coef_ref, ...), custom_call_target="tpu_custom_call", output_to_operand_aliasing={{0}: (4, {}), {1}: (5, {})} | custom-call | tf_op jit(solution)/shard_map/second_sweeps/pallas_call | solution.py:624
  (4 shorter events, 0.0 us)
Async XLA Ops:
  2.7 3.4 %collective-permute-start = (f32[56,128]{1,0:T(8,128)S(1)}, f32[56,128]{1,0:T(8,128)S(1)}, u32[]{:S(2)}, u32[]{:S(2)}) collective-permute-start(f32[56,128]{1,0:T(8,128)S(1)} %get-tuple-element.52), channel_id=1, source_target_pairs={{0,4},{1,5},{2,6},{3,7},{4,0},{5,1},{6,2},{7,3},{8,12},{9,13},{10,... | collective-permute-start | bytes 86024 | tf_op jit(solution)/shard_map/ppermute | solution.py:594
  6.1 7.5 %collective-permute-start.2 = (f32[120,128]{1,0:T(8,128)S(1)}, f32[120,128]{1,0:T(8,128)S(1)}, u32[]{:S(2)}, u32[]{:S(2)}) collective-permute-start(f32[120,128]{1,0:T(8,128)S(1)} %get-tuple-element.75), channel_id=1, source_target_pairs={{0,3},{1,2},{2,1},{3,0},{4,7},{5,6},{6,5},{7,4},{8,11},{9,10},{10,... | collective-permute-start | bytes 184328 | tf_op jit(solution)/shard_map/ppermute | solution.py:594
  9.6 4.0 %collective-permute-start.1 = (f32[120,128]{1,0:T(8,128)S(1)}, f32[120,128]{1,0:T(8,128)S(1)}, u32[]{:S(2)}, u32[]{:S(2)}) collective-permute-start(f32[120,128]{1,0:T(8,128)S(1)} %get-tuple-element.76), channel_id=1, source_target_pairs={{0,1},{1,0},{2,3},{3,2},{4,5},{5,4},{6,7},{7,6},{8,9},{9,8},{10,11... | collective-permute-start | bytes 184328 | tf_op jit(solution)/shard_map/ppermute | solution.py:594
  9.6 4.0 %collective-permute-start.3 = (f32[36,8,128]{2,1,0:T(8,128)S(1)}, f32[36,8,128]{2,1,0:T(8,128)S(1)}, u32[]{:S(2)}, u32[]{:S(2)}) collective-permute-start(f32[36,8,128]{2,1,0:T(8,128)S(1)} %get-tuple-element.56), channel_id=1, source_target_pairs={{0,4},{1,5},{2,6},{3,7},{4,0},{5,1},{6,2},{7,3},{8,12},{9,13},{10,... | collective-permute-start | bytes 442376 | tf_op jit(solution)/shard_map/ppermute | solution.py:594
  10.9 2.7 %collective-permute-start.4 = (f32[40,128]{1,0:T(8,128)S(1)}, f32[40,128]{1,0:T(8,128)S(1)}, u32[]{:S(2)}, u32[]{:S(2)}) collective-permute-start(f32[40,128]{1,0:T(8,128)S(1)} %slice_dynamic-update-slice_fusion.2), channel_id=1, source_target_pairs={{0,1},{1,0},{2,3},{3,2},{4,5},{5,4},{6,7},{7,6},{8,9},{9,8},{10,11... | collective-permute-start | bytes 61448 | tf_op jit(solution)/shard_map/ppermute | solution.py:594
  15.5 10.8 %collective-permute-start.6 = (f32[40,128]{1,0:T(8,128)S(1)}, f32[40,128]{1,0:T(8,128)S(1)}, u32[]{:S(2)}, u32[]{:S(2)}) collective-permute-start(f32[40,128]{1,0:T(8,128)S(1)} %add.6), channel_id=1, source_target_pairs={{8,2},{9,3},{10,0},{11,1},{12,6},{13,7},{14,4},{15,5},{16,10},{17,... | collective-permute-start | bytes 61448 | tf_op jit(solution)/shard_map/ppermute | solution.py:594
  21.3 5.1 %collective-permute-start.5 = (f32[40,128]{1,0:T(8,128)S(1)}, f32[40,128]{1,0:T(8,128)S(1)}, u32[]{:S(2)}, u32[]{:S(2)}) collective-permute-start(f32[40,128]{1,0:T(8,128)S(1)} %add.6), channel_id=1, source_target_pairs={{8,0},{9,1},{10,2},{11,3},{12,4},{13,5},{14,6},{15,7},{16,8},{17,9... | collective-permute-start | bytes 61448 | tf_op jit(solution)/shard_map/ppermute | solution.py:594
  27.7 3.5 %collective-permute-start.7 = (f32[136,128]{1,0:T(8,128)S(1)}, f32[136,128]{1,0:T(8,128)S(1)}, u32[]{:S(2)}, u32[]{:S(2)}) collective-permute-start(f32[136,128]{1,0:T(8,128)S(1)} %late_modes.1.more_ref), channel_id=1, source_target_pairs={{0,1},{1,0},{2,3},{3,2},{4,5},{5,4},{6,7},{7,6},{8,9},{9,8},{10,11... | collective-permute-start | bytes 208904 | tf_op jit(solution)/shard_map/ppermute | solution.py:594
  31.2 10.5 %collective-permute-start.9 = (f32[136,128]{1,0:T(8,128)S(1)}, f32[136,128]{1,0:T(8,128)S(1)}, u32[]{:S(2)}, u32[]{:S(2)}) collective-permute-start(f32[136,128]{1,0:T(8,128)S(1)} %add.7), channel_id=1, source_target_pairs={{8,2},{9,3},{10,0},{11,1},{12,6},{13,7},{14,4},{15,5},{16,10},{17,... | collective-permute-start | bytes 208904 | tf_op jit(solution)/shard_map/ppermute | solution.py:594
  34.1 7.7 %collective-permute-start.8 = (f32[136,128]{1,0:T(8,128)S(1)}, f32[136,128]{1,0:T(8,128)S(1)}, u32[]{:S(2)}, u32[]{:S(2)}) collective-permute-start(f32[136,128]{1,0:T(8,128)S(1)} %add.7), channel_id=1, source_target_pairs={{8,0},{9,1},{10,2},{11,3},{12,4},{13,5},{14,6},{15,7},{16,8},{17,9... | collective-permute-start | bytes 208904 | tf_op jit(solution)/shard_map/ppermute | solution.py:594

commit v8 on v6

--- a/solution.py
+++ b/solution.py
@@ -465,11 +465,11 @@
 
 
 def late_kernel(
-    jac_ref, coef_ref, inv_ref, part_ref, more_ref, modes_a_ref, modes_b_ref, synth_ref, table_ref, modes_ref,
+    jac_ref, coef_ref, inv_ref, part_ref, more_ref, first_ref, synth_ref, table_ref, modes_ref,
 ):
     span, pitch = part_ref.shape
     components, axial = coef_ref.shape[0] - 6, coef_ref.shape[1]
-    field = synthesised(modes_a_ref[EDGE:] + modes_b_ref[EDGE:], synth_ref[:components * pitch])
+    field = synthesised(first_ref[EDGE:], synth_ref[:components * pitch])
     delta = [inv_ref[:span] * field[:, c * pitch:(c + 1) * pitch] for c in range(components)]
     for a in range(axial - 2, -1, -1):
         delta = along_axis(jac_ref, coef_ref, delta, a, span)
@@ -479,13 +479,13 @@
 
 
 def between_kernel(
-    jac_ref, coef_ref, inv_ref, edge_coef_ref, state_in_ref, edge_in_ref, modes_a_ref, modes_b_ref, synth_ref, more_ref,
+    jac_ref, coef_ref, inv_ref, edge_coef_ref, state_in_ref, edge_in_ref, modes_ref, synth_ref, more_ref,
     state_ref, edge_ref, sent_ref,
 ):
     sent_ref[...] = more_ref[...]
     components, axial = state_ref.shape[1], state_ref.shape[2] - 2
     wide, pitch = state_ref.shape[3:]
-    modes = modes_a_ref[...] + modes_b_ref[...]
+    modes = modes_ref[...]
     field = synthesised(jnp.concatenate([modes[EDGE:], modes[:EDGE]], 0), synth_ref[...])
     delta = [inv_ref[...] * field[:, c * pitch:(c + 1) * pitch] for c in range(components)]
     for t in range(1, axial + 1):
@@ -657,11 +657,10 @@
     outer = moved(outer, lambda r, s, p: (r, s, (p - 1 + 2 * (p % 2)) % place_count))
     inner = moved(inner, lambda r, s, p: (r, s, p ^ 1))
 
-    modes = modes + inner[groups * span + corner_rows:] if steps else modes
-    for step in steps[1:]:
+    modes = modes + inner[groups * span + corner_rows:]
+    for step in [1 << n for n in range(1, place_count.bit_length() - 1)]:
         modes = modes + moved(modes, lambda r, s, p: (r, s, p ^ step))
-    modes_b = far(modes)
-    modes_a = near(modes)
+    modes = near(modes)
 
     synth, jac = call(
         synth_kernel, "synth",
@@ -689,11 +688,11 @@
     more_shape = struct(axial * span + EDGE, pitch)
     more = call(
         late_kernel, "late_modes", more_shape,
-        [(vmem, x) for x in (jac, coef, inv, part, more, modes_a, modes_b, synth, table)],
+        [(vmem, x) for x in (jac, coef, inv, part, more, modes, synth, table)],
     )
     state, edge, sent = call(
         between_kernel, "between_sweeps", (state_shape, edge_shape, more_shape),
-        [(vmem, x) for x in (jac, coef, inv, edge_coef, state, edge, modes_a, modes_b, synth, more)],
+        [(vmem, x) for x in (jac, coef, inv, edge_coef, state, edge, modes, synth, more)],
         aliases={4: 0, 5: 1},
     )
     for step in steps:

time: 43.6 us -> 44.4 us (1.018)
  starting transfers between devices: 20.3 us -> 21.7 us
  waiting for transfers between devices: 6.84 us -> 6.35 us
    ppermute x9, starting transfers between devices: 20.3 us -> 21.7 us  [moved(): return lax.ppermute(x, AXES, pairs)]
    ppermute x9, waiting for transfers between devices: 6.84 us -> 6.35 us  [moved(): return lax.ppermute(x, AXES, pairs)]
  transfers between devices with their start and end apart: 9 -> 9, of which waited for: 2 -> 4; matrix products, arithmetic and copies ran while one was open for 0% -> 0% of each run, Pallas kernels for 19% -> 19%
where the time goes in v8:
time: 44.4 us; the launch traced here: 44.3 us
  starting transfers between devices  21.7 us (49%)
  Pallas kernels  16.1 us (36%)
  waiting for transfers between devices  6.35 us (14%)
    ppermute x9, starting transfers between devices, moved(): return lax.ppermute(x, AXES, pairs)  21.7 us
    pallas_call x6, Pallas kernels, call(): pl.pallas_call(functools.partial(kernel, **fixed), out_shape=outs, in_spe...  16.1 us
    ppermute x9, waiting for transfers between devices, moved(): return lax.ppermute(x, AXES, pairs)  6.35 us
  transfers between devices with their start and end apart: 9, of which 4 were waited for; matrix products, arithmetic and copies ran while one was open for 0% of the time, Pallas kernels for 19%

profile of v8, /device:TPU:1, one launch (start us, length us, event | category | flops | bytes accessed | tf_op | source)
XLA Modules:
  0.0 44.3 jit_solution(9820014282057234548)
XLA Ops:
  0.0 2.7 %pack.1 = (f32[5,4,32,128]{3,2,1,0:T(8,128)S(1)}, f32[11,4,32,128]{3,2,1,0:T(8,128)S(1)}, f32[32,128]{1,0:T(8,128)S(1)}, f32[17,32,128]{2,1,0:T(8,128)S(1)}, f32...) custom-call(f32[5,4,32,128]{3,2,1,0:T(8,128)} %adjoint_hbm.1, ...), custom_call_target="tpu_custom_call" | custom-call | tf_op jit(solution)/shard_map/pack/pallas_call | solution.py:611
  2.7 2.1 %collective-permute-start.1 = (f32[56,128]{1,0:T(8,128)S(1)}, f32[56,128]{1,0:T(8,128)S(1)}, u32[]{:S(2)}, u32[]{:S(2)}) collective-permute-start(f32[56,128]{1,0:T(8,128)S(1)} %get-tuple-element.46), channel_id=1, source_target_pairs={{0,4},{1,5},{2,6},{3,7},{4,0},{5,1},{6,2},{7,3},{8,12},{9,13},{10,... | collective-permute-start | bytes 86024 | tf_op jit(solution)/shard_map/ppermute | solution.py:581
  4.8 0.1 collective-permute-start
  4.9 1.2 %collective-permute-done.1 = f32[56,128]{1,0:T(8,128)S(1)} collective-permute-done((f32[56,128]{1,0:T(8,128)S(1)}, f32[56,128]{1,0:T(8,128)S(1)}, u32[]{:S(2)}, u32[]{:S(2)}) %collective-permute-start.1) | collective-permute-done | bytes 28704 | tf_op jit(solution)/shard_map/ppermute | solution.py:581
  6.1 1.5 %collective-permute-start.2 = (f32[160,128]{1,0:T(8,128)S(1)}, f32[160,128]{1,0:T(8,128)S(1)}, u32[]{:S(2)}, u32[]{:S(2)}) collective-permute-start(f32[160,128]{1,0:T(8,128)S(1)} %slice_dynamic-update-slice_fusion), channel_id=1, source_target_pairs={{0,1},{1,0},{2,3},{3,2},{4,5},{5,4},{6,7},{7,6},{8,9},{9,8},{10,11... | collective-permute-start | bytes 245768 | tf_op jit(solution)/shard_map/ppermute | solution.py:581
  7.6 2.2 %collective-permute-start.3 = (f32[120,128]{1,0:T(8,128)S(1)}, f32[120,128]{1,0:T(8,128)S(1)}, u32[]{:S(2)}, u32[]{:S(2)}) collective-permute-start(f32[120,128]{1,0:T(8,128)S(1)} %slice_dynamic-update-slice_fusion.1), channel_id=1, source_target_pairs={{0,3},{1,2},{2,1},{3,0},{4,7},{5,6},{6,5},{7,4},{8,11},{9,10},{10,... | collective-permute-start | bytes 184328 | tf_op jit(solution)/shard_map/ppermute | solution.py:581
  9.8 0.0 collective-permute-done.2.inner_ref
  9.8 2.4 %collective-permute-start.4 = (f32[40,128]{1,0:T(8,128)S(1)}, f32[40,128]{1,0:T(8,128)S(1)}, u32[]{:S(2)}, u32[]{:S(2)}) collective-permute-start(f32[40,128]{1,0:T(8,128)S(1)} %slice_add_fusion), channel_id=1, source_target_pairs={{0,2},{1,3},{2,0},{3,1},{4,6},{5,7},{6,4},{7,5},{8,10},{9,11},{10,... | collective-permute-start | bytes 61448 | tf_op jit(solution)/shard_map/ppermute | solution.py:581
  12.2 1.2 %collective-permute-done.4 = f32[40,128]{1,0:T(8,128)S(1)} collective-permute-done((f32[40,128]{1,0:T(8,128)S(1)}, f32[40,128]{1,0:T(8,128)S(1)}, u32[]{:S(2)}, u32[]{:S(2)}) %collective-permute-start.4) | collective-permute-done | bytes 20512 | tf_op jit(solution)/shard_map/ppermute | solution.py:581
  13.5 5.6 %collective-permute-start.5 = (f32[40,128]{1,0:T(8,128)S(1)}, f32[40,128]{1,0:T(8,128)S(1)}, u32[]{:S(2)}, u32[]{:S(2)}) collective-permute-start(f32[40,128]{1,0:T(8,128)S(1)} %add.10), channel_id=1, source_target_pairs={{8,0},{9,1},{10,2},{11,3},{12,4},{13,5},{14,6},{15,7},{16,8},{17,9... | collective-permute-start | bytes 61448 | tf_op jit(solution)/shard_map/ppermute | solution.py:581
  19.0 0.6 %synth.1 = (f32[896,128]{1,0:T(8,128)S(1)}, f32[152,128]{1,0:T(8,128)S(1)}) custom-call(s32[1,4]{1,0:T(1,128)S(1)} %get-tuple-element.33.blades_ref, f32[5,5,1,6]{3,2,1,0:T(1,128)S(1)} %get-tuple-element.34.jacobians_ref, f32[5,5,3,64]{3,2,1,0:T(4,128)S(1)} %get-tuple-element.35.giles_re_ref, f32[5,5,3,64]{3,2,1,0:T(4,128)S(1)} %get-tuple-element.36.giles_im_ref, ...), custom_call_target="tpu_custom_call" | custom-call | tf_op jit(solution)/shard_map/synth/pallas_call | solution.py:611
  19.6 0.0 collective-permute-done.3.outer_ref
  19.6 0.0 collective-permute-done.span_ref
  19.6 5.1 %first_sweeps.1 = (f32[11,4,40,128]{3,2,1,0:T(8,128)S(1)}, f32[40,128]{1,0:T(8,128)S(1)}, f32[12,40,128]{2,1,0:T(8,128)S(1)}, f32[6,5,6,40,128]{4,3,2,1,0:T(8,12...) custom-call(f32[152,128]{1,0:T(8,128)S(1)} %get-tuple-element.39.jac_ref, ...), custom_call_target="tpu_custom_call" | custom-call | tf_op jit(solution)/shard_map/first_sweeps/pallas_call | solution.py:611
  24.7 0.0 collective-permute-done.5.first_ref.modes_ref
  24.8 1.3 %late_modes.1.more_ref = f32[136,128]{1,0:T(8,128)S(1)} custom-call(f32[152,128]{1,0:T(8,128)S(1)} %get-tuple-element.39.jac_ref, f32[11,4,40,128]{3,2,1,0:T(8,128)S(1)} %get-tuple-element.49.coef_ref, f32[40,128]{1,0:T(8,128)S(1)} %get-tuple-element.50.inv_ref, f32[32,128]{1,0:T(8,128)S(1)} %get-tuple-element.55.part_ref, ...), custom_call_target="tpu_custom_call" | custom-call | tf_op jit(solution)/shard_map/late_modes/pallas_call | solution.py:611
  26.1 2.0 %collective-permute-start.6 = (f32[136,128]{1,0:T(8,128)S(1)}, f32[136,128]{1,0:T(8,128)S(1)}, u32[]{:S(2)}, u32[]{:S(2)}) collective-permute-start(f32[136,128]{1,0:T(8,128)S(1)} %late_modes.1.more_ref), channel_id=1, source_target_pairs={{0,1},{1,0},{2,3},{3,2},{4,5},{5,4},{6,7},{7,6},{8,9},{9,8},{10,11... | collective-permute-start | bytes 208904 | tf_op jit(solution)/shard_map/ppermute | solution.py:581
  28.1 2.8 %between_sweeps.1 = (f32[6,5,6,40,128]{4,3,2,1,0:T(8,128)S(1)}, f32[5,5,40,128]{3,2,1,0:T(8,128)S(1)}, f32[136,128]{1,0:T(8,128)S(1)}) custom-call(f32[152,128]{1,0:T(8,128)S(1)} %get-tuple-element.39.jac_ref, f32[11,4,40,128]{3,2,1,0:T(8,128)S(1)} %get-tuple-element.49.coef_ref, ...), custom_call_target="tpu_custom_call", output_to_operand_aliasing={{0}: (4, {}), {1}: (5, {})} | custom-call | tf_op jit(solution)/shard_map/between_sweeps/pallas_call | solution.py:611
  30.8 0.0 collective-permute-done.6
  30.9 3.8 %collective-permute-start.8 = (f32[136,128]{1,0:T(8,128)S(1)}, f32[136,128]{1,0:T(8,128)S(1)}, u32[]{:S(2)}, u32[]{:S(2)}) collective-permute-start(f32[136,128]{1,0:T(8,128)S(1)} %add.11), channel_id=1, source_target_pairs={{8,2},{9,3},{10,0},{11,1},{12,6},{13,7},{14,4},{15,5},{16,10},{17,... | collective-permute-start | bytes 208904 | tf_op jit(solution)/shard_map/ppermute | solution.py:581
  34.7 1.9 %collective-permute-start.7 = (f32[136,128]{1,0:T(8,128)S(1)}, f32[136,128]{1,0:T(8,128)S(1)}, u32[]{:S(2)}, u32[]{:S(2)}) collective-permute-start(f32[136,128]{1,0:T(8,128)S(1)} %add.11), channel_id=1, source_target_pairs={{8,0},{9,1},{10,2},{11,3},{12,4},{13,5},{14,6},{15,7},{16,8},{17,9... | collective-permute-start | bytes 208904 | tf_op jit(solution)/shard_map/ppermute | solution.py:581
  36.6 3.8 %collective-permute-done.8.more_b_ref = f32[136,128]{1,0:T(8,128)S(1)} collective-permute-done((f32[136,128]{1,0:T(8,128)S(1)}, f32[136,128]{1,0:T(8,128)S(1)}, u32[]{:S(2)}, u32[]{:S(2)}) %collective-permute-start.8) | collective-permute-done | bytes 69664 | tf_op jit(solution)/shard_map/ppermute | solution.py:581
  40.4 0.1 collective-permute-done.7.more_a_ref
  40.6 3.7 %second_sweeps.1 = (f32[6,5,6,40,128]{4,3,2,1,0:T(8,128)S(1)}, f32[5,5,40,128]{3,2,1,0:T(8,128)S(1)}, f32[5,4,32,128]{3,2,1,0:T(8,128)}) custom-call(f32[152,128]{1,0:T(8,128)S(1)} %get-tuple-element.39.jac_ref, f32[11,4,40,128]{3,2,1,0:T(8,128)S(1)} %get-tuple-element.49.coef_ref, ...), custom_call_target="tpu_custom_call", output_to_operand_aliasing={{0}: (4, {}), {1}: (5, {})} | custom-call | tf_op jit(solution)/shard_map/second_sweeps/pallas_call | solution.py:611
  (5 shorter events, 0.0 us)
Async XLA Ops:
  2.7 3.4 %collective-permute-start.1 = (f32[56,128]{1,0:T(8,128)S(1)}, f32[56,128]{1,0:T(8,128)S(1)}, u32[]{:S(2)}, u32[]{:S(2)}) collective-permute-start(f32[56,128]{1,0:T(8,128)S(1)} %get-tuple-element.46), channel_id=1, source_target_pairs={{0,4},{1,5},{2,6},{3,7},{4,0},{5,1},{6,2},{7,3},{8,12},{9,13},{10,... | collective-permute-start | bytes 86024 | tf_op jit(solution)/shard_map/ppermute | solution.py:581
  4.8 14.8 %collective-permute-start = (f32[36,8,128]{2,1,0:T(8,128)S(1)}, f32[36,8,128]{2,1,0:T(8,128)S(1)}, u32[]{:S(2)}, u32[]{:S(2)}) collective-permute-start(f32[36,8,128]{2,1,0:T(8,128)S(1)} %get-tuple-element.44), channel_id=1, source_target_pairs={{0,4},{1,5},{2,6},{3,7},{4,0},{5,1},{6,2},{7,3},{8,12},{9,13},{10,... | collective-permute-start | bytes 442376 | tf_op jit(solution)/shard_map/ppermute | solution.py:581
  6.1 3.7 %collective-permute-start.2 = (f32[160,128]{1,0:T(8,128)S(1)}, f32[160,128]{1,0:T(8,128)S(1)}, u32[]{:S(2)}, u32[]{:S(2)}) collective-permute-start(f32[160,128]{1,0:T(8,128)S(1)} %slice_dynamic-update-slice_fusion), channel_id=1, source_target_pairs={{0,1},{1,0},{2,3},{3,2},{4,5},{5,4},{6,7},{7,6},{8,9},{9,8},{10,11... | collective-permute-start | bytes 245768 | tf_op jit(solution)/shard_map/ppermute | solution.py:581
  7.6 12.0 %collective-permute-start.3 = (f32[120,128]{1,0:T(8,128)S(1)}, f32[120,128]{1,0:T(8,128)S(1)}, u32[]{:S(2)}, u32[]{:S(2)}) collective-permute-start(f32[120,128]{1,0:T(8,128)S(1)} %slice_dynamic-update-slice_fusion.1), channel_id=1, source_target_pairs={{0,3},{1,2},{2,1},{3,0},{4,7},{5,6},{6,5},{7,4},{8,11},{9,10},{10,... | collective-permute-start | bytes 184328 | tf_op jit(solution)/shard_map/ppermute | solution.py:581
  9.8 3.6 %collective-permute-start.4 = (f32[40,128]{1,0:T(8,128)S(1)}, f32[40,128]{1,0:T(8,128)S(1)}, u32[]{:S(2)}, u32[]{:S(2)}) collective-permute-start(f32[40,128]{1,0:T(8,128)S(1)} %slice_add_fusion), channel_id=1, source_target_pairs={{0,2},{1,3},{2,0},{3,1},{4,6},{5,7},{6,4},{7,5},{8,10},{9,11},{10,... | collective-permute-start | bytes 61448 | tf_op jit(solution)/shard_map/ppermute | solution.py:581
  13.5 11.3 %collective-permute-start.5 = (f32[40,128]{1,0:T(8,128)S(1)}, f32[40,128]{1,0:T(8,128)S(1)}, u32[]{:S(2)}, u32[]{:S(2)}) collective-permute-start(f32[40,128]{1,0:T(8,128)S(1)} %add.10), channel_id=1, source_target_pairs={{8,0},{9,1},{10,2},{11,3},{12,4},{13,5},{14,6},{15,7},{16,8},{17,9... | collective-permute-start | bytes 61448 | tf_op jit(solution)/shard_map/ppermute | solution.py:581
  26.1 4.8 %collective-permute-start.6 = (f32[136,128]{1,0:T(8,128)S(1)}, f32[136,128]{1,0:T(8,128)S(1)}, u32[]{:S(2)}, u32[]{:S(2)}) collective-permute-start(f32[136,128]{1,0:T(8,128)S(1)} %late_modes.1.more_ref), channel_id=1, source_target_pairs={{0,1},{1,0},{2,3},{3,2},{4,5},{5,4},{6,7},{7,6},{8,9},{9,8},{10,11... | collective-permute-start | bytes 208904 | tf_op jit(solution)/shard_map/ppermute | solution.py:581
  30.9 9.5 %collective-permute-start.8 = (f32[136,128]{1,0:T(8,128)S(1)}, f32[136,128]{1,0:T(8,128)S(1)}, u32[]{:S(2)}, u32[]{:S(2)}) collective-permute-start(f32[136,128]{1,0:T(8,128)S(1)} %add.11), channel_id=1, source_target_pairs={{8,2},{9,3},{10,0},{11,1},{12,6},{13,7},{14,4},{15,5},{16,10},{17,... | collective-permute-start | bytes 208904 | tf_op jit(solution)/shard_map/ppermute | solution.py:581
  34.7 5.8 %collective-permute-start.7 = (f32[136,128]{1,0:T(8,128)S(1)}, f32[136,128]{1,0:T(8,128)S(1)}, u32[]{:S(2)}, u32[]{:S(2)}) collective-permute-start(f32[136,128]{1,0:T(8,128)S(1)} %add.11), channel_id=1, source_target_pairs={{8,0},{9,1},{10,2},{11,3},{12,4},{13,5},{14,6},{15,7},{16,8},{17,9... | collective-permute-start | bytes 208904 | tf_op jit(solution)/shard_map/ppermute | solution.py:581

commit v9 on v6

--- a/solution.py
+++ b/solution.py
@@ -158,9 +158,11 @@
     number = mode_number(mode, [picked(blades_ref[...], face + n) for n in range(2)])
     cos_table, sin_table = waves(number * (place * pitch + rows((pitch, pitch))), length)
     table = jnp.where(component < components, jnp.where(sine, sin_table, cos_table), 0.0)
-    table_ref[...] = table
+    for c in range(components):
+        for n, value in enumerate(split(jnp.where(component == c, table, 0.0))):
+            table_ref[n, pl.ds(c * pitch, pitch), :] = value
     start = groups * span + (groups + 1) * EDGE
-    inner_ref[pl.ds(start, span), :] = projected([adjoint_ref[c, 0] for c in range(components)], table)
+    inner_ref[pl.ds(start, span), :] = projected([adjoint_ref[c, 0] for c in range(components)], table_ref)
     small_ref[pl.ds(groups * EDGE, EDGE), :] = inner_ref[pl.ds(start + edge_row, EDGE), :]
 
     to_low, to_high = half_rows(side)
@@ -189,20 +191,24 @@
     return jnp.sum(chosen, axis=1, keepdims=True).astype(jnp.int32)
 
 
-def projected(strips, table):
-    component, _, _ = column(lanes(table.shape))
-    total = jnp.zeros((strips[0].shape[0], table.shape[1]), jnp.float32)
-    for c, strip in enumerate(strips):
-        total += jnp.dot(
-            strip, jnp.where(component == c, table, 0.0), precision=EXACT, preferred_element_type=jnp.float32,
-        )
-    return total
-
-
-def synthesised(modes, synth):
-    return lax.dot_general(
-        modes, synth, (((1,), (1,)), ((), ())), precision=EXACT, preferred_element_type=jnp.float32,
-    )
+def split(x):
+    high = x.astype(jnp.bfloat16)
+    return high, (x - high.astype(jnp.float32)).astype(jnp.bfloat16)
+
+
+def product(x, table, dims):
+    x_high, x_low = split(x)
+    table_high, table_low = table
+    dot = functools.partial(lax.dot_general, dimension_numbers=(dims, ((), ())), preferred_element_type=jnp.float32)
+    return dot(x_high, table_high) + (dot(x_low, table_high) + dot(x_high, table_low))
+
+
+def projected(strips, table_ref):
+    return product(jnp.concatenate(strips, 1), (table_ref[0], table_ref[1]), ((1,), (0,)))
+
+
+def synthesised(modes, synth_ref, count):
+    return product(modes, (synth_ref[0, :count], synth_ref[1, :count]), ((1,), (1,)))
 
 
 def synth_kernel(
@@ -265,12 +271,13 @@
             row_cos = jnp.where(component == b, with_cos[at:at + 1], row_cos)
             row_sin = jnp.where(component == b, with_sin[at:at + 1], row_sin)
         part = row_cos * cos_table + row_sin * sin_table
-        synth_ref[pl.ds(c * pitch, pitch), :] = part[:pitch]
-        synth_ref[pl.ds(components * pitch + c * SEGMENT_LANES, SEGMENT_LANES), :] = part[pitch:]
+        for n, value in enumerate(split(part)):
+            synth_ref[n, pl.ds(c * pitch, pitch), :] = value[:pitch]
+            synth_ref[n, pl.ds(components * pitch + c * SEGMENT_LANES, SEGMENT_LANES), :] = value[pitch:]
     used = components * (pitch + SEGMENT_LANES)
-    rest = synth_ref.shape[0] - used
+    rest = synth_ref.shape[1] - used
     if rest:
-        synth_ref[pl.ds(used, rest), :] = jnp.zeros((rest, pitch), jnp.float32)
+        synth_ref[:, pl.ds(used, rest), :] = jnp.zeros((2, rest, pitch), jnp.bfloat16)
 
 
 def jacobian(jac_ref, components, b, c, d):
@@ -289,16 +296,17 @@
     return total
 
 
-def layer_update(jac_ref, state_ref, edge_ref, coef_ref, t, a):
+def layer_update(jac_ref, state_ref, edge_ref, coef_ref, t, a, height):
     components, wide, pitch = state_ref.shape[1], state_ref.shape[3], state_ref.shape[4]
-    lane = lanes((wide, pitch))
+    lane = lanes((height, pitch))
     start = a * SEGMENT_LANES
     own = [state_ref[t, c, a + 1] for c in range(components)]
-    above = [state_ref[t, c, a + 2] for c in range(components)]
-    below = [state_ref[t, c, a] for c in range(components)]
-    edge = [edge_ref[t, c] for c in range(components)]
-    span_next = [pltpu.roll(x, wide - 1, 0) for x in own]
-    span_prev = [pltpu.roll(x, 1, 0) for x in own]
+    above = [state_ref[t, c, a + 2, :height] for c in range(components)]
+    below = [state_ref[t, c, a, :height] for c in range(components)]
+    edge = [edge_ref[t, c, :height] for c in range(components)]
+    span_next = [pltpu.roll(x, wide - 1, 0)[:height] for x in own]
+    span_prev = [pltpu.roll(x, 1, 0)[:height] for x in own]
+    own = [x[:height] for x in own]
     to_end = 2 * pitch - 1 - (start + 3 * EDGE)
     to_begin = 2 * pitch - (start + EDGE - 1)
     pitch_next = [
@@ -309,8 +317,8 @@
         jnp.where(lane == 0, pltpu.roll(e, lax.rem(to_begin, pitch), 1), pltpu.roll(x, 1, 1))
         for e, x in zip(edge, own)
     ]
-    source = [coef_ref[c, a] for c in range(components)]
-    couplings = [coef_ref[components + d, a] for d in range(6)]
+    source = [coef_ref[c, a, :height] for c in range(components)]
+    couplings = [coef_ref[components + d, a, :height] for d in range(6)]
     return mixed(jac_ref, source, couplings, (above, below, span_next, span_prev, pitch_next, pitch_prev))
 
 
@@ -335,10 +343,11 @@
     return pltpu.roll(tile, ((axial - 1) * SEGMENT_LANES - at % pitch) % pitch, 1)
 
 
-def advance(refs, t, a):
+def advance(refs, t, a, height=None):
     state_ref = refs[1]
-    for c, value in enumerate(layer_update(*refs, t, a)):
-        state_ref[t + 1, c, a + 1] = value
+    height = height or state_ref.shape[3]
+    for c, value in enumerate(layer_update(*refs, t, a, height)):
+        state_ref[t + 1, c, a + 1, :height] = value
 
 
 def first_kernel(
@@ -421,19 +430,17 @@
 
         lax.fori_loop(0, axial - t, body, 0)
 
-        @pl.when(t < axial - 1)
-        def _():
-            for c, value in enumerate(edge_update(jac_ref, edge_ref, edge_coef_ref, t, axial)):
-                edge_ref[t + 1, c] = value
-
+        for c, value in enumerate(edge_update(jac_ref, edge_ref, edge_coef_ref, t, axial)):
+            edge_ref[t + 1, c] = value
         return carry
 
-    lax.fori_loop(0, axial, sweep, 0)
+    lax.fori_loop(0, axial - 1, sweep, 0)
+    advance(refs, axial - 1, 0)
     strips = [
         jnp.concatenate([state_ref[t, c, 1] for t in range(1, axial)] + [state_ref[axial, c, 1, :span]], 0)
         for c in range(components)
     ]
-    total = projected(strips, table_ref[...])
+    total = projected(strips, table_ref)
     ghosts = jnp.zeros((EDGE, pitch), jnp.float32)
     for t in range(1, axial):
         part = total[(t - 1) * wide:t * wide]
@@ -469,13 +476,13 @@
 ):
     span, pitch = part_ref.shape
     components, axial = coef_ref.shape[0] - 6, coef_ref.shape[1]
-    field = synthesised(modes_a_ref[EDGE:] + modes_b_ref[EDGE:], synth_ref[:components * pitch])
+    field = synthesised(modes_a_ref[EDGE:] + modes_b_ref[EDGE:], synth_ref, components * pitch)
     delta = [inv_ref[:span] * field[:, c * pitch:(c + 1) * pitch] for c in range(components)]
     for a in range(axial - 2, -1, -1):
         delta = along_axis(jac_ref, coef_ref, delta, a, span)
     before = more_ref.shape[0]
     modes_ref[:before] = more_ref[...]
-    modes_ref[before:] = part_ref[...] + projected(delta, table_ref[...])
+    modes_ref[before:] = part_ref[...] + projected(delta, table_ref)
 
 
 def between_kernel(
@@ -486,7 +493,7 @@
     components, axial = state_ref.shape[1], state_ref.shape[2] - 2
     wide, pitch = state_ref.shape[3:]
     modes = modes_a_ref[...] + modes_b_ref[...]
-    field = synthesised(jnp.concatenate([modes[EDGE:], modes[:EDGE]], 0), synth_ref[...])
+    field = synthesised(jnp.concatenate([modes[EDGE:], modes[:EDGE]], 0), synth_ref, synth_ref.shape[1])
     delta = [inv_ref[...] * field[:, c * pitch:(c + 1) * pitch] for c in range(components)]
     for t in range(1, axial + 1):
         for c in range(components):
@@ -495,19 +502,25 @@
             delta = along_axis(jac_ref, coef_ref, delta, axial - 1 - t, wide)
     for c in range(components):
         edge_ref[1, c] += edge_coef_ref[components + 6] * edge_boundary(field, c, components, pitch, axial)
-    refs = (jac_ref, state_ref, edge_ref, coef_ref)
+    diagonal_sweeps(jac_ref, state_ref, edge_ref, coef_ref, edge_coef_ref, 1, axial // 2 + 1)
+
+
+def beside_kernel(jac_ref, coef_ref, edge_coef_ref, state_in_ref, edge_in_ref, state_ref, edge_ref):
+    axial, span = state_ref.shape[2] - 2, state_ref.shape[3] - EDGE
+    diagonal_sweeps(jac_ref, state_ref, edge_ref, coef_ref, edge_coef_ref, axial // 2 + 1, axial)
+    advance((jac_ref, state_ref, edge_ref, coef_ref), axial, 0, span)
+
+
+def diagonal_sweeps(jac_ref, state_ref, edge_ref, coef_ref, edge_coef_ref, first, last):
+    axial = state_ref.shape[2] - 2
 
     def sweep(t, carry):
-        advance(refs, t, axial - t)
-
-        @pl.when(t < axial)
-        def _():
-            for c, value in enumerate(edge_update(jac_ref, edge_ref, edge_coef_ref, t, axial)):
-                edge_ref[t + 1, c] = value
-
+        advance((jac_ref, state_ref, edge_ref, coef_ref), t, axial - t)
+        for c, value in enumerate(edge_update(jac_ref, edge_ref, edge_coef_ref, t, axial)):
+            edge_ref[t + 1, c] = value
         return carry
 
-    lax.fori_loop(1, axial + 1, sweep, 0)
+    lax.fori_loop(first, last, sweep, 0)
 
 
 def second_kernel(
@@ -523,7 +536,7 @@
     for t in range(1, axial):
         _, _, from_packed = ghost_rows(side, t, axial)
         parts += [more[(t - 1) * span:t * span], pltpu.roll(more[start:start + EDGE], from_packed, 0)]
-    field = synthesised(jnp.concatenate(parts + [more[start + EDGE:]], 0), synth_ref[...])
+    field = synthesised(jnp.concatenate(parts + [more[start + EDGE:]], 0), synth_ref, synth_ref.shape[1])
     for t in range(1, axial):
         part = field[(t - 1) * wide:t * wide]
         for c in range(components):
@@ -532,8 +545,9 @@
         bound_ref[axial, c, :span] = inv_ref[:span] * field[(axial - 1) * wide:, c * pitch:(c + 1) * pitch]
     delta = [bound_ref[1, c] for c in range(components)]
     for t in range(2, axial + 2):
+        height = wide if t <= axial else span
         for c in range(components):
-            state_ref[t, c, axial + 2 - t] += delta[c]
+            state_ref[t, c, axial + 2 - t, :height] += delta[c][:height]
         if t < axial + 1:
             delta = along_axis(jac_ref, coef_ref, delta, axial - t, wide)
     for t in range(1, axial):
@@ -558,8 +572,8 @@
     lax.fori_loop(2, axial, sweep, 0)
 
     def final(a, carry):
-        for c, value in enumerate(layer_update(*refs, axial, a)):
-            out_ref[c, a] = value[:span]
+        for c, value in enumerate(layer_update(*refs, axial, a, span)):
+            out_ref[c, a] = value
         return carry
 
     lax.fori_loop(1, axial, final, 0)
@@ -631,7 +645,7 @@
             struct(components, axial, span, pitch), struct(components + 6, axial, span, pitch), struct(span, pitch),
             struct(fields + 1, span, pitch), struct(span_tiles, EDGE, pitch), struct(2 * corner_rows + EDGE, pitch),
             struct(groups * span + corner_rows + EDGE + span, pitch), struct(groups * span + corner_rows, pitch),
-            struct(pitch, pitch), *(jax.ShapeDtypeStruct(x.shape, x.dtype) for x in (blades, *tables)),
+            jax.ShapeDtypeStruct((2, components * pitch, pitch), jnp.bfloat16), *(jax.ShapeDtypeStruct(x.shape, x.dtype) for x in (blades, *tables)),
         ),
         [(hbm, in_hbm(x)) for x in (adjoint_start, source, couplings, damping, blades, *tables)],
         scratch=[
@@ -666,7 +680,9 @@
     synth, jac = call(
         synth_kernel, "synth",
         (
-            struct(-(-components * (pitch + SEGMENT_LANES) // pitch) * pitch, pitch),
+            jax.ShapeDtypeStruct(
+                (2, -(-components * (pitch + SEGMENT_LANES) // pitch) * pitch, pitch), jnp.bfloat16
+            ),
             struct(-(-6 * components * components // EDGE) * EDGE, pitch),
         ),
         [(vmem, x) for x in (blades, *tables)],
@@ -695,6 +711,11 @@
         between_kernel, "between_sweeps", (state_shape, edge_shape, more_shape),
         [(vmem, x) for x in (jac, coef, inv, edge_coef, state, edge, modes_a, modes_b, synth, more)],
         aliases={4: 0, 5: 1},
+    )
+    state, edge = call(
+        beside_kernel, "beside_sweeps", (state_shape, edge_shape),
+        [(vmem, x) for x in (jac, coef, edge_coef, state, edge)],
+        aliases={3: 0, 4: 1},
     )
     for step in steps:
         got = moved(more, lambda r, s, p: (r, s, p ^ step))

time: 43.6 us -> 40.1 us (0.920)
  Pallas kernels: 16.1 us -> 14.1 us
  waiting for transfers between devices: 6.84 us -> 5.29 us
    pallas_call x6 -> x7, Pallas kernels: 16.1 us -> 14.1 us  [call(): pl.pallas_call(functools.partial(kernel, **fixed), out_shape=outs, in_spe...]
    ppermute x9, waiting for transfers between devices: 6.84 us -> 5.29 us  [moved(): return lax.ppermute(x, AXES, pairs)]
  transfers between devices with their start and end apart: 9 -> 9, of which waited for: 2 -> 4; matrix products, arithmetic and copies ran while one was open for 0% -> 0% of each run, Pallas kernels for 19% -> 19%
where the time goes in v9:
time: 40.1 us; the launch traced here: 39.9 us
  starting transfers between devices  20.4 us (51%)
  Pallas kernels  14.1 us (35%)
  waiting for transfers between devices  5.29 us (13%)
    ppermute x9, starting transfers between devices, moved(): return lax.ppermute(x, AXES, pairs)  20.4 us
    pallas_call x7, Pallas kernels, call(): pl.pallas_call(functools.partial(kernel, **fixed), out_shape=outs, in_spe...  14.1 us
    ppermute x9, waiting for transfers between devices, moved(): return lax.ppermute(x, AXES, pairs)  5.29 us
  transfers between devices with their start and end apart: 9, of which 4 were waited for; matrix products, arithmetic and copies ran while one was open for 0% of the time, Pallas kernels for 19%

profile of v9, /device:TPU:1, one launch (start us, length us, event | category | flops | bytes accessed | tf_op | source)
XLA Modules:
  0.0 39.9 jit_solution(3674144287230951791)
XLA Ops:
  0.0 2.6 %pack.1 = (f32[5,4,32,128]{3,2,1,0:T(8,128)S(1)}, f32[11,4,32,128]{3,2,1,0:T(8,128)S(1)}, f32[32,128]{1,0:T(8,128)S(1)}, f32[17,32,128]{2,1,0:T(8,128)S(1)}, f32...) custom-call(f32[5,4,32,128]{3,2,1,0:T(8,128)} %adjoint_hbm.1, ...), custom_call_target="tpu_custom_call" | custom-call | tf_op jit(solution)/shard_map/pack/pallas_call | solution.py:625
  2.6 2.1 %collective-permute-start.1 = (f32[56,128]{1,0:T(8,128)S(1)}, f32[56,128]{1,0:T(8,128)S(1)}, u32[]{:S(2)}, u32[]{:S(2)}) collective-permute-start(f32[56,128]{1,0:T(8,128)S(1)} %get-tuple-element.48), channel_id=1, source_target_pairs={{0,4},{1,5},{2,6},{3,7},{4,0},{5,1},{6,2},{7,3},{8,12},{9,13},{10,... | collective-permute-start | bytes 86024 | tf_op jit(solution)/shard_map/ppermute | solution.py:595
  4.7 0.1 collective-permute-start
  4.8 1.2 %collective-permute-done.1 = f32[56,128]{1,0:T(8,128)S(1)} collective-permute-done((f32[56,128]{1,0:T(8,128)S(1)}, f32[56,128]{1,0:T(8,128)S(1)}, u32[]{:S(2)}, u32[]{:S(2)}) %collective-permute-start.1) | collective-permute-done | bytes 28704 | tf_op jit(solution)/shard_map/ppermute | solution.py:595
  6.0 1.5 %collective-permute-start.2 = (f32[160,128]{1,0:T(8,128)S(1)}, f32[160,128]{1,0:T(8,128)S(1)}, u32[]{:S(2)}, u32[]{:S(2)}) collective-permute-start(f32[160,128]{1,0:T(8,128)S(1)} %slice_dynamic-update-slice_fusion), channel_id=1, source_target_pairs={{0,1},{1,0},{2,3},{3,2},{4,5},{5,4},{6,7},{7,6},{8,9},{9,8},{10,11... | collective-permute-start | bytes 245768 | tf_op jit(solution)/shard_map/ppermute | solution.py:595
  7.5 2.2 %collective-permute-start.3 = (f32[120,128]{1,0:T(8,128)S(1)}, f32[120,128]{1,0:T(8,128)S(1)}, u32[]{:S(2)}, u32[]{:S(2)}) collective-permute-start(f32[120,128]{1,0:T(8,128)S(1)} %slice_dynamic-update-slice_fusion.1), channel_id=1, source_target_pairs={{0,3},{1,2},{2,1},{3,0},{4,7},{5,6},{6,5},{7,4},{8,11},{9,10},{10,... | collective-permute-start | bytes 184328 | tf_op jit(solution)/shard_map/ppermute | solution.py:595
  9.7 0.0 collective-permute-done.2.inner_ref
  9.7 7.1 %collective-permute-start.5 = (f32[40,128]{1,0:T(8,128)S(1)}, f32[40,128]{1,0:T(8,128)S(1)}, u32[]{:S(2)}, u32[]{:S(2)}) collective-permute-start(f32[40,128]{1,0:T(8,128)S(1)} %slice_add_fusion), channel_id=1, source_target_pairs={{8,2},{9,3},{10,0},{11,1},{12,6},{13,7},{14,4},{15,5},{16,10},{17,... | collective-permute-start | bytes 61448 | tf_op jit(solution)/shard_map/ppermute | solution.py:595
  16.8 1.9 %collective-permute-start.4 = (f32[40,128]{1,0:T(8,128)S(1)}, f32[40,128]{1,0:T(8,128)S(1)}, u32[]{:S(2)}, u32[]{:S(2)}) collective-permute-start(f32[40,128]{1,0:T(8,128)S(1)} %slice_add_fusion), channel_id=1, source_target_pairs={{8,0},{9,1},{10,2},{11,3},{12,4},{13,5},{14,6},{15,7},{16,8},{17,9... | collective-permute-start | bytes 61448 | tf_op jit(solution)/shard_map/ppermute | solution.py:595
  18.7 0.6 %synth.1 = (bf16[2,896,128]{2,1,0:T(8,128)(2,1)S(1)}, f32[152,128]{1,0:T(8,128)S(1)}) custom-call(s32[1,4]{1,0:T(1,128)S(1)} %get-tuple-element.35.blades_ref, f32[5,5,1,6]{3,2,1,0:T(1,128)S(1)} %get-tuple-element.36.jacobians_ref, f32[5,5,3,64]{3,2,1,0:T(4,128)S(1)} %get-tuple-element.37.giles_re_ref, f32[5,5,3,64]{3,2,1,0:T(4,128)S(1)} %get-tuple-element.38.giles_im_ref, ...), custom_call_target="tpu_custom_call" | custom-call | tf_op jit(solution)/shard_map/synth/pallas_call | solution.py:625
  19.3 0.0 collective-permute-done.3.outer_ref
  19.4 0.0 collective-permute-done.span_ref
  19.4 4.5 %first_sweeps.1 = (f32[11,4,40,128]{3,2,1,0:T(8,128)S(1)}, f32[40,128]{1,0:T(8,128)S(1)}, f32[12,40,128]{2,1,0:T(8,128)S(1)}, f32[6,5,6,40,128]{4,3,2,1,0:T(8,12...) custom-call(f32[152,128]{1,0:T(8,128)S(1)} %get-tuple-element.41.jac_ref, ...), custom_call_target="tpu_custom_call" | custom-call | tf_op jit(solution)/shard_map/first_sweeps/pallas_call | solution.py:625
  23.9 0.0 collective-permute-done.5.modes_b_ref
  23.9 0.0 collective-permute-done.4.modes_a_ref
  23.9 0.6 %late_modes.1.more_ref = f32[136,128]{1,0:T(8,128)S(1)} custom-call(f32[152,128]{1,0:T(8,128)S(1)} %get-tuple-element.41.jac_ref, f32[11,4,40,128]{3,2,1,0:T(8,128)S(1)} %get-tuple-element.51.coef_ref, f32[40,128]{1,0:T(8,128)S(1)} %get-tuple-element.52.inv_ref, f32[32,128]{1,0:T(8,128)S(1)} %get-tuple-element.57.part_ref, ...), custom_call_target="tpu_custom_call" | custom-call | tf_op jit(solution)/shard_map/late_modes/pallas_call | solution.py:625
  24.5 1.6 %collective-permute-start.6 = (f32[136,128]{1,0:T(8,128)S(1)}, f32[136,128]{1,0:T(8,128)S(1)}, u32[]{:S(2)}, u32[]{:S(2)}) collective-permute-start(f32[136,128]{1,0:T(8,128)S(1)} %late_modes.1.more_ref), channel_id=1, source_target_pairs={{0,1},{1,0},{2,3},{3,2},{4,5},{5,4},{6,7},{7,6},{8,9},{9,8},{10,11... | collective-permute-start | bytes 208904 | tf_op jit(solution)/shard_map/ppermute | solution.py:595
  26.1 1.6 %between_sweeps.1 = (f32[6,5,6,40,128]{4,3,2,1,0:T(8,128)S(1)}, f32[5,5,40,128]{3,2,1,0:T(8,128)S(1)}, f32[136,128]{1,0:T(8,128)S(1)}) custom-call(f32[152,128]{1,0:T(8,128)S(1)} %get-tuple-element.41.jac_ref, f32[11,4,40,128]{3,2,1,0:T(8,128)S(1)} %get-tuple-element.51.coef_ref, ...), custom_call_target="tpu_custom_call", output_to_operand_aliasing={{0}: (4, {}), {1}: (5, {})} | custom-call | tf_op jit(solution)/shard_map/between_sweeps/pallas_call | solution.py:625
  27.7 0.1 collective-permute-done.6
  27.9 1.9 %collective-permute-start.8 = (f32[136,128]{1,0:T(8,128)S(1)}, f32[136,128]{1,0:T(8,128)S(1)}, u32[]{:S(2)}, u32[]{:S(2)}) collective-permute-start(f32[136,128]{1,0:T(8,128)S(1)} %add.7), channel_id=1, source_target_pairs={{8,2},{9,3},{10,0},{11,1},{12,6},{13,7},{14,4},{15,5},{16,10},{17,... | collective-permute-start | bytes 208904 | tf_op jit(solution)/shard_map/ppermute | solution.py:595
  29.8 1.9 %collective-permute-start.7 = (f32[136,128]{1,0:T(8,128)S(1)}, f32[136,128]{1,0:T(8,128)S(1)}, u32[]{:S(2)}, u32[]{:S(2)}) collective-permute-start(f32[136,128]{1,0:T(8,128)S(1)} %add.7), channel_id=1, source_target_pairs={{8,0},{9,1},{10,2},{11,3},{12,4},{13,5},{14,6},{15,7},{16,8},{17,9... | collective-permute-start | bytes 208904 | tf_op jit(solution)/shard_map/ppermute | solution.py:595
  31.7 0.8 %beside_sweeps.1 = (f32[6,5,6,40,128]{4,3,2,1,0:T(8,128)S(1)}, f32[5,5,40,128]{3,2,1,0:T(8,128)S(1)}) custom-call(f32[152,128]{1,0:T(8,128)S(1)} %get-tuple-element.41.jac_ref, f32[11,4,40,128]{3,2,1,0:T(8,128)S(1)} %get-tuple-element.51.coef_ref, f32[12,40,128]{2,1,0:T(8,128)S(1)} %get-tuple-element.53.edge_coef_ref, ...), custom_call_target="tpu_custom_call", output_to_operand_aliasing={{0}: (3, {}), {1}: (4, {})} | custom-call | tf_op jit(solution)/shard_map/beside_sweeps/pallas_call | solution.py:625
  32.5 2.8 %collective-permute-done.8.more_b_ref = f32[136,128]{1,0:T(8,128)S(1)} collective-permute-done((f32[136,128]{1,0:T(8,128)S(1)}, f32[136,128]{1,0:T(8,128)S(1)}, u32[]{:S(2)}, u32[]{:S(2)}) %collective-permute-start.8) | collective-permute-done | bytes 69664 | tf_op jit(solution)/shard_map/ppermute | solution.py:595
  35.3 1.2 %collective-permute-done.7.more_a_ref = f32[136,128]{1,0:T(8,128)S(1)} collective-permute-done((f32[136,128]{1,0:T(8,128)S(1)}, f32[136,128]{1,0:T(8,128)S(1)}, u32[]{:S(2)}, u32[]{:S(2)}) %collective-permute-start.7) | collective-permute-done | bytes 69664 | tf_op jit(solution)/shard_map/ppermute | solution.py:595
  36.5 3.4 %second_sweeps.1 = (f32[6,5,6,40,128]{4,3,2,1,0:T(8,128)S(1)}, f32[5,5,40,128]{3,2,1,0:T(8,128)S(1)}, f32[5,4,32,128]{3,2,1,0:T(8,128)}) custom-call(f32[152,128]{1,0:T(8,128)S(1)} %get-tuple-element.41.jac_ref, f32[11,4,40,128]{3,2,1,0:T(8,128)S(1)} %get-tuple-element.51.coef_ref, ...), custom_call_target="tpu_custom_call", output_to_operand_aliasing={{0}: (4, {}), {1}: (5, {})} | custom-call | tf_op jit(solution)/shard_map/second_sweeps/pallas_call | solution.py:625
  (4 shorter events, 0.0 us)
Async XLA Ops:
  2.6 3.4 %collective-permute-start.1 = (f32[56,128]{1,0:T(8,128)S(1)}, f32[56,128]{1,0:T(8,128)S(1)}, u32[]{:S(2)}, u32[]{:S(2)}) collective-permute-start(f32[56,128]{1,0:T(8,128)S(1)} %get-tuple-element.48), channel_id=1, source_target_pairs={{0,4},{1,5},{2,6},{3,7},{4,0},{5,1},{6,2},{7,3},{8,12},{9,13},{10,... | collective-permute-start | bytes 86024 | tf_op jit(solution)/shard_map/ppermute | solution.py:595
  4.7 14.6 %collective-permute-start = (f32[36,8,128]{2,1,0:T(8,128)S(1)}, f32[36,8,128]{2,1,0:T(8,128)S(1)}, u32[]{:S(2)}, u32[]{:S(2)}) collective-permute-start(f32[36,8,128]{2,1,0:T(8,128)S(1)} %get-tuple-element.46), channel_id=1, source_target_pairs={{0,4},{1,5},{2,6},{3,7},{4,0},{5,1},{6,2},{7,3},{8,12},{9,13},{10,... | collective-permute-start | bytes 442376 | tf_op jit(solution)/shard_map/ppermute | solution.py:595
  6.0 3.7 %collective-permute-start.2 = (f32[160,128]{1,0:T(8,128)S(1)}, f32[160,128]{1,0:T(8,128)S(1)}, u32[]{:S(2)}, u32[]{:S(2)}) collective-permute-start(f32[160,128]{1,0:T(8,128)S(1)} %slice_dynamic-update-slice_fusion), channel_id=1, source_target_pairs={{0,1},{1,0},{2,3},{3,2},{4,5},{5,4},{6,7},{7,6},{8,9},{9,8},{10,11... | collective-permute-start | bytes 245768 | tf_op jit(solution)/shard_map/ppermute | solution.py:595
  7.5 11.9 %collective-permute-start.3 = (f32[120,128]{1,0:T(8,128)S(1)}, f32[120,128]{1,0:T(8,128)S(1)}, u32[]{:S(2)}, u32[]{:S(2)}) collective-permute-start(f32[120,128]{1,0:T(8,128)S(1)} %slice_dynamic-update-slice_fusion.1), channel_id=1, source_target_pairs={{0,3},{1,2},{2,1},{3,0},{4,7},{5,6},{6,5},{7,4},{8,11},{9,10},{10,... | collective-permute-start | bytes 184328 | tf_op jit(solution)/shard_map/ppermute | solution.py:595
  9.7 14.2 %collective-permute-start.5 = (f32[40,128]{1,0:T(8,128)S(1)}, f32[40,128]{1,0:T(8,128)S(1)}, u32[]{:S(2)}, u32[]{:S(2)}) collective-permute-start(f32[40,128]{1,0:T(8,128)S(1)} %slice_add_fusion), channel_id=1, source_target_pairs={{8,2},{9,3},{10,0},{11,1},{12,6},{13,7},{14,4},{15,5},{16,10},{17,... | collective-permute-start | bytes 61448 | tf_op jit(solution)/shard_map/ppermute | solution.py:595
  16.8 7.1 %collective-permute-start.4 = (f32[40,128]{1,0:T(8,128)S(1)}, f32[40,128]{1,0:T(8,128)S(1)}, u32[]{:S(2)}, u32[]{:S(2)}) collective-permute-start(f32[40,128]{1,0:T(8,128)S(1)} %slice_add_fusion), channel_id=1, source_target_pairs={{8,0},{9,1},{10,2},{11,3},{12,4},{13,5},{14,6},{15,7},{16,8},{17,9... | collective-permute-start | bytes 61448 | tf_op jit(solution)/shard_map/ppermute | solution.py:595
  24.5 3.3 %collective-permute-start.6 = (f32[136,128]{1,0:T(8,128)S(1)}, f32[136,128]{1,0:T(8,128)S(1)}, u32[]{:S(2)}, u32[]{:S(2)}) collective-permute-start(f32[136,128]{1,0:T(8,128)S(1)} %late_modes.1.more_ref), channel_id=1, source_target_pairs={{0,1},{1,0},{2,3},{3,2},{4,5},{5,4},{6,7},{7,6},{8,9},{9,8},{10,11... | collective-permute-start | bytes 208904 | tf_op jit(solution)/shard_map/ppermute | solution.py:595
  27.9 7.4 %collective-permute-start.8 = (f32[136,128]{1,0:T(8,128)S(1)}, f32[136,128]{1,0:T(8,128)S(1)}, u32[]{:S(2)}, u32[]{:S(2)}) collective-permute-start(f32[136,128]{1,0:T(8,128)S(1)} %add.7), channel_id=1, source_target_pairs={{8,2},{9,3},{10,0},{11,1},{12,6},{13,7},{14,4},{15,5},{16,10},{17,... | collective-permute-start | bytes 208904 | tf_op jit(solution)/shard_map/ppermute | solution.py:595
  29.8 6.7 %collective-permute-start.7 = (f32[136,128]{1,0:T(8,128)S(1)}, f32[136,128]{1,0:T(8,128)S(1)}, u32[]{:S(2)}, u32[]{:S(2)}) collective-permute-start(f32[136,128]{1,0:T(8,128)S(1)} %add.7), channel_id=1, source_target_pairs={{8,0},{9,1},{10,2},{11,3},{12,4},{13,5},{14,6},{15,7},{16,8},{17,9... | collective-permute-start | bytes 208904 | tf_op jit(solution)/shard_map/ppermute | solution.py:595

commit v10 on v9

--- a/solution.py
+++ b/solution.py
@@ -97,9 +97,10 @@
 def pack_kernel(
     adjoint_hbm, source_hbm, couplings_hbm, damping_hbm, blades_hbm, *refs, groups, length,
 ):
-    (adjoint_ref, coef_ref, inv_ref, edges_ref, span_ref, small_ref, inner_ref, outer_ref, table_ref, blades_ref) = refs[5:15]
+    (state_ref, coef_ref, inv_ref, edges_ref, span_ref, small_ref, inner_ref, outer_ref, table_ref, blades_ref) = refs[5:15]
     source_ref, couplings_ref, damping_ref, sems = refs[20:]
-    components, axial, span, pitch = adjoint_ref.shape
+    components, axial, span, pitch = source_ref.shape
+    adjoint_ref = state_ref.at[0, :, :, pl.ds(0, span), :]
     copies = [
         pltpu.make_async_copy(src, dst, sems.at[n])
         for n, (src, dst) in enumerate((
@@ -117,18 +118,18 @@
         diag = diag + couplings_ref[d]
     inverse = 1.0 / diag
     for d in range(6):
-        coef_ref[components + d] = couplings_ref[d] * inverse
-    inv_ref[...] = inverse[axial - 1]
+        coef_ref[components + d, :, :span] = couplings_ref[d] * inverse
+    inv_ref[:span] = inverse[axial - 1]
     copies[2].wait()
     for c in range(components):
-        coef_ref[c] = source_ref[c] * inverse
+        coef_ref[c, :, :span] = source_ref[c] * inverse
     copies[3].wait()
 
     fields = 2 * components + 6
     for f in range(fields):
         ref, at = (adjoint_ref, f) if f < components else (coef_ref, f - components)
-        edges_ref[f] = to_edges([ref[at, a] for a in range(axial)], pitch)
-    last = inv_ref[...]
+        edges_ref[f] = to_edges([ref[at, a, :span] for a in range(axial)], pitch)
+    last = inv_ref[:span]
     edges_ref[fields] = jnp.where(
         lanes(last.shape) >= (axial - 1) * SEGMENT_LANES,
         to_edges([jnp.zeros_like(last)] * (axial - 1) + [last], pitch), 0.0,
@@ -288,6 +289,8 @@
     total = list(source)
     jac = functools.partial(jacobian, jac_ref, len(total))
     for d, neighbour in enumerate(neighbours):
+        if neighbour is None:
+            continue
         for c in range(len(total)):
             term = jac(0, c, d) * neighbour[0]
             for b in range(1, len(total)):
@@ -297,24 +300,24 @@
 
 
 def layer_update(jac_ref, state_ref, edge_ref, coef_ref, t, a, height):
-    components, wide, pitch = state_ref.shape[1], state_ref.shape[3], state_ref.shape[4]
+    _, components, axial, wide, pitch = state_ref.shape
     lane = lanes((height, pitch))
     start = a * SEGMENT_LANES
-    own = [state_ref[t, c, a + 1] for c in range(components)]
-    above = [state_ref[t, c, a + 2, :height] for c in range(components)]
-    below = [state_ref[t, c, a, :height] for c in range(components)]
+    own = [state_ref[t, c, a] for c in range(components)]
+    above = [state_ref[t, c, a + 1, :height] for c in range(components)] if a < axial - 1 else None
+    below = [state_ref[t, c, a - 1, :height] for c in range(components)] if a else None
     edge = [edge_ref[t, c, :height] for c in range(components)]
     span_next = [pltpu.roll(x, wide - 1, 0)[:height] for x in own]
     span_prev = [pltpu.roll(x, 1, 0)[:height] for x in own]
     own = [x[:height] for x in own]
-    to_end = 2 * pitch - 1 - (start + 3 * EDGE)
-    to_begin = 2 * pitch - (start + EDGE - 1)
+    to_end = (pitch - 1 - (start + 3 * EDGE)) % pitch
+    to_begin = (pitch - (start + EDGE - 1)) % pitch
     pitch_next = [
-        jnp.where(lane == pitch - 1, pltpu.roll(e, lax.rem(to_end, pitch), 1), pltpu.roll(x, pitch - 1, 1))
+        jnp.where(lane == pitch - 1, pltpu.roll(e, to_end, 1), pltpu.roll(x, pitch - 1, 1))
         for e, x in zip(edge, own)
     ]
     pitch_prev = [
-        jnp.where(lane == 0, pltpu.roll(e, lax.rem(to_begin, pitch), 1), pltpu.roll(x, 1, 1))
+        jnp.where(lane == 0, pltpu.roll(e, to_begin, 1), pltpu.roll(x, 1, 1))
         for e, x in zip(edge, own)
     ]
     source = [coef_ref[c, a, :height] for c in range(components)]
@@ -347,15 +350,15 @@
     state_ref = refs[1]
     height = height or state_ref.shape[3]
     for c, value in enumerate(layer_update(*refs, t, a, height)):
-        state_ref[t + 1, c, a + 1, :height] = value
+        state_ref[t + 1, c, a, :height] = value
 
 
 def first_kernel(
-    jac_ref, adjoint_ref, coef_in_ref, inv_in_ref, edges_ref, span_ref, inner_ref, outer_ref, table_ref,
+    jac_ref, state_in_ref, coef_in_ref, inv_in_ref, edges_ref, span_ref, inner_ref, outer_ref, table_ref,
     coef_ref, inv_ref, edge_coef_ref, state_ref, edge_ref, modes_ref, part_ref, *, groups,
 ):
-    components, axial, span, pitch = adjoint_ref.shape
-    wide = span + EDGE
+    _, components, axial, wide, pitch = state_ref.shape
+    span = wide - EDGE
     side = lax.axis_index("span")
     fields = 2 * components + 6
     line = rows((EDGE, pitch))
@@ -390,14 +393,11 @@
             layers = [jnp.zeros((EDGE, pitch), jnp.float32)] * (axial - 1) + [ghost(fields * axial)]
         if f < components:
             for a in range(axial):
-                state_ref[0, f, a + 1, :span] = adjoint_ref[f, a]
-                state_ref[0, f, a + 1, span:] = layers[a]
+                state_ref[0, f, a, span:] = layers[a]
         elif f < fields:
             for a in range(axial):
-                coef_ref[f - components, a, :span] = coef_in_ref[f - components, a]
                 coef_ref[f - components, a, span:] = layers[a]
         else:
-            inv_ref[:span] = inv_in_ref[...]
             inv_ref[span:] = layers[-1]
         g, at = near[f]
         value = jnp.concatenate([edges_ref[f], to_edges(layers, pitch)], 0)
@@ -416,28 +416,15 @@
         target, at = (edge_ref.at[0], f) if f < components else (edge_coef_ref, f - components)
         target[at, :span] = value[:span]
         target[at, span:] = jnp.where(keep_five if f < components else keep_half, value[span:], 0.0)
-    for t in range(state_ref.shape[0]):
-        for c in range(components):
-            state_ref[t, c, 0] = jnp.zeros((wide, pitch), jnp.float32)
-            state_ref[t, c, axial + 1] = jnp.zeros((wide, pitch), jnp.float32)
-
     refs = (jac_ref, state_ref, edge_ref, coef_ref)
-
-    def sweep(t, carry):
-        def body(a, inner):
+    for t in range(axial):
+        for a in range(axial - t):
             advance(refs, t, a)
-            return inner
-
-        lax.fori_loop(0, axial - t, body, 0)
-
-        for c, value in enumerate(edge_update(jac_ref, edge_ref, edge_coef_ref, t, axial)):
-            edge_ref[t + 1, c] = value
-        return carry
-
-    lax.fori_loop(0, axial - 1, sweep, 0)
-    advance(refs, axial - 1, 0)
+        if t < axial - 1:
+            for c, value in enumerate(edge_update(jac_ref, edge_ref, edge_coef_ref, t, axial)):
+                edge_ref[t + 1, c] = value
     strips = [
-        jnp.concatenate([state_ref[t, c, 1] for t in range(1, axial)] + [state_ref[axial, c, 1, :span]], 0)
+        jnp.concatenate([state_ref[t, c, 0] for t in range(1, axial)] + [state_ref[axial, c, 0, :span]], 0)
         for c in range(components)
     ]
     total = projected(strips, table_ref)
@@ -490,14 +477,14 @@
     state_ref, edge_ref, sent_ref,
 ):
     sent_ref[...] = more_ref[...]
-    components, axial = state_ref.shape[1], state_ref.shape[2] - 2
+    components, axial = state_ref.shape[1], state_ref.shape[2]
     wide, pitch = state_ref.shape[3:]
     modes = modes_a_ref[...] + modes_b_ref[...]
     field = synthesised(jnp.concatenate([modes[EDGE:], modes[:EDGE]], 0), synth_ref, synth_ref.shape[1])
     delta = [inv_ref[...] * field[:, c * pitch:(c + 1) * pitch] for c in range(components)]
     for t in range(1, axial + 1):
         for c in range(components):
-            state_ref[t, c, axial + 1 - t] += delta[c]
+            state_ref[t, c, axial - t] += delta[c]
         if t < axial:
             delta = along_axis(jac_ref, coef_ref, delta, axial - 1 - t, wide)
     for c in range(components):
@@ -506,21 +493,17 @@
 
 
 def beside_kernel(jac_ref, coef_ref, edge_coef_ref, state_in_ref, edge_in_ref, state_ref, edge_ref):
-    axial, span = state_ref.shape[2] - 2, state_ref.shape[3] - EDGE
+    axial, span = state_ref.shape[2], state_ref.shape[3] - EDGE
     diagonal_sweeps(jac_ref, state_ref, edge_ref, coef_ref, edge_coef_ref, axial // 2 + 1, axial)
     advance((jac_ref, state_ref, edge_ref, coef_ref), axial, 0, span)
 
 
 def diagonal_sweeps(jac_ref, state_ref, edge_ref, coef_ref, edge_coef_ref, first, last):
-    axial = state_ref.shape[2] - 2
-
-    def sweep(t, carry):
+    axial = state_ref.shape[2]
+    for t in range(first, last):
         advance((jac_ref, state_ref, edge_ref, coef_ref), t, axial - t)
         for c, value in enumerate(edge_update(jac_ref, edge_ref, edge_coef_ref, t, axial)):
             edge_ref[t + 1, c] = value
-        return carry
-
-    lax.fori_loop(first, last, sweep, 0)
 
 
 def second_kernel(
@@ -547,7 +530,7 @@
     for t in range(2, axial + 2):
         height = wide if t <= axial else span
         for c in range(components):
-            state_ref[t, c, axial + 2 - t, :height] += delta[c][:height]
+            state_ref[t, c, axial + 1 - t, :height] += delta[c][:height]
         if t < axial + 1:
             delta = along_axis(jac_ref, coef_ref, delta, axial - t, wide)
     for t in range(1, axial):
@@ -559,27 +542,16 @@
             edge_ref[t + 1, c] += edge_coef_ref[components + 6] * edge_boundary(part, c, components, pitch, axial)
     refs = (jac_ref, state_ref, edge_ref, coef_ref)
 
-    def sweep(t, carry):
-        def body(a, inner):
+    for t in range(2, axial):
+        for a in range(axial + 1 - t, axial):
             advance(refs, t, a)
-            return inner
-
-        lax.fori_loop(axial + 1 - t, axial, body, 0)
         for c in range(components):
-            state_ref[t + 1, c, axial] += bound_ref[t, c]
-        return carry
-
-    lax.fori_loop(2, axial, sweep, 0)
-
-    def final(a, carry):
+            state_ref[t + 1, c, axial - 1] += bound_ref[t, c]
+    for a in range(1, axial):
         for c, value in enumerate(layer_update(*refs, axial, a, span)):
-            out_ref[c, a] = value
-        return carry
-
-    lax.fori_loop(1, axial, final, 0)
+            out_ref[c, a] = value + bound_ref[axial, c, :span] if a == axial - 1 else value
     for c in range(components):
-        out_ref[c, 0] = state_ref[axial + 1, c, 1, :span]
-        out_ref[c, axial - 1] += bound_ref[axial, c, :span]
+        out_ref[c, 0] = state_ref[axial + 1, c, 0, :span]
 
 
 def moved(x, to):
@@ -639,10 +611,11 @@
     )
     blades = blades.reshape(1, -1)
     corner_rows = groups * EDGE
-    adjoint, coef, inv, edges, span_out, small, inner, outer, table, blades, *tables = call(
+    state_shape = struct(axial + 2, components, axial, wide, pitch)
+    state, coef, inv, edges, span_out, small, inner, outer, table, blades, *tables = call(
         pack_kernel, "pack",
         (
-            struct(components, axial, span, pitch), struct(components + 6, axial, span, pitch), struct(span, pitch),
+            state_shape, struct(components + 6, axial, wide, pitch), struct(wide, pitch),
             struct(fields + 1, span, pitch), struct(span_tiles, EDGE, pitch), struct(2 * corner_rows + EDGE, pitch),
             struct(groups * span + corner_rows + EDGE + span, pitch), struct(groups * span + corner_rows, pitch),
             jax.ShapeDtypeStruct((2, components * pitch, pitch), jnp.bfloat16), *(jax.ShapeDtypeStruct(x.shape, x.dtype) for x in (blades, *tables)),
@@ -689,7 +662,6 @@
         scratch=[pltpu.VMEM((2, components * components, mode_orders.shape[1]), jnp.float32)],
         row_count=row_count, place_count=place_count, components=components, pitch=pitch, length=length, axial=axial,
     )
-    state_shape = struct(axial + 2, components, axial + 2, wide, pitch)
     edge_shape = struct(axial + 1, components, wide, pitch)
     coef, inv, edge_coef, state, edge, more, part = call(
         first_kernel, "first_sweeps",
@@ -698,7 +670,8 @@
             state_shape, edge_shape,
             struct((axial - 1) * span + EDGE, pitch), struct(span, pitch),
         ),
-        [(vmem, jac)] + [(vmem, x) for x in (adjoint, coef, inv, edges, from_span, inner, outer, table)],
+        [(vmem, jac)] + [(vmem, x) for x in (state, coef, inv, edges, from_span, inner, outer, table)],
+        aliases={1: 3, 2: 0, 3: 1},
         groups=groups,
     )
 

time: 40.1 us -> 39.7 us (0.990)
  transfers between devices with their start and end apart: 9 -> 9, of which waited for: 4 -> 3; matrix products, arithmetic and copies ran while one was open for 0% -> 0% of each run, Pallas kernels for 19% -> 18%
where the time goes in v10:
time: 39.7 us; the launch traced here: 39.5 us
  starting transfers between devices  20.4 us (51%)
  Pallas kernels  13.7 us (35%)
  waiting for transfers between devices  5.24 us (13%)
    ppermute x9, starting transfers between devices, moved(): return lax.ppermute(x, AXES, pairs)  20.4 us
    pallas_call x7, Pallas kernels, call(): pl.pallas_call(functools.partial(kernel, **fixed), out_shape=outs, in_spe...  13.7 us
    ppermute x9, waiting for transfers between devices, moved(): return lax.ppermute(x, AXES, pairs)  5.24 us
  transfers between devices with their start and end apart: 9, of which 3 were waited for; matrix products, arithmetic and copies ran while one was open for 0% of the time, Pallas kernels for 18%

profile of v10, /device:TPU:1, one launch (start us, length us, event | category | flops | bytes accessed | tf_op | source)
XLA Modules:
  0.0 39.5 jit_solution(10180676234444977929)
XLA Ops:
  0.0 2.6 %pack.1 = (f32[6,5,4,40,128]{4,3,2,1,0:T(8,128)S(1)}, f32[11,4,40,128]{3,2,1,0:T(8,128)S(1)}, f32[40,128]{1,0:T(8,128)S(1)}, f32[17,32,128]{2,1,0:T(8,128)S(1)},...) custom-call(f32[5,4,32,128]{3,2,1,0:T(8,128)} %adjoint_hbm.1, ...), custom_call_target="tpu_custom_call" | custom-call | tf_op jit(solution)/shard_map/pack/pallas_call | solution.py:597
  2.6 2.1 %collective-permute-start.1 = (f32[56,128]{1,0:T(8,128)S(1)}, f32[56,128]{1,0:T(8,128)S(1)}, u32[]{:S(2)}, u32[]{:S(2)}) collective-permute-start(f32[56,128]{1,0:T(8,128)S(1)} %get-tuple-element.48), channel_id=1, source_target_pairs={{0,4},{1,5},{2,6},{3,7},{4,0},{5,1},{6,2},{7,3},{8,12},{9,13},{10,... | collective-permute-start | bytes 86024 | tf_op jit(solution)/shard_map/ppermute | solution.py:567
  4.7 0.1 collective-permute-start
  4.8 1.2 %collective-permute-done.1 = f32[56,128]{1,0:T(8,128)S(1)} collective-permute-done((f32[56,128]{1,0:T(8,128)S(1)}, f32[56,128]{1,0:T(8,128)S(1)}, u32[]{:S(2)}, u32[]{:S(2)}) %collective-permute-start.1) | collective-permute-done | bytes 28704 | tf_op jit(solution)/shard_map/ppermute | solution.py:567
  6.0 1.5 %collective-permute-start.2 = (f32[160,128]{1,0:T(8,128)S(1)}, f32[160,128]{1,0:T(8,128)S(1)}, u32[]{:S(2)}, u32[]{:S(2)}) collective-permute-start(f32[160,128]{1,0:T(8,128)S(1)} %slice_dynamic-update-slice_fusion), channel_id=1, source_target_pairs={{0,1},{1,0},{2,3},{3,2},{4,5},{5,4},{6,7},{7,6},{8,9},{9,8},{10,11... | collective-permute-start | bytes 245768 | tf_op jit(solution)/shard_map/ppermute | solution.py:567
  7.5 2.2 %collective-permute-start.3 = (f32[120,128]{1,0:T(8,128)S(1)}, f32[120,128]{1,0:T(8,128)S(1)}, u32[]{:S(2)}, u32[]{:S(2)}) collective-permute-start(f32[120,128]{1,0:T(8,128)S(1)} %slice_dynamic-update-slice_fusion.1), channel_id=1, source_target_pairs={{0,3},{1,2},{2,1},{3,0},{4,7},{5,6},{6,5},{7,4},{8,11},{9,10},{10,... | collective-permute-start | bytes 184328 | tf_op jit(solution)/shard_map/ppermute | solution.py:567
  9.7 0.0 collective-permute-done.2.inner_ref
  9.7 7.1 %collective-permute-start.5 = (f32[40,128]{1,0:T(8,128)S(1)}, f32[40,128]{1,0:T(8,128)S(1)}, u32[]{:S(2)}, u32[]{:S(2)}) collective-permute-start(f32[40,128]{1,0:T(8,128)S(1)} %slice_add_fusion), channel_id=1, source_target_pairs={{8,2},{9,3},{10,0},{11,1},{12,6},{13,7},{14,4},{15,5},{16,10},{17,... | collective-permute-start | bytes 61448 | tf_op jit(solution)/shard_map/ppermute | solution.py:567
  16.8 1.9 %collective-permute-start.4 = (f32[40,128]{1,0:T(8,128)S(1)}, f32[40,128]{1,0:T(8,128)S(1)}, u32[]{:S(2)}, u32[]{:S(2)}) collective-permute-start(f32[40,128]{1,0:T(8,128)S(1)} %slice_add_fusion), channel_id=1, source_target_pairs={{8,0},{9,1},{10,2},{11,3},{12,4},{13,5},{14,6},{15,7},{16,8},{17,9... | collective-permute-start | bytes 61448 | tf_op jit(solution)/shard_map/ppermute | solution.py:567
  18.7 0.6 %synth.1 = (bf16[2,896,128]{2,1,0:T(8,128)(2,1)S(1)}, f32[152,128]{1,0:T(8,128)S(1)}) custom-call(s32[1,4]{1,0:T(1,128)S(1)} %get-tuple-element.35.blades_ref, f32[5,5,1,6]{3,2,1,0:T(1,128)S(1)} %get-tuple-element.36.jacobians_ref, f32[5,5,3,64]{3,2,1,0:T(4,128)S(1)} %get-tuple-element.37.giles_re_ref, f32[5,5,3,64]{3,2,1,0:T(4,128)S(1)} %get-tuple-element.38.giles_im_ref, ...), custom_call_target="tpu_custom_call" | custom-call | tf_op jit(solution)/shard_map/synth/pallas_call | solution.py:597
  19.3 0.0 collective-permute-done.3.outer_ref
  19.4 0.0 collective-permute-done.span_ref
  19.4 4.1 %first_sweeps.1 = (f32[11,4,40,128]{3,2,1,0:T(8,128)S(1)}, f32[40,128]{1,0:T(8,128)S(1)}, f32[12,40,128]{2,1,0:T(8,128)S(1)}, f32[6,5,4,40,128]{4,3,2,1,0:T(8,12...) custom-call(f32[152,128]{1,0:T(8,128)S(1)} %get-tuple-element.41.jac, ...), custom_call_target="tpu_custom_call", output_to_operand_aliasing={{3}: (1, {}), {0}: (2, {}), {1}: (3, {})} | custom-call | tf_op jit(solution)/shard_map/first_sweeps/pallas_call | solution.py:597
  23.5 0.0 collective-permute-done.5.modes_b_ref
  23.5 0.0 collective-permute-done.4.modes_a_ref
  23.5 0.6 %late_modes.1.more_ref = f32[136,128]{1,0:T(8,128)S(1)} custom-call(f32[152,128]{1,0:T(8,128)S(1)} %get-tuple-element.41.jac_ref, f32[11,4,40,128]{3,2,1,0:T(8,128)S(1)} %get-tuple-element.51.coef_ref, f32[40,128]{1,0:T(8,128)S(1)} %get-tuple-element.52.inv_ref, f32[32,128]{1,0:T(8,128)S(1)} %get-tuple-element.57.part_ref, ...), custom_call_target="tpu_custom_call" | custom-call | tf_op jit(solution)/shard_map/late_modes/pallas_call | solution.py:597
  24.1 1.6 %collective-permute-start.6 = (f32[136,128]{1,0:T(8,128)S(1)}, f32[136,128]{1,0:T(8,128)S(1)}, u32[]{:S(2)}, u32[]{:S(2)}) collective-permute-start(f32[136,128]{1,0:T(8,128)S(1)} %late_modes.1.more_ref), channel_id=1, source_target_pairs={{0,1},{1,0},{2,3},{3,2},{4,5},{5,4},{6,7},{7,6},{8,9},{9,8},{10,11... | collective-permute-start | bytes 208904 | tf_op jit(solution)/shard_map/ppermute | solution.py:567
  25.8 1.7 %between_sweeps.1 = (f32[6,5,4,40,128]{4,3,2,1,0:T(8,128)S(1)}, f32[5,5,40,128]{3,2,1,0:T(8,128)S(1)}, f32[136,128]{1,0:T(8,128)S(1)}) custom-call(f32[152,128]{1,0:T(8,128)S(1)} %get-tuple-element.41.jac_ref, f32[11,4,40,128]{3,2,1,0:T(8,128)S(1)} %get-tuple-element.51.coef_ref, ...), custom_call_target="tpu_custom_call", output_to_operand_aliasing={{0}: (4, {}), {1}: (5, {})} | custom-call | tf_op jit(solution)/shard_map/between_sweeps/pallas_call | solution.py:597
  27.4 0.0 collective-permute-done.6
  27.5 1.9 %collective-permute-start.8 = (f32[136,128]{1,0:T(8,128)S(1)}, f32[136,128]{1,0:T(8,128)S(1)}, u32[]{:S(2)}, u32[]{:S(2)}) collective-permute-start(f32[136,128]{1,0:T(8,128)S(1)} %add.7), channel_id=1, source_target_pairs={{8,2},{9,3},{10,0},{11,1},{12,6},{13,7},{14,4},{15,5},{16,10},{17,... | collective-permute-start | bytes 208904 | tf_op jit(solution)/shard_map/ppermute | solution.py:567
  29.4 1.9 %collective-permute-start.7 = (f32[136,128]{1,0:T(8,128)S(1)}, f32[136,128]{1,0:T(8,128)S(1)}, u32[]{:S(2)}, u32[]{:S(2)}) collective-permute-start(f32[136,128]{1,0:T(8,128)S(1)} %add.7), channel_id=1, source_target_pairs={{8,0},{9,1},{10,2},{11,3},{12,4},{13,5},{14,6},{15,7},{16,8},{17,9... | collective-permute-start | bytes 208904 | tf_op jit(solution)/shard_map/ppermute | solution.py:567
  31.3 0.7 %beside_sweeps.1 = (f32[6,5,4,40,128]{4,3,2,1,0:T(8,128)S(1)}, f32[5,5,40,128]{3,2,1,0:T(8,128)S(1)}) custom-call(f32[152,128]{1,0:T(8,128)S(1)} %get-tuple-element.41.jac_ref, f32[11,4,40,128]{3,2,1,0:T(8,128)S(1)} %get-tuple-element.51.coef_ref, f32[12,40,128]{2,1,0:T(8,128)S(1)} %get-tuple-element.53.edge_coef_ref, ...), custom_call_target="tpu_custom_call", output_to_operand_aliasing={{0}: (3, {}), {1}: (4, {})} | custom-call | tf_op jit(solution)/shard_map/beside_sweeps/pallas_call | solution.py:597
  32.1 2.8 %collective-permute-done.8.more_b_ref = f32[136,128]{1,0:T(8,128)S(1)} collective-permute-done((f32[136,128]{1,0:T(8,128)S(1)}, f32[136,128]{1,0:T(8,128)S(1)}, u32[]{:S(2)}, u32[]{:S(2)}) %collective-permute-start.8) | collective-permute-done | bytes 69664 | tf_op jit(solution)/shard_map/ppermute | solution.py:567
  34.9 1.2 %collective-permute-done.7.more_a_ref = f32[136,128]{1,0:T(8,128)S(1)} collective-permute-done((f32[136,128]{1,0:T(8,128)S(1)}, f32[136,128]{1,0:T(8,128)S(1)}, u32[]{:S(2)}, u32[]{:S(2)}) %collective-permute-start.7) | collective-permute-done | bytes 69664 | tf_op jit(solution)/shard_map/ppermute | solution.py:567
  36.1 3.4 %second_sweeps.1 = (f32[6,5,4,40,128]{4,3,2,1,0:T(8,128)S(1)}, f32[5,5,40,128]{3,2,1,0:T(8,128)S(1)}, f32[5,4,32,128]{3,2,1,0:T(8,128)}) custom-call(f32[152,128]{1,0:T(8,128)S(1)} %get-tuple-element.41.jac_ref, f32[11,4,40,128]{3,2,1,0:T(8,128)S(1)} %get-tuple-element.51.coef_ref, ...), custom_call_target="tpu_custom_call", output_to_operand_aliasing={{0}: (4, {}), {1}: (5, {})} | custom-call | tf_op jit(solution)/shard_map/second_sweeps/pallas_call | solution.py:597
  (4 shorter events, 0.0 us)
Async XLA Ops:
  2.6 3.4 %collective-permute-start.1 = (f32[56,128]{1,0:T(8,128)S(1)}, f32[56,128]{1,0:T(8,128)S(1)}, u32[]{:S(2)}, u32[]{:S(2)}) collective-permute-start(f32[56,128]{1,0:T(8,128)S(1)} %get-tuple-element.48), channel_id=1, source_target_pairs={{0,4},{1,5},{2,6},{3,7},{4,0},{5,1},{6,2},{7,3},{8,12},{9,13},{10,... | collective-permute-start | bytes 86024 | tf_op jit(solution)/shard_map/ppermute | solution.py:567
  4.7 14.6 %collective-permute-start = (f32[36,8,128]{2,1,0:T(8,128)S(1)}, f32[36,8,128]{2,1,0:T(8,128)S(1)}, u32[]{:S(2)}, u32[]{:S(2)}) collective-permute-start(f32[36,8,128]{2,1,0:T(8,128)S(1)} %get-tuple-element.46), channel_id=1, source_target_pairs={{0,4},{1,5},{2,6},{3,7},{4,0},{5,1},{6,2},{7,3},{8,12},{9,13},{10,... | collective-permute-start | bytes 442376 | tf_op jit(solution)/shard_map/ppermute | solution.py:567
  6.0 3.7 %collective-permute-start.2 = (f32[160,128]{1,0:T(8,128)S(1)}, f32[160,128]{1,0:T(8,128)S(1)}, u32[]{:S(2)}, u32[]{:S(2)}) collective-permute-start(f32[160,128]{1,0:T(8,128)S(1)} %slice_dynamic-update-slice_fusion), channel_id=1, source_target_pairs={{0,1},{1,0},{2,3},{3,2},{4,5},{5,4},{6,7},{7,6},{8,9},{9,8},{10,11... | collective-permute-start | bytes 245768 | tf_op jit(solution)/shard_map/ppermute | solution.py:567
  7.5 11.9 %collective-permute-start.3 = (f32[120,128]{1,0:T(8,128)S(1)}, f32[120,128]{1,0:T(8,128)S(1)}, u32[]{:S(2)}, u32[]{:S(2)}) collective-permute-start(f32[120,128]{1,0:T(8,128)S(1)} %slice_dynamic-update-slice_fusion.1), channel_id=1, source_target_pairs={{0,3},{1,2},{2,1},{3,0},{4,7},{5,6},{6,5},{7,4},{8,11},{9,10},{10,... | collective-permute-start | bytes 184328 | tf_op jit(solution)/shard_map/ppermute | solution.py:567
  9.7 13.8 %collective-permute-start.5 = (f32[40,128]{1,0:T(8,128)S(1)}, f32[40,128]{1,0:T(8,128)S(1)}, u32[]{:S(2)}, u32[]{:S(2)}) collective-permute-start(f32[40,128]{1,0:T(8,128)S(1)} %slice_add_fusion), channel_id=1, source_target_pairs={{8,2},{9,3},{10,0},{11,1},{12,6},{13,7},{14,4},{15,5},{16,10},{17,... | collective-permute-start | bytes 61448 | tf_op jit(solution)/shard_map/ppermute | solution.py:567
  16.8 6.8 %collective-permute-start.4 = (f32[40,128]{1,0:T(8,128)S(1)}, f32[40,128]{1,0:T(8,128)S(1)}, u32[]{:S(2)}, u32[]{:S(2)}) collective-permute-start(f32[40,128]{1,0:T(8,128)S(1)} %slice_add_fusion), channel_id=1, source_target_pairs={{8,0},{9,1},{10,2},{11,3},{12,4},{13,5},{14,6},{15,7},{16,8},{17,9... | collective-permute-start | bytes 61448 | tf_op jit(solution)/shard_map/ppermute | solution.py:567
  24.1 3.3 %collective-permute-start.6 = (f32[136,128]{1,0:T(8,128)S(1)}, f32[136,128]{1,0:T(8,128)S(1)}, u32[]{:S(2)}, u32[]{:S(2)}) collective-permute-start(f32[136,128]{1,0:T(8,128)S(1)} %late_modes.1.more_ref), channel_id=1, source_target_pairs={{0,1},{1,0},{2,3},{3,2},{4,5},{5,4},{6,7},{7,6},{8,9},{9,8},{10,11... | collective-permute-start | bytes 208904 | tf_op jit(solution)/shard_map/ppermute | solution.py:567
  27.5 7.4 %collective-permute-start.8 = (f32[136,128]{1,0:T(8,128)S(1)}, f32[136,128]{1,0:T(8,128)S(1)}, u32[]{:S(2)}, u32[]{:S(2)}) collective-permute-start(f32[136,128]{1,0:T(8,128)S(1)} %add.7), channel_id=1, source_target_pairs={{8,2},{9,3},{10,0},{11,1},{12,6},{13,7},{14,4},{15,5},{16,10},{17,... | collective-permute-start | bytes 208904 | tf_op jit(solution)/shard_map/ppermute | solution.py:567
  29.4 6.7 %collective-permute-start.7 = (f32[136,128]{1,0:T(8,128)S(1)}, f32[136,128]{1,0:T(8,128)S(1)}, u32[]{:S(2)}, u32[]{:S(2)}) collective-permute-start(f32[136,128]{1,0:T(8,128)S(1)} %add.7), channel_id=1, source_target_pairs={{8,0},{9,1},{10,2},{11,3},{12,4},{13,5},{14,6},{15,7},{16,8},{17,9... | collective-permute-start | bytes 208904 | tf_op jit(solution)/shard_map/ppermute | solution.py:567

commit v11 on v10

--- a/solution.py
+++ b/solution.py
@@ -69,8 +69,8 @@
 
 
 def to_edges(layers, pitch):
-    lane = lanes(layers[0].shape)
-    block = jnp.zeros_like(layers[0])
+    lane = lanes(layers[-1].shape)
+    block = jnp.zeros_like(layers[-1])
     for a, layer in enumerate(layers):
         if layer is None:
             continue
@@ -94,23 +94,58 @@
     return near, far
 
 
-def pack_kernel(
+def packed_edges(blocks, place, components):
+    near, far = slots(len(blocks), components)
+    pitch = blocks[0].shape[1]
+    lane = lanes(blocks[0].shape) % SEGMENT_LANES
+    sides = []
+    for near_at, far_at in ((3 * EDGE - HALF, 3 * EDGE - HALF - 1), (EDGE, EDGE + HALF)):
+        packed = [jnp.zeros_like(blocks[0]) for _ in range(far[-1][0] + 1)]
+        for f, (g, to) in enumerate(near):
+            value = pltpu.roll(blocks[f], (to - near_at) % pitch, 1)
+            packed[g] = jnp.where((lane >= to) & (lane < to + HALF), value, packed[g])
+        for f, (g, to) in enumerate(far):
+            packed[g] = jnp.where(lane == to, pltpu.roll(blocks[f], (to - far_at) % pitch, 1), packed[g])
+        sides.append(packed)
+    even = lax.rem(place, 2) == 0
+    inner = [jnp.where(even, right, left) for right, left in zip(*sides)]
+    outer = [jnp.where(even, left, right) for right, left in zip(*sides)]
+    return inner, outer
+
+
+def edge_blocks(state_ref, coef_ref, inv_ref, at):
+    components, axial, pitch = state_ref.shape[1], state_ref.shape[2], state_ref.shape[4]
+    blocks = [to_edges([state_ref[0, c, a, at, :] for a in range(axial)], pitch) for c in range(components)]
+    blocks += [to_edges([coef_ref[f, a, at, :] for a in range(axial)], pitch) for f in range(components + 6)]
+    return blocks + [to_edges([None] * (axial - 1) + [inv_ref[at, :]], pitch)]
+
+
+def start_kernel(
     adjoint_hbm, source_hbm, couplings_hbm, damping_hbm, blades_hbm, *refs, groups, length,
 ):
-    (state_ref, coef_ref, inv_ref, edges_ref, span_ref, small_ref, inner_ref, outer_ref, table_ref, blades_ref) = refs[5:15]
-    source_ref, couplings_ref, damping_ref, sems = refs[20:]
+    state_ref, coef_ref, inv_ref, small_ref, modes_ref, table_ref, blades_ref = refs[5:12]
+    source_ref, couplings_ref, damping_ref, sems = refs[17:]
     components, axial, span, pitch = source_ref.shape
     adjoint_ref = state_ref.at[0, :, :, pl.ds(0, span), :]
     copies = [
         pltpu.make_async_copy(src, dst, sems.at[n])
         for n, (src, dst) in enumerate((
             (couplings_hbm, couplings_ref), (damping_hbm, damping_ref), (source_hbm, source_ref),
-            (adjoint_hbm, adjoint_ref), (blades_hbm, blades_ref), *zip(refs[:5], refs[15:20]),
+            (adjoint_hbm, adjoint_ref), (blades_hbm, blades_ref), *zip(refs[:5], refs[12:17]),
         ))
     ]
     for copy in copies:
         copy.start()
     row, side, place = (lax.axis_index(name) for name in AXES)
+    copies[4].wait()
+    face = jnp.maximum(row - 1, 0)
+    component, mode, sine = column(lanes((pitch, pitch)))
+    number = mode_number(mode, [picked(blades_ref[...], face + n) for n in range(2)])
+    cos_table, sin_table = waves(number * (place * pitch + rows((pitch, pitch))), length)
+    table = jnp.where(component < components, jnp.where(sine, sin_table, cos_table), 0.0)
+    for c in range(components):
+        for n, value in enumerate(split(jnp.where(component == c, table, 0.0))):
+            table_ref[n, pl.ds(c * pitch, pitch), :] = value
     copies[0].wait()
     copies[1].wait()
     diag = damping_ref[...]
@@ -124,53 +159,34 @@
     for c in range(components):
         coef_ref[c, :, :span] = source_ref[c] * inverse
     copies[3].wait()
-
-    fields = 2 * components + 6
-    for f in range(fields):
-        ref, at = (adjoint_ref, f) if f < components else (coef_ref, f - components)
-        edges_ref[f] = to_edges([ref[at, a, :span] for a in range(axial)], pitch)
-    last = inv_ref[:span]
-    edges_ref[fields] = jnp.where(
-        lanes(last.shape) >= (axial - 1) * SEGMENT_LANES,
-        to_edges([jnp.zeros_like(last)] * (axial - 1) + [last], pitch), 0.0,
-    )
     edge_row = pl.multiple_of(jnp.where(side == 0, span - EDGE, 0), EDGE)
-    near, far = slots(fields + 1, components)
-    lane = lanes((span, pitch)) % SEGMENT_LANES
-    sides = []
-    for near_at, far_at in ((3 * EDGE - HALF, 3 * EDGE - HALF - 1), (EDGE, EDGE + HALF)):
-        packed = [jnp.zeros((span, pitch), jnp.float32) for _ in range(groups)]
-        for f, (g, to) in enumerate(near):
-            value = pltpu.roll(edges_ref[f], (to - near_at) % pitch, 1)
-            packed[g] = jnp.where((lane >= to) & (lane < to + HALF), value, packed[g])
-        for f, (g, to) in enumerate(far):
-            packed[g] = jnp.where(lane == to, pltpu.roll(edges_ref[f], (to - far_at) % pitch, 1), packed[g])
-        sides.append(packed)
-    even = lax.rem(place, 2) == 0
-    for g in range(groups):
-        for n, (out_ref, value) in enumerate((
-            (inner_ref, jnp.where(even, sides[0][g], sides[1][g])), (outer_ref, jnp.where(even, sides[1][g], sides[0][g])),
-        )):
+    blocks = edge_blocks(state_ref, coef_ref, inv_ref, pl.ds(edge_row, EDGE))
+    for n, packed in enumerate(packed_edges(blocks, place, components)):
+        for g, value in enumerate(packed):
+            small_ref[pl.ds((n * groups + g) * EDGE, EDGE), :] = value
+    modes_ref[:span] = projected([adjoint_ref[c, 0] for c in range(components)], table_ref)
+    small_ref[pl.ds(2 * groups * EDGE, EDGE), :] = modes_ref[pl.ds(edge_row, EDGE), :]
+    for copy in copies[5:]:
+        copy.wait()
+
+
+def pack_kernel(state_ref, coef_ref, inv_ref, edges_ref, span_ref, inner_ref, outer_ref):
+    _, components, axial, wide, pitch = state_ref.shape
+    span = wide - EDGE
+    side, place = lax.axis_index("span"), lax.axis_index("pitch")
+    blocks = edge_blocks(state_ref, coef_ref, inv_ref, pl.ds(0, span))
+    for f, block in enumerate(blocks):
+        edges_ref[f] = block
+    for out_ref, packed in zip((inner_ref, outer_ref), packed_edges(blocks, place, components)):
+        for g, value in enumerate(packed):
             out_ref[pl.ds(g * span, span), :] = value
-            small_ref[pl.ds((n * (groups + 1) + g) * EDGE, EDGE), :] = out_ref[pl.ds(g * span + edge_row, EDGE), :]
-    copies[4].wait()
-    face = jnp.maximum(row - 1, 0)
-    component, mode, sine = column(lanes((pitch, pitch)))
-    number = mode_number(mode, [picked(blades_ref[...], face + n) for n in range(2)])
-    cos_table, sin_table = waves(number * (place * pitch + rows((pitch, pitch))), length)
-    table = jnp.where(component < components, jnp.where(sine, sin_table, cos_table), 0.0)
-    for c in range(components):
-        for n, value in enumerate(split(jnp.where(component == c, table, 0.0))):
-            table_ref[n, pl.ds(c * pitch, pitch), :] = value
-    start = groups * span + (groups + 1) * EDGE
-    inner_ref[pl.ds(start, span), :] = projected([adjoint_ref[c, 0] for c in range(components)], table_ref)
-    small_ref[pl.ds(groups * EDGE, EDGE), :] = inner_ref[pl.ds(start + edge_row, EDGE), :]
-
+
+    edge_row = pl.multiple_of(jnp.where(side == 0, span - EDGE, 0), EDGE)
     to_low, to_high = half_rows(side)
     line = rows((EDGE, pitch))
-    tiles = [(adjoint_ref, c, a) for c in range(components) for a in range(axial)]
-    tiles += [(coef_ref, f, a) for f in range(components + 6) for a in range(axial)]
-    tiles = [ref[f, a, pl.ds(edge_row, EDGE), :] for ref, f, a in tiles] + [inv_ref[pl.ds(edge_row, EDGE), :]]
+    tiles = [state_ref[0, c, a, pl.ds(edge_row, EDGE), :] for c in range(components) for a in range(axial)]
+    tiles += [coef_ref[f, a, pl.ds(edge_row, EDGE), :] for f in range(components + 6) for a in range(axial)]
+    tiles += [inv_ref[pl.ds(edge_row, EDGE), :]]
     pairs = -(-len(tiles) // 2)
     for n in range(pairs):
         value = pltpu.roll(tiles[2 * n], to_low, 0)
@@ -183,8 +199,6 @@
         for k in range(min(EDGE, components * axial - n * EDGE)):
             value = jnp.where(line == k, pltpu.roll(tiles[n * EDGE + k], lax.rem(k + EDGE - fifth, EDGE), 0), value)
         span_ref[pairs + n] = value
-    for copy in copies[5:]:
-        copy.wait()
 
 
 def picked(values, at):
@@ -463,7 +477,7 @@
 ):
     span, pitch = part_ref.shape
     components, axial = coef_ref.shape[0] - 6, coef_ref.shape[1]
-    field = synthesised(modes_a_ref[EDGE:] + modes_b_ref[EDGE:], synth_ref, components * pitch)
+    field = synthesised(modes_a_ref[:span] + modes_b_ref[:span], synth_ref, components * pitch)
     delta = [inv_ref[:span] * field[:, c * pitch:(c + 1) * pitch] for c in range(components)]
     for a in range(axial - 2, -1, -1):
         delta = along_axis(jac_ref, coef_ref, delta, a, span)
@@ -479,8 +493,7 @@
     sent_ref[...] = more_ref[...]
     components, axial = state_ref.shape[1], state_ref.shape[2]
     wide, pitch = state_ref.shape[3:]
-    modes = modes_a_ref[...] + modes_b_ref[...]
-    field = synthesised(jnp.concatenate([modes[EDGE:], modes[:EDGE]], 0), synth_ref, synth_ref.shape[1])
+    field = synthesised(modes_a_ref[...] + modes_b_ref[...], synth_ref, synth_ref.shape[1])
     delta = [inv_ref[...] * field[:, c * pitch:(c + 1) * pitch] for c in range(components)]
     for t in range(1, axial + 1):
         for c in range(components):
@@ -612,13 +625,13 @@
     blades = blades.reshape(1, -1)
     corner_rows = groups * EDGE
     state_shape = struct(axial + 2, components, axial, wide, pitch)
-    state, coef, inv, edges, span_out, small, inner, outer, table, blades, *tables = call(
-        pack_kernel, "pack",
+    state, coef, inv, small, modes, table, blades, *tables = call(
+        start_kernel, "start",
         (
             state_shape, struct(components + 6, axial, wide, pitch), struct(wide, pitch),
-            struct(fields + 1, span, pitch), struct(span_tiles, EDGE, pitch), struct(2 * corner_rows + EDGE, pitch),
-            struct(groups * span + corner_rows + EDGE + span, pitch), struct(groups * span + corner_rows, pitch),
-            jax.ShapeDtypeStruct((2, components * pitch, pitch), jnp.bfloat16), *(jax.ShapeDtypeStruct(x.shape, x.dtype) for x in (blades, *tables)),
+            struct(2 * corner_rows + EDGE, pitch), struct(wide, pitch),
+            jax.ShapeDtypeStruct((2, components * pitch, pitch), jnp.bfloat16),
+            *(jax.ShapeDtypeStruct(x.shape, x.dtype) for x in (blades, *tables)),
         ),
         [(hbm, in_hbm(x)) for x in (adjoint_start, source, couplings, damping, blades, *tables)],
         scratch=[
@@ -627,6 +640,14 @@
         ],
         groups=groups, length=length,
     )
+    edges, span_out, inner, outer = call(
+        pack_kernel, "pack",
+        (
+            struct(fields + 1, span, pitch), struct(span_tiles, EDGE, pitch), struct(groups * wide, pitch),
+            struct(groups * wide, pitch),
+        ),
+        [(vmem, x) for x in (state, coef, inv)],
+    )
     steps = [1 << n for n in range(place_count.bit_length() - 2)]
     last_step = place_count // 2
 
@@ -636,20 +657,8 @@
     def far(x):
         return moved(x, lambda r, s, p: (r - 1, s, p ^ last_step))
 
-    small = moved(small, lambda r, s, p: (r, 1 - s, p))
+    small, edges = lax.optimization_barrier((moved(small, lambda r, s, p: (r, 1 - s, p)), edges))
     from_span = moved(span_out, lambda r, s, p: (r, 1 - s, p))
-    inner = lax.dynamic_update_slice(inner, small[:corner_rows + EDGE], (groups * span, 0))
-    outer = lax.dynamic_update_slice(outer, small[corner_rows + EDGE:], (groups * span, 0))
-    modes = inner[groups * span + corner_rows:]
-    outer = moved(outer, lambda r, s, p: (r, s, (p - 1 + 2 * (p % 2)) % place_count))
-    inner = moved(inner, lambda r, s, p: (r, s, p ^ 1))
-
-    modes = modes + inner[groups * span + corner_rows:] if steps else modes
-    for step in steps[1:]:
-        modes = modes + moved(modes, lambda r, s, p: (r, s, p ^ step))
-    modes_b = far(modes)
-    modes_a = near(modes)
-
     synth, jac = call(
         synth_kernel, "synth",
         (
@@ -663,6 +672,19 @@
         row_count=row_count, place_count=place_count, components=components, pitch=pitch, length=length, axial=axial,
     )
     edge_shape = struct(axial + 1, components, wide, pitch)
+    modes = lax.dynamic_update_slice(modes, small[2 * corner_rows:], (span, 0))
+    for n, step in enumerate(steps):
+        got = moved(modes, lambda r, s, p: (r, s, p ^ step))
+        if n == 0:
+            got, jac, inner, outer = lax.optimization_barrier((got, jac, inner, outer))
+        modes = modes + got
+    modes_b = far(modes)
+    modes_a = near(modes)
+    inner = lax.dynamic_update_slice(inner, small[:corner_rows], (groups * span, 0))
+    outer = lax.dynamic_update_slice(outer, small[corner_rows:2 * corner_rows], (groups * span, 0))
+    outer = moved(outer, lambda r, s, p: (r, s, (p - 1 + 2 * (p % 2)) % place_count))
+    inner = moved(inner, lambda r, s, p: (r, s, p ^ 1))
+
     coef, inv, edge_coef, state, edge, more, part = call(
         first_kernel, "first_sweeps",
         (

time: 39.7 us -> 40.7 us (1.025)
  waiting for transfers between devices: 5.24 us -> 6.77 us
    ppermute x9 -> x10, waiting for transfers between devices: 5.24 us -> 6.77 us  [moved(): return lax.ppermute(x, AXES, pairs)]
    ppermute x9 -> x10, starting transfers between devices: 20.4 us -> 20 us  [moved(): return lax.ppermute(x, AXES, pairs)]
    pallas_call x7 -> x8, Pallas kernels: 13.7 us -> 13.6 us  [call(): pl.pallas_call(functools.partial(kernel, **fixed), out_shape=outs, in_spe...]
  transfers between devices with their start and end apart: 9 -> 10, of which waited for: 3 -> 3; matrix products, arithmetic and copies ran while one was open for 0% -> 0% of each run, Pallas kernels for 18% -> 19%
where the time goes in v11:
time: 40.7 us; the launch traced here: 40.5 us
  starting transfers between devices  20 us (49%)
  Pallas kernels  13.6 us (33%)
  waiting for transfers between devices  6.77 us (17%)
    ppermute x10, starting transfers between devices, moved(): return lax.ppermute(x, AXES, pairs)  20 us
    pallas_call x8, Pallas kernels, call(): pl.pallas_call(functools.partial(kernel, **fixed), out_shape=outs, in_spe...  13.6 us
    ppermute x10, waiting for transfers between devices, moved(): return lax.ppermute(x, AXES, pairs)  6.77 us
  transfers between devices with their start and end apart: 10, of which 3 were waited for; matrix products, arithmetic and copies ran while one was open for 0% of the time, Pallas kernels for 19%

profile of v11, /device:TPU:1, one launch (start us, length us, event | category | flops | bytes accessed | tf_op | source)
XLA Modules:
  0.0 40.5 jit_solution(7131217342447928755)
XLA Ops:
  0.0 1.7 %start.1 = (f32[6,5,4,40,128]{4,3,2,1,0:T(8,128)S(1)}, f32[11,4,40,128]{3,2,1,0:T(8,128)S(1)}, f32[40,128]{1,0:T(8,128)S(1)}, f32[56,128]{1,0:T(8,128)S(1)}, f32...) custom-call(f32[5,4,32,128]{3,2,1,0:T(8,128)} %adjoint_hbm.1, ...), custom_call_target="tpu_custom_call" | custom-call | tf_op jit(solution)/shard_map/start/pallas_call | solution.py:610
  1.7 2.1 %collective-permute-start = (f32[56,128]{1,0:T(8,128)S(1)}, f32[56,128]{1,0:T(8,128)S(1)}, u32[]{:S(2)}, u32[]{:S(2)}) collective-permute-start(f32[56,128]{1,0:T(8,128)S(1)} %get-tuple-element.43), channel_id=1, source_target_pairs={{0,4},{1,5},{2,6},{3,7},{4,0},{5,1},{6,2},{7,3},{8,12},{9,13},{10,... | collective-permute-start | bytes 86024 | tf_op jit(solution)/shard_map/ppermute | solution.py:580
  3.9 0.8 %pack.1 = (f32[17,32,128]{2,1,0:T(8,128)S(1)}, f32[36,8,128]{2,1,0:T(8,128)S(1)}, f32[120,128]{1,0:T(8,128)S(1)}, f32[120,128]{1,0:T(8,128)S(1)}) custom-call(f32[6,5,4,40,128]{4,3,2,1,0:T(8,128)S(1)} %get-tuple-element.44.state_ref.state_in_ref, f32[11,4,40,128]{3,2,1,0:T(8,128)S(1)} %get-tuple-element.45.coef_ref.coef_in_ref, ...), custom_call_target="tpu_custom_call" | custom-call | tf_op jit(solution)/shard_map/pack/pallas_call | solution.py:610
  4.6 0.5 %collective-permute-done = f32[56,128]{1,0:T(8,128)S(1)} collective-permute-done((f32[56,128]{1,0:T(8,128)S(1)}, f32[56,128]{1,0:T(8,128)S(1)}, u32[]{:S(2)}, u32[]{:S(2)}) %collective-permute-start) | collective-permute-done | bytes 28704 | tf_op jit(solution)/shard_map/ppermute | solution.py:580
  5.1 1.5 %collective-permute-start.1 = (f32[40,128]{1,0:T(8,128)S(1)}, f32[40,128]{1,0:T(8,128)S(1)}, u32[]{:S(2)}, u32[]{:S(2)}) collective-permute-start(f32[40,128]{1,0:T(8,128)S(1)} %slice_dynamic-update-slice_fusion.2), channel_id=1, source_target_pairs={{0,1},{1,0},{2,3},{3,2},{4,5},{5,4},{6,7},{7,6},{8,9},{9,8},{10,11... | collective-permute-start | bytes 61448 | tf_op jit(solution)/shard_map/ppermute | solution.py:580
  6.6 1.2 %collective-permute-start.2 = (f32[36,8,128]{2,1,0:T(8,128)S(1)}, f32[36,8,128]{2,1,0:T(8,128)S(1)}, u32[]{:S(2)}, u32[]{:S(2)}) collective-permute-start(f32[36,8,128]{2,1,0:T(8,128)S(1)} %get-tuple-element.60), channel_id=1, source_target_pairs={{0,4},{1,5},{2,6},{3,7},{4,0},{5,1},{6,2},{7,3},{8,12},{9,13},{10,... | collective-permute-start | bytes 442376 | tf_op jit(solution)/shard_map/ppermute | solution.py:580
  7.9 0.6 %synth.1 = (bf16[2,896,128]{2,1,0:T(8,128)(2,1)S(1)}, f32[152,128]{1,0:T(8,128)S(1)}) custom-call(s32[1,4]{1,0:T(1,128)S(1)} %get-tuple-element.49.blades_ref, f32[5,5,1,6]{3,2,1,0:T(1,128)S(1)} %get-tuple-element.50.jacobians_ref, f32[5,5,3,64]{3,2,1,0:T(4,128)S(1)} %get-tuple-element.51.giles_re_ref, f32[5,5,3,64]{3,2,1,0:T(4,128)S(1)} %get-tuple-element.52.giles_im_ref, ...), custom_call_target="tpu_custom_call" | custom-call | tf_op jit(solution)/shard_map/synth/pallas_call | solution.py:610
  8.5 0.0 collective-permute-done.1
  8.5 2.8 %collective-permute-start.4 = (f32[120,128]{1,0:T(8,128)S(1)}, f32[120,128]{1,0:T(8,128)S(1)}, u32[]{:S(2)}, u32[]{:S(2)}) collective-permute-start(f32[120,128]{1,0:T(8,128)S(1)} %get-tuple-element.79), channel_id=1, source_target_pairs={{0,3},{1,2},{2,1},{3,0},{4,7},{5,6},{6,5},{7,4},{8,11},{9,10},{10,... | collective-permute-start | bytes 184328 | tf_op jit(solution)/shard_map/ppermute | solution.py:580
  11.3 0.0 collective-permute-start.3
  11.3 5.6 %collective-permute-start.6 = (f32[40,128]{1,0:T(8,128)S(1)}, f32[40,128]{1,0:T(8,128)S(1)}, u32[]{:S(2)}, u32[]{:S(2)}) collective-permute-start(f32[40,128]{1,0:T(8,128)S(1)} %add.6), channel_id=1, source_target_pairs={{8,2},{9,3},{10,0},{11,1},{12,6},{13,7},{14,4},{15,5},{16,10},{17,... | collective-permute-start | bytes 61448 | tf_op jit(solution)/shard_map/ppermute | solution.py:580
  16.9 1.9 %collective-permute-start.5 = (f32[40,128]{1,0:T(8,128)S(1)}, f32[40,128]{1,0:T(8,128)S(1)}, u32[]{:S(2)}, u32[]{:S(2)}) collective-permute-start(f32[40,128]{1,0:T(8,128)S(1)} %add.6), channel_id=1, source_target_pairs={{8,0},{9,1},{10,2},{11,3},{12,4},{13,5},{14,6},{15,7},{16,8},{17,9... | collective-permute-start | bytes 61448 | tf_op jit(solution)/shard_map/ppermute | solution.py:580
  18.8 0.0 collective-permute-done.4.outer_ref
  18.8 0.0 collective-permute-done.3.inner_ref
  18.8 0.0 collective-permute-done.2.span_ref
  18.9 4.1 %first_sweeps.1 = (f32[11,4,40,128]{3,2,1,0:T(8,128)S(1)}, f32[40,128]{1,0:T(8,128)S(1)}, f32[12,40,128]{2,1,0:T(8,128)S(1)}, f32[6,5,4,40,128]{4,3,2,1,0:T(8,12...) custom-call(f32[152,128]{1,0:T(8,128)S(1)} %get-tuple-element.58.jac, ...), custom_call_target="tpu_custom_call", output_to_operand_aliasing={{3}: (1, {}), {0}: (2, {}), {1}: (3, {})} | custom-call | tf_op jit(solution)/shard_map/first_sweeps/pallas_call | solution.py:610
  22.9 0.0 collective-permute-done.6.modes_b_ref
  23.0 0.0 collective-permute-done.5.modes_a_ref
  23.0 0.6 %late_modes.1.more_ref = f32[136,128]{1,0:T(8,128)S(1)} custom-call(f32[152,128]{1,0:T(8,128)S(1)} %get-tuple-element.58.jac_ref, f32[11,4,40,128]{3,2,1,0:T(8,128)S(1)} %get-tuple-element.64.coef_ref, f32[40,128]{1,0:T(8,128)S(1)} %get-tuple-element.65.inv_ref, f32[32,128]{1,0:T(8,128)S(1)} %get-tuple-element.71.part_ref, ...), custom_call_target="tpu_custom_call" | custom-call | tf_op jit(solution)/shard_map/late_modes/pallas_call | solution.py:610
  23.6 0.7 %collective-permute-start.7 = (f32[136,128]{1,0:T(8,128)S(1)}, f32[136,128]{1,0:T(8,128)S(1)}, u32[]{:S(2)}, u32[]{:S(2)}) collective-permute-start(f32[136,128]{1,0:T(8,128)S(1)} %late_modes.1.more_ref), channel_id=1, source_target_pairs={{0,1},{1,0},{2,3},{3,2},{4,5},{5,4},{6,7},{7,6},{8,9},{9,8},{10,11... | collective-permute-start | bytes 208904 | tf_op jit(solution)/shard_map/ppermute | solution.py:580
  24.3 1.7 %between_sweeps.1 = (f32[6,5,4,40,128]{4,3,2,1,0:T(8,128)S(1)}, f32[5,5,40,128]{3,2,1,0:T(8,128)S(1)}, f32[136,128]{1,0:T(8,128)S(1)}) custom-call(f32[152,128]{1,0:T(8,128)S(1)} %get-tuple-element.58.jac_ref, f32[11,4,40,128]{3,2,1,0:T(8,128)S(1)} %get-tuple-element.64.coef_ref, ...), custom_call_target="tpu_custom_call", output_to_operand_aliasing={{0}: (4, {}), {1}: (5, {})} | custom-call | tf_op jit(solution)/shard_map/between_sweeps/pallas_call | solution.py:610
  26.0 1.6 %collective-permute-done.7 = f32[136,128]{1,0:T(8,128)S(1)} collective-permute-done((f32[136,128]{1,0:T(8,128)S(1)}, f32[136,128]{1,0:T(8,128)S(1)}, u32[]{:S(2)}, u32[]{:S(2)}) %collective-permute-start.7) | collective-permute-done | bytes 69664 | tf_op jit(solution)/shard_map/ppermute | solution.py:580
  27.6 2.2 %collective-permute-start.9 = (f32[136,128]{1,0:T(8,128)S(1)}, f32[136,128]{1,0:T(8,128)S(1)}, u32[]{:S(2)}, u32[]{:S(2)}) collective-permute-start(f32[136,128]{1,0:T(8,128)S(1)} %add.7), channel_id=1, source_target_pairs={{8,2},{9,3},{10,0},{11,1},{12,6},{13,7},{14,4},{15,5},{16,10},{17,... | collective-permute-start | bytes 208904 | tf_op jit(solution)/shard_map/ppermute | solution.py:580
  29.8 1.9 %collective-permute-start.8 = (f32[136,128]{1,0:T(8,128)S(1)}, f32[136,128]{1,0:T(8,128)S(1)}, u32[]{:S(2)}, u32[]{:S(2)}) collective-permute-start(f32[136,128]{1,0:T(8,128)S(1)} %add.7), channel_id=1, source_target_pairs={{8,0},{9,1},{10,2},{11,3},{12,4},{13,5},{14,6},{15,7},{16,8},{17,9... | collective-permute-start | bytes 208904 | tf_op jit(solution)/shard_map/ppermute | solution.py:580
  31.7 0.7 %beside_sweeps.1 = (f32[6,5,4,40,128]{4,3,2,1,0:T(8,128)S(1)}, f32[5,5,40,128]{3,2,1,0:T(8,128)S(1)}) custom-call(f32[152,128]{1,0:T(8,128)S(1)} %get-tuple-element.58.jac_ref, f32[11,4,40,128]{3,2,1,0:T(8,128)S(1)} %get-tuple-element.64.coef_ref, f32[12,40,128]{2,1,0:T(8,128)S(1)} %get-tuple-element.66.edge_coef_ref, ...), custom_call_target="tpu_custom_call", output_to_operand_aliasing={{0}: (3, {}), {1}: (4, {})} | custom-call | tf_op jit(solution)/shard_map/beside_sweeps/pallas_call | solution.py:610
  32.4 4.7 %collective-permute-done.9.more_b_ref = f32[136,128]{1,0:T(8,128)S(1)} collective-permute-done((f32[136,128]{1,0:T(8,128)S(1)}, f32[136,128]{1,0:T(8,128)S(1)}, u32[]{:S(2)}, u32[]{:S(2)}) %collective-permute-start.9) | collective-permute-done | bytes 69664 | tf_op jit(solution)/shard_map/ppermute | solution.py:580
  37.1 0.0 collective-permute-done.8.more_a_ref
  37.1 3.4 %second_sweeps.1 = (f32[6,5,4,40,128]{4,3,2,1,0:T(8,128)S(1)}, f32[5,5,40,128]{3,2,1,0:T(8,128)S(1)}, f32[5,4,32,128]{3,2,1,0:T(8,128)}) custom-call(f32[152,128]{1,0:T(8,128)S(1)} %get-tuple-element.58.jac_ref, f32[11,4,40,128]{3,2,1,0:T(8,128)S(1)} %get-tuple-element.64.coef_ref, ...), custom_call_target="tpu_custom_call", output_to_operand_aliasing={{0}: (4, {}), {1}: (5, {})} | custom-call | tf_op jit(solution)/shard_map/second_sweeps/pallas_call | solution.py:610
  (4 shorter events, 0.0 us)
Async XLA Ops:
  1.7 3.4 %collective-permute-start = (f32[56,128]{1,0:T(8,128)S(1)}, f32[56,128]{1,0:T(8,128)S(1)}, u32[]{:S(2)}, u32[]{:S(2)}) collective-permute-start(f32[56,128]{1,0:T(8,128)S(1)} %get-tuple-element.43), channel_id=1, source_target_pairs={{0,4},{1,5},{2,6},{3,7},{4,0},{5,1},{6,2},{7,3},{8,12},{9,13},{10,... | collective-permute-start | bytes 86024 | tf_op jit(solution)/shard_map/ppermute | solution.py:580
  5.1 3.4 %collective-permute-start.1 = (f32[40,128]{1,0:T(8,128)S(1)}, f32[40,128]{1,0:T(8,128)S(1)}, u32[]{:S(2)}, u32[]{:S(2)}) collective-permute-start(f32[40,128]{1,0:T(8,128)S(1)} %slice_dynamic-update-slice_fusion.2), channel_id=1, source_target_pairs={{0,1},{1,0},{2,3},{3,2},{4,5},{5,4},{6,7},{7,6},{8,9},{9,8},{10,11... | collective-permute-start | bytes 61448 | tf_op jit(solution)/shard_map/ppermute | solution.py:580
  6.6 12.2 %collective-permute-start.2 = (f32[36,8,128]{2,1,0:T(8,128)S(1)}, f32[36,8,128]{2,1,0:T(8,128)S(1)}, u32[]{:S(2)}, u32[]{:S(2)}) collective-permute-start(f32[36,8,128]{2,1,0:T(8,128)S(1)} %get-tuple-element.60), channel_id=1, source_target_pairs={{0,4},{1,5},{2,6},{3,7},{4,0},{5,1},{6,2},{7,3},{8,12},{9,13},{10,... | collective-permute-start | bytes 442376 | tf_op jit(solution)/shard_map/ppermute | solution.py:580
  8.5 10.3 %collective-permute-start.4 = (f32[120,128]{1,0:T(8,128)S(1)}, f32[120,128]{1,0:T(8,128)S(1)}, u32[]{:S(2)}, u32[]{:S(2)}) collective-permute-start(f32[120,128]{1,0:T(8,128)S(1)} %get-tuple-element.79), channel_id=1, source_target_pairs={{0,3},{1,2},{2,1},{3,0},{4,7},{5,6},{6,5},{7,4},{8,11},{9,10},{10,... | collective-permute-start | bytes 184328 | tf_op jit(solution)/shard_map/ppermute | solution.py:580
  11.3 7.5 %collective-permute-start.3 = (f32[120,128]{1,0:T(8,128)S(1)}, f32[120,128]{1,0:T(8,128)S(1)}, u32[]{:S(2)}, u32[]{:S(2)}) collective-permute-start(f32[120,128]{1,0:T(8,128)S(1)} %get-tuple-element.80), channel_id=1, source_target_pairs={{0,1},{1,0},{2,3},{3,2},{4,5},{5,4},{6,7},{7,6},{8,9},{9,8},{10,11... | collective-permute-start | bytes 184328 | tf_op jit(solution)/shard_map/ppermute | solution.py:580
  11.3 11.6 %collective-permute-start.6 = (f32[40,128]{1,0:T(8,128)S(1)}, f32[40,128]{1,0:T(8,128)S(1)}, u32[]{:S(2)}, u32[]{:S(2)}) collective-permute-start(f32[40,128]{1,0:T(8,128)S(1)} %add.6), channel_id=1, source_target_pairs={{8,2},{9,3},{10,0},{11,1},{12,6},{13,7},{14,4},{15,5},{16,10},{17,... | collective-permute-start | bytes 61448 | tf_op jit(solution)/shard_map/ppermute | solution.py:580
  16.9 6.1 %collective-permute-start.5 = (f32[40,128]{1,0:T(8,128)S(1)}, f32[40,128]{1,0:T(8,128)S(1)}, u32[]{:S(2)}, u32[]{:S(2)}) collective-permute-start(f32[40,128]{1,0:T(8,128)S(1)} %add.6), channel_id=1, source_target_pairs={{8,0},{9,1},{10,2},{11,3},{12,4},{13,5},{14,6},{15,7},{16,8},{17,9... | collective-permute-start | bytes 61448 | tf_op jit(solution)/shard_map/ppermute | solution.py:580
  23.6 4.0 %collective-permute-start.7 = (f32[136,128]{1,0:T(8,128)S(1)}, f32[136,128]{1,0:T(8,128)S(1)}, u32[]{:S(2)}, u32[]{:S(2)}) collective-permute-start(f32[136,128]{1,0:T(8,128)S(1)} %late_modes.1.more_ref), channel_id=1, source_target_pairs={{0,1},{1,0},{2,3},{3,2},{4,5},{5,4},{6,7},{7,6},{8,9},{9,8},{10,11... | collective-permute-start | bytes 208904 | tf_op jit(solution)/shard_map/ppermute | solution.py:580
  27.6 9.6 %collective-permute-start.9 = (f32[136,128]{1,0:T(8,128)S(1)}, f32[136,128]{1,0:T(8,128)S(1)}, u32[]{:S(2)}, u32[]{:S(2)}) collective-permute-start(f32[136,128]{1,0:T(8,128)S(1)} %add.7), channel_id=1, source_target_pairs={{8,2},{9,3},{10,0},{11,1},{12,6},{13,7},{14,4},{15,5},{16,10},{17,... | collective-permute-start | bytes 208904 | tf_op jit(solution)/shard_map/ppermute | solution.py:580
  29.8 7.4 %collective-permute-start.8 = (f32[136,128]{1,0:T(8,128)S(1)}, f32[136,128]{1,0:T(8,128)S(1)}, u32[]{:S(2)}, u32[]{:S(2)}) collective-permute-start(f32[136,128]{1,0:T(8,128)S(1)} %add.7), channel_id=1, source_target_pairs={{8,0},{9,1},{10,2},{11,3},{12,4},{13,5},{14,6},{15,7},{16,8},{17,9... | collective-permute-start | bytes 208904 | tf_op jit(solution)/shard_map/ppermute | solution.py:580

commit v12 on v11

--- a/solution.py
+++ b/solution.py
@@ -123,15 +123,15 @@
 def start_kernel(
     adjoint_hbm, source_hbm, couplings_hbm, damping_hbm, blades_hbm, *refs, groups, length,
 ):
-    state_ref, coef_ref, inv_ref, small_ref, modes_ref, table_ref, blades_ref = refs[5:12]
-    source_ref, couplings_ref, damping_ref, sems = refs[17:]
+    state_ref, coef_ref, inv_ref, span_ref, small_ref, modes_ref, table_ref, blades_ref = refs[5:13]
+    source_ref, couplings_ref, damping_ref, sems = refs[18:]
     components, axial, span, pitch = source_ref.shape
     adjoint_ref = state_ref.at[0, :, :, pl.ds(0, span), :]
     copies = [
         pltpu.make_async_copy(src, dst, sems.at[n])
         for n, (src, dst) in enumerate((
             (couplings_hbm, couplings_ref), (damping_hbm, damping_ref), (source_hbm, source_ref),
-            (adjoint_hbm, adjoint_ref), (blades_hbm, blades_ref), *zip(refs[:5], refs[12:17]),
+            (adjoint_hbm, adjoint_ref), (blades_hbm, blades_ref), *zip(refs[:5], refs[13:18]),
         ))
     ]
     for copy in copies:
@@ -163,25 +163,10 @@
     blocks = edge_blocks(state_ref, coef_ref, inv_ref, pl.ds(edge_row, EDGE))
     for n, packed in enumerate(packed_edges(blocks, place, components)):
         for g, value in enumerate(packed):
-            small_ref[pl.ds((n * groups + g) * EDGE, EDGE), :] = value
-    modes_ref[:span] = projected([adjoint_ref[c, 0] for c in range(components)], table_ref)
-    small_ref[pl.ds(2 * groups * EDGE, EDGE), :] = modes_ref[pl.ds(edge_row, EDGE), :]
-    for copy in copies[5:]:
-        copy.wait()
-
-
-def pack_kernel(state_ref, coef_ref, inv_ref, edges_ref, span_ref, inner_ref, outer_ref):
-    _, components, axial, wide, pitch = state_ref.shape
-    span = wide - EDGE
-    side, place = lax.axis_index("span"), lax.axis_index("pitch")
-    blocks = edge_blocks(state_ref, coef_ref, inv_ref, pl.ds(0, span))
-    for f, block in enumerate(blocks):
-        edges_ref[f] = block
-    for out_ref, packed in zip((inner_ref, outer_ref), packed_edges(blocks, place, components)):
-        for g, value in enumerate(packed):
-            out_ref[pl.ds(g * span, span), :] = value
-
-    edge_row = pl.multiple_of(jnp.where(side == 0, span - EDGE, 0), EDGE)
+            small_ref[pl.ds((n * (groups + 1) + g) * EDGE, EDGE), :] = value
+    modes_ref[...] = projected([adjoint_ref[c, 0] for c in range(components)], table_ref)
+    small_ref[pl.ds(groups * EDGE, EDGE), :] = modes_ref[pl.ds(edge_row, EDGE), :]
+
     to_low, to_high = half_rows(side)
     line = rows((EDGE, pitch))
     tiles = [state_ref[0, c, a, pl.ds(edge_row, EDGE), :] for c in range(components) for a in range(axial)]
@@ -199,6 +184,22 @@
         for k in range(min(EDGE, components * axial - n * EDGE)):
             value = jnp.where(line == k, pltpu.roll(tiles[n * EDGE + k], lax.rem(k + EDGE - fifth, EDGE), 0), value)
         span_ref[pairs + n] = value
+    for copy in copies[5:]:
+        copy.wait()
+
+
+def pack_kernel(state_ref, coef_ref, inv_ref, modes_ref, edges_ref, inner_ref, outer_ref, *, groups):
+    _, components, axial, wide, pitch = state_ref.shape
+    span = wide - EDGE
+    place = lax.axis_index("pitch")
+    blocks = edge_blocks(state_ref, coef_ref, inv_ref, pl.ds(0, span))
+    for f, block in enumerate(blocks):
+        edges_ref[f] = block
+    for out_ref, packed in zip((inner_ref, outer_ref), packed_edges(blocks, place, components)):
+        for g, value in enumerate(packed):
+            out_ref[pl.ds(g * span, span), :] = value
+    start = groups * span + (groups + 1) * EDGE
+    inner_ref[pl.ds(start, span), :] = modes_ref[...]
 
 
 def picked(values, at):
@@ -473,11 +474,11 @@
 
 
 def late_kernel(
-    jac_ref, coef_ref, inv_ref, part_ref, more_ref, modes_a_ref, modes_b_ref, synth_ref, table_ref, modes_ref,
+    jac_ref, coef_ref, inv_ref, part_ref, more_ref, modes_b_ref, modes_a_ref, synth_ref, table_ref, modes_ref,
 ):
     span, pitch = part_ref.shape
     components, axial = coef_ref.shape[0] - 6, coef_ref.shape[1]
-    field = synthesised(modes_a_ref[:span] + modes_b_ref[:span], synth_ref, components * pitch)
+    field = synthesised(modes_a_ref[EDGE:] + modes_b_ref[EDGE:], synth_ref, components * pitch)
     delta = [inv_ref[:span] * field[:, c * pitch:(c + 1) * pitch] for c in range(components)]
     for a in range(axial - 2, -1, -1):
         delta = along_axis(jac_ref, coef_ref, delta, a, span)
@@ -487,13 +488,14 @@
 
 
 def between_kernel(
-    jac_ref, coef_ref, inv_ref, edge_coef_ref, state_in_ref, edge_in_ref, modes_a_ref, modes_b_ref, synth_ref, more_ref,
+    jac_ref, coef_ref, inv_ref, edge_coef_ref, state_in_ref, edge_in_ref, modes_b_ref, modes_a_ref, synth_ref, more_ref,
     state_ref, edge_ref, sent_ref,
 ):
     sent_ref[...] = more_ref[...]
     components, axial = state_ref.shape[1], state_ref.shape[2]
     wide, pitch = state_ref.shape[3:]
-    field = synthesised(modes_a_ref[...] + modes_b_ref[...], synth_ref, synth_ref.shape[1])
+    modes = modes_a_ref[...] + modes_b_ref[...]
+    field = synthesised(jnp.concatenate([modes[EDGE:], modes[:EDGE]], 0), synth_ref, synth_ref.shape[1])
     delta = [inv_ref[...] * field[:, c * pitch:(c + 1) * pitch] for c in range(components)]
     for t in range(1, axial + 1):
         for c in range(components):
@@ -593,7 +595,7 @@
     assert sum(axial - t for t in range(1, axial)) <= EDGE
     assert components == COMPONENTS and components * WAVES <= pitch
     assert axial == ITERS - 1 and ITERS <= EDGE and axial * SEGMENT_LANES == pitch
-    assert span_count == 2 and place_count > 1 and place_count & (place_count - 1) == 0
+    assert span_count == 2 and place_count > 2 and place_count & (place_count - 1) == 0
     wide = span + EDGE
     fields = 2 * components + 6
     groups = slots(fields + 1, components)[1][-1][0] + 1
@@ -625,11 +627,11 @@
     blades = blades.reshape(1, -1)
     corner_rows = groups * EDGE
     state_shape = struct(axial + 2, components, axial, wide, pitch)
-    state, coef, inv, small, modes, table, blades, *tables = call(
+    state, coef, inv, span_out, small, modes, table, blades, *tables = call(
         start_kernel, "start",
         (
             state_shape, struct(components + 6, axial, wide, pitch), struct(wide, pitch),
-            struct(2 * corner_rows + EDGE, pitch), struct(wide, pitch),
+            struct(span_tiles, EDGE, pitch), struct(2 * corner_rows + EDGE, pitch), struct(span, pitch),
             jax.ShapeDtypeStruct((2, components * pitch, pitch), jnp.bfloat16),
             *(jax.ShapeDtypeStruct(x.shape, x.dtype) for x in (blades, *tables)),
         ),
@@ -640,13 +642,11 @@
         ],
         groups=groups, length=length,
     )
-    edges, span_out, inner, outer = call(
+    edges, inner, outer = call(
         pack_kernel, "pack",
-        (
-            struct(fields + 1, span, pitch), struct(span_tiles, EDGE, pitch), struct(groups * wide, pitch),
-            struct(groups * wide, pitch),
-        ),
-        [(vmem, x) for x in (state, coef, inv)],
+        (struct(fields + 1, span, pitch), struct((groups + 1) * wide, pitch), struct(groups * wide, pitch)),
+        [(vmem, x) for x in (state, coef, inv, modes)],
+        groups=groups,
     )
     steps = [1 << n for n in range(place_count.bit_length() - 2)]
     last_step = place_count // 2
@@ -672,18 +672,16 @@
         row_count=row_count, place_count=place_count, components=components, pitch=pitch, length=length, axial=axial,
     )
     edge_shape = struct(axial + 1, components, wide, pitch)
-    modes = lax.dynamic_update_slice(modes, small[2 * corner_rows:], (span, 0))
-    for n, step in enumerate(steps):
-        got = moved(modes, lambda r, s, p: (r, s, p ^ step))
-        if n == 0:
-            got, jac, inner, outer = lax.optimization_barrier((got, jac, inner, outer))
-        modes = modes + got
+    inner = lax.dynamic_update_slice(inner, small[:corner_rows + EDGE], (groups * span, 0))
+    outer = lax.dynamic_update_slice(outer, small[corner_rows + EDGE:], (groups * span, 0))
+    modes = inner[groups * span + corner_rows:]
+    outer = moved(outer, lambda r, s, p: (r, s, (p - 1 + 2 * (p % 2)) % place_count))
+    inner = moved(inner, lambda r, s, p: (r, s, p ^ 1))
+    modes = modes + inner[groups * span + corner_rows:]
+    for step in steps[1:]:
+        modes = modes + moved(modes, lambda r, s, p: (r, s, p ^ step))
     modes_b = far(modes)
     modes_a = near(modes)
-    inner = lax.dynamic_update_slice(inner, small[:corner_rows], (groups * span, 0))
-    outer = lax.dynamic_update_slice(outer, small[corner_rows:2 * corner_rows], (groups * span, 0))
-    outer = moved(outer, lambda r, s, p: (r, s, (p - 1 + 2 * (p % 2)) % place_count))
-    inner = moved(inner, lambda r, s, p: (r, s, p ^ 1))
 
     coef, inv, edge_coef, state, edge, more, part = call(
         first_kernel, "first_sweeps",
@@ -700,11 +698,11 @@
     more_shape = struct(axial * span + EDGE, pitch)
     more = call(
         late_kernel, "late_modes", more_shape,
-        [(vmem, x) for x in (jac, coef, inv, part, more, modes_a, modes_b, synth, table)],
+        [(vmem, x) for x in (jac, coef, inv, part, more, modes_b, modes_a, synth, table)],
     )
     state, edge, sent = call(
         between_kernel, "between_sweeps", (state_shape, edge_shape, more_shape),
-        [(vmem, x) for x in (jac, coef, inv, edge_coef, state, edge, modes_a, modes_b, synth, more)],
+        [(vmem, x) for x in (jac, coef, inv, edge_coef, state, edge, modes_b, modes_a, synth, more)],
         aliases={4: 0, 5: 1},
     )
     state, edge = call(

time: 40.7 us -> 38.7 us (0.951)
  waiting for transfers between devices: 6.77 us -> 4.49 us
    ppermute x10 -> x9, waiting for transfers between devices: 6.77 us -> 4.49 us  [moved(): return lax.ppermute(x, AXES, pairs)]
    ppermute x10 -> x9, starting transfers between devices: 20 us -> 20.2 us  [moved(): return lax.ppermute(x, AXES, pairs)]
  transfers between devices with their start and end apart: 10 -> 9, of which waited for: 3 -> 3; matrix products, arithmetic and copies ran while one was open for 0% -> 0% of each run, Pallas kernels for 19% -> 21%
where the time goes in v12:
time: 38.7 us; the launch traced here: 38.4 us
  starting transfers between devices  20.2 us (52%)
  Pallas kernels  13.7 us (35%)
  waiting for transfers between devices  4.49 us (12%)
    ppermute x9, starting transfers between devices, moved(): return lax.ppermute(x, AXES, pairs)  20.2 us
    pallas_call x8, Pallas kernels, call(): pl.pallas_call(functools.partial(kernel, **fixed), out_shape=outs, in_spe...  13.7 us
    ppermute x9, waiting for transfers between devices, moved(): return lax.ppermute(x, AXES, pairs)  4.49 us
  transfers between devices with their start and end apart: 9, of which 3 were waited for; matrix products, arithmetic and copies ran while one was open for 0% of the time, Pallas kernels for 21%

profile of v12, /device:TPU:1, one launch (start us, length us, event | category | flops | bytes accessed | tf_op | source)
XLA Modules:
  0.0 38.4 jit_solution(2241071909921444100)
XLA Ops:
  0.0 1.7 %start.1 = (f32[6,5,4,40,128]{4,3,2,1,0:T(8,128)S(1)}, f32[11,4,40,128]{3,2,1,0:T(8,128)S(1)}, f32[40,128]{1,0:T(8,128)S(1)}, f32[36,8,128]{2,1,0:T(8,128)S(1)},...) custom-call(f32[5,4,32,128]{3,2,1,0:T(8,128)} %adjoint_hbm.1, ...), custom_call_target="tpu_custom_call" | custom-call | tf_op jit(solution)/shard_map/start/pallas_call | solution.py:612
  1.7 2.1 %collective-permute-start = (f32[56,128]{1,0:T(8,128)S(1)}, f32[56,128]{1,0:T(8,128)S(1)}, u32[]{:S(2)}, u32[]{:S(2)}) collective-permute-start(f32[56,128]{1,0:T(8,128)S(1)} %get-tuple-element.48), channel_id=1, source_target_pairs={{0,4},{1,5},{2,6},{3,7},{4,0},{5,1},{6,2},{7,3},{8,12},{9,13},{10,... | collective-permute-start | bytes 86024 | tf_op jit(solution)/shard_map/ppermute | solution.py:582
  3.9 0.1 collective-permute-start.1
  3.9 0.8 %pack.1 = (f32[17,32,128]{2,1,0:T(8,128)S(1)}, f32[160,128]{1,0:T(8,128)S(1)}, f32[120,128]{1,0:T(8,128)S(1)}) custom-call(f32[6,5,4,40,128]{4,3,2,1,0:T(8,128)S(1)} %get-tuple-element.45.state_ref.state_in_ref, f32[11,4,40,128]{3,2,1,0:T(8,128)S(1)} %get-tuple-element.46.coef_ref.coef_in_ref, f32[40,128]{1,0:T(8,128)S(1)} %get-tuple-element.47.inv_ref.inv_in_ref, ...), custom_call_target="tpu_custom_call" | custom-call | tf_op jit(solution)/shard_map/pack/pallas_call | solution.py:612
  4.7 0.4 %collective-permute-done = f32[56,128]{1,0:T(8,128)S(1)} collective-permute-done((f32[56,128]{1,0:T(8,128)S(1)}, f32[56,128]{1,0:T(8,128)S(1)}, u32[]{:S(2)}, u32[]{:S(2)}) %collective-permute-start) | collective-permute-done | bytes 28704 | tf_op jit(solution)/shard_map/ppermute | solution.py:582
  5.1 1.5 %collective-permute-start.2 = (f32[160,128]{1,0:T(8,128)S(1)}, f32[160,128]{1,0:T(8,128)S(1)}, u32[]{:S(2)}, u32[]{:S(2)}) collective-permute-start(f32[160,128]{1,0:T(8,128)S(1)} %slice_dynamic-update-slice_fusion), channel_id=1, source_target_pairs={{0,1},{1,0},{2,3},{3,2},{4,5},{5,4},{6,7},{7,6},{8,9},{9,8},{10,11... | collective-permute-start | bytes 245768 | tf_op jit(solution)/shard_map/ppermute | solution.py:582
  6.6 2.2 %collective-permute-start.3 = (f32[120,128]{1,0:T(8,128)S(1)}, f32[120,128]{1,0:T(8,128)S(1)}, u32[]{:S(2)}, u32[]{:S(2)}) collective-permute-start(f32[120,128]{1,0:T(8,128)S(1)} %slice_dynamic-update-slice_fusion.1), channel_id=1, source_target_pairs={{0,3},{1,2},{2,1},{3,0},{4,7},{5,6},{6,5},{7,4},{8,11},{9,10},{10,... | collective-permute-start | bytes 184328 | tf_op jit(solution)/shard_map/ppermute | solution.py:582
  8.8 0.0 collective-permute-done.2.inner_ref
  8.8 4.5 %collective-permute-start.5 = (f32[40,128]{1,0:T(8,128)S(1)}, f32[40,128]{1,0:T(8,128)S(1)}, u32[]{:S(2)}, u32[]{:S(2)}) collective-permute-start(f32[40,128]{1,0:T(8,128)S(1)} %slice_add_fusion), channel_id=1, source_target_pairs={{8,0},{9,1},{10,2},{11,3},{12,4},{13,5},{14,6},{15,7},{16,8},{17,9... | collective-permute-start | bytes 61448 | tf_op jit(solution)/shard_map/ppermute | solution.py:582
  13.3 3.9 %collective-permute-start.4 = (f32[40,128]{1,0:T(8,128)S(1)}, f32[40,128]{1,0:T(8,128)S(1)}, u32[]{:S(2)}, u32[]{:S(2)}) collective-permute-start(f32[40,128]{1,0:T(8,128)S(1)} %slice_add_fusion), channel_id=1, source_target_pairs={{8,2},{9,3},{10,0},{11,1},{12,6},{13,7},{14,4},{15,5},{16,10},{17,... | collective-permute-start | bytes 61448 | tf_op jit(solution)/shard_map/ppermute | solution.py:582
  17.2 0.6 %synth.1 = (bf16[2,896,128]{2,1,0:T(8,128)(2,1)S(1)}, f32[152,128]{1,0:T(8,128)S(1)}) custom-call(s32[1,4]{1,0:T(1,128)S(1)} %get-tuple-element.38.blades_ref, f32[5,5,1,6]{3,2,1,0:T(1,128)S(1)} %get-tuple-element.39.jacobians_ref, f32[5,5,3,64]{3,2,1,0:T(4,128)S(1)} %get-tuple-element.40.giles_re_ref, f32[5,5,3,64]{3,2,1,0:T(4,128)S(1)} %get-tuple-element.41.giles_im_ref, ...), custom_call_target="tpu_custom_call" | custom-call | tf_op jit(solution)/shard_map/synth/pallas_call | solution.py:612
  17.9 0.0 collective-permute-done.3.outer_ref
  17.9 0.0 collective-permute-done.1.span_ref
  17.9 4.1 %first_sweeps.1 = (f32[11,4,40,128]{3,2,1,0:T(8,128)S(1)}, f32[40,128]{1,0:T(8,128)S(1)}, f32[12,40,128]{2,1,0:T(8,128)S(1)}, f32[6,5,4,40,128]{4,3,2,1,0:T(8,12...) custom-call(f32[152,128]{1,0:T(8,128)S(1)} %get-tuple-element.44.jac, ...), custom_call_target="tpu_custom_call", output_to_operand_aliasing={{3}: (1, {}), {0}: (2, {}), {1}: (3, {})} | custom-call | tf_op jit(solution)/shard_map/first_sweeps/pallas_call | solution.py:612
  22.0 0.0 collective-permute-done.5.modes_a_ref
  22.0 0.0 collective-permute-done.4.modes_b_ref
  22.1 0.6 %late_modes.1.more_ref = f32[136,128]{1,0:T(8,128)S(1)} custom-call(f32[152,128]{1,0:T(8,128)S(1)} %get-tuple-element.44.jac_ref, f32[11,4,40,128]{3,2,1,0:T(8,128)S(1)} %get-tuple-element.57.coef_ref, f32[40,128]{1,0:T(8,128)S(1)} %get-tuple-element.58.inv_ref, f32[32,128]{1,0:T(8,128)S(1)} %get-tuple-element.63.part_ref, ...), custom_call_target="tpu_custom_call" | custom-call | tf_op jit(solution)/shard_map/late_modes/pallas_call | solution.py:612
  22.7 1.6 %collective-permute-start.6 = (f32[136,128]{1,0:T(8,128)S(1)}, f32[136,128]{1,0:T(8,128)S(1)}, u32[]{:S(2)}, u32[]{:S(2)}) collective-permute-start(f32[136,128]{1,0:T(8,128)S(1)} %late_modes.1.more_ref), channel_id=1, source_target_pairs={{0,1},{1,0},{2,3},{3,2},{4,5},{5,4},{6,7},{7,6},{8,9},{9,8},{10,11... | collective-permute-start | bytes 208904 | tf_op jit(solution)/shard_map/ppermute | solution.py:582
  24.3 1.7 %between_sweeps.1 = (f32[6,5,4,40,128]{4,3,2,1,0:T(8,128)S(1)}, f32[5,5,40,128]{3,2,1,0:T(8,128)S(1)}, f32[136,128]{1,0:T(8,128)S(1)}) custom-call(f32[152,128]{1,0:T(8,128)S(1)} %get-tuple-element.44.jac_ref, f32[11,4,40,128]{3,2,1,0:T(8,128)S(1)} %get-tuple-element.57.coef_ref, ...), custom_call_target="tpu_custom_call", output_to_operand_aliasing={{0}: (4, {}), {1}: (5, {})} | custom-call | tf_op jit(solution)/shard_map/between_sweeps/pallas_call | solution.py:612
  25.9 0.0 collective-permute-done.6
  26.0 2.4 %collective-permute-start.8 = (f32[136,128]{1,0:T(8,128)S(1)}, f32[136,128]{1,0:T(8,128)S(1)}, u32[]{:S(2)}, u32[]{:S(2)}) collective-permute-start(f32[136,128]{1,0:T(8,128)S(1)} %add.7), channel_id=1, source_target_pairs={{8,2},{9,3},{10,0},{11,1},{12,6},{13,7},{14,4},{15,5},{16,10},{17,... | collective-permute-start | bytes 208904 | tf_op jit(solution)/shard_map/ppermute | solution.py:582
  28.4 1.9 %collective-permute-start.7 = (f32[136,128]{1,0:T(8,128)S(1)}, f32[136,128]{1,0:T(8,128)S(1)}, u32[]{:S(2)}, u32[]{:S(2)}) collective-permute-start(f32[136,128]{1,0:T(8,128)S(1)} %add.7), channel_id=1, source_target_pairs={{8,0},{9,1},{10,2},{11,3},{12,4},{13,5},{14,6},{15,7},{16,8},{17,9... | collective-permute-start | bytes 208904 | tf_op jit(solution)/shard_map/ppermute | solution.py:582
  30.3 0.7 %beside_sweeps.1 = (f32[6,5,4,40,128]{4,3,2,1,0:T(8,128)S(1)}, f32[5,5,40,128]{3,2,1,0:T(8,128)S(1)}) custom-call(f32[152,128]{1,0:T(8,128)S(1)} %get-tuple-element.44.jac_ref, f32[11,4,40,128]{3,2,1,0:T(8,128)S(1)} %get-tuple-element.57.coef_ref, f32[12,40,128]{2,1,0:T(8,128)S(1)} %get-tuple-element.59.edge_coef_ref, ...), custom_call_target="tpu_custom_call", output_to_operand_aliasing={{0}: (3, {}), {1}: (4, {})} | custom-call | tf_op jit(solution)/shard_map/beside_sweeps/pallas_call | solution.py:612
  31.0 2.4 %collective-permute-done.8.more_b_ref = f32[136,128]{1,0:T(8,128)S(1)} collective-permute-done((f32[136,128]{1,0:T(8,128)S(1)}, f32[136,128]{1,0:T(8,128)S(1)}, u32[]{:S(2)}, u32[]{:S(2)}) %collective-permute-start.8) | collective-permute-done | bytes 69664 | tf_op jit(solution)/shard_map/ppermute | solution.py:582
  33.4 1.6 %collective-permute-done.7.more_a_ref = f32[136,128]{1,0:T(8,128)S(1)} collective-permute-done((f32[136,128]{1,0:T(8,128)S(1)}, f32[136,128]{1,0:T(8,128)S(1)}, u32[]{:S(2)}, u32[]{:S(2)}) %collective-permute-start.7) | collective-permute-done | bytes 69664 | tf_op jit(solution)/shard_map/ppermute | solution.py:582
  35.1 3.4 %second_sweeps.1 = (f32[6,5,4,40,128]{4,3,2,1,0:T(8,128)S(1)}, f32[5,5,40,128]{3,2,1,0:T(8,128)S(1)}, f32[5,4,32,128]{3,2,1,0:T(8,128)}) custom-call(f32[152,128]{1,0:T(8,128)S(1)} %get-tuple-element.44.jac_ref, f32[11,4,40,128]{3,2,1,0:T(8,128)S(1)} %get-tuple-element.57.coef_ref, ...), custom_call_target="tpu_custom_call", output_to_operand_aliasing={{0}: (4, {}), {1}: (5, {})} | custom-call | tf_op jit(solution)/shard_map/second_sweeps/pallas_call | solution.py:612
  (4 shorter events, 0.0 us)
Async XLA Ops:
  1.7 3.4 %collective-permute-start = (f32[56,128]{1,0:T(8,128)S(1)}, f32[56,128]{1,0:T(8,128)S(1)}, u32[]{:S(2)}, u32[]{:S(2)}) collective-permute-start(f32[56,128]{1,0:T(8,128)S(1)} %get-tuple-element.48), channel_id=1, source_target_pairs={{0,4},{1,5},{2,6},{3,7},{4,0},{5,1},{6,2},{7,3},{8,12},{9,13},{10,... | collective-permute-start | bytes 86024 | tf_op jit(solution)/shard_map/ppermute | solution.py:582
  3.9 14.0 %collective-permute-start.1 = (f32[36,8,128]{2,1,0:T(8,128)S(1)}, f32[36,8,128]{2,1,0:T(8,128)S(1)}, u32[]{:S(2)}, u32[]{:S(2)}) collective-permute-start(f32[36,8,128]{2,1,0:T(8,128)S(1)} %get-tuple-element.52), channel_id=1, source_target_pairs={{0,4},{1,5},{2,6},{3,7},{4,0},{5,1},{6,2},{7,3},{8,12},{9,13},{10,... | collective-permute-start | bytes 442376 | tf_op jit(solution)/shard_map/ppermute | solution.py:582
  5.1 3.7 %collective-permute-start.2 = (f32[160,128]{1,0:T(8,128)S(1)}, f32[160,128]{1,0:T(8,128)S(1)}, u32[]{:S(2)}, u32[]{:S(2)}) collective-permute-start(f32[160,128]{1,0:T(8,128)S(1)} %slice_dynamic-update-slice_fusion), channel_id=1, source_target_pairs={{0,1},{1,0},{2,3},{3,2},{4,5},{5,4},{6,7},{7,6},{8,9},{9,8},{10,11... | collective-permute-start | bytes 245768 | tf_op jit(solution)/shard_map/ppermute | solution.py:582
  6.6 11.2 %collective-permute-start.3 = (f32[120,128]{1,0:T(8,128)S(1)}, f32[120,128]{1,0:T(8,128)S(1)}, u32[]{:S(2)}, u32[]{:S(2)}) collective-permute-start(f32[120,128]{1,0:T(8,128)S(1)} %slice_dynamic-update-slice_fusion.1), channel_id=1, source_target_pairs={{0,3},{1,2},{2,1},{3,0},{4,7},{5,6},{6,5},{7,4},{8,11},{9,10},{10,... | collective-permute-start | bytes 184328 | tf_op jit(solution)/shard_map/ppermute | solution.py:582
  8.8 13.2 %collective-permute-start.5 = (f32[40,128]{1,0:T(8,128)S(1)}, f32[40,128]{1,0:T(8,128)S(1)}, u32[]{:S(2)}, u32[]{:S(2)}) collective-permute-start(f32[40,128]{1,0:T(8,128)S(1)} %slice_add_fusion), channel_id=1, source_target_pairs={{8,0},{9,1},{10,2},{11,3},{12,4},{13,5},{14,6},{15,7},{16,8},{17,9... | collective-permute-start | bytes 61448 | tf_op jit(solution)/shard_map/ppermute | solution.py:582
  13.3 8.7 %collective-permute-start.4 = (f32[40,128]{1,0:T(8,128)S(1)}, f32[40,128]{1,0:T(8,128)S(1)}, u32[]{:S(2)}, u32[]{:S(2)}) collective-permute-start(f32[40,128]{1,0:T(8,128)S(1)} %slice_add_fusion), channel_id=1, source_target_pairs={{8,2},{9,3},{10,0},{11,1},{12,6},{13,7},{14,4},{15,5},{16,10},{17,... | collective-permute-start | bytes 61448 | tf_op jit(solution)/shard_map/ppermute | solution.py:582
  22.7 3.3 %collective-permute-start.6 = (f32[136,128]{1,0:T(8,128)S(1)}, f32[136,128]{1,0:T(8,128)S(1)}, u32[]{:S(2)}, u32[]{:S(2)}) collective-permute-start(f32[136,128]{1,0:T(8,128)S(1)} %late_modes.1.more_ref), channel_id=1, source_target_pairs={{0,1},{1,0},{2,3},{3,2},{4,5},{5,4},{6,7},{7,6},{8,9},{9,8},{10,11... | collective-permute-start | bytes 208904 | tf_op jit(solution)/shard_map/ppermute | solution.py:582
  26.0 7.4 %collective-permute-start.8 = (f32[136,128]{1,0:T(8,128)S(1)}, f32[136,128]{1,0:T(8,128)S(1)}, u32[]{:S(2)}, u32[]{:S(2)}) collective-permute-start(f32[136,128]{1,0:T(8,128)S(1)} %add.7), channel_id=1, source_target_pairs={{8,2},{9,3},{10,0},{11,1},{12,6},{13,7},{14,4},{15,5},{16,10},{17,... | collective-permute-start | bytes 208904 | tf_op jit(solution)/shard_map/ppermute | solution.py:582
  28.4 6.7 %collective-permute-start.7 = (f32[136,128]{1,0:T(8,128)S(1)}, f32[136,128]{1,0:T(8,128)S(1)}, u32[]{:S(2)}, u32[]{:S(2)}) collective-permute-start(f32[136,128]{1,0:T(8,128)S(1)} %add.7), channel_id=1, source_target_pairs={{8,0},{9,1},{10,2},{11,3},{12,4},{13,5},{14,6},{15,7},{16,8},{17,9... | collective-permute-start | bytes 208904 | tf_op jit(solution)/shard_map/ppermute | solution.py:582

commit v13 on v12

--- a/solution.py
+++ b/solution.py
@@ -164,8 +164,8 @@
     for n, packed in enumerate(packed_edges(blocks, place, components)):
         for g, value in enumerate(packed):
             small_ref[pl.ds((n * (groups + 1) + g) * EDGE, EDGE), :] = value
-    modes_ref[...] = projected([adjoint_ref[c, 0] for c in range(components)], table_ref)
-    small_ref[pl.ds(groups * EDGE, EDGE), :] = modes_ref[pl.ds(edge_row, EDGE), :]
+    modes_ref[:span] = projected([adjoint_ref[c, 0] for c in range(components)], table_ref)
+    modes_ref[span:] = modes_ref[pl.ds(edge_row, EDGE), :]
 
     to_low, to_high = half_rows(side)
     line = rows((EDGE, pitch))
@@ -188,7 +188,7 @@
         copy.wait()
 
 
-def pack_kernel(state_ref, coef_ref, inv_ref, modes_ref, edges_ref, inner_ref, outer_ref, *, groups):
+def pack_kernel(state_ref, coef_ref, inv_ref, edges_ref, inner_ref, outer_ref):
     _, components, axial, wide, pitch = state_ref.shape
     span = wide - EDGE
     place = lax.axis_index("pitch")
@@ -198,8 +198,6 @@
     for out_ref, packed in zip((inner_ref, outer_ref), packed_edges(blocks, place, components)):
         for g, value in enumerate(packed):
             out_ref[pl.ds(g * span, span), :] = value
-    start = groups * span + (groups + 1) * EDGE
-    inner_ref[pl.ds(start, span), :] = modes_ref[...]
 
 
 def picked(values, at):
@@ -631,7 +629,7 @@
         start_kernel, "start",
         (
             state_shape, struct(components + 6, axial, wide, pitch), struct(wide, pitch),
-            struct(span_tiles, EDGE, pitch), struct(2 * corner_rows + EDGE, pitch), struct(span, pitch),
+            struct(span_tiles, EDGE, pitch), struct(2 * corner_rows + EDGE, pitch), struct(wide, pitch),
             jax.ShapeDtypeStruct((2, components * pitch, pitch), jnp.bfloat16),
             *(jax.ShapeDtypeStruct(x.shape, x.dtype) for x in (blades, *tables)),
         ),
@@ -645,8 +643,7 @@
     edges, inner, outer = call(
         pack_kernel, "pack",
         (struct(fields + 1, span, pitch), struct((groups + 1) * wide, pitch), struct(groups * wide, pitch)),
-        [(vmem, x) for x in (state, coef, inv, modes)],
-        groups=groups,
+        [(vmem, x) for x in (state, coef, inv)],
     )
     steps = [1 << n for n in range(place_count.bit_length() - 2)]
     last_step = place_count // 2
@@ -657,8 +654,12 @@
     def far(x):
         return moved(x, lambda r, s, p: (r - 1, s, p ^ last_step))
 
-    small, edges = lax.optimization_barrier((moved(small, lambda r, s, p: (r, 1 - s, p)), edges))
+    modes, edges = lax.optimization_barrier((near(modes), edges))
+    small = lax.dynamic_update_slice(small, modes[span:], (corner_rows, 0))
+    small, span_out = lax.optimization_barrier((small, span_out))
+    small = moved(small, lambda r, s, p: (r, 1 - s, p))
     from_span = moved(span_out, lambda r, s, p: (r, 1 - s, p))
+    inner = lax.dynamic_update_slice(inner, modes[:span], (groups * wide + EDGE, 0))
     synth, jac = call(
         synth_kernel, "synth",
         (
@@ -680,8 +681,7 @@
     modes = modes + inner[groups * span + corner_rows:]
     for step in steps[1:]:
         modes = modes + moved(modes, lambda r, s, p: (r, s, p ^ step))
-    modes_b = far(modes)
-    modes_a = near(modes)
+    modes_a, modes_b = modes, moved(modes, lambda r, s, p: (r, s, p ^ last_step))
 
     coef, inv, edge_coef, state, edge, more, part = call(
         first_kernel, "first_sweeps",

time: 38.7 us -> 39.9 us (1.031)
  waiting for transfers between devices: 4.49 us -> 8.89 us
  starting transfers between devices: 20.2 us -> 17.1 us
    ppermute x9, waiting for transfers between devices: 4.49 us -> 8.89 us  [moved(): return lax.ppermute(x, AXES, pairs)]
    ppermute x9, starting transfers between devices: 20.2 us -> 17.1 us  [moved(): return lax.ppermute(x, AXES, pairs)]
  transfers between devices with their start and end apart: 9 -> 9, of which waited for: 3 -> 6; matrix products, arithmetic and copies ran while one was open for 0% -> 0% of each run, Pallas kernels for 21% -> 20%
where the time goes in v13:
time: 39.9 us; the launch traced here: 39.7 us
  starting transfers between devices  17.1 us (43%)
  Pallas kernels  13.6 us (34%)
  waiting for transfers between devices  8.89 us (22%)
    ppermute x9, starting transfers between devices, moved(): return lax.ppermute(x, AXES, pairs)  17.1 us
    pallas_call x8, Pallas kernels, call(): pl.pallas_call(functools.partial(kernel, **fixed), out_shape=outs, in_spe...  13.6 us
    ppermute x9, waiting for transfers between devices, moved(): return lax.ppermute(x, AXES, pairs)  8.89 us
  transfers between devices with their start and end apart: 9, of which 6 were waited for; matrix products, arithmetic and copies ran while one was open for 0% of the time, Pallas kernels for 20%

profile of v13, /device:TPU:1, one launch (start us, length us, event | category | flops | bytes accessed | tf_op | source)
XLA Modules:
  0.0 39.7 jit_solution(3770962194653405906)
XLA Ops:
  0.0 1.7 %start.1 = (f32[6,5,4,40,128]{4,3,2,1,0:T(8,128)S(1)}, f32[11,4,40,128]{3,2,1,0:T(8,128)S(1)}, f32[40,128]{1,0:T(8,128)S(1)}, f32[36,8,128]{2,1,0:T(8,128)S(1)},...) custom-call(f32[5,4,32,128]{3,2,1,0:T(8,128)} %adjoint_hbm.1, ...), custom_call_target="tpu_custom_call" | custom-call | tf_op jit(solution)/shard_map/start/pallas_call | solution.py:610
  1.7 2.0 %collective-permute-start = (f32[40,128]{1,0:T(8,128)S(1)}, f32[40,128]{1,0:T(8,128)S(1)}, u32[]{:S(2)}, u32[]{:S(2)}) collective-permute-start(f32[40,128]{1,0:T(8,128)S(1)} %get-tuple-element.50), channel_id=1, source_target_pairs={{8,0},{9,1},{10,2},{11,3},{12,4},{13,5},{14,6},{15,7},{16,8},{17,9... | collective-permute-start | bytes 61448 | tf_op jit(solution)/shard_map/ppermute | solution.py:580
  3.7 0.8 %pack.1 = (f32[17,32,128]{2,1,0:T(8,128)S(1)}, f32[160,128]{1,0:T(8,128)S(1)}, f32[120,128]{1,0:T(8,128)S(1)}) custom-call(f32[6,5,4,40,128]{4,3,2,1,0:T(8,128)S(1)} %get-tuple-element.47.state_ref.state_in_ref, f32[11,4,40,128]{3,2,1,0:T(8,128)S(1)} %get-tuple-element.48.coef_ref.coef_in_ref, f32[40,128]{1,0:T(8,128)S(1)} %get-tuple-element.49.inv_ref.inv_in_ref), custom_call_target="tpu_custom_call" | custom-call | tf_op jit(solution)/shard_map/pack/pallas_call | solution.py:610
  4.5 3.2 %collective-permute-done = f32[40,128]{1,0:T(8,128)S(1)} collective-permute-done((f32[40,128]{1,0:T(8,128)S(1)}, f32[40,128]{1,0:T(8,128)S(1)}, u32[]{:S(2)}, u32[]{:S(2)}) %collective-permute-start) | collective-permute-done | bytes 20512 | tf_op jit(solution)/shard_map/ppermute | solution.py:580
  7.7 1.2 %collective-permute-start.2 = (f32[56,128]{1,0:T(8,128)S(1)}, f32[56,128]{1,0:T(8,128)S(1)}, u32[]{:S(2)}, u32[]{:S(2)}) collective-permute-start(f32[56,128]{1,0:T(8,128)S(1)} %slice_dynamic-update-slice_fusion.3), channel_id=1, source_target_pairs={{0,4},{1,5},{2,6},{3,7},{4,0},{5,1},{6,2},{7,3},{8,12},{9,13},{10,... | collective-permute-start | bytes 86024 | tf_op jit(solution)/shard_map/ppermute | solution.py:580
  8.9 0.2 collective-permute-start.1
  9.2 1.3 %collective-permute-done.2 = f32[56,128]{1,0:T(8,128)S(1)} collective-permute-done((f32[56,128]{1,0:T(8,128)S(1)}, f32[56,128]{1,0:T(8,128)S(1)}, u32[]{:S(2)}, u32[]{:S(2)}) %collective-permute-start.2) | collective-permute-done | bytes 28704 | tf_op jit(solution)/shard_map/ppermute | solution.py:580
  10.4 1.3 %collective-permute-start.3 = (f32[160,128]{1,0:T(8,128)S(1)}, f32[160,128]{1,0:T(8,128)S(1)}, u32[]{:S(2)}, u32[]{:S(2)}) collective-permute-start(f32[160,128]{1,0:T(8,128)S(1)} %slice_dynamic-update-slice_fusion), channel_id=1, source_target_pairs={{0,1},{1,0},{2,3},{3,2},{4,5},{5,4},{6,7},{7,6},{8,9},{9,8},{10,11... | collective-permute-start | bytes 245768 | tf_op jit(solution)/shard_map/ppermute | solution.py:580
  11.7 2.2 %collective-permute-start.4 = (f32[120,128]{1,0:T(8,128)S(1)}, f32[120,128]{1,0:T(8,128)S(1)}, u32[]{:S(2)}, u32[]{:S(2)}) collective-permute-start(f32[120,128]{1,0:T(8,128)S(1)} %slice_dynamic-update-slice_fusion.2), channel_id=1, source_target_pairs={{0,3},{1,2},{2,1},{3,0},{4,7},{5,6},{6,5},{7,4},{8,11},{9,10},{10,... | collective-permute-start | bytes 184328 | tf_op jit(solution)/shard_map/ppermute | solution.py:580
  13.9 0.5 %collective-permute-done.3.inner_ref = f32[160,128]{1,0:T(8,128)S(1)} collective-permute-done((f32[160,128]{1,0:T(8,128)S(1)}, f32[160,128]{1,0:T(8,128)S(1)}, u32[]{:S(2)}, u32[]{:S(2)}) %collective-permute-start.3) | collective-permute-done | bytes 81952 | tf_op jit(solution)/shard_map/ppermute | solution.py:580
  14.5 2.5 %collective-permute-start.5 = (f32[40,128]{1,0:T(8,128)S(1)}, f32[40,128]{1,0:T(8,128)S(1)}, u32[]{:S(2)}, u32[]{:S(2)}) collective-permute-start(f32[40,128]{1,0:T(8,128)S(1)} %slice_add_fusion.modes_a_ref), channel_id=1, source_target_pairs={{0,2},{1,3},{2,0},{3,1},{4,6},{5,7},{6,4},{7,5},{8,10},{9,11},{10,... | collective-permute-start | bytes 61448 | tf_op jit(solution)/shard_map/ppermute | solution.py:580
  17.0 0.6 %synth.1 = (bf16[2,896,128]{2,1,0:T(8,128)(2,1)S(1)}, f32[152,128]{1,0:T(8,128)S(1)}) custom-call(s32[1,4]{1,0:T(1,128)S(1)} %get-tuple-element.40.blades_ref, f32[5,5,1,6]{3,2,1,0:T(1,128)S(1)} %get-tuple-element.41.jacobians_ref, f32[5,5,3,64]{3,2,1,0:T(4,128)S(1)} %get-tuple-element.42.giles_re_ref, f32[5,5,3,64]{3,2,1,0:T(4,128)S(1)} %get-tuple-element.43.giles_im_ref, ...), custom_call_target="tpu_custom_call" | custom-call | tf_op jit(solution)/shard_map/synth/pallas_call | solution.py:610
  17.6 0.4 collective-permute-done.4.outer_ref
  18.0 0.0 collective-permute-done.1.span_ref
  18.0 4.1 %first_sweeps.1 = (f32[11,4,40,128]{3,2,1,0:T(8,128)S(1)}, f32[40,128]{1,0:T(8,128)S(1)}, f32[12,40,128]{2,1,0:T(8,128)S(1)}, f32[6,5,4,40,128]{4,3,2,1,0:T(8,12...) custom-call(f32[152,128]{1,0:T(8,128)S(1)} %get-tuple-element.46.jac, ...), custom_call_target="tpu_custom_call", output_to_operand_aliasing={{3}: (1, {}), {0}: (2, {}), {1}: (3, {})} | custom-call | tf_op jit(solution)/shard_map/first_sweeps/pallas_call | solution.py:610
  22.1 0.0 collective-permute-done.5.modes_b_ref
  22.1 0.6 %late_modes.1.more_ref = f32[136,128]{1,0:T(8,128)S(1)} custom-call(f32[152,128]{1,0:T(8,128)S(1)} %get-tuple-element.46.jac_ref, f32[11,4,40,128]{3,2,1,0:T(8,128)S(1)} %get-tuple-element.61.coef_ref, f32[40,128]{1,0:T(8,128)S(1)} %get-tuple-element.62.inv_ref, f32[32,128]{1,0:T(8,128)S(1)} %get-tuple-element.67.part_ref, ...), custom_call_target="tpu_custom_call" | custom-call | tf_op jit(solution)/shard_map/late_modes/pallas_call | solution.py:610
  22.8 1.0 %collective-permute-start.6 = (f32[136,128]{1,0:T(8,128)S(1)}, f32[136,128]{1,0:T(8,128)S(1)}, u32[]{:S(2)}, u32[]{:S(2)}) collective-permute-start(f32[136,128]{1,0:T(8,128)S(1)} %late_modes.1.more_ref), channel_id=1, source_target_pairs={{0,1},{1,0},{2,3},{3,2},{4,5},{5,4},{6,7},{7,6},{8,9},{9,8},{10,11... | collective-permute-start | bytes 208904 | tf_op jit(solution)/shard_map/ppermute | solution.py:580
  23.8 1.7 %between_sweeps.1 = (f32[6,5,4,40,128]{4,3,2,1,0:T(8,128)S(1)}, f32[5,5,40,128]{3,2,1,0:T(8,128)S(1)}, f32[136,128]{1,0:T(8,128)S(1)}) custom-call(f32[152,128]{1,0:T(8,128)S(1)} %get-tuple-element.46.jac_ref, f32[11,4,40,128]{3,2,1,0:T(8,128)S(1)} %get-tuple-element.61.coef_ref, ...), custom_call_target="tpu_custom_call", output_to_operand_aliasing={{0}: (4, {}), {1}: (5, {})} | custom-call | tf_op jit(solution)/shard_map/between_sweeps/pallas_call | solution.py:610
  25.4 0.6 %collective-permute-done.6 = f32[136,128]{1,0:T(8,128)S(1)} collective-permute-done((f32[136,128]{1,0:T(8,128)S(1)}, f32[136,128]{1,0:T(8,128)S(1)}, u32[]{:S(2)}, u32[]{:S(2)}) %collective-permute-start.6) | collective-permute-done | bytes 69664 | tf_op jit(solution)/shard_map/ppermute | solution.py:580
  26.0 4.7 %collective-permute-start.8 = (f32[136,128]{1,0:T(8,128)S(1)}, f32[136,128]{1,0:T(8,128)S(1)}, u32[]{:S(2)}, u32[]{:S(2)}) collective-permute-start(f32[136,128]{1,0:T(8,128)S(1)} %add.7), channel_id=1, source_target_pairs={{8,2},{9,3},{10,0},{11,1},{12,6},{13,7},{14,4},{15,5},{16,10},{17,... | collective-permute-start | bytes 208904 | tf_op jit(solution)/shard_map/ppermute | solution.py:580
  30.7 1.9 %collective-permute-start.7 = (f32[136,128]{1,0:T(8,128)S(1)}, f32[136,128]{1,0:T(8,128)S(1)}, u32[]{:S(2)}, u32[]{:S(2)}) collective-permute-start(f32[136,128]{1,0:T(8,128)S(1)} %add.7), channel_id=1, source_target_pairs={{8,0},{9,1},{10,2},{11,3},{12,4},{13,5},{14,6},{15,7},{16,8},{17,9... | collective-permute-start | bytes 208904 | tf_op jit(solution)/shard_map/ppermute | solution.py:580
  32.7 0.7 %beside_sweeps.1 = (f32[6,5,4,40,128]{4,3,2,1,0:T(8,128)S(1)}, f32[5,5,40,128]{3,2,1,0:T(8,128)S(1)}) custom-call(f32[152,128]{1,0:T(8,128)S(1)} %get-tuple-element.46.jac_ref, f32[11,4,40,128]{3,2,1,0:T(8,128)S(1)} %get-tuple-element.61.coef_ref, f32[12,40,128]{2,1,0:T(8,128)S(1)} %get-tuple-element.63.edge_coef_ref, ...), custom_call_target="tpu_custom_call", output_to_operand_aliasing={{0}: (3, {}), {1}: (4, {})} | custom-call | tf_op jit(solution)/shard_map/beside_sweeps/pallas_call | solution.py:610
  33.4 0.0 collective-permute-done.8.more_b_ref
  33.4 2.9 %collective-permute-done.7.more_a_ref = f32[136,128]{1,0:T(8,128)S(1)} collective-permute-done((f32[136,128]{1,0:T(8,128)S(1)}, f32[136,128]{1,0:T(8,128)S(1)}, u32[]{:S(2)}, u32[]{:S(2)}) %collective-permute-start.7) | collective-permute-done | bytes 69664 | tf_op jit(solution)/shard_map/ppermute | solution.py:580
  36.4 3.4 %second_sweeps.1 = (f32[6,5,4,40,128]{4,3,2,1,0:T(8,128)S(1)}, f32[5,5,40,128]{3,2,1,0:T(8,128)S(1)}, f32[5,4,32,128]{3,2,1,0:T(8,128)}) custom-call(f32[152,128]{1,0:T(8,128)S(1)} %get-tuple-element.46.jac_ref, f32[11,4,40,128]{3,2,1,0:T(8,128)S(1)} %get-tuple-element.61.coef_ref, ...), custom_call_target="tpu_custom_call", output_to_operand_aliasing={{0}: (4, {}), {1}: (5, {})} | custom-call | tf_op jit(solution)/shard_map/second_sweeps/pallas_call | solution.py:610
  (6 shorter events, 0.0 us)
Async XLA Ops:
  1.7 6.0 %collective-permute-start = (f32[40,128]{1,0:T(8,128)S(1)}, f32[40,128]{1,0:T(8,128)S(1)}, u32[]{:S(2)}, u32[]{:S(2)}) collective-permute-start(f32[40,128]{1,0:T(8,128)S(1)} %get-tuple-element.50), channel_id=1, source_target_pairs={{8,0},{9,1},{10,2},{11,3},{12,4},{13,5},{14,6},{15,7},{16,8},{17,9... | collective-permute-start | bytes 61448 | tf_op jit(solution)/shard_map/ppermute | solution.py:580
  7.7 2.7 %collective-permute-start.2 = (f32[56,128]{1,0:T(8,128)S(1)}, f32[56,128]{1,0:T(8,128)S(1)}, u32[]{:S(2)}, u32[]{:S(2)}) collective-permute-start(f32[56,128]{1,0:T(8,128)S(1)} %slice_dynamic-update-slice_fusion.3), channel_id=1, source_target_pairs={{0,4},{1,5},{2,6},{3,7},{4,0},{5,1},{6,2},{7,3},{8,12},{9,13},{10,... | collective-permute-start | bytes 86024 | tf_op jit(solution)/shard_map/ppermute | solution.py:580
  8.9 9.1 %collective-permute-start.1 = (f32[36,8,128]{2,1,0:T(8,128)S(1)}, f32[36,8,128]{2,1,0:T(8,128)S(1)}, u32[]{:S(2)}, u32[]{:S(2)}) collective-permute-start(f32[36,8,128]{2,1,0:T(8,128)S(1)} %get-tuple-element.56), channel_id=1, source_target_pairs={{0,4},{1,5},{2,6},{3,7},{4,0},{5,1},{6,2},{7,3},{8,12},{9,13},{10,... | collective-permute-start | bytes 442376 | tf_op jit(solution)/shard_map/ppermute | solution.py:580
  10.4 4.0 %collective-permute-start.3 = (f32[160,128]{1,0:T(8,128)S(1)}, f32[160,128]{1,0:T(8,128)S(1)}, u32[]{:S(2)}, u32[]{:S(2)}) collective-permute-start(f32[160,128]{1,0:T(8,128)S(1)} %slice_dynamic-update-slice_fusion), channel_id=1, source_target_pairs={{0,1},{1,0},{2,3},{3,2},{4,5},{5,4},{6,7},{7,6},{8,9},{9,8},{10,11... | collective-permute-start | bytes 245768 | tf_op jit(solution)/shard_map/ppermute | solution.py:580
  11.7 6.3 %collective-permute-start.4 = (f32[120,128]{1,0:T(8,128)S(1)}, f32[120,128]{1,0:T(8,128)S(1)}, u32[]{:S(2)}, u32[]{:S(2)}) collective-permute-start(f32[120,128]{1,0:T(8,128)S(1)} %slice_dynamic-update-slice_fusion.2), channel_id=1, source_target_pairs={{0,3},{1,2},{2,1},{3,0},{4,7},{5,6},{6,5},{7,4},{8,11},{9,10},{10,... | collective-permute-start | bytes 184328 | tf_op jit(solution)/shard_map/ppermute | solution.py:580
  14.5 7.7 %collective-permute-start.5 = (f32[40,128]{1,0:T(8,128)S(1)}, f32[40,128]{1,0:T(8,128)S(1)}, u32[]{:S(2)}, u32[]{:S(2)}) collective-permute-start(f32[40,128]{1,0:T(8,128)S(1)} %slice_add_fusion.modes_a_ref), channel_id=1, source_target_pairs={{0,2},{1,3},{2,0},{3,1},{4,6},{5,7},{6,4},{7,5},{8,10},{9,11},{10,... | collective-permute-start | bytes 61448 | tf_op jit(solution)/shard_map/ppermute | solution.py:580
  22.8 3.2 %collective-permute-start.6 = (f32[136,128]{1,0:T(8,128)S(1)}, f32[136,128]{1,0:T(8,128)S(1)}, u32[]{:S(2)}, u32[]{:S(2)}) collective-permute-start(f32[136,128]{1,0:T(8,128)S(1)} %late_modes.1.more_ref), channel_id=1, source_target_pairs={{0,1},{1,0},{2,3},{3,2},{4,5},{5,4},{6,7},{7,6},{8,9},{9,8},{10,11... | collective-permute-start | bytes 208904 | tf_op jit(solution)/shard_map/ppermute | solution.py:580
  26.0 7.4 %collective-permute-start.8 = (f32[136,128]{1,0:T(8,128)S(1)}, f32[136,128]{1,0:T(8,128)S(1)}, u32[]{:S(2)}, u32[]{:S(2)}) collective-permute-start(f32[136,128]{1,0:T(8,128)S(1)} %add.7), channel_id=1, source_target_pairs={{8,2},{9,3},{10,0},{11,1},{12,6},{13,7},{14,4},{15,5},{16,10},{17,... | collective-permute-start | bytes 208904 | tf_op jit(solution)/shard_map/ppermute | solution.py:580
  30.7 5.6 %collective-permute-start.7 = (f32[136,128]{1,0:T(8,128)S(1)}, f32[136,128]{1,0:T(8,128)S(1)}, u32[]{:S(2)}, u32[]{:S(2)}) collective-permute-start(f32[136,128]{1,0:T(8,128)S(1)} %add.7), channel_id=1, source_target_pairs={{8,0},{9,1},{10,2},{11,3},{12,4},{13,5},{14,6},{15,7},{16,8},{17,9... | collective-permute-start | bytes 208904 | tf_op jit(solution)/shard_map/ppermute | solution.py:580

commit v14 on v12

--- a/solution.py
+++ b/solution.py
@@ -369,8 +369,8 @@
 
 
 def first_kernel(
-    jac_ref, state_in_ref, coef_in_ref, inv_in_ref, edges_ref, span_ref, inner_ref, outer_ref, table_ref,
-    coef_ref, inv_ref, edge_coef_ref, state_ref, edge_ref, modes_ref, part_ref, *, groups,
+    jac_ref, state_in_ref, coef_in_ref, inv_in_ref, edges_ref, span_ref, inner_ref, outer_ref,
+    coef_ref, inv_ref, edge_coef_ref, state_ref, edge_ref, *, groups,
 ):
     _, components, axial, wide, pitch = state_ref.shape
     span = wide - EDGE
@@ -431,13 +431,26 @@
         target, at = (edge_ref.at[0], f) if f < components else (edge_coef_ref, f - components)
         target[at, :span] = value[:span]
         target[at, span:] = jnp.where(keep_five if f < components else keep_half, value[span:], 0.0)
-    refs = (jac_ref, state_ref, edge_ref, coef_ref)
-    for t in range(axial):
+    sweeps_without_boundaries(jac_ref, state_ref, edge_ref, coef_ref, edge_coef_ref, 0, 1)
+
+
+def sweeps_without_boundaries(jac_ref, state_ref, edge_ref, coef_ref, edge_coef_ref, first, last):
+    axial = state_ref.shape[2]
+    for t in range(first, last):
         for a in range(axial - t):
-            advance(refs, t, a)
+            advance((jac_ref, state_ref, edge_ref, coef_ref), t, a)
         if t < axial - 1:
             for c, value in enumerate(edge_update(jac_ref, edge_ref, edge_coef_ref, t, axial)):
                 edge_ref[t + 1, c] = value
+
+
+def more_kernel(
+    jac_ref, coef_ref, edge_coef_ref, state_in_ref, edge_in_ref, table_ref, state_ref, edge_ref, modes_ref, part_ref,
+):
+    _, components, axial, wide, pitch = state_ref.shape
+    span = wide - EDGE
+    side = lax.axis_index("span")
+    sweeps_without_boundaries(jac_ref, state_ref, edge_ref, coef_ref, edge_coef_ref, 1, axial)
     strips = [
         jnp.concatenate([state_ref[t, c, 0] for t in range(1, axial)] + [state_ref[axial, c, 0, :span]], 0)
         for c in range(components)
@@ -474,11 +487,11 @@
 
 
 def late_kernel(
-    jac_ref, coef_ref, inv_ref, part_ref, more_ref, modes_b_ref, modes_a_ref, synth_ref, table_ref, modes_ref,
+    jac_ref, coef_ref, inv_ref, part_ref, more_ref, first_ref, synth_ref, table_ref, modes_ref,
 ):
     span, pitch = part_ref.shape
     components, axial = coef_ref.shape[0] - 6, coef_ref.shape[1]
-    field = synthesised(modes_a_ref[EDGE:] + modes_b_ref[EDGE:], synth_ref, components * pitch)
+    field = synthesised(first_ref[EDGE:], synth_ref, components * pitch)
     delta = [inv_ref[:span] * field[:, c * pitch:(c + 1) * pitch] for c in range(components)]
     for a in range(axial - 2, -1, -1):
         delta = along_axis(jac_ref, coef_ref, delta, a, span)
@@ -488,13 +501,13 @@
 
 
 def between_kernel(
-    jac_ref, coef_ref, inv_ref, edge_coef_ref, state_in_ref, edge_in_ref, modes_b_ref, modes_a_ref, synth_ref, more_ref,
+    jac_ref, coef_ref, inv_ref, edge_coef_ref, state_in_ref, edge_in_ref, modes_ref, synth_ref, more_ref,
     state_ref, edge_ref, sent_ref,
 ):
     sent_ref[...] = more_ref[...]
     components, axial = state_ref.shape[1], state_ref.shape[2]
     wide, pitch = state_ref.shape[3:]
-    modes = modes_a_ref[...] + modes_b_ref[...]
+    modes = modes_ref[...]
     field = synthesised(jnp.concatenate([modes[EDGE:], modes[:EDGE]], 0), synth_ref, synth_ref.shape[1])
     delta = [inv_ref[...] * field[:, c * pitch:(c + 1) * pitch] for c in range(components)]
     for t in range(1, axial + 1):
@@ -680,29 +693,33 @@
     modes = modes + inner[groups * span + corner_rows:]
     for step in steps[1:]:
         modes = modes + moved(modes, lambda r, s, p: (r, s, p ^ step))
-    modes_b = far(modes)
-    modes_a = near(modes)
-
-    coef, inv, edge_coef, state, edge, more, part = call(
-        first_kernel, "first_sweeps",
+    got = moved(modes, lambda r, s, p: (r, s, p ^ last_step))
+    coef, inv, edge_coef, state, edge = call(
+        first_kernel, "first_sweep",
         (
             struct(components + 6, axial, wide, pitch), struct(wide, pitch), struct(components + 7, wide, pitch),
             state_shape, edge_shape,
-            struct((axial - 1) * span + EDGE, pitch), struct(span, pitch),
         ),
-        [(vmem, jac)] + [(vmem, x) for x in (state, coef, inv, edges, from_span, inner, outer, table)],
+        [(vmem, x) for x in (jac, state, coef, inv, edges, from_span, inner, outer)],
         aliases={1: 3, 2: 0, 3: 1},
         groups=groups,
     )
-
+    got, inv = lax.optimization_barrier((got, inv))
+    modes = near(modes + got)
+    state, edge, more, part = call(
+        more_kernel, "more_sweeps",
+        (state_shape, edge_shape, struct((axial - 1) * span + EDGE, pitch), struct(span, pitch)),
+        [(vmem, x) for x in (jac, coef, edge_coef, state, edge, table)],
+        aliases={3: 0, 4: 1},
+    )
     more_shape = struct(axial * span + EDGE, pitch)
     more = call(
         late_kernel, "late_modes", more_shape,
-        [(vmem, x) for x in (jac, coef, inv, part, more, modes_b, modes_a, synth, table)],
+        [(vmem, x) for x in (jac, coef, inv, part, more, modes, synth, table)],
     )
     state, edge, sent = call(
         between_kernel, "between_sweeps", (state_shape, edge_shape, more_shape),
-        [(vmem, x) for x in (jac, coef, inv, edge_coef, state, edge, modes_b, modes_a, synth, more)],
+        [(vmem, x) for x in (jac, coef, inv, edge_coef, state, edge, modes, synth, more)],
         aliases={4: 0, 5: 1},
     )
     state, edge = call(

time: 38.7 us -> 38.9 us (level)
  starting transfers between devices: 20.2 us -> 20.8 us
    ppermute x9, starting transfers between devices: 20.2 us -> 20.8 us  [moved(): return lax.ppermute(x, AXES, pairs)]
    pallas_call x8 -> x9, Pallas kernels: 13.7 us -> 13.5 us  [call(): pl.pallas_call(functools.partial(kernel, **fixed), out_shape=outs, in_spe...]
  transfers between devices with their start and end apart: 9 -> 9, of which waited for: 3 -> 5; matrix products, arithmetic and copies ran while one was open for 0% -> 0% of each run, Pallas kernels for 21% -> 20%
where the time goes in v14:
time: 38.9 us; the launch traced here: 38.7 us
  starting transfers between devices  20.8 us (53%)
  Pallas kernels  13.5 us (35%)
  waiting for transfers between devices  4.31 us (11%)
    ppermute x9, starting transfers between devices, moved(): return lax.ppermute(x, AXES, pairs)  20.8 us
    pallas_call x9, Pallas kernels, call(): pl.pallas_call(functools.partial(kernel, **fixed), out_shape=outs, in_spe...  13.5 us
    ppermute x9, waiting for transfers between devices, moved(): return lax.ppermute(x, AXES, pairs)  4.31 us
  transfers between devices with their start and end apart: 9, of which 5 were waited for; matrix products, arithmetic and copies ran while one was open for 0% of the time, Pallas kernels for 20%

profile of v14, /device:TPU:1, one launch (start us, length us, event | category | flops | bytes accessed | tf_op | source)
XLA Modules:
  0.0 38.7 jit_solution(2123225646061159281)
XLA Ops:
  0.0 1.7 %start.1 = (f32[6,5,4,40,128]{4,3,2,1,0:T(8,128)S(1)}, f32[11,4,40,128]{3,2,1,0:T(8,128)S(1)}, f32[40,128]{1,0:T(8,128)S(1)}, f32[36,8,128]{2,1,0:T(8,128)S(1)},...) custom-call(f32[5,4,32,128]{3,2,1,0:T(8,128)} %adjoint_hbm.1, ...), custom_call_target="tpu_custom_call" | custom-call | tf_op jit(solution)/shard_map/start/pallas_call | solution.py:625
  1.7 2.1 %collective-permute-start = (f32[56,128]{1,0:T(8,128)S(1)}, f32[56,128]{1,0:T(8,128)S(1)}, u32[]{:S(2)}, u32[]{:S(2)}) collective-permute-start(f32[56,128]{1,0:T(8,128)S(1)} %get-tuple-element.52), channel_id=1, source_target_pairs={{0,4},{1,5},{2,6},{3,7},{4,0},{5,1},{6,2},{7,3},{8,12},{9,13},{10,... | collective-permute-start | bytes 86024 | tf_op jit(solution)/shard_map/ppermute | solution.py:595
  3.9 0.1 collective-permute-start.1
  3.9 0.8 %pack.1 = (f32[17,32,128]{2,1,0:T(8,128)S(1)}, f32[160,128]{1,0:T(8,128)S(1)}, f32[120,128]{1,0:T(8,128)S(1)}) custom-call(f32[6,5,4,40,128]{4,3,2,1,0:T(8,128)S(1)} %get-tuple-element.49.state_ref.state_in_ref, f32[11,4,40,128]{3,2,1,0:T(8,128)S(1)} %get-tuple-element.50.coef_ref.coef_in_ref, f32[40,128]{1,0:T(8,128)S(1)} %get-tuple-element.51.inv_ref.inv_in_ref, ...), custom_call_target="tpu_custom_call" | custom-call | tf_op jit(solution)/shard_map/pack/pallas_call | solution.py:625
  4.7 0.4 %collective-permute-done = f32[56,128]{1,0:T(8,128)S(1)} collective-permute-done((f32[56,128]{1,0:T(8,128)S(1)}, f32[56,128]{1,0:T(8,128)S(1)}, u32[]{:S(2)}, u32[]{:S(2)}) %collective-permute-start) | collective-permute-done | bytes 28704 | tf_op jit(solution)/shard_map/ppermute | solution.py:595
  5.1 1.5 %collective-permute-start.2 = (f32[160,128]{1,0:T(8,128)S(1)}, f32[160,128]{1,0:T(8,128)S(1)}, u32[]{:S(2)}, u32[]{:S(2)}) collective-permute-start(f32[160,128]{1,0:T(8,128)S(1)} %slice_dynamic-update-slice_fusion), channel_id=1, source_target_pairs={{0,1},{1,0},{2,3},{3,2},{4,5},{5,4},{6,7},{7,6},{8,9},{9,8},{10,11... | collective-permute-start | bytes 245768 | tf_op jit(solution)/shard_map/ppermute | solution.py:595
  6.7 2.2 %collective-permute-start.3 = (f32[120,128]{1,0:T(8,128)S(1)}, f32[120,128]{1,0:T(8,128)S(1)}, u32[]{:S(2)}, u32[]{:S(2)}) collective-permute-start(f32[120,128]{1,0:T(8,128)S(1)} %slice_dynamic-update-slice_fusion.1), channel_id=1, source_target_pairs={{0,3},{1,2},{2,1},{3,0},{4,7},{5,6},{6,5},{7,4},{8,11},{9,10},{10,... | collective-permute-start | bytes 184328 | tf_op jit(solution)/shard_map/ppermute | solution.py:595
  8.8 0.0 collective-permute-done.2.inner_ref
  8.9 2.4 %collective-permute-start.4 = (f32[40,128]{1,0:T(8,128)S(1)}, f32[40,128]{1,0:T(8,128)S(1)}, u32[]{:S(2)}, u32[]{:S(2)}) collective-permute-start(f32[40,128]{1,0:T(8,128)S(1)} %slice_add_fusion), channel_id=1, source_target_pairs={{0,2},{1,3},{2,0},{3,1},{4,6},{5,7},{6,4},{7,5},{8,10},{9,11},{10,... | collective-permute-start | bytes 61448 | tf_op jit(solution)/shard_map/ppermute | solution.py:595
  11.3 0.6 %synth.1 = (bf16[2,896,128]{2,1,0:T(8,128)(2,1)S(1)}, f32[152,128]{1,0:T(8,128)S(1)}) custom-call(s32[1,4]{1,0:T(1,128)S(1)} %get-tuple-element.42.blades_ref, f32[5,5,1,6]{3,2,1,0:T(1,128)S(1)} %get-tuple-element.43.jacobians_ref, f32[5,5,3,64]{3,2,1,0:T(4,128)S(1)} %get-tuple-element.44.giles_re_ref, f32[5,5,3,64]{3,2,1,0:T(4,128)S(1)} %get-tuple-element.45.giles_im_ref, ...), custom_call_target="tpu_custom_call" | custom-call | tf_op jit(solution)/shard_map/synth/pallas_call | solution.py:625
  11.9 0.0 collective-permute-done.3.outer_ref
  11.9 0.0 collective-permute-done.1.span_ref
  11.9 1.7 %first_sweep.1 = (f32[11,4,40,128]{3,2,1,0:T(8,128)S(1)}, f32[40,128]{1,0:T(8,128)S(1)}, f32[12,40,128]{2,1,0:T(8,128)S(1)}, f32[6,5,4,40,128]{4,3,2,1,0:T(8,128)S(1)}, f32[5,5,40,128]{3,2,1,0:T(8,128)S(1)}) custom-call(f32[152,128]{1,0:T(8,128)S(1)} %get-tuple-element.48.jac_ref, ...), custom_call_target="tpu_custom_call", output_to_operand_aliasing={{3}: (1, {}), {0}: (2, {}), {1}: (3, {})} | custom-call | tf_op jit(solution)/shard_map/first_sweep/pallas_call | solution.py:625
  13.6 0.0 collective-permute-done.4
  13.6 5.1 %collective-permute-start.5 = (f32[40,128]{1,0:T(8,128)S(1)}, f32[40,128]{1,0:T(8,128)S(1)}, u32[]{:S(2)}, u32[]{:S(2)}) collective-permute-start(f32[40,128]{1,0:T(8,128)S(1)} %add.10), channel_id=1, source_target_pairs={{8,0},{9,1},{10,2},{11,3},{12,4},{13,5},{14,6},{15,7},{16,8},{17,9... | collective-permute-start | bytes 61448 | tf_op jit(solution)/shard_map/ppermute | solution.py:595
  18.7 2.4 %more_sweeps.1 = (f32[6,5,4,40,128]{4,3,2,1,0:T(8,128)S(1)}, f32[5,5,40,128]{3,2,1,0:T(8,128)S(1)}, f32[104,128]{1,0:T(8,128)S(1)}, f32[32,128]{1,0:T(8,128)S(1)}) custom-call(f32[152,128]{1,0:T(8,128)S(1)} %get-tuple-element.48.jac_ref, f32[11,4,40,128]{3,2,1,0:T(8,128)S(1)} %get-tuple-element.60.coef_ref, ...), custom_call_target="tpu_custom_call", output_to_operand_aliasing={{0}: (3, {}), {1}: (4, {})} | custom-call | tf_op jit(solution)/shard_map/more_sweeps/pallas_call | solution.py:625
  21.1 0.5 %collective-permute-done.5.first_ref.modes_ref = f32[40,128]{1,0:T(8,128)S(1)} collective-permute-done((f32[40,128]{1,0:T(8,128)S(1)}, f32[40,128]{1,0:T(8,128)S(1)}, u32[]{:S(2)}, u32[]{:S(2)}) %collective-permute-start.5) | collective-permute-done | bytes 20512 | tf_op jit(solution)/shard_map/ppermute | solution.py:595
  21.6 0.6 %late_modes.1.more_ref = f32[136,128]{1,0:T(8,128)S(1)} custom-call(f32[152,128]{1,0:T(8,128)S(1)} %get-tuple-element.48.jac_ref, f32[11,4,40,128]{3,2,1,0:T(8,128)S(1)} %get-tuple-element.60.coef_ref, f32[40,128]{1,0:T(8,128)S(1)} %get-tuple-element.62.inv_ref, f32[32,128]{1,0:T(8,128)S(1)} %get-tuple-element.71.part_ref, ...), custom_call_target="tpu_custom_call" | custom-call | tf_op jit(solution)/shard_map/late_modes/pallas_call | solution.py:625
  22.2 1.2 %collective-permute-start.6 = (f32[136,128]{1,0:T(8,128)S(1)}, f32[136,128]{1,0:T(8,128)S(1)}, u32[]{:S(2)}, u32[]{:S(2)}) collective-permute-start(f32[136,128]{1,0:T(8,128)S(1)} %late_modes.1.more_ref), channel_id=1, source_target_pairs={{0,1},{1,0},{2,3},{3,2},{4,5},{5,4},{6,7},{7,6},{8,9},{9,8},{10,11... | collective-permute-start | bytes 208904 | tf_op jit(solution)/shard_map/ppermute | solution.py:595
  23.5 1.6 %between_sweeps.1 = (f32[6,5,4,40,128]{4,3,2,1,0:T(8,128)S(1)}, f32[5,5,40,128]{3,2,1,0:T(8,128)S(1)}, f32[136,128]{1,0:T(8,128)S(1)}) custom-call(f32[152,128]{1,0:T(8,128)S(1)} %get-tuple-element.48.jac_ref, f32[11,4,40,128]{3,2,1,0:T(8,128)S(1)} %get-tuple-element.60.coef_ref, ...), custom_call_target="tpu_custom_call", output_to_operand_aliasing={{0}: (4, {}), {1}: (5, {})} | custom-call | tf_op jit(solution)/shard_map/between_sweeps/pallas_call | solution.py:625
  25.1 0.4 %collective-permute-done.6 = f32[136,128]{1,0:T(8,128)S(1)} collective-permute-done((f32[136,128]{1,0:T(8,128)S(1)}, f32[136,128]{1,0:T(8,128)S(1)}, u32[]{:S(2)}, u32[]{:S(2)}) %collective-permute-start.6) | collective-permute-done | bytes 69664 | tf_op jit(solution)/shard_map/ppermute | solution.py:595
  25.5 4.2 %collective-permute-start.8 = (f32[136,128]{1,0:T(8,128)S(1)}, f32[136,128]{1,0:T(8,128)S(1)}, u32[]{:S(2)}, u32[]{:S(2)}) collective-permute-start(f32[136,128]{1,0:T(8,128)S(1)} %add.11), channel_id=1, source_target_pairs={{8,2},{9,3},{10,0},{11,1},{12,6},{13,7},{14,4},{15,5},{16,10},{17,... | collective-permute-start | bytes 208904 | tf_op jit(solution)/shard_map/ppermute | solution.py:595
  29.7 1.9 %collective-permute-start.7 = (f32[136,128]{1,0:T(8,128)S(1)}, f32[136,128]{1,0:T(8,128)S(1)}, u32[]{:S(2)}, u32[]{:S(2)}) collective-permute-start(f32[136,128]{1,0:T(8,128)S(1)} %add.11), channel_id=1, source_target_pairs={{8,0},{9,1},{10,2},{11,3},{12,4},{13,5},{14,6},{15,7},{16,8},{17,9... | collective-permute-start | bytes 208904 | tf_op jit(solution)/shard_map/ppermute | solution.py:595
  31.7 0.7 %beside_sweeps.1 = (f32[6,5,4,40,128]{4,3,2,1,0:T(8,128)S(1)}, f32[5,5,40,128]{3,2,1,0:T(8,128)S(1)}) custom-call(f32[152,128]{1,0:T(8,128)S(1)} %get-tuple-element.48.jac_ref, f32[11,4,40,128]{3,2,1,0:T(8,128)S(1)} %get-tuple-element.60.coef_ref, f32[12,40,128]{2,1,0:T(8,128)S(1)} %get-tuple-element.63.edge_coef_ref, ...), custom_call_target="tpu_custom_call", output_to_operand_aliasing={{0}: (3, {}), {1}: (4, {})} | custom-call | tf_op jit(solution)/shard_map/beside_sweeps/pallas_call | solution.py:625
  32.4 1.2 %collective-permute-done.8.more_b_ref = f32[136,128]{1,0:T(8,128)S(1)} collective-permute-done((f32[136,128]{1,0:T(8,128)S(1)}, f32[136,128]{1,0:T(8,128)S(1)}, u32[]{:S(2)}, u32[]{:S(2)}) %collective-permute-start.8) | collective-permute-done | bytes 69664 | tf_op jit(solution)/shard_map/ppermute | solution.py:595
  33.6 1.7 %collective-permute-done.7.more_a_ref = f32[136,128]{1,0:T(8,128)S(1)} collective-permute-done((f32[136,128]{1,0:T(8,128)S(1)}, f32[136,128]{1,0:T(8,128)S(1)}, u32[]{:S(2)}, u32[]{:S(2)}) %collective-permute-start.7) | collective-permute-done | bytes 69664 | tf_op jit(solution)/shard_map/ppermute | solution.py:595
  35.4 3.3 %second_sweeps.1 = (f32[6,5,4,40,128]{4,3,2,1,0:T(8,128)S(1)}, f32[5,5,40,128]{3,2,1,0:T(8,128)S(1)}, f32[5,4,32,128]{3,2,1,0:T(8,128)}) custom-call(f32[152,128]{1,0:T(8,128)S(1)} %get-tuple-element.48.jac_ref, f32[11,4,40,128]{3,2,1,0:T(8,128)S(1)} %get-tuple-element.60.coef_ref, ...), custom_call_target="tpu_custom_call", output_to_operand_aliasing={{0}: (4, {}), {1}: (5, {})} | custom-call | tf_op jit(solution)/shard_map/second_sweeps/pallas_call | solution.py:625
  (5 shorter events, 0.0 us)
Async XLA Ops:
  1.7 3.4 %collective-permute-start = (f32[56,128]{1,0:T(8,128)S(1)}, f32[56,128]{1,0:T(8,128)S(1)}, u32[]{:S(2)}, u32[]{:S(2)}) collective-permute-start(f32[56,128]{1,0:T(8,128)S(1)} %get-tuple-element.52), channel_id=1, source_target_pairs={{0,4},{1,5},{2,6},{3,7},{4,0},{5,1},{6,2},{7,3},{8,12},{9,13},{10,... | collective-permute-start | bytes 86024 | tf_op jit(solution)/shard_map/ppermute | solution.py:595
  3.9 8.0 %collective-permute-start.1 = (f32[36,8,128]{2,1,0:T(8,128)S(1)}, f32[36,8,128]{2,1,0:T(8,128)S(1)}, u32[]{:S(2)}, u32[]{:S(2)}) collective-permute-start(f32[36,8,128]{2,1,0:T(8,128)S(1)} %get-tuple-element.56), channel_id=1, source_target_pairs={{0,4},{1,5},{2,6},{3,7},{4,0},{5,1},{6,2},{7,3},{8,12},{9,13},{10,... | collective-permute-start | bytes 442376 | tf_op jit(solution)/shard_map/ppermute | solution.py:595
  5.1 3.7 %collective-permute-start.2 = (f32[160,128]{1,0:T(8,128)S(1)}, f32[160,128]{1,0:T(8,128)S(1)}, u32[]{:S(2)}, u32[]{:S(2)}) collective-permute-start(f32[160,128]{1,0:T(8,128)S(1)} %slice_dynamic-update-slice_fusion), channel_id=1, source_target_pairs={{0,1},{1,0},{2,3},{3,2},{4,5},{5,4},{6,7},{7,6},{8,9},{9,8},{10,11... | collective-permute-start | bytes 245768 | tf_op jit(solution)/shard_map/ppermute | solution.py:595
  6.7 5.2 %collective-permute-start.3 = (f32[120,128]{1,0:T(8,128)S(1)}, f32[120,128]{1,0:T(8,128)S(1)}, u32[]{:S(2)}, u32[]{:S(2)}) collective-permute-start(f32[120,128]{1,0:T(8,128)S(1)} %slice_dynamic-update-slice_fusion.1), channel_id=1, source_target_pairs={{0,3},{1,2},{2,1},{3,0},{4,7},{5,6},{6,5},{7,4},{8,11},{9,10},{10,... | collective-permute-start | bytes 184328 | tf_op jit(solution)/shard_map/ppermute | solution.py:595
  8.9 4.7 %collective-permute-start.4 = (f32[40,128]{1,0:T(8,128)S(1)}, f32[40,128]{1,0:T(8,128)S(1)}, u32[]{:S(2)}, u32[]{:S(2)}) collective-permute-start(f32[40,128]{1,0:T(8,128)S(1)} %slice_add_fusion), channel_id=1, source_target_pairs={{0,2},{1,3},{2,0},{3,1},{4,6},{5,7},{6,4},{7,5},{8,10},{9,11},{10,... | collective-permute-start | bytes 61448 | tf_op jit(solution)/shard_map/ppermute | solution.py:595
  13.6 8.0 %collective-permute-start.5 = (f32[40,128]{1,0:T(8,128)S(1)}, f32[40,128]{1,0:T(8,128)S(1)}, u32[]{:S(2)}, u32[]{:S(2)}) collective-permute-start(f32[40,128]{1,0:T(8,128)S(1)} %add.10), channel_id=1, source_target_pairs={{8,0},{9,1},{10,2},{11,3},{12,4},{13,5},{14,6},{15,7},{16,8},{17,9... | collective-permute-start | bytes 61448 | tf_op jit(solution)/shard_map/ppermute | solution.py:595
  22.2 3.3 %collective-permute-start.6 = (f32[136,128]{1,0:T(8,128)S(1)}, f32[136,128]{1,0:T(8,128)S(1)}, u32[]{:S(2)}, u32[]{:S(2)}) collective-permute-start(f32[136,128]{1,0:T(8,128)S(1)} %late_modes.1.more_ref), channel_id=1, source_target_pairs={{0,1},{1,0},{2,3},{3,2},{4,5},{5,4},{6,7},{7,6},{8,9},{9,8},{10,11... | collective-permute-start | bytes 208904 | tf_op jit(solution)/shard_map/ppermute | solution.py:595
  25.5 8.1 %collective-permute-start.8 = (f32[136,128]{1,0:T(8,128)S(1)}, f32[136,128]{1,0:T(8,128)S(1)}, u32[]{:S(2)}, u32[]{:S(2)}) collective-permute-start(f32[136,128]{1,0:T(8,128)S(1)} %add.11), channel_id=1, source_target_pairs={{8,2},{9,3},{10,0},{11,1},{12,6},{13,7},{14,4},{15,5},{16,10},{17,... | collective-permute-start | bytes 208904 | tf_op jit(solution)/shard_map/ppermute | solution.py:595
  29.7 5.6 %collective-permute-start.7 = (f32[136,128]{1,0:T(8,128)S(1)}, f32[136,128]{1,0:T(8,128)S(1)}, u32[]{:S(2)}, u32[]{:S(2)}) collective-permute-start(f32[136,128]{1,0:T(8,128)S(1)} %add.11), channel_id=1, source_target_pairs={{8,0},{9,1},{10,2},{11,3},{12,4},{13,5},{14,6},{15,7},{16,8},{17,9... | collective-permute-start | bytes 208904 | tf_op jit(solution)/shard_map/ppermute | solution.py:595

commit v15 on v14

--- a/solution.py
+++ b/solution.py
@@ -536,9 +536,10 @@
 
 def second_kernel(
     jac_ref, coef_ref, inv_ref, edge_coef_ref, state_in_ref, edge_in_ref, more_a_ref, more_b_ref, synth_ref,
-    state_ref, edge_ref, out_ref, bound_ref,
+    state_ref, edge_ref, out_hbm, bound_ref, out_ref, sems,
 ):
-    components, axial, span, pitch = out_ref.shape
+    axial, components, span, pitch = out_ref.shape
+    copies = [pltpu.make_async_copy(out_ref.at[a], out_hbm.at[:, a], sems.at[a]) for a in range(axial)]
     wide = span + EDGE
     side = lax.axis_index("span")
     more = more_a_ref[...] + more_b_ref[...]
@@ -561,6 +562,9 @@
             state_ref[t, c, axial + 1 - t, :height] += delta[c][:height]
         if t < axial + 1:
             delta = along_axis(jac_ref, coef_ref, delta, axial - t, wide)
+    for c in range(components):
+        out_ref[0, c] = state_ref[axial + 1, c, 0, :span]
+    copies[0].start()
     for t in range(1, axial):
         if t > 1:
             for c, value in enumerate(edge_update(jac_ref, edge_ref, edge_coef_ref, t, axial)):
@@ -577,9 +581,10 @@
             state_ref[t + 1, c, axial - 1] += bound_ref[t, c]
     for a in range(1, axial):
         for c, value in enumerate(layer_update(*refs, axial, a, span)):
-            out_ref[c, a] = value + bound_ref[axial, c, :span] if a == axial - 1 else value
-    for c in range(components):
-        out_ref[c, 0] = state_ref[axial + 1, c, 0, :span]
+            out_ref[a, c] = value + bound_ref[axial, c, :span] if a == axial - 1 else value
+        copies[a].start()
+    for copy in copies:
+        copy.wait()
 
 
 def moved(x, to):
@@ -620,13 +625,13 @@
     def in_hbm(x):
         return pltpu.with_memory_space_constraint(x, pltpu.HBM)
 
-    def call(kernel, name, outs, ins, aliases=None, scratch=(), limit=40 * MIB, **fixed):
+    def call(kernel, name, outs, ins, aliases=None, scratch=(), limit=40 * MIB, out_specs=None, **fixed):
         specs = [spec for spec, _ in ins]
         return pl.pallas_call(
             functools.partial(kernel, **fixed),
             out_shape=outs,
             in_specs=specs,
-            out_specs=jax.tree.map(lambda _: vmem, outs),
+            out_specs=out_specs or jax.tree.map(lambda _: vmem, outs),
             scratch_shapes=scratch,
             input_output_aliases=aliases or {},
             compiler_params=params(limit),
@@ -670,8 +675,6 @@
     def far(x):
         return moved(x, lambda r, s, p: (r - 1, s, p ^ last_step))
 
-    small, edges = lax.optimization_barrier((moved(small, lambda r, s, p: (r, 1 - s, p)), edges))
-    from_span = moved(span_out, lambda r, s, p: (r, 1 - s, p))
     synth, jac = call(
         synth_kernel, "synth",
         (
@@ -684,6 +687,8 @@
         scratch=[pltpu.VMEM((2, components * components, mode_orders.shape[1]), jnp.float32)],
         row_count=row_count, place_count=place_count, components=components, pitch=pitch, length=length, axial=axial,
     )
+    small, edges, jac = lax.optimization_barrier((moved(small, lambda r, s, p: (r, 1 - s, p)), edges, jac))
+    from_span = moved(span_out, lambda r, s, p: (r, 1 - s, p))
     edge_shape = struct(axial + 1, components, wide, pitch)
     inner = lax.dynamic_update_slice(inner, small[:corner_rows + EDGE], (groups * span, 0))
     outer = lax.dynamic_update_slice(outer, small[corner_rows + EDGE:], (groups * span, 0))
@@ -736,7 +741,11 @@
         second_kernel, "second_sweeps", (state_shape, edge_shape, struct(components, axial, span, pitch)),
         [(vmem, x) for x in (jac, coef, inv, edge_coef, state, edge, more_a, more_b, synth)],
         aliases={4: 0, 5: 1},
-        scratch=[pltpu.VMEM((axial + 1, components, wide, pitch), jnp.float32)],
+        scratch=[
+            pltpu.VMEM((axial + 1, components, wide, pitch), jnp.float32),
+            pltpu.VMEM((axial, components, span, pitch), jnp.float32), pltpu.SemaphoreType.DMA((axial,)),
+        ],
+        out_specs=(vmem, vmem, hbm),
     )[2]
 
 

time: 38.9 us -> 39.1 us (level)
  starting transfers between devices: 20.8 us -> 21.2 us
    ppermute x9, starting transfers between devices: 20.8 us -> 21.2 us  [moved(): return lax.ppermute(x, AXES, pairs)]
  transfers between devices with their start and end apart: 9 -> 9, of which waited for: 5 -> 4; matrix products, arithmetic and copies ran while one was open for 0% -> 0% of each run, Pallas kernels for 20% -> 20%
where the time goes in v15:
time: 39.1 us; the launch traced here: 38.9 us
  starting transfers between devices  21.2 us (54%)
  Pallas kernels  13.5 us (35%)
  waiting for transfers between devices  4.05 us (10%)
    ppermute x9, starting transfers between devices, moved(): return lax.ppermute(x, AXES, pairs)  21.2 us
    pallas_call x9, Pallas kernels, call(): pl.pallas_call(functools.partial(kernel, **fixed), out_shape=outs, in_spe...  13.5 us
    ppermute x9, waiting for transfers between devices, moved(): return lax.ppermute(x, AXES, pairs)  4.05 us
  transfers between devices with their start and end apart: 9, of which 4 were waited for; matrix products, arithmetic and copies ran while one was open for 0% of the time, Pallas kernels for 20%

profile of v15, /device:TPU:1, one launch (start us, length us, event | category | flops | bytes accessed | tf_op | source)
XLA Modules:
  0.0 38.9 jit_solution(1350277330842056168)
XLA Ops:
  0.0 1.7 %start.1 = (f32[6,5,4,40,128]{4,3,2,1,0:T(8,128)S(1)}, f32[11,4,40,128]{3,2,1,0:T(8,128)S(1)}, f32[40,128]{1,0:T(8,128)S(1)}, f32[36,8,128]{2,1,0:T(8,128)S(1)},...) custom-call(f32[5,4,32,128]{3,2,1,0:T(8,128)} %adjoint_hbm.1, ...), custom_call_target="tpu_custom_call" | custom-call | tf_op jit(solution)/shard_map/start/pallas_call | solution.py:630
  1.7 2.1 %collective-permute-start = (f32[56,128]{1,0:T(8,128)S(1)}, f32[56,128]{1,0:T(8,128)S(1)}, u32[]{:S(2)}, u32[]{:S(2)}) collective-permute-start(f32[56,128]{1,0:T(8,128)S(1)} %get-tuple-element.43), channel_id=1, source_target_pairs={{0,4},{1,5},{2,6},{3,7},{4,0},{5,1},{6,2},{7,3},{8,12},{9,13},{10,... | collective-permute-start | bytes 86024 | tf_op jit(solution)/shard_map/ppermute | solution.py:600
  3.9 0.1 collective-permute-start.1
  3.9 0.8 %pack.1 = (f32[17,32,128]{2,1,0:T(8,128)S(1)}, f32[160,128]{1,0:T(8,128)S(1)}, f32[120,128]{1,0:T(8,128)S(1)}) custom-call(f32[6,5,4,40,128]{4,3,2,1,0:T(8,128)S(1)} %get-tuple-element.44.state_ref.state_in_ref, f32[11,4,40,128]{3,2,1,0:T(8,128)S(1)} %get-tuple-element.45.coef_ref.coef_in_ref, f32[40,128]{1,0:T(8,128)S(1)} %get-tuple-element.46.inv_ref.inv_in_ref, ...), custom_call_target="tpu_custom_call" | custom-call | tf_op jit(solution)/shard_map/pack/pallas_call | solution.py:630
  4.7 0.6 %synth.1 = (bf16[2,896,128]{2,1,0:T(8,128)(2,1)S(1)}, f32[152,128]{1,0:T(8,128)S(1)}) custom-call(s32[1,4]{1,0:T(1,128)S(1)} %get-tuple-element.49.blades_ref, f32[5,5,1,6]{3,2,1,0:T(1,128)S(1)} %get-tuple-element.50.jacobians_ref, f32[5,5,3,64]{3,2,1,0:T(4,128)S(1)} %get-tuple-element.51.giles_re_ref, f32[5,5,3,64]{3,2,1,0:T(4,128)S(1)} %get-tuple-element.52.giles_im_ref, ...), custom_call_target="tpu_custom_call" | custom-call | tf_op jit(solution)/shard_map/synth/pallas_call | solution.py:630
  5.4 0.0 collective-permute-done
  5.4 1.5 %collective-permute-start.2 = (f32[160,128]{1,0:T(8,128)S(1)}, f32[160,128]{1,0:T(8,128)S(1)}, u32[]{:S(2)}, u32[]{:S(2)}) collective-permute-start(f32[160,128]{1,0:T(8,128)S(1)} %slice_dynamic-update-slice_fusion), channel_id=1, source_target_pairs={{0,1},{1,0},{2,3},{3,2},{4,5},{5,4},{6,7},{7,6},{8,9},{9,8},{10,11... | collective-permute-start | bytes 245768 | tf_op jit(solution)/shard_map/ppermute | solution.py:600
  6.9 2.2 %collective-permute-start.3 = (f32[120,128]{1,0:T(8,128)S(1)}, f32[120,128]{1,0:T(8,128)S(1)}, u32[]{:S(2)}, u32[]{:S(2)}) collective-permute-start(f32[120,128]{1,0:T(8,128)S(1)} %slice_dynamic-update-slice_fusion.1), channel_id=1, source_target_pairs={{0,3},{1,2},{2,1},{3,0},{4,7},{5,6},{6,5},{7,4},{8,11},{9,10},{10,... | collective-permute-start | bytes 184328 | tf_op jit(solution)/shard_map/ppermute | solution.py:600
  9.1 0.0 collective-permute-done.2.inner_ref
  9.1 2.4 %collective-permute-start.4 = (f32[40,128]{1,0:T(8,128)S(1)}, f32[40,128]{1,0:T(8,128)S(1)}, u32[]{:S(2)}, u32[]{:S(2)}) collective-permute-start(f32[40,128]{1,0:T(8,128)S(1)} %slice_add_fusion), channel_id=1, source_target_pairs={{0,2},{1,3},{2,0},{3,1},{4,6},{5,7},{6,4},{7,5},{8,10},{9,11},{10,... | collective-permute-start | bytes 61448 | tf_op jit(solution)/shard_map/ppermute | solution.py:600
  11.5 0.3 collective-permute-done.3.outer_ref
  11.8 0.0 collective-permute-done.1.span_ref
  11.8 1.7 %first_sweep.1 = (f32[11,4,40,128]{3,2,1,0:T(8,128)S(1)}, f32[40,128]{1,0:T(8,128)S(1)}, f32[12,40,128]{2,1,0:T(8,128)S(1)}, f32[6,5,4,40,128]{4,3,2,1,0:T(8,128)S(1)}, f32[5,5,40,128]{3,2,1,0:T(8,128)S(1)}) custom-call(f32[152,128]{1,0:T(8,128)S(1)} %get-tuple-element.56.jac_ref, ...), custom_call_target="tpu_custom_call", output_to_operand_aliasing={{3}: (1, {}), {0}: (2, {}), {1}: (3, {})} | custom-call | tf_op jit(solution)/shard_map/first_sweep/pallas_call | solution.py:630
  13.4 0.0 collective-permute-done.4
  13.5 5.2 %collective-permute-start.5 = (f32[40,128]{1,0:T(8,128)S(1)}, f32[40,128]{1,0:T(8,128)S(1)}, u32[]{:S(2)}, u32[]{:S(2)}) collective-permute-start(f32[40,128]{1,0:T(8,128)S(1)} %add.10), channel_id=1, source_target_pairs={{8,0},{9,1},{10,2},{11,3},{12,4},{13,5},{14,6},{15,7},{16,8},{17,9... | collective-permute-start | bytes 61448 | tf_op jit(solution)/shard_map/ppermute | solution.py:600
  18.7 2.4 %more_sweeps.1 = (f32[6,5,4,40,128]{4,3,2,1,0:T(8,128)S(1)}, f32[5,5,40,128]{3,2,1,0:T(8,128)S(1)}, f32[104,128]{1,0:T(8,128)S(1)}, f32[32,128]{1,0:T(8,128)S(1)}) custom-call(f32[152,128]{1,0:T(8,128)S(1)} %get-tuple-element.56.jac_ref, f32[11,4,40,128]{3,2,1,0:T(8,128)S(1)} %get-tuple-element.62.coef_ref, ...), custom_call_target="tpu_custom_call", output_to_operand_aliasing={{0}: (3, {}), {1}: (4, {})} | custom-call | tf_op jit(solution)/shard_map/more_sweeps/pallas_call | solution.py:630
  21.1 0.2 collective-permute-done.5.first_ref.modes_ref
  21.3 0.6 %late_modes.1.more_ref = f32[136,128]{1,0:T(8,128)S(1)} custom-call(f32[152,128]{1,0:T(8,128)S(1)} %get-tuple-element.56.jac_ref, f32[11,4,40,128]{3,2,1,0:T(8,128)S(1)} %get-tuple-element.62.coef_ref, f32[40,128]{1,0:T(8,128)S(1)} %get-tuple-element.64.inv_ref, f32[32,128]{1,0:T(8,128)S(1)} %get-tuple-element.73.part_ref, ...), custom_call_target="tpu_custom_call" | custom-call | tf_op jit(solution)/shard_map/late_modes/pallas_call | solution.py:630
  21.9 1.7 %collective-permute-start.6 = (f32[136,128]{1,0:T(8,128)S(1)}, f32[136,128]{1,0:T(8,128)S(1)}, u32[]{:S(2)}, u32[]{:S(2)}) collective-permute-start(f32[136,128]{1,0:T(8,128)S(1)} %late_modes.1.more_ref), channel_id=1, source_target_pairs={{0,1},{1,0},{2,3},{3,2},{4,5},{5,4},{6,7},{7,6},{8,9},{9,8},{10,11... | collective-permute-start | bytes 208904 | tf_op jit(solution)/shard_map/ppermute | solution.py:600
  23.6 1.6 %between_sweeps.1 = (f32[6,5,4,40,128]{4,3,2,1,0:T(8,128)S(1)}, f32[5,5,40,128]{3,2,1,0:T(8,128)S(1)}, f32[136,128]{1,0:T(8,128)S(1)}) custom-call(f32[152,128]{1,0:T(8,128)S(1)} %get-tuple-element.56.jac_ref, f32[11,4,40,128]{3,2,1,0:T(8,128)S(1)} %get-tuple-element.62.coef_ref, ...), custom_call_target="tpu_custom_call", output_to_operand_aliasing={{0}: (4, {}), {1}: (5, {})} | custom-call | tf_op jit(solution)/shard_map/between_sweeps/pallas_call | solution.py:630
  25.2 0.3 collective-permute-done.6
  25.5 4.1 %collective-permute-start.8 = (f32[136,128]{1,0:T(8,128)S(1)}, f32[136,128]{1,0:T(8,128)S(1)}, u32[]{:S(2)}, u32[]{:S(2)}) collective-permute-start(f32[136,128]{1,0:T(8,128)S(1)} %add.11), channel_id=1, source_target_pairs={{8,2},{9,3},{10,0},{11,1},{12,6},{13,7},{14,4},{15,5},{16,10},{17,... | collective-permute-start | bytes 208904 | tf_op jit(solution)/shard_map/ppermute | solution.py:600
  29.6 1.9 %collective-permute-start.7 = (f32[136,128]{1,0:T(8,128)S(1)}, f32[136,128]{1,0:T(8,128)S(1)}, u32[]{:S(2)}, u32[]{:S(2)}) collective-permute-start(f32[136,128]{1,0:T(8,128)S(1)} %add.11), channel_id=1, source_target_pairs={{8,0},{9,1},{10,2},{11,3},{12,4},{13,5},{14,6},{15,7},{16,8},{17,9... | collective-permute-start | bytes 208904 | tf_op jit(solution)/shard_map/ppermute | solution.py:600
  31.5 0.7 %beside_sweeps.1 = (f32[6,5,4,40,128]{4,3,2,1,0:T(8,128)S(1)}, f32[5,5,40,128]{3,2,1,0:T(8,128)S(1)}) custom-call(f32[152,128]{1,0:T(8,128)S(1)} %get-tuple-element.56.jac_ref, f32[11,4,40,128]{3,2,1,0:T(8,128)S(1)} %get-tuple-element.62.coef_ref, f32[12,40,128]{2,1,0:T(8,128)S(1)} %get-tuple-element.65.edge_coef_ref, ...), custom_call_target="tpu_custom_call", output_to_operand_aliasing={{0}: (3, {}), {1}: (4, {})} | custom-call | tf_op jit(solution)/shard_map/beside_sweeps/pallas_call | solution.py:630
  32.3 3.3 %collective-permute-done.8.more_b_ref = f32[136,128]{1,0:T(8,128)S(1)} collective-permute-done((f32[136,128]{1,0:T(8,128)S(1)}, f32[136,128]{1,0:T(8,128)S(1)}, u32[]{:S(2)}, u32[]{:S(2)}) %collective-permute-start.8) | collective-permute-done | bytes 69664 | tf_op jit(solution)/shard_map/ppermute | solution.py:600
  35.6 0.0 collective-permute-done.7.more_a_ref
  35.6 3.3 %second_sweeps.1 = (f32[6,5,4,40,128]{4,3,2,1,0:T(8,128)S(1)}, f32[5,5,40,128]{3,2,1,0:T(8,128)S(1)}, f32[5,4,32,128]{3,2,1,0:T(8,128)}) custom-call(f32[152,128]{1,0:T(8,128)S(1)} %get-tuple-element.56.jac_ref, f32[11,4,40,128]{3,2,1,0:T(8,128)S(1)} %get-tuple-element.62.coef_ref, ...), custom_call_target="tpu_custom_call", output_to_operand_aliasing={{0}: (4, {}), {1}: (5, {})} | custom-call | tf_op jit(solution)/shard_map/second_sweeps/pallas_call | solution.py:630
  (5 shorter events, 0.0 us)
Async XLA Ops:
  1.7 3.6 %collective-permute-start = (f32[56,128]{1,0:T(8,128)S(1)}, f32[56,128]{1,0:T(8,128)S(1)}, u32[]{:S(2)}, u32[]{:S(2)}) collective-permute-start(f32[56,128]{1,0:T(8,128)S(1)} %get-tuple-element.43), channel_id=1, source_target_pairs={{0,4},{1,5},{2,6},{3,7},{4,0},{5,1},{6,2},{7,3},{8,12},{9,13},{10,... | collective-permute-start | bytes 86024 | tf_op jit(solution)/shard_map/ppermute | solution.py:600
  3.9 7.9 %collective-permute-start.1 = (f32[36,8,128]{2,1,0:T(8,128)S(1)}, f32[36,8,128]{2,1,0:T(8,128)S(1)}, u32[]{:S(2)}, u32[]{:S(2)}) collective-permute-start(f32[36,8,128]{2,1,0:T(8,128)S(1)} %get-tuple-element.58), channel_id=1, source_target_pairs={{0,4},{1,5},{2,6},{3,7},{4,0},{5,1},{6,2},{7,3},{8,12},{9,13},{10,... | collective-permute-start | bytes 442376 | tf_op jit(solution)/shard_map/ppermute | solution.py:600
  5.4 3.7 %collective-permute-start.2 = (f32[160,128]{1,0:T(8,128)S(1)}, f32[160,128]{1,0:T(8,128)S(1)}, u32[]{:S(2)}, u32[]{:S(2)}) collective-permute-start(f32[160,128]{1,0:T(8,128)S(1)} %slice_dynamic-update-slice_fusion), channel_id=1, source_target_pairs={{0,1},{1,0},{2,3},{3,2},{4,5},{5,4},{6,7},{7,6},{8,9},{9,8},{10,11... | collective-permute-start | bytes 245768 | tf_op jit(solution)/shard_map/ppermute | solution.py:600
  6.9 4.9 %collective-permute-start.3 = (f32[120,128]{1,0:T(8,128)S(1)}, f32[120,128]{1,0:T(8,128)S(1)}, u32[]{:S(2)}, u32[]{:S(2)}) collective-permute-start(f32[120,128]{1,0:T(8,128)S(1)} %slice_dynamic-update-slice_fusion.1), channel_id=1, source_target_pairs={{0,3},{1,2},{2,1},{3,0},{4,7},{5,6},{6,5},{7,4},{8,11},{9,10},{10,... | collective-permute-start | bytes 184328 | tf_op jit(solution)/shard_map/ppermute | solution.py:600
  9.1 4.3 %collective-permute-start.4 = (f32[40,128]{1,0:T(8,128)S(1)}, f32[40,128]{1,0:T(8,128)S(1)}, u32[]{:S(2)}, u32[]{:S(2)}) collective-permute-start(f32[40,128]{1,0:T(8,128)S(1)} %slice_add_fusion), channel_id=1, source_target_pairs={{0,2},{1,3},{2,0},{3,1},{4,6},{5,7},{6,4},{7,5},{8,10},{9,11},{10,... | collective-permute-start | bytes 61448 | tf_op jit(solution)/shard_map/ppermute | solution.py:600
  13.5 7.8 %collective-permute-start.5 = (f32[40,128]{1,0:T(8,128)S(1)}, f32[40,128]{1,0:T(8,128)S(1)}, u32[]{:S(2)}, u32[]{:S(2)}) collective-permute-start(f32[40,128]{1,0:T(8,128)S(1)} %add.10), channel_id=1, source_target_pairs={{8,0},{9,1},{10,2},{11,3},{12,4},{13,5},{14,6},{15,7},{16,8},{17,9... | collective-permute-start | bytes 61448 | tf_op jit(solution)/shard_map/ppermute | solution.py:600
  21.9 3.7 %collective-permute-start.6 = (f32[136,128]{1,0:T(8,128)S(1)}, f32[136,128]{1,0:T(8,128)S(1)}, u32[]{:S(2)}, u32[]{:S(2)}) collective-permute-start(f32[136,128]{1,0:T(8,128)S(1)} %late_modes.1.more_ref), channel_id=1, source_target_pairs={{0,1},{1,0},{2,3},{3,2},{4,5},{5,4},{6,7},{7,6},{8,9},{9,8},{10,11... | collective-permute-start | bytes 208904 | tf_op jit(solution)/shard_map/ppermute | solution.py:600
  25.5 10.0 %collective-permute-start.8 = (f32[136,128]{1,0:T(8,128)S(1)}, f32[136,128]{1,0:T(8,128)S(1)}, u32[]{:S(2)}, u32[]{:S(2)}) collective-permute-start(f32[136,128]{1,0:T(8,128)S(1)} %add.11), channel_id=1, source_target_pairs={{8,2},{9,3},{10,0},{11,1},{12,6},{13,7},{14,4},{15,5},{16,10},{17,... | collective-permute-start | bytes 208904 | tf_op jit(solution)/shard_map/ppermute | solution.py:600
  29.6 6.0 %collective-permute-start.7 = (f32[136,128]{1,0:T(8,128)S(1)}, f32[136,128]{1,0:T(8,128)S(1)}, u32[]{:S(2)}, u32[]{:S(2)}) collective-permute-start(f32[136,128]{1,0:T(8,128)S(1)} %add.11), channel_id=1, source_target_pairs={{8,0},{9,1},{10,2},{11,3},{12,4},{13,5},{14,6},{15,7},{16,8},{17,9... | collective-permute-start | bytes 208904 | tf_op jit(solution)/shard_map/ppermute | solution.py:600

commit v16 on v15

--- a/solution.py
+++ b/solution.py
@@ -502,9 +502,8 @@
 
 def between_kernel(
     jac_ref, coef_ref, inv_ref, edge_coef_ref, state_in_ref, edge_in_ref, modes_ref, synth_ref, more_ref,
-    state_ref, edge_ref, sent_ref,
+    state_ref, edge_ref,
 ):
-    sent_ref[...] = more_ref[...]
     components, axial = state_ref.shape[1], state_ref.shape[2]
     wide, pitch = state_ref.shape[3:]
     modes = modes_ref[...]
@@ -672,9 +671,6 @@
     def near(x):
         return moved(x, lambda r, s, p: (r - 1, s, p))
 
-    def far(x):
-        return moved(x, lambda r, s, p: (r - 1, s, p ^ last_step))
-
     synth, jac = call(
         synth_kernel, "synth",
         (
@@ -722,21 +718,22 @@
         late_kernel, "late_modes", more_shape,
         [(vmem, x) for x in (jac, coef, inv, part, more, modes, synth, table)],
     )
-    state, edge, sent = call(
-        between_kernel, "between_sweeps", (state_shape, edge_shape, more_shape),
+    up, up_across = near(more), moved(more, lambda r, s, p: (r - 1, s, p ^ 1))
+    state, edge = call(
+        between_kernel, "between_sweeps", (state_shape, edge_shape),
         [(vmem, x) for x in (jac, coef, inv, edge_coef, state, edge, modes, synth, more)],
         aliases={4: 0, 5: 1},
     )
+    up, edge = lax.optimization_barrier((up, edge))
+    more_a = up + up_across
     state, edge = call(
         beside_kernel, "beside_sweeps", (state_shape, edge_shape),
         [(vmem, x) for x in (jac, coef, edge_coef, state, edge)],
         aliases={3: 0, 4: 1},
     )
-    for step in steps:
-        got = moved(more, lambda r, s, p: (r, s, p ^ step))
-        more, sent = sent + got, sent + got
-    more_b = far(more)
-    more_a = near(more)
+    for step in steps[1:]:
+        more_a = more_a + moved(more_a, lambda r, s, p: (r, s, p ^ step))
+    more_b = moved(more_a, lambda r, s, p: (r, s, p ^ last_step))
     return call(
         second_kernel, "second_sweeps", (state_shape, edge_shape, struct(components, axial, span, pitch)),
         [(vmem, x) for x in (jac, coef, inv, edge_coef, state, edge, more_a, more_b, synth)],

time: 39.1 us -> 39.4 us (level)
  starting transfers between devices: 21.2 us -> 19.5 us
  waiting for transfers between devices: 4.05 us -> 5.51 us
    ppermute x9, starting transfers between devices: 21.2 us -> 19.5 us  [moved(): return lax.ppermute(x, AXES, pairs)]
    ppermute x9, waiting for transfers between devices: 4.05 us -> 5.51 us  [moved(): return lax.ppermute(x, AXES, pairs)]
  transfers between devices with their start and end apart: 9 -> 9, of which waited for: 4 -> 4; matrix products, arithmetic and copies ran while one was open for 0% -> 0% of each run, Pallas kernels for 20% -> 21%
where the time goes in v16:
time: 39.4 us; the launch traced here: 39 us
  starting transfers between devices  19.5 us (49%)
  Pallas kernels  13.8 us (35%)
  waiting for transfers between devices  5.51 us (14%)
    ppermute x9, starting transfers between devices, moved(): return lax.ppermute(x, AXES, pairs)  19.5 us
    pallas_call x9, Pallas kernels, call(): pl.pallas_call(functools.partial(kernel, **fixed), out_shape=outs, in_spe...  13.8 us
    ppermute x9, waiting for transfers between devices, moved(): return lax.ppermute(x, AXES, pairs)  5.51 us
  transfers between devices with their start and end apart: 9, of which 4 were waited for; matrix products, arithmetic and copies ran while one was open for 0% of the time, Pallas kernels for 21%

profile of v16, /device:TPU:1, one launch (start us, length us, event | category | flops | bytes accessed | tf_op | source)
XLA Modules:
  0.0 39.0 jit_solution(18077811405290609289)
XLA Ops:
  0.0 1.7 %start.1 = (f32[6,5,4,40,128]{4,3,2,1,0:T(8,128)S(1)}, f32[11,4,40,128]{3,2,1,0:T(8,128)S(1)}, f32[40,128]{1,0:T(8,128)S(1)}, f32[36,8,128]{2,1,0:T(8,128)S(1)},...) custom-call(f32[5,4,32,128]{3,2,1,0:T(8,128)} %adjoint_hbm.1, ...), custom_call_target="tpu_custom_call" | custom-call | tf_op jit(solution)/shard_map/start/pallas_call | solution.py:629
  1.7 2.1 %collective-permute-start = (f32[56,128]{1,0:T(8,128)S(1)}, f32[56,128]{1,0:T(8,128)S(1)}, u32[]{:S(2)}, u32[]{:S(2)}) collective-permute-start(f32[56,128]{1,0:T(8,128)S(1)} %get-tuple-element.44), channel_id=1, source_target_pairs={{0,4},{1,5},{2,6},{3,7},{4,0},{5,1},{6,2},{7,3},{8,12},{9,13},{10,... | collective-permute-start | bytes 86024 | tf_op jit(solution)/shard_map/ppermute | solution.py:599
  3.9 0.1 collective-permute-start.1
  3.9 0.8 %pack.1 = (f32[17,32,128]{2,1,0:T(8,128)S(1)}, f32[160,128]{1,0:T(8,128)S(1)}, f32[120,128]{1,0:T(8,128)S(1)}) custom-call(f32[6,5,4,40,128]{4,3,2,1,0:T(8,128)S(1)} %get-tuple-element.45.state_ref.state_in_ref, f32[11,4,40,128]{3,2,1,0:T(8,128)S(1)} %get-tuple-element.46.coef_ref.coef_in_ref, f32[40,128]{1,0:T(8,128)S(1)} %get-tuple-element.47.inv_ref.inv_in_ref, ...), custom_call_target="tpu_custom_call" | custom-call | tf_op jit(solution)/shard_map/pack/pallas_call | solution.py:629
  4.7 0.6 %synth.1 = (bf16[2,896,128]{2,1,0:T(8,128)(2,1)S(1)}, f32[152,128]{1,0:T(8,128)S(1)}) custom-call(s32[1,4]{1,0:T(1,128)S(1)} %get-tuple-element.50.blades_ref, f32[5,5,1,6]{3,2,1,0:T(1,128)S(1)} %get-tuple-element.51.jacobians_ref, f32[5,5,3,64]{3,2,1,0:T(4,128)S(1)} %get-tuple-element.52.giles_re_ref, f32[5,5,3,64]{3,2,1,0:T(4,128)S(1)} %get-tuple-element.53.giles_im_ref, ...), custom_call_target="tpu_custom_call" | custom-call | tf_op jit(solution)/shard_map/synth/pallas_call | solution.py:629
  5.4 0.0 collective-permute-done
  5.4 1.5 %collective-permute-start.2 = (f32[160,128]{1,0:T(8,128)S(1)}, f32[160,128]{1,0:T(8,128)S(1)}, u32[]{:S(2)}, u32[]{:S(2)}) collective-permute-start(f32[160,128]{1,0:T(8,128)S(1)} %slice_dynamic-update-slice_fusion), channel_id=1, source_target_pairs={{0,1},{1,0},{2,3},{3,2},{4,5},{5,4},{6,7},{7,6},{8,9},{9,8},{10,11... | collective-permute-start | bytes 245768 | tf_op jit(solution)/shard_map/ppermute | solution.py:599
  6.9 2.2 %collective-permute-start.3 = (f32[120,128]{1,0:T(8,128)S(1)}, f32[120,128]{1,0:T(8,128)S(1)}, u32[]{:S(2)}, u32[]{:S(2)}) collective-permute-start(f32[120,128]{1,0:T(8,128)S(1)} %slice_dynamic-update-slice_fusion.1), channel_id=1, source_target_pairs={{0,3},{1,2},{2,1},{3,0},{4,7},{5,6},{6,5},{7,4},{8,11},{9,10},{10,... | collective-permute-start | bytes 184328 | tf_op jit(solution)/shard_map/ppermute | solution.py:599
  9.1 0.0 collective-permute-done.2.inner_ref
  9.1 2.4 %collective-permute-start.4 = (f32[40,128]{1,0:T(8,128)S(1)}, f32[40,128]{1,0:T(8,128)S(1)}, u32[]{:S(2)}, u32[]{:S(2)}) collective-permute-start(f32[40,128]{1,0:T(8,128)S(1)} %slice_add_fusion), channel_id=1, source_target_pairs={{0,2},{1,3},{2,0},{3,1},{4,6},{5,7},{6,4},{7,5},{8,10},{9,11},{10,... | collective-permute-start | bytes 61448 | tf_op jit(solution)/shard_map/ppermute | solution.py:599
  11.5 0.3 collective-permute-done.3.outer_ref
  11.8 0.0 collective-permute-done.1.span_ref
  11.8 1.7 %first_sweep.1 = (f32[11,4,40,128]{3,2,1,0:T(8,128)S(1)}, f32[40,128]{1,0:T(8,128)S(1)}, f32[12,40,128]{2,1,0:T(8,128)S(1)}, f32[6,5,4,40,128]{4,3,2,1,0:T(8,128)S(1)}, f32[5,5,40,128]{3,2,1,0:T(8,128)S(1)}) custom-call(f32[152,128]{1,0:T(8,128)S(1)} %get-tuple-element.57.jac_ref, ...), custom_call_target="tpu_custom_call", output_to_operand_aliasing={{3}: (1, {}), {0}: (2, {}), {1}: (3, {})} | custom-call | tf_op jit(solution)/shard_map/first_sweep/pallas_call | solution.py:629
  13.5 0.0 collective-permute-done.4
  13.5 5.2 %collective-permute-start.5 = (f32[40,128]{1,0:T(8,128)S(1)}, f32[40,128]{1,0:T(8,128)S(1)}, u32[]{:S(2)}, u32[]{:S(2)}) collective-permute-start(f32[40,128]{1,0:T(8,128)S(1)} %add.10), channel_id=1, source_target_pairs={{8,0},{9,1},{10,2},{11,3},{12,4},{13,5},{14,6},{15,7},{16,8},{17,9... | collective-permute-start | bytes 61448 | tf_op jit(solution)/shard_map/ppermute | solution.py:599
  18.8 2.5 %more_sweeps.1 = (f32[6,5,4,40,128]{4,3,2,1,0:T(8,128)S(1)}, f32[5,5,40,128]{3,2,1,0:T(8,128)S(1)}, f32[104,128]{1,0:T(8,128)S(1)}, f32[32,128]{1,0:T(8,128)S(1)}) custom-call(f32[152,128]{1,0:T(8,128)S(1)} %get-tuple-element.57.jac_ref, f32[11,4,40,128]{3,2,1,0:T(8,128)S(1)} %get-tuple-element.63.coef_ref, ...), custom_call_target="tpu_custom_call", output_to_operand_aliasing={{0}: (3, {}), {1}: (4, {})} | custom-call | tf_op jit(solution)/shard_map/more_sweeps/pallas_call | solution.py:629
  21.2 0.1 collective-permute-done.5.first_ref.modes_ref
  21.3 0.6 %late_modes.1.more_ref = f32[136,128]{1,0:T(8,128)S(1)} custom-call(f32[152,128]{1,0:T(8,128)S(1)} %get-tuple-element.57.jac_ref, f32[11,4,40,128]{3,2,1,0:T(8,128)S(1)} %get-tuple-element.63.coef_ref, f32[40,128]{1,0:T(8,128)S(1)} %get-tuple-element.65.inv_ref, f32[32,128]{1,0:T(8,128)S(1)} %get-tuple-element.74.part_ref, ...), custom_call_target="tpu_custom_call" | custom-call | tf_op jit(solution)/shard_map/late_modes/pallas_call | solution.py:629
  21.9 1.9 %collective-permute-start.6 = (f32[136,128]{1,0:T(8,128)S(1)}, f32[136,128]{1,0:T(8,128)S(1)}, u32[]{:S(2)}, u32[]{:S(2)}) collective-permute-start(f32[136,128]{1,0:T(8,128)S(1)} %late_modes.1.more_ref), channel_id=1, source_target_pairs={{8,0},{9,1},{10,2},{11,3},{12,4},{13,5},{14,6},{15,7},{16,8},{17,9... | collective-permute-start | bytes 208904 | tf_op jit(solution)/shard_map/ppermute | solution.py:599
  23.9 2.1 %collective-permute-start.7 = (f32[136,128]{1,0:T(8,128)S(1)}, f32[136,128]{1,0:T(8,128)S(1)}, u32[]{:S(2)}, u32[]{:S(2)}) collective-permute-start(f32[136,128]{1,0:T(8,128)S(1)} %late_modes.1.more_ref), channel_id=1, source_target_pairs={{8,1},{9,0},{10,3},{11,2},{12,5},{13,4},{14,7},{15,6},{16,9},{17,8... | collective-permute-start | bytes 208904 | tf_op jit(solution)/shard_map/ppermute | solution.py:599
  25.9 1.7 %between_sweeps.1 = (f32[6,5,4,40,128]{4,3,2,1,0:T(8,128)S(1)}, f32[5,5,40,128]{3,2,1,0:T(8,128)S(1)}) custom-call(f32[152,128]{1,0:T(8,128)S(1)} %get-tuple-element.57.jac_ref, f32[11,4,40,128]{3,2,1,0:T(8,128)S(1)} %get-tuple-element.63.coef_ref, f32[40,128]{1,0:T(8,128)S(1)} %get-tuple-element.65.inv_ref, ...), custom_call_target="tpu_custom_call", output_to_operand_aliasing={{0}: (4, {}), {1}: (5, {})} | custom-call | tf_op jit(solution)/shard_map/between_sweeps/pallas_call | solution.py:629
  27.6 0.0 collective-permute-done.6
  27.6 3.5 %collective-permute-done.7 = f32[136,128]{1,0:T(8,128)S(1)} collective-permute-done((f32[136,128]{1,0:T(8,128)S(1)}, f32[136,128]{1,0:T(8,128)S(1)}, u32[]{:S(2)}, u32[]{:S(2)}) %collective-permute-start.7) | collective-permute-done | bytes 69664 | tf_op jit(solution)/shard_map/ppermute | solution.py:599
  31.1 2.0 %collective-permute-start.8 = (f32[136,128]{1,0:T(8,128)S(1)}, f32[136,128]{1,0:T(8,128)S(1)}, u32[]{:S(2)}, u32[]{:S(2)}) collective-permute-start(f32[136,128]{1,0:T(8,128)S(1)} %add.11.more_a_ref), channel_id=1, source_target_pairs={{0,2},{1,3},{2,0},{3,1},{4,6},{5,7},{6,4},{7,5},{8,10},{9,11},{10,... | collective-permute-start | bytes 208904 | tf_op jit(solution)/shard_map/ppermute | solution.py:599
  33.1 0.8 %beside_sweeps.1 = (f32[6,5,4,40,128]{4,3,2,1,0:T(8,128)S(1)}, f32[5,5,40,128]{3,2,1,0:T(8,128)S(1)}) custom-call(f32[152,128]{1,0:T(8,128)S(1)} %get-tuple-element.57.jac_ref, f32[11,4,40,128]{3,2,1,0:T(8,128)S(1)} %get-tuple-element.63.coef_ref, f32[12,40,128]{2,1,0:T(8,128)S(1)} %get-tuple-element.66.edge_coef_ref, ...), custom_call_target="tpu_custom_call", output_to_operand_aliasing={{0}: (3, {}), {1}: (4, {})} | custom-call | tf_op jit(solution)/shard_map/beside_sweeps/pallas_call | solution.py:629
  33.9 1.7 %collective-permute-done.8.more_b_ref = f32[136,128]{1,0:T(8,128)S(1)} collective-permute-done((f32[136,128]{1,0:T(8,128)S(1)}, f32[136,128]{1,0:T(8,128)S(1)}, u32[]{:S(2)}, u32[]{:S(2)}) %collective-permute-start.8) | collective-permute-done | bytes 69664 | tf_op jit(solution)/shard_map/ppermute | solution.py:599
  35.6 3.4 %second_sweeps.1 = (f32[6,5,4,40,128]{4,3,2,1,0:T(8,128)S(1)}, f32[5,5,40,128]{3,2,1,0:T(8,128)S(1)}, f32[5,4,32,128]{3,2,1,0:T(8,128)}) custom-call(f32[152,128]{1,0:T(8,128)S(1)} %get-tuple-element.57.jac_ref, f32[11,4,40,128]{3,2,1,0:T(8,128)S(1)} %get-tuple-element.63.coef_ref, ...), custom_call_target="tpu_custom_call", output_to_operand_aliasing={{0}: (4, {}), {1}: (5, {})} | custom-call | tf_op jit(solution)/shard_map/second_sweeps/pallas_call | solution.py:629
  (5 shorter events, 0.0 us)
Async XLA Ops:
  1.7 3.7 %collective-permute-start = (f32[56,128]{1,0:T(8,128)S(1)}, f32[56,128]{1,0:T(8,128)S(1)}, u32[]{:S(2)}, u32[]{:S(2)}) collective-permute-start(f32[56,128]{1,0:T(8,128)S(1)} %get-tuple-element.44), channel_id=1, source_target_pairs={{0,4},{1,5},{2,6},{3,7},{4,0},{5,1},{6,2},{7,3},{8,12},{9,13},{10,... | collective-permute-start | bytes 86024 | tf_op jit(solution)/shard_map/ppermute | solution.py:599
  3.9 7.9 %collective-permute-start.1 = (f32[36,8,128]{2,1,0:T(8,128)S(1)}, f32[36,8,128]{2,1,0:T(8,128)S(1)}, u32[]{:S(2)}, u32[]{:S(2)}) collective-permute-start(f32[36,8,128]{2,1,0:T(8,128)S(1)} %get-tuple-element.59), channel_id=1, source_target_pairs={{0,4},{1,5},{2,6},{3,7},{4,0},{5,1},{6,2},{7,3},{8,12},{9,13},{10,... | collective-permute-start | bytes 442376 | tf_op jit(solution)/shard_map/ppermute | solution.py:599
  5.4 3.7 %collective-permute-start.2 = (f32[160,128]{1,0:T(8,128)S(1)}, f32[160,128]{1,0:T(8,128)S(1)}, u32[]{:S(2)}, u32[]{:S(2)}) collective-permute-start(f32[160,128]{1,0:T(8,128)S(1)} %slice_dynamic-update-slice_fusion), channel_id=1, source_target_pairs={{0,1},{1,0},{2,3},{3,2},{4,5},{5,4},{6,7},{7,6},{8,9},{9,8},{10,11... | collective-permute-start | bytes 245768 | tf_op jit(solution)/shard_map/ppermute | solution.py:599
  6.9 4.9 %collective-permute-start.3 = (f32[120,128]{1,0:T(8,128)S(1)}, f32[120,128]{1,0:T(8,128)S(1)}, u32[]{:S(2)}, u32[]{:S(2)}) collective-permute-start(f32[120,128]{1,0:T(8,128)S(1)} %slice_dynamic-update-slice_fusion.1), channel_id=1, source_target_pairs={{0,3},{1,2},{2,1},{3,0},{4,7},{5,6},{6,5},{7,4},{8,11},{9,10},{10,... | collective-permute-start | bytes 184328 | tf_op jit(solution)/shard_map/ppermute | solution.py:599
  9.1 4.4 %collective-permute-start.4 = (f32[40,128]{1,0:T(8,128)S(1)}, f32[40,128]{1,0:T(8,128)S(1)}, u32[]{:S(2)}, u32[]{:S(2)}) collective-permute-start(f32[40,128]{1,0:T(8,128)S(1)} %slice_add_fusion), channel_id=1, source_target_pairs={{0,2},{1,3},{2,0},{3,1},{4,6},{5,7},{6,4},{7,5},{8,10},{9,11},{10,... | collective-permute-start | bytes 61448 | tf_op jit(solution)/shard_map/ppermute | solution.py:599
  13.5 7.8 %collective-permute-start.5 = (f32[40,128]{1,0:T(8,128)S(1)}, f32[40,128]{1,0:T(8,128)S(1)}, u32[]{:S(2)}, u32[]{:S(2)}) collective-permute-start(f32[40,128]{1,0:T(8,128)S(1)} %add.10), channel_id=1, source_target_pairs={{8,0},{9,1},{10,2},{11,3},{12,4},{13,5},{14,6},{15,7},{16,8},{17,9... | collective-permute-start | bytes 61448 | tf_op jit(solution)/shard_map/ppermute | solution.py:599
  21.9 5.7 %collective-permute-start.6 = (f32[136,128]{1,0:T(8,128)S(1)}, f32[136,128]{1,0:T(8,128)S(1)}, u32[]{:S(2)}, u32[]{:S(2)}) collective-permute-start(f32[136,128]{1,0:T(8,128)S(1)} %late_modes.1.more_ref), channel_id=1, source_target_pairs={{8,0},{9,1},{10,2},{11,3},{12,4},{13,5},{14,6},{15,7},{16,8},{17,9... | collective-permute-start | bytes 208904 | tf_op jit(solution)/shard_map/ppermute | solution.py:599
  23.9 7.2 %collective-permute-start.7 = (f32[136,128]{1,0:T(8,128)S(1)}, f32[136,128]{1,0:T(8,128)S(1)}, u32[]{:S(2)}, u32[]{:S(2)}) collective-permute-start(f32[136,128]{1,0:T(8,128)S(1)} %late_modes.1.more_ref), channel_id=1, source_target_pairs={{8,1},{9,0},{10,3},{11,2},{12,5},{13,4},{14,7},{15,6},{16,9},{17,8... | collective-permute-start | bytes 208904 | tf_op jit(solution)/shard_map/ppermute | solution.py:599
  31.1 4.4 %collective-permute-start.8 = (f32[136,128]{1,0:T(8,128)S(1)}, f32[136,128]{1,0:T(8,128)S(1)}, u32[]{:S(2)}, u32[]{:S(2)}) collective-permute-start(f32[136,128]{1,0:T(8,128)S(1)} %add.11.more_a_ref), channel_id=1, source_target_pairs={{0,2},{1,3},{2,0},{3,1},{4,6},{5,7},{6,4},{7,5},{8,10},{9,11},{10,... | collective-permute-start | bytes 208904 | tf_op jit(solution)/shard_map/ppermute | solution.py:599

commit v17 on v16

--- a/solution.py
+++ b/solution.py
@@ -718,14 +718,14 @@
         late_kernel, "late_modes", more_shape,
         [(vmem, x) for x in (jac, coef, inv, part, more, modes, synth, table)],
     )
-    up, up_across = near(more), moved(more, lambda r, s, p: (r - 1, s, p ^ 1))
+    up_across, up = moved(more, lambda r, s, p: (r - 1, s, p ^ 1)), near(more)
     state, edge = call(
         between_kernel, "between_sweeps", (state_shape, edge_shape),
         [(vmem, x) for x in (jac, coef, inv, edge_coef, state, edge, modes, synth, more)],
         aliases={4: 0, 5: 1},
     )
-    up, edge = lax.optimization_barrier((up, edge))
-    more_a = up + up_across
+    up_across, edge = lax.optimization_barrier((up_across, edge))
+    more_a = up_across + up
     state, edge = call(
         beside_kernel, "beside_sweeps", (state_shape, edge_shape),
         [(vmem, x) for x in (jac, coef, edge_coef, state, edge)],

time: 39.4 us -> 39.3 us (level)
  starting transfers between devices: 19.5 us -> 20.4 us
  waiting for transfers between devices: 5.51 us -> 4.74 us
    ppermute x9, starting transfers between devices: 19.5 us -> 20.4 us  [moved(): return lax.ppermute(x, AXES, pairs)]
    ppermute x9, waiting for transfers between devices: 5.51 us -> 4.74 us  [moved(): return lax.ppermute(x, AXES, pairs)]
  transfers between devices with their start and end apart: 9 -> 9, of which waited for: 4 -> 5; matrix products, arithmetic and copies ran while one was open for 0% -> 0% of each run, Pallas kernels for 21% -> 21%
where the time goes in v17:
time: 39.3 us; the launch traced here: 39.1 us
  starting transfers between devices  20.4 us (52%)
  Pallas kernels  13.8 us (35%)
  waiting for transfers between devices  4.74 us (12%)
    ppermute x9, starting transfers between devices, moved(): return lax.ppermute(x, AXES, pairs)  20.4 us
    pallas_call x9, Pallas kernels, call(): pl.pallas_call(functools.partial(kernel, **fixed), out_shape=outs, in_spe...  13.8 us
    ppermute x9, waiting for transfers between devices, moved(): return lax.ppermute(x, AXES, pairs)  4.74 us
  transfers between devices with their start and end apart: 9, of which 5 were waited for; matrix products, arithmetic and copies ran while one was open for 0% of the time, Pallas kernels for 21%

profile of v17, /device:TPU:1, one launch (start us, length us, event | category | flops | bytes accessed | tf_op | source)
XLA Modules:
  0.0 39.1 jit_solution(9204746281122622930)
XLA Ops:
  0.0 1.7 %start.1 = (f32[6,5,4,40,128]{4,3,2,1,0:T(8,128)S(1)}, f32[11,4,40,128]{3,2,1,0:T(8,128)S(1)}, f32[40,128]{1,0:T(8,128)S(1)}, f32[36,8,128]{2,1,0:T(8,128)S(1)},...) custom-call(f32[5,4,32,128]{3,2,1,0:T(8,128)} %adjoint_hbm.1, ...), custom_call_target="tpu_custom_call" | custom-call | tf_op jit(solution)/shard_map/start/pallas_call | solution.py:629
  1.7 2.1 %collective-permute-start = (f32[56,128]{1,0:T(8,128)S(1)}, f32[56,128]{1,0:T(8,128)S(1)}, u32[]{:S(2)}, u32[]{:S(2)}) collective-permute-start(f32[56,128]{1,0:T(8,128)S(1)} %get-tuple-element.44), channel_id=1, source_target_pairs={{0,4},{1,5},{2,6},{3,7},{4,0},{5,1},{6,2},{7,3},{8,12},{9,13},{10,... | collective-permute-start | bytes 86024 | tf_op jit(solution)/shard_map/ppermute | solution.py:599
  3.9 0.1 collective-permute-start.1
  3.9 0.8 %pack.1 = (f32[17,32,128]{2,1,0:T(8,128)S(1)}, f32[160,128]{1,0:T(8,128)S(1)}, f32[120,128]{1,0:T(8,128)S(1)}) custom-call(f32[6,5,4,40,128]{4,3,2,1,0:T(8,128)S(1)} %get-tuple-element.45.state_ref.state_in_ref, f32[11,4,40,128]{3,2,1,0:T(8,128)S(1)} %get-tuple-element.46.coef_ref.coef_in_ref, f32[40,128]{1,0:T(8,128)S(1)} %get-tuple-element.47.inv_ref.inv_in_ref, ...), custom_call_target="tpu_custom_call" | custom-call | tf_op jit(solution)/shard_map/pack/pallas_call | solution.py:629
  4.7 0.6 %synth.1 = (bf16[2,896,128]{2,1,0:T(8,128)(2,1)S(1)}, f32[152,128]{1,0:T(8,128)S(1)}) custom-call(s32[1,4]{1,0:T(1,128)S(1)} %get-tuple-element.50.blades_ref, f32[5,5,1,6]{3,2,1,0:T(1,128)S(1)} %get-tuple-element.51.jacobians_ref, f32[5,5,3,64]{3,2,1,0:T(4,128)S(1)} %get-tuple-element.52.giles_re_ref, f32[5,5,3,64]{3,2,1,0:T(4,128)S(1)} %get-tuple-element.53.giles_im_ref, ...), custom_call_target="tpu_custom_call" | custom-call | tf_op jit(solution)/shard_map/synth/pallas_call | solution.py:629
  5.4 0.0 collective-permute-done
  5.4 1.5 %collective-permute-start.2 = (f32[160,128]{1,0:T(8,128)S(1)}, f32[160,128]{1,0:T(8,128)S(1)}, u32[]{:S(2)}, u32[]{:S(2)}) collective-permute-start(f32[160,128]{1,0:T(8,128)S(1)} %slice_dynamic-update-slice_fusion), channel_id=1, source_target_pairs={{0,1},{1,0},{2,3},{3,2},{4,5},{5,4},{6,7},{7,6},{8,9},{9,8},{10,11... | collective-permute-start | bytes 245768 | tf_op jit(solution)/shard_map/ppermute | solution.py:599
  6.9 2.2 %collective-permute-start.3 = (f32[120,128]{1,0:T(8,128)S(1)}, f32[120,128]{1,0:T(8,128)S(1)}, u32[]{:S(2)}, u32[]{:S(2)}) collective-permute-start(f32[120,128]{1,0:T(8,128)S(1)} %slice_dynamic-update-slice_fusion.1), channel_id=1, source_target_pairs={{0,3},{1,2},{2,1},{3,0},{4,7},{5,6},{6,5},{7,4},{8,11},{9,10},{10,... | collective-permute-start | bytes 184328 | tf_op jit(solution)/shard_map/ppermute | solution.py:599
  9.1 0.0 collective-permute-done.2.inner_ref
  9.1 2.4 %collective-permute-start.4 = (f32[40,128]{1,0:T(8,128)S(1)}, f32[40,128]{1,0:T(8,128)S(1)}, u32[]{:S(2)}, u32[]{:S(2)}) collective-permute-start(f32[40,128]{1,0:T(8,128)S(1)} %slice_add_fusion), channel_id=1, source_target_pairs={{0,2},{1,3},{2,0},{3,1},{4,6},{5,7},{6,4},{7,5},{8,10},{9,11},{10,... | collective-permute-start | bytes 61448 | tf_op jit(solution)/shard_map/ppermute | solution.py:599
  11.5 0.3 collective-permute-done.3.outer_ref
  11.8 0.0 collective-permute-done.1.span_ref
  11.8 1.7 %first_sweep.1 = (f32[11,4,40,128]{3,2,1,0:T(8,128)S(1)}, f32[40,128]{1,0:T(8,128)S(1)}, f32[12,40,128]{2,1,0:T(8,128)S(1)}, f32[6,5,4,40,128]{4,3,2,1,0:T(8,128)S(1)}, f32[5,5,40,128]{3,2,1,0:T(8,128)S(1)}) custom-call(f32[152,128]{1,0:T(8,128)S(1)} %get-tuple-element.57.jac_ref, ...), custom_call_target="tpu_custom_call", output_to_operand_aliasing={{3}: (1, {}), {0}: (2, {}), {1}: (3, {})} | custom-call | tf_op jit(solution)/shard_map/first_sweep/pallas_call | solution.py:629
  13.5 0.0 collective-permute-done.4
  13.5 5.2 %collective-permute-start.5 = (f32[40,128]{1,0:T(8,128)S(1)}, f32[40,128]{1,0:T(8,128)S(1)}, u32[]{:S(2)}, u32[]{:S(2)}) collective-permute-start(f32[40,128]{1,0:T(8,128)S(1)} %add.10), channel_id=1, source_target_pairs={{8,0},{9,1},{10,2},{11,3},{12,4},{13,5},{14,6},{15,7},{16,8},{17,9... | collective-permute-start | bytes 61448 | tf_op jit(solution)/shard_map/ppermute | solution.py:599
  18.8 2.5 %more_sweeps.1 = (f32[6,5,4,40,128]{4,3,2,1,0:T(8,128)S(1)}, f32[5,5,40,128]{3,2,1,0:T(8,128)S(1)}, f32[104,128]{1,0:T(8,128)S(1)}, f32[32,128]{1,0:T(8,128)S(1)}) custom-call(f32[152,128]{1,0:T(8,128)S(1)} %get-tuple-element.57.jac_ref, f32[11,4,40,128]{3,2,1,0:T(8,128)S(1)} %get-tuple-element.63.coef_ref, ...), custom_call_target="tpu_custom_call", output_to_operand_aliasing={{0}: (3, {}), {1}: (4, {})} | custom-call | tf_op jit(solution)/shard_map/more_sweeps/pallas_call | solution.py:629
  21.2 0.1 collective-permute-done.5.first_ref.modes_ref
  21.3 0.6 %late_modes.1.more_ref = f32[136,128]{1,0:T(8,128)S(1)} custom-call(f32[152,128]{1,0:T(8,128)S(1)} %get-tuple-element.57.jac_ref, f32[11,4,40,128]{3,2,1,0:T(8,128)S(1)} %get-tuple-element.63.coef_ref, f32[40,128]{1,0:T(8,128)S(1)} %get-tuple-element.65.inv_ref, f32[32,128]{1,0:T(8,128)S(1)} %get-tuple-element.74.part_ref, ...), custom_call_target="tpu_custom_call" | custom-call | tf_op jit(solution)/shard_map/late_modes/pallas_call | solution.py:629
  21.9 2.7 %collective-permute-start.6 = (f32[136,128]{1,0:T(8,128)S(1)}, f32[136,128]{1,0:T(8,128)S(1)}, u32[]{:S(2)}, u32[]{:S(2)}) collective-permute-start(f32[136,128]{1,0:T(8,128)S(1)} %late_modes.1.more_ref), channel_id=1, source_target_pairs={{8,1},{9,0},{10,3},{11,2},{12,5},{13,4},{14,7},{15,6},{16,9},{17,8... | collective-permute-start | bytes 208904 | tf_op jit(solution)/shard_map/ppermute | solution.py:599
  24.6 1.9 %collective-permute-start.7 = (f32[136,128]{1,0:T(8,128)S(1)}, f32[136,128]{1,0:T(8,128)S(1)}, u32[]{:S(2)}, u32[]{:S(2)}) collective-permute-start(f32[136,128]{1,0:T(8,128)S(1)} %late_modes.1.more_ref), channel_id=1, source_target_pairs={{8,0},{9,1},{10,2},{11,3},{12,4},{13,5},{14,6},{15,7},{16,8},{17,9... | collective-permute-start | bytes 208904 | tf_op jit(solution)/shard_map/ppermute | solution.py:599
  26.6 1.7 %between_sweeps.1 = (f32[6,5,4,40,128]{4,3,2,1,0:T(8,128)S(1)}, f32[5,5,40,128]{3,2,1,0:T(8,128)S(1)}) custom-call(f32[152,128]{1,0:T(8,128)S(1)} %get-tuple-element.57.jac_ref, f32[11,4,40,128]{3,2,1,0:T(8,128)S(1)} %get-tuple-element.63.coef_ref, f32[40,128]{1,0:T(8,128)S(1)} %get-tuple-element.65.inv_ref, ...), custom_call_target="tpu_custom_call", output_to_operand_aliasing={{0}: (4, {}), {1}: (5, {})} | custom-call | tf_op jit(solution)/shard_map/between_sweeps/pallas_call | solution.py:629
  28.2 0.3 collective-permute-done.6
  28.5 2.3 %collective-permute-done.7 = f32[136,128]{1,0:T(8,128)S(1)} collective-permute-done((f32[136,128]{1,0:T(8,128)S(1)}, f32[136,128]{1,0:T(8,128)S(1)}, u32[]{:S(2)}, u32[]{:S(2)}) %collective-permute-start.7) | collective-permute-done | bytes 69664 | tf_op jit(solution)/shard_map/ppermute | solution.py:599
  30.8 2.3 %collective-permute-start.8 = (f32[136,128]{1,0:T(8,128)S(1)}, f32[136,128]{1,0:T(8,128)S(1)}, u32[]{:S(2)}, u32[]{:S(2)}) collective-permute-start(f32[136,128]{1,0:T(8,128)S(1)} %add.11.more_a_ref), channel_id=1, source_target_pairs={{0,2},{1,3},{2,0},{3,1},{4,6},{5,7},{6,4},{7,5},{8,10},{9,11},{10,... | collective-permute-start | bytes 208904 | tf_op jit(solution)/shard_map/ppermute | solution.py:599
  33.1 0.8 %beside_sweeps.1 = (f32[6,5,4,40,128]{4,3,2,1,0:T(8,128)S(1)}, f32[5,5,40,128]{3,2,1,0:T(8,128)S(1)}) custom-call(f32[152,128]{1,0:T(8,128)S(1)} %get-tuple-element.57.jac_ref, f32[11,4,40,128]{3,2,1,0:T(8,128)S(1)} %get-tuple-element.63.coef_ref, f32[12,40,128]{2,1,0:T(8,128)S(1)} %get-tuple-element.66.edge_coef_ref, ...), custom_call_target="tpu_custom_call", output_to_operand_aliasing={{0}: (3, {}), {1}: (4, {})} | custom-call | tf_op jit(solution)/shard_map/beside_sweeps/pallas_call | solution.py:629
  33.8 1.8 %collective-permute-done.8.more_b_ref = f32[136,128]{1,0:T(8,128)S(1)} collective-permute-done((f32[136,128]{1,0:T(8,128)S(1)}, f32[136,128]{1,0:T(8,128)S(1)}, u32[]{:S(2)}, u32[]{:S(2)}) %collective-permute-start.8) | collective-permute-done | bytes 69664 | tf_op jit(solution)/shard_map/ppermute | solution.py:599
  35.7 3.4 %second_sweeps.1 = (f32[6,5,4,40,128]{4,3,2,1,0:T(8,128)S(1)}, f32[5,5,40,128]{3,2,1,0:T(8,128)S(1)}, f32[5,4,32,128]{3,2,1,0:T(8,128)}) custom-call(f32[152,128]{1,0:T(8,128)S(1)} %get-tuple-element.57.jac_ref, f32[11,4,40,128]{3,2,1,0:T(8,128)S(1)} %get-tuple-element.63.coef_ref, ...), custom_call_target="tpu_custom_call", output_to_operand_aliasing={{0}: (4, {}), {1}: (5, {})} | custom-call | tf_op jit(solution)/shard_map/second_sweeps/pallas_call | solution.py:629
  (5 shorter events, 0.0 us)
Async XLA Ops:
  1.7 3.7 %collective-permute-start = (f32[56,128]{1,0:T(8,128)S(1)}, f32[56,128]{1,0:T(8,128)S(1)}, u32[]{:S(2)}, u32[]{:S(2)}) collective-permute-start(f32[56,128]{1,0:T(8,128)S(1)} %get-tuple-element.44), channel_id=1, source_target_pairs={{0,4},{1,5},{2,6},{3,7},{4,0},{5,1},{6,2},{7,3},{8,12},{9,13},{10,... | collective-permute-start | bytes 86024 | tf_op jit(solution)/shard_map/ppermute | solution.py:599
  3.9 7.9 %collective-permute-start.1 = (f32[36,8,128]{2,1,0:T(8,128)S(1)}, f32[36,8,128]{2,1,0:T(8,128)S(1)}, u32[]{:S(2)}, u32[]{:S(2)}) collective-permute-start(f32[36,8,128]{2,1,0:T(8,128)S(1)} %get-tuple-element.59), channel_id=1, source_target_pairs={{0,4},{1,5},{2,6},{3,7},{4,0},{5,1},{6,2},{7,3},{8,12},{9,13},{10,... | collective-permute-start | bytes 442376 | tf_op jit(solution)/shard_map/ppermute | solution.py:599
  5.4 3.7 %collective-permute-start.2 = (f32[160,128]{1,0:T(8,128)S(1)}, f32[160,128]{1,0:T(8,128)S(1)}, u32[]{:S(2)}, u32[]{:S(2)}) collective-permute-start(f32[160,128]{1,0:T(8,128)S(1)} %slice_dynamic-update-slice_fusion), channel_id=1, source_target_pairs={{0,1},{1,0},{2,3},{3,2},{4,5},{5,4},{6,7},{7,6},{8,9},{9,8},{10,11... | collective-permute-start | bytes 245768 | tf_op jit(solution)/shard_map/ppermute | solution.py:599
  6.9 4.9 %collective-permute-start.3 = (f32[120,128]{1,0:T(8,128)S(1)}, f32[120,128]{1,0:T(8,128)S(1)}, u32[]{:S(2)}, u32[]{:S(2)}) collective-permute-start(f32[120,128]{1,0:T(8,128)S(1)} %slice_dynamic-update-slice_fusion.1), channel_id=1, source_target_pairs={{0,3},{1,2},{2,1},{3,0},{4,7},{5,6},{6,5},{7,4},{8,11},{9,10},{10,... | collective-permute-start | bytes 184328 | tf_op jit(solution)/shard_map/ppermute | solution.py:599
  9.1 4.4 %collective-permute-start.4 = (f32[40,128]{1,0:T(8,128)S(1)}, f32[40,128]{1,0:T(8,128)S(1)}, u32[]{:S(2)}, u32[]{:S(2)}) collective-permute-start(f32[40,128]{1,0:T(8,128)S(1)} %slice_add_fusion), channel_id=1, source_target_pairs={{0,2},{1,3},{2,0},{3,1},{4,6},{5,7},{6,4},{7,5},{8,10},{9,11},{10,... | collective-permute-start | bytes 61448 | tf_op jit(solution)/shard_map/ppermute | solution.py:599
  13.5 7.8 %collective-permute-start.5 = (f32[40,128]{1,0:T(8,128)S(1)}, f32[40,128]{1,0:T(8,128)S(1)}, u32[]{:S(2)}, u32[]{:S(2)}) collective-permute-start(f32[40,128]{1,0:T(8,128)S(1)} %add.10), channel_id=1, source_target_pairs={{8,0},{9,1},{10,2},{11,3},{12,4},{13,5},{14,6},{15,7},{16,8},{17,9... | collective-permute-start | bytes 61448 | tf_op jit(solution)/shard_map/ppermute | solution.py:599
  21.9 6.6 %collective-permute-start.6 = (f32[136,128]{1,0:T(8,128)S(1)}, f32[136,128]{1,0:T(8,128)S(1)}, u32[]{:S(2)}, u32[]{:S(2)}) collective-permute-start(f32[136,128]{1,0:T(8,128)S(1)} %late_modes.1.more_ref), channel_id=1, source_target_pairs={{8,1},{9,0},{10,3},{11,2},{12,5},{13,4},{14,7},{15,6},{16,9},{17,8... | collective-permute-start | bytes 208904 | tf_op jit(solution)/shard_map/ppermute | solution.py:599
  24.6 6.1 %collective-permute-start.7 = (f32[136,128]{1,0:T(8,128)S(1)}, f32[136,128]{1,0:T(8,128)S(1)}, u32[]{:S(2)}, u32[]{:S(2)}) collective-permute-start(f32[136,128]{1,0:T(8,128)S(1)} %late_modes.1.more_ref), channel_id=1, source_target_pairs={{8,0},{9,1},{10,2},{11,3},{12,4},{13,5},{14,6},{15,7},{16,8},{17,9... | collective-permute-start | bytes 208904 | tf_op jit(solution)/shard_map/ppermute | solution.py:599
  30.8 4.9 %collective-permute-start.8 = (f32[136,128]{1,0:T(8,128)S(1)}, f32[136,128]{1,0:T(8,128)S(1)}, u32[]{:S(2)}, u32[]{:S(2)}) collective-permute-start(f32[136,128]{1,0:T(8,128)S(1)} %add.11.more_a_ref), channel_id=1, source_target_pairs={{0,2},{1,3},{2,0},{3,1},{4,6},{5,7},{6,4},{7,5},{8,10},{9,11},{10,... | collective-permute-start | bytes 208904 | tf_op jit(solution)/shard_map/ppermute | solution.py:599

commit v18 on v15

--- a/solution.py
+++ b/solution.py
@@ -144,8 +144,9 @@
     cos_table, sin_table = waves(number * (place * pitch + rows((pitch, pitch))), length)
     table = jnp.where(component < components, jnp.where(sine, sin_table, cos_table), 0.0)
     for c in range(components):
-        for n, value in enumerate(split(jnp.where(component == c, table, 0.0))):
-            table_ref[n, pl.ds(c * pitch, pitch), :] = value
+        high, low = split(jnp.where(component == c, table, 0.0))
+        for n, value in enumerate((high, high, low)):
+            table_ref[pl.ds((n * components + c) * pitch, pitch), :] = value
     copies[0].wait()
     copies[1].wait()
     diag = damping_ref[...]
@@ -212,19 +213,18 @@
     return high, (x - high.astype(jnp.float32)).astype(jnp.bfloat16)
 
 
-def product(x, table, dims):
-    x_high, x_low = split(x)
-    table_high, table_low = table
-    dot = functools.partial(lax.dot_general, dimension_numbers=(dims, ((), ())), preferred_element_type=jnp.float32)
-    return dot(x_high, table_high) + (dot(x_low, table_high) + dot(x_high, table_low))
+def thrice(x):
+    high, low = split(x)
+    return jnp.concatenate([high, low, high], 1)
 
 
 def projected(strips, table_ref):
-    return product(jnp.concatenate(strips, 1), (table_ref[0], table_ref[1]), ((1,), (0,)))
+    return jnp.dot(thrice(jnp.concatenate(strips, 1)), table_ref[...], preferred_element_type=jnp.float32)
 
 
 def synthesised(modes, synth_ref, count):
-    return product(modes, (synth_ref[0, :count], synth_ref[1, :count]), ((1,), (1,)))
+    dims = (((1,), (1,)), ((), ()))
+    return lax.dot_general(thrice(modes), synth_ref[:count], dims, preferred_element_type=jnp.float32)
 
 
 def synth_kernel(
@@ -287,13 +287,14 @@
             row_cos = jnp.where(component == b, with_cos[at:at + 1], row_cos)
             row_sin = jnp.where(component == b, with_sin[at:at + 1], row_sin)
         part = row_cos * cos_table + row_sin * sin_table
-        for n, value in enumerate(split(part)):
-            synth_ref[n, pl.ds(c * pitch, pitch), :] = value[:pitch]
-            synth_ref[n, pl.ds(components * pitch + c * SEGMENT_LANES, SEGMENT_LANES), :] = value[pitch:]
+        high, low = split(part)
+        value = jnp.concatenate([high, high, low], 1)
+        synth_ref[pl.ds(c * pitch, pitch), :] = value[:pitch]
+        synth_ref[pl.ds(components * pitch + c * SEGMENT_LANES, SEGMENT_LANES), :] = value[pitch:]
     used = components * (pitch + SEGMENT_LANES)
-    rest = synth_ref.shape[1] - used
+    rest = synth_ref.shape[0] - used
     if rest:
-        synth_ref[:, pl.ds(used, rest), :] = jnp.zeros((2, rest, pitch), jnp.bfloat16)
+        synth_ref[pl.ds(used, rest), :] = jnp.zeros((rest, 3 * pitch), jnp.bfloat16)
 
 
 def jacobian(jac_ref, components, b, c, d):
@@ -508,7 +509,7 @@
     components, axial = state_ref.shape[1], state_ref.shape[2]
     wide, pitch = state_ref.shape[3:]
     modes = modes_ref[...]
-    field = synthesised(jnp.concatenate([modes[EDGE:], modes[:EDGE]], 0), synth_ref, synth_ref.shape[1])
+    field = synthesised(jnp.concatenate([modes[EDGE:], modes[:EDGE]], 0), synth_ref, synth_ref.shape[0])
     delta = [inv_ref[...] * field[:, c * pitch:(c + 1) * pitch] for c in range(components)]
     for t in range(1, axial + 1):
         for c in range(components):
@@ -548,7 +549,7 @@
     for t in range(1, axial):
         _, _, from_packed = ghost_rows(side, t, axial)
         parts += [more[(t - 1) * span:t * span], pltpu.roll(more[start:start + EDGE], from_packed, 0)]
-    field = synthesised(jnp.concatenate(parts + [more[start + EDGE:]], 0), synth_ref, synth_ref.shape[1])
+    field = synthesised(jnp.concatenate(parts + [more[start + EDGE:]], 0), synth_ref, synth_ref.shape[0])
     for t in range(1, axial):
         part = field[(t - 1) * wide:t * wide]
         for c in range(components):
@@ -650,7 +651,7 @@
         (
             state_shape, struct(components + 6, axial, wide, pitch), struct(wide, pitch),
             struct(span_tiles, EDGE, pitch), struct(2 * corner_rows + EDGE, pitch), struct(span, pitch),
-            jax.ShapeDtypeStruct((2, components * pitch, pitch), jnp.bfloat16),
+            jax.ShapeDtypeStruct((3 * components * pitch, pitch), jnp.bfloat16),
             *(jax.ShapeDtypeStruct(x.shape, x.dtype) for x in (blades, *tables)),
         ),
         [(hbm, in_hbm(x)) for x in (adjoint_start, source, couplings, damping, blades, *tables)],
@@ -679,7 +680,7 @@
         synth_kernel, "synth",
         (
             jax.ShapeDtypeStruct(
-                (2, -(-components * (pitch + SEGMENT_LANES) // pitch) * pitch, pitch), jnp.bfloat16
+                (-(-components * (pitch + SEGMENT_LANES) // pitch) * pitch, 3 * pitch), jnp.bfloat16
             ),
             struct(-(-6 * components * components // EDGE) * EDGE, pitch),
         ),

time: 39.1 us -> 38.9 us (level)
  no operation moved by 1% of the time
where the time goes in v18:
time: 38.9 us; the launch traced here: 38.7 us
  starting transfers between devices  21.2 us (54%)
  Pallas kernels  13.2 us (34%)
  waiting for transfers between devices  4.13 us (11%)
    ppermute x9, starting transfers between devices, moved(): return lax.ppermute(x, AXES, pairs)  21.2 us
    pallas_call x9, Pallas kernels, call(): pl.pallas_call(functools.partial(kernel, **fixed), out_shape=outs, in_spe...  13.2 us
    ppermute x9, waiting for transfers between devices, moved(): return lax.ppermute(x, AXES, pairs)  4.13 us
  transfers between devices with their start and end apart: 9, of which 4 were waited for; matrix products, arithmetic and copies ran while one was open for 0% of the time, Pallas kernels for 20%

profile of v18, /device:TPU:1, one launch (start us, length us, event | category | flops | bytes accessed | tf_op | source)
XLA Modules:
  0.0 38.7 jit_solution(15201557592843714728)
XLA Ops:
  0.0 1.7 %start.1 = (f32[6,5,4,40,128]{4,3,2,1,0:T(8,128)S(1)}, f32[11,4,40,128]{3,2,1,0:T(8,128)S(1)}, f32[40,128]{1,0:T(8,128)S(1)}, f32[36,8,128]{2,1,0:T(8,128)S(1)},...) custom-call(f32[5,4,32,128]{3,2,1,0:T(8,128)} %adjoint_hbm.1, ...), custom_call_target="tpu_custom_call" | custom-call | tf_op jit(solution)/shard_map/start/pallas_call | solution.py:631
  1.7 2.1 %collective-permute-start = (f32[56,128]{1,0:T(8,128)S(1)}, f32[56,128]{1,0:T(8,128)S(1)}, u32[]{:S(2)}, u32[]{:S(2)}) collective-permute-start(f32[56,128]{1,0:T(8,128)S(1)} %get-tuple-element.43), channel_id=1, source_target_pairs={{0,4},{1,5},{2,6},{3,7},{4,0},{5,1},{6,2},{7,3},{8,12},{9,13},{10,... | collective-permute-start | bytes 86024 | tf_op jit(solution)/shard_map/ppermute | solution.py:601
  3.9 0.1 collective-permute-start.1
  3.9 0.8 %pack.1 = (f32[17,32,128]{2,1,0:T(8,128)S(1)}, f32[160,128]{1,0:T(8,128)S(1)}, f32[120,128]{1,0:T(8,128)S(1)}) custom-call(f32[6,5,4,40,128]{4,3,2,1,0:T(8,128)S(1)} %get-tuple-element.44.state_ref.state_in_ref, f32[11,4,40,128]{3,2,1,0:T(8,128)S(1)} %get-tuple-element.45.coef_ref.coef_in_ref, f32[40,128]{1,0:T(8,128)S(1)} %get-tuple-element.46.inv_ref.inv_in_ref, ...), custom_call_target="tpu_custom_call" | custom-call | tf_op jit(solution)/shard_map/pack/pallas_call | solution.py:631
  4.7 0.7 %synth.1 = (bf16[896,384]{1,0:T(8,128)(2,1)S(1)}, f32[152,128]{1,0:T(8,128)S(1)}) custom-call(s32[1,4]{1,0:T(1,128)S(1)} %get-tuple-element.49.blades_ref, f32[5,5,1,6]{3,2,1,0:T(1,128)S(1)} %get-tuple-element.50.jacobians_ref, f32[5,5,3,64]{3,2,1,0:T(4,128)S(1)} %get-tuple-element.51.giles_re_ref, f32[5,5,3,64]{3,2,1,0:T(4,128)S(1)} %get-tuple-element.52.giles_im_ref, ...), custom_call_target="tpu_custom_call" | custom-call | tf_op jit(solution)/shard_map/synth/pallas_call | solution.py:631
  5.4 0.0 collective-permute-done
  5.4 1.5 %collective-permute-start.2 = (f32[160,128]{1,0:T(8,128)S(1)}, f32[160,128]{1,0:T(8,128)S(1)}, u32[]{:S(2)}, u32[]{:S(2)}) collective-permute-start(f32[160,128]{1,0:T(8,128)S(1)} %slice_dynamic-update-slice_fusion), channel_id=1, source_target_pairs={{0,1},{1,0},{2,3},{3,2},{4,5},{5,4},{6,7},{7,6},{8,9},{9,8},{10,11... | collective-permute-start | bytes 245768 | tf_op jit(solution)/shard_map/ppermute | solution.py:601
  6.9 2.2 %collective-permute-start.3 = (f32[120,128]{1,0:T(8,128)S(1)}, f32[120,128]{1,0:T(8,128)S(1)}, u32[]{:S(2)}, u32[]{:S(2)}) collective-permute-start(f32[120,128]{1,0:T(8,128)S(1)} %slice_dynamic-update-slice_fusion.1), channel_id=1, source_target_pairs={{0,3},{1,2},{2,1},{3,0},{4,7},{5,6},{6,5},{7,4},{8,11},{9,10},{10,... | collective-permute-start | bytes 184328 | tf_op jit(solution)/shard_map/ppermute | solution.py:601
  9.1 0.0 collective-permute-done.2.inner_ref
  9.1 2.4 %collective-permute-start.4 = (f32[40,128]{1,0:T(8,128)S(1)}, f32[40,128]{1,0:T(8,128)S(1)}, u32[]{:S(2)}, u32[]{:S(2)}) collective-permute-start(f32[40,128]{1,0:T(8,128)S(1)} %slice_add_fusion), channel_id=1, source_target_pairs={{0,2},{1,3},{2,0},{3,1},{4,6},{5,7},{6,4},{7,5},{8,10},{9,11},{10,... | collective-permute-start | bytes 61448 | tf_op jit(solution)/shard_map/ppermute | solution.py:601
  11.5 0.3 collective-permute-done.3.outer_ref
  11.8 0.0 collective-permute-done.1.span_ref
  11.8 1.7 %first_sweep.1 = (f32[11,4,40,128]{3,2,1,0:T(8,128)S(1)}, f32[40,128]{1,0:T(8,128)S(1)}, f32[12,40,128]{2,1,0:T(8,128)S(1)}, f32[6,5,4,40,128]{4,3,2,1,0:T(8,128)S(1)}, f32[5,5,40,128]{3,2,1,0:T(8,128)S(1)}) custom-call(f32[152,128]{1,0:T(8,128)S(1)} %get-tuple-element.56.jac_ref, ...), custom_call_target="tpu_custom_call", output_to_operand_aliasing={{3}: (1, {}), {0}: (2, {}), {1}: (3, {})} | custom-call | tf_op jit(solution)/shard_map/first_sweep/pallas_call | solution.py:631
  13.5 0.0 collective-permute-done.4
  13.5 5.2 %collective-permute-start.5 = (f32[40,128]{1,0:T(8,128)S(1)}, f32[40,128]{1,0:T(8,128)S(1)}, u32[]{:S(2)}, u32[]{:S(2)}) collective-permute-start(f32[40,128]{1,0:T(8,128)S(1)} %add.10), channel_id=1, source_target_pairs={{8,0},{9,1},{10,2},{11,3},{12,4},{13,5},{14,6},{15,7},{16,8},{17,9... | collective-permute-start | bytes 61448 | tf_op jit(solution)/shard_map/ppermute | solution.py:601
  18.7 2.4 %more_sweeps.1 = (f32[6,5,4,40,128]{4,3,2,1,0:T(8,128)S(1)}, f32[5,5,40,128]{3,2,1,0:T(8,128)S(1)}, f32[104,128]{1,0:T(8,128)S(1)}, f32[32,128]{1,0:T(8,128)S(1)}) custom-call(f32[152,128]{1,0:T(8,128)S(1)} %get-tuple-element.56.jac_ref, f32[11,4,40,128]{3,2,1,0:T(8,128)S(1)} %get-tuple-element.62.coef_ref, ...), custom_call_target="tpu_custom_call", output_to_operand_aliasing={{0}: (3, {}), {1}: (4, {})} | custom-call | tf_op jit(solution)/shard_map/more_sweeps/pallas_call | solution.py:631
  21.1 0.1 collective-permute-done.5.first_ref.modes_ref
  21.3 0.5 %late_modes.1.more_ref = f32[136,128]{1,0:T(8,128)S(1)} custom-call(f32[152,128]{1,0:T(8,128)S(1)} %get-tuple-element.56.jac_ref, f32[11,4,40,128]{3,2,1,0:T(8,128)S(1)} %get-tuple-element.62.coef_ref, f32[40,128]{1,0:T(8,128)S(1)} %get-tuple-element.64.inv_ref, f32[32,128]{1,0:T(8,128)S(1)} %get-tuple-element.73.part_ref, ...), custom_call_target="tpu_custom_call" | custom-call | tf_op jit(solution)/shard_map/late_modes/pallas_call | solution.py:631
  21.8 1.7 %collective-permute-start.6 = (f32[136,128]{1,0:T(8,128)S(1)}, f32[136,128]{1,0:T(8,128)S(1)}, u32[]{:S(2)}, u32[]{:S(2)}) collective-permute-start(f32[136,128]{1,0:T(8,128)S(1)} %late_modes.1.more_ref), channel_id=1, source_target_pairs={{0,1},{1,0},{2,3},{3,2},{4,5},{5,4},{6,7},{7,6},{8,9},{9,8},{10,11... | collective-permute-start | bytes 208904 | tf_op jit(solution)/shard_map/ppermute | solution.py:601
  23.5 1.5 %between_sweeps.1 = (f32[6,5,4,40,128]{4,3,2,1,0:T(8,128)S(1)}, f32[5,5,40,128]{3,2,1,0:T(8,128)S(1)}, f32[136,128]{1,0:T(8,128)S(1)}) custom-call(f32[152,128]{1,0:T(8,128)S(1)} %get-tuple-element.56.jac_ref, f32[11,4,40,128]{3,2,1,0:T(8,128)S(1)} %get-tuple-element.62.coef_ref, ...), custom_call_target="tpu_custom_call", output_to_operand_aliasing={{0}: (4, {}), {1}: (5, {})} | custom-call | tf_op jit(solution)/shard_map/between_sweeps/pallas_call | solution.py:631
  25.0 0.4 %collective-permute-done.6 = f32[136,128]{1,0:T(8,128)S(1)} collective-permute-done((f32[136,128]{1,0:T(8,128)S(1)}, f32[136,128]{1,0:T(8,128)S(1)}, u32[]{:S(2)}, u32[]{:S(2)}) %collective-permute-start.6) | collective-permute-done | bytes 69664 | tf_op jit(solution)/shard_map/ppermute | solution.py:601
  25.5 4.1 %collective-permute-start.8 = (f32[136,128]{1,0:T(8,128)S(1)}, f32[136,128]{1,0:T(8,128)S(1)}, u32[]{:S(2)}, u32[]{:S(2)}) collective-permute-start(f32[136,128]{1,0:T(8,128)S(1)} %add.11), channel_id=1, source_target_pairs={{8,2},{9,3},{10,0},{11,1},{12,6},{13,7},{14,4},{15,5},{16,10},{17,... | collective-permute-start | bytes 208904 | tf_op jit(solution)/shard_map/ppermute | solution.py:601
  29.6 1.9 %collective-permute-start.7 = (f32[136,128]{1,0:T(8,128)S(1)}, f32[136,128]{1,0:T(8,128)S(1)}, u32[]{:S(2)}, u32[]{:S(2)}) collective-permute-start(f32[136,128]{1,0:T(8,128)S(1)} %add.11), channel_id=1, source_target_pairs={{8,0},{9,1},{10,2},{11,3},{12,4},{13,5},{14,6},{15,7},{16,8},{17,9... | collective-permute-start | bytes 208904 | tf_op jit(solution)/shard_map/ppermute | solution.py:601
  31.5 0.7 %beside_sweeps.1 = (f32[6,5,4,40,128]{4,3,2,1,0:T(8,128)S(1)}, f32[5,5,40,128]{3,2,1,0:T(8,128)S(1)}) custom-call(f32[152,128]{1,0:T(8,128)S(1)} %get-tuple-element.56.jac_ref, f32[11,4,40,128]{3,2,1,0:T(8,128)S(1)} %get-tuple-element.62.coef_ref, f32[12,40,128]{2,1,0:T(8,128)S(1)} %get-tuple-element.65.edge_coef_ref, ...), custom_call_target="tpu_custom_call", output_to_operand_aliasing={{0}: (3, {}), {1}: (4, {})} | custom-call | tf_op jit(solution)/shard_map/beside_sweeps/pallas_call | solution.py:631
  32.2 3.3 %collective-permute-done.8.more_b_ref = f32[136,128]{1,0:T(8,128)S(1)} collective-permute-done((f32[136,128]{1,0:T(8,128)S(1)}, f32[136,128]{1,0:T(8,128)S(1)}, u32[]{:S(2)}, u32[]{:S(2)}) %collective-permute-start.8) | collective-permute-done | bytes 69664 | tf_op jit(solution)/shard_map/ppermute | solution.py:601
  35.5 0.0 collective-permute-done.7.more_a_ref
  35.5 3.2 %second_sweeps.1 = (f32[6,5,4,40,128]{4,3,2,1,0:T(8,128)S(1)}, f32[5,5,40,128]{3,2,1,0:T(8,128)S(1)}, f32[5,4,32,128]{3,2,1,0:T(8,128)}) custom-call(f32[152,128]{1,0:T(8,128)S(1)} %get-tuple-element.56.jac_ref, f32[11,4,40,128]{3,2,1,0:T(8,128)S(1)} %get-tuple-element.62.coef_ref, ...), custom_call_target="tpu_custom_call", output_to_operand_aliasing={{0}: (4, {}), {1}: (5, {})} | custom-call | tf_op jit(solution)/shard_map/second_sweeps/pallas_call | solution.py:631
  (5 shorter events, 0.0 us)
Async XLA Ops:
  1.7 3.7 %collective-permute-start = (f32[56,128]{1,0:T(8,128)S(1)}, f32[56,128]{1,0:T(8,128)S(1)}, u32[]{:S(2)}, u32[]{:S(2)}) collective-permute-start(f32[56,128]{1,0:T(8,128)S(1)} %get-tuple-element.43), channel_id=1, source_target_pairs={{0,4},{1,5},{2,6},{3,7},{4,0},{5,1},{6,2},{7,3},{8,12},{9,13},{10,... | collective-permute-start | bytes 86024 | tf_op jit(solution)/shard_map/ppermute | solution.py:601
  3.9 7.9 %collective-permute-start.1 = (f32[36,8,128]{2,1,0:T(8,128)S(1)}, f32[36,8,128]{2,1,0:T(8,128)S(1)}, u32[]{:S(2)}, u32[]{:S(2)}) collective-permute-start(f32[36,8,128]{2,1,0:T(8,128)S(1)} %get-tuple-element.58), channel_id=1, source_target_pairs={{0,4},{1,5},{2,6},{3,7},{4,0},{5,1},{6,2},{7,3},{8,12},{9,13},{10,... | collective-permute-start | bytes 442376 | tf_op jit(solution)/shard_map/ppermute | solution.py:601
  5.4 3.7 %collective-permute-start.2 = (f32[160,128]{1,0:T(8,128)S(1)}, f32[160,128]{1,0:T(8,128)S(1)}, u32[]{:S(2)}, u32[]{:S(2)}) collective-permute-start(f32[160,128]{1,0:T(8,128)S(1)} %slice_dynamic-update-slice_fusion), channel_id=1, source_target_pairs={{0,1},{1,0},{2,3},{3,2},{4,5},{5,4},{6,7},{7,6},{8,9},{9,8},{10,11... | collective-permute-start | bytes 245768 | tf_op jit(solution)/shard_map/ppermute | solution.py:601
  6.9 4.9 %collective-permute-start.3 = (f32[120,128]{1,0:T(8,128)S(1)}, f32[120,128]{1,0:T(8,128)S(1)}, u32[]{:S(2)}, u32[]{:S(2)}) collective-permute-start(f32[120,128]{1,0:T(8,128)S(1)} %slice_dynamic-update-slice_fusion.1), channel_id=1, source_target_pairs={{0,3},{1,2},{2,1},{3,0},{4,7},{5,6},{6,5},{7,4},{8,11},{9,10},{10,... | collective-permute-start | bytes 184328 | tf_op jit(solution)/shard_map/ppermute | solution.py:601
  9.1 4.3 %collective-permute-start.4 = (f32[40,128]{1,0:T(8,128)S(1)}, f32[40,128]{1,0:T(8,128)S(1)}, u32[]{:S(2)}, u32[]{:S(2)}) collective-permute-start(f32[40,128]{1,0:T(8,128)S(1)} %slice_add_fusion), channel_id=1, source_target_pairs={{0,2},{1,3},{2,0},{3,1},{4,6},{5,7},{6,4},{7,5},{8,10},{9,11},{10,... | collective-permute-start | bytes 61448 | tf_op jit(solution)/shard_map/ppermute | solution.py:601
  13.5 7.8 %collective-permute-start.5 = (f32[40,128]{1,0:T(8,128)S(1)}, f32[40,128]{1,0:T(8,128)S(1)}, u32[]{:S(2)}, u32[]{:S(2)}) collective-permute-start(f32[40,128]{1,0:T(8,128)S(1)} %add.10), channel_id=1, source_target_pairs={{8,0},{9,1},{10,2},{11,3},{12,4},{13,5},{14,6},{15,7},{16,8},{17,9... | collective-permute-start | bytes 61448 | tf_op jit(solution)/shard_map/ppermute | solution.py:601
  21.8 3.7 %collective-permute-start.6 = (f32[136,128]{1,0:T(8,128)S(1)}, f32[136,128]{1,0:T(8,128)S(1)}, u32[]{:S(2)}, u32[]{:S(2)}) collective-permute-start(f32[136,128]{1,0:T(8,128)S(1)} %late_modes.1.more_ref), channel_id=1, source_target_pairs={{0,1},{1,0},{2,3},{3,2},{4,5},{5,4},{6,7},{7,6},{8,9},{9,8},{10,11... | collective-permute-start | bytes 208904 | tf_op jit(solution)/shard_map/ppermute | solution.py:601
  25.5 10.0 %collective-permute-start.8 = (f32[136,128]{1,0:T(8,128)S(1)}, f32[136,128]{1,0:T(8,128)S(1)}, u32[]{:S(2)}, u32[]{:S(2)}) collective-permute-start(f32[136,128]{1,0:T(8,128)S(1)} %add.11), channel_id=1, source_target_pairs={{8,2},{9,3},{10,0},{11,1},{12,6},{13,7},{14,4},{15,5},{16,10},{17,... | collective-permute-start | bytes 208904 | tf_op jit(solution)/shard_map/ppermute | solution.py:601
  29.6 5.9 %collective-permute-start.7 = (f32[136,128]{1,0:T(8,128)S(1)}, f32[136,128]{1,0:T(8,128)S(1)}, u32[]{:S(2)}, u32[]{:S(2)}) collective-permute-start(f32[136,128]{1,0:T(8,128)S(1)} %add.11), channel_id=1, source_target_pairs={{8,0},{9,1},{10,2},{11,3},{12,4},{13,5},{14,6},{15,7},{16,8},{17,9... | collective-permute-start | bytes 208904 | tf_op jit(solution)/shard_map/ppermute | solution.py:601

commit v19 on v18

--- a/solution.py
+++ b/solution.py
@@ -19,6 +19,7 @@
 EDGE = 8
 HALF = EDGE // 2
 SEGMENT_LANES = 4 * EDGE
+SHARED_LANES = SEGMENT_LANES // 2
 EXACT = lax.Precision.HIGHEST
 MIB = 1024 * 1024
 
@@ -197,9 +198,12 @@
     for f, block in enumerate(blocks):
         edges_ref[f] = block
     for out_ref, packed in zip((inner_ref, outer_ref), packed_edges(blocks, place, components)):
-        for g, value in enumerate(packed):
+        for g, value in enumerate(packed[:-1]):
             out_ref[pl.ds(g * span, span), :] = value
-    start = groups * span + (groups + 1) * EDGE
+        low, high = packed[-1][:span // 2], packed[-1][span // 2:]
+        shared = jnp.where(lanes(low.shape) % SEGMENT_LANES < SHARED_LANES, low, pltpu.roll(high, SHARED_LANES, 1))
+        out_ref[pl.ds((len(packed) - 1) * span, span // 2), :] = shared
+    start = (groups - 1) * span + span // 2 + (groups + 1) * EDGE
     inner_ref[pl.ds(start, span), :] = modes_ref[...]
 
 
@@ -394,8 +398,11 @@
     even = lax.rem(lax.axis_index("pitch"), 2) == 0
 
     def group(ref, g):
-        corner = ref[pl.ds(groups * span + g * EDGE, EDGE), :]
-        return jnp.concatenate([ref[pl.ds(g * span, span), :], corner], 0)
+        corner = ref[pl.ds((groups - 1) * span + span // 2 + g * EDGE, EDGE), :]
+        if g < groups - 1:
+            return jnp.concatenate([ref[pl.ds(g * span, span), :], corner], 0)
+        shared = ref[pl.ds(g * span, span // 2), :]
+        return jnp.concatenate([shared, pltpu.roll(shared, pitch - SHARED_LANES, 1), corner], 0)
 
     halves = [(group(inner_ref, g), group(outer_ref, g)) for g in range(groups)]
     from_left = [jnp.where(even, outer, inner) for inner, outer in halves]
@@ -645,6 +652,8 @@
     )
     blades = blades.reshape(1, -1)
     corner_rows = groups * EDGE
+    own_rows = (groups - 1) * span + span // 2
+    assert slots(fields + 1, components)[1][-1][1] < SHARED_LANES
     state_shape = struct(axial + 2, components, axial, wide, pitch)
     state, coef, inv, span_out, small, modes, table, blades, *tables = call(
         start_kernel, "start",
@@ -663,7 +672,7 @@
     )
     edges, inner, outer = call(
         pack_kernel, "pack",
-        (struct(fields + 1, span, pitch), struct((groups + 1) * wide, pitch), struct(groups * wide, pitch)),
+        (struct(fields + 1, span, pitch), struct(own_rows + corner_rows + wide, pitch), struct(own_rows + corner_rows, pitch)),
         [(vmem, x) for x in (state, coef, inv, modes)],
         groups=groups,
     )
@@ -691,12 +700,12 @@
     small, edges, jac = lax.optimization_barrier((moved(small, lambda r, s, p: (r, 1 - s, p)), edges, jac))
     from_span = moved(span_out, lambda r, s, p: (r, 1 - s, p))
     edge_shape = struct(axial + 1, components, wide, pitch)
-    inner = lax.dynamic_update_slice(inner, small[:corner_rows + EDGE], (groups * span, 0))
-    outer = lax.dynamic_update_slice(outer, small[corner_rows + EDGE:], (groups * span, 0))
-    modes = inner[groups * span + corner_rows:]
+    inner = lax.dynamic_update_slice(inner, small[:corner_rows + EDGE], (own_rows, 0))
+    outer = lax.dynamic_update_slice(outer, small[corner_rows + EDGE:], (own_rows, 0))
+    modes = inner[own_rows + corner_rows:]
     outer = moved(outer, lambda r, s, p: (r, s, (p - 1 + 2 * (p % 2)) % place_count))
     inner = moved(inner, lambda r, s, p: (r, s, p ^ 1))
-    modes = modes + inner[groups * span + corner_rows:]
+    modes = modes + inner[own_rows + corner_rows:]
     for step in steps[1:]:
         modes = modes + moved(modes, lambda r, s, p: (r, s, p ^ step))
     got = moved(modes, lambda r, s, p: (r, s, p ^ last_step))

time: 38.9 us -> 38.7 us (level)
  no operation moved by 1% of the time
where the time goes in v19:
time: 38.7 us; the launch traced here: 38.5 us
  starting transfers between devices  21.1 us (55%)
  Pallas kernels  13.2 us (34%)
  waiting for transfers between devices  4.14 us (11%)
    ppermute x9, starting transfers between devices, moved(): return lax.ppermute(x, AXES, pairs)  21.1 us
    pallas_call x9, Pallas kernels, call(): pl.pallas_call(functools.partial(kernel, **fixed), out_shape=outs, in_spe...  13.2 us
    ppermute x9, waiting for transfers between devices, moved(): return lax.ppermute(x, AXES, pairs)  4.14 us
  transfers between devices with their start and end apart: 9, of which 4 were waited for; matrix products, arithmetic and copies ran while one was open for 0% of the time, Pallas kernels for 20%

profile of v19, /device:TPU:1, one launch (start us, length us, event | category | flops | bytes accessed | tf_op | source)
XLA Modules:
  0.0 38.5 jit_solution(14445555119403884230)
XLA Ops:
  0.0 1.7 %start.1 = (f32[6,5,4,40,128]{4,3,2,1,0:T(8,128)S(1)}, f32[11,4,40,128]{3,2,1,0:T(8,128)S(1)}, f32[40,128]{1,0:T(8,128)S(1)}, f32[36,8,128]{2,1,0:T(8,128)S(1)},...) custom-call(f32[5,4,32,128]{3,2,1,0:T(8,128)} %adjoint_hbm.1, ...), custom_call_target="tpu_custom_call" | custom-call | tf_op jit(solution)/shard_map/start/pallas_call | solution.py:638
  1.7 2.1 %collective-permute-start = (f32[56,128]{1,0:T(8,128)S(1)}, f32[56,128]{1,0:T(8,128)S(1)}, u32[]{:S(2)}, u32[]{:S(2)}) collective-permute-start(f32[56,128]{1,0:T(8,128)S(1)} %get-tuple-element.43), channel_id=1, source_target_pairs={{0,4},{1,5},{2,6},{3,7},{4,0},{5,1},{6,2},{7,3},{8,12},{9,13},{10,... | collective-permute-start | bytes 86024 | tf_op jit(solution)/shard_map/ppermute | solution.py:608
  3.9 0.1 collective-permute-start.1
  3.9 0.8 %pack.1 = (f32[17,32,128]{2,1,0:T(8,128)S(1)}, f32[144,128]{1,0:T(8,128)S(1)}, f32[104,128]{1,0:T(8,128)S(1)}) custom-call(f32[6,5,4,40,128]{4,3,2,1,0:T(8,128)S(1)} %get-tuple-element.44.state_ref.state_in_ref, f32[11,4,40,128]{3,2,1,0:T(8,128)S(1)} %get-tuple-element.45.coef_ref.coef_in_ref, f32[40,128]{1,0:T(8,128)S(1)} %get-tuple-element.46.inv_ref.inv_in_ref, ...), custom_call_target="tpu_custom_call" | custom-call | tf_op jit(solution)/shard_map/pack/pallas_call | solution.py:638
  4.7 0.7 %synth.1 = (bf16[896,384]{1,0:T(8,128)(2,1)S(1)}, f32[152,128]{1,0:T(8,128)S(1)}) custom-call(s32[1,4]{1,0:T(1,128)S(1)} %get-tuple-element.49.blades_ref, f32[5,5,1,6]{3,2,1,0:T(1,128)S(1)} %get-tuple-element.50.jacobians_ref, f32[5,5,3,64]{3,2,1,0:T(4,128)S(1)} %get-tuple-element.51.giles_re_ref, f32[5,5,3,64]{3,2,1,0:T(4,128)S(1)} %get-tuple-element.52.giles_im_ref, ...), custom_call_target="tpu_custom_call" | custom-call | tf_op jit(solution)/shard_map/synth/pallas_call | solution.py:638
  5.4 0.0 collective-permute-done
  5.4 1.5 %collective-permute-start.2 = (f32[144,128]{1,0:T(8,128)S(1)}, f32[144,128]{1,0:T(8,128)S(1)}, u32[]{:S(2)}, u32[]{:S(2)}) collective-permute-start(f32[144,128]{1,0:T(8,128)S(1)} %slice_dynamic-update-slice_fusion), channel_id=1, source_target_pairs={{0,1},{1,0},{2,3},{3,2},{4,5},{5,4},{6,7},{7,6},{8,9},{9,8},{10,11... | collective-permute-start | bytes 221192 | tf_op jit(solution)/shard_map/ppermute | solution.py:608
  6.9 2.2 %collective-permute-start.3 = (f32[104,128]{1,0:T(8,128)S(1)}, f32[104,128]{1,0:T(8,128)S(1)}, u32[]{:S(2)}, u32[]{:S(2)}) collective-permute-start(f32[104,128]{1,0:T(8,128)S(1)} %slice_dynamic-update-slice_fusion.1), channel_id=1, source_target_pairs={{0,3},{1,2},{2,1},{3,0},{4,7},{5,6},{6,5},{7,4},{8,11},{9,10},{10,... | collective-permute-start | bytes 159752 | tf_op jit(solution)/shard_map/ppermute | solution.py:608
  9.1 0.0 collective-permute-done.2.inner_ref
  9.1 2.3 %collective-permute-start.4 = (f32[40,128]{1,0:T(8,128)S(1)}, f32[40,128]{1,0:T(8,128)S(1)}, u32[]{:S(2)}, u32[]{:S(2)}) collective-permute-start(f32[40,128]{1,0:T(8,128)S(1)} %slice_add_fusion), channel_id=1, source_target_pairs={{0,2},{1,3},{2,0},{3,1},{4,6},{5,7},{6,4},{7,5},{8,10},{9,11},{10,... | collective-permute-start | bytes 61448 | tf_op jit(solution)/shard_map/ppermute | solution.py:608
  11.5 0.3 collective-permute-done.3.outer_ref
  11.7 0.0 collective-permute-done.1.span_ref
  11.7 1.7 %first_sweep.1 = (f32[11,4,40,128]{3,2,1,0:T(8,128)S(1)}, f32[40,128]{1,0:T(8,128)S(1)}, f32[12,40,128]{2,1,0:T(8,128)S(1)}, f32[6,5,4,40,128]{4,3,2,1,0:T(8,128)S(1)}, f32[5,5,40,128]{3,2,1,0:T(8,128)S(1)}) custom-call(f32[152,128]{1,0:T(8,128)S(1)} %get-tuple-element.56.jac_ref, ...), custom_call_target="tpu_custom_call", output_to_operand_aliasing={{3}: (1, {}), {0}: (2, {}), {1}: (3, {})} | custom-call | tf_op jit(solution)/shard_map/first_sweep/pallas_call | solution.py:638
  13.4 0.0 collective-permute-done.4
  13.4 5.1 %collective-permute-start.5 = (f32[40,128]{1,0:T(8,128)S(1)}, f32[40,128]{1,0:T(8,128)S(1)}, u32[]{:S(2)}, u32[]{:S(2)}) collective-permute-start(f32[40,128]{1,0:T(8,128)S(1)} %add.10), channel_id=1, source_target_pairs={{8,0},{9,1},{10,2},{11,3},{12,4},{13,5},{14,6},{15,7},{16,8},{17,9... | collective-permute-start | bytes 61448 | tf_op jit(solution)/shard_map/ppermute | solution.py:608
  18.6 2.4 %more_sweeps.1 = (f32[6,5,4,40,128]{4,3,2,1,0:T(8,128)S(1)}, f32[5,5,40,128]{3,2,1,0:T(8,128)S(1)}, f32[104,128]{1,0:T(8,128)S(1)}, f32[32,128]{1,0:T(8,128)S(1)}) custom-call(f32[152,128]{1,0:T(8,128)S(1)} %get-tuple-element.56.jac_ref, f32[11,4,40,128]{3,2,1,0:T(8,128)S(1)} %get-tuple-element.62.coef_ref, ...), custom_call_target="tpu_custom_call", output_to_operand_aliasing={{0}: (3, {}), {1}: (4, {})} | custom-call | tf_op jit(solution)/shard_map/more_sweeps/pallas_call | solution.py:638
  21.0 0.1 collective-permute-done.5.first_ref.modes_ref
  21.1 0.5 %late_modes.1.more_ref = f32[136,128]{1,0:T(8,128)S(1)} custom-call(f32[152,128]{1,0:T(8,128)S(1)} %get-tuple-element.56.jac_ref, f32[11,4,40,128]{3,2,1,0:T(8,128)S(1)} %get-tuple-element.62.coef_ref, f32[40,128]{1,0:T(8,128)S(1)} %get-tuple-element.64.inv_ref, f32[32,128]{1,0:T(8,128)S(1)} %get-tuple-element.73.part_ref, ...), custom_call_target="tpu_custom_call" | custom-call | tf_op jit(solution)/shard_map/late_modes/pallas_call | solution.py:638
  21.6 1.7 %collective-permute-start.6 = (f32[136,128]{1,0:T(8,128)S(1)}, f32[136,128]{1,0:T(8,128)S(1)}, u32[]{:S(2)}, u32[]{:S(2)}) collective-permute-start(f32[136,128]{1,0:T(8,128)S(1)} %late_modes.1.more_ref), channel_id=1, source_target_pairs={{0,1},{1,0},{2,3},{3,2},{4,5},{5,4},{6,7},{7,6},{8,9},{9,8},{10,11... | collective-permute-start | bytes 208904 | tf_op jit(solution)/shard_map/ppermute | solution.py:608
  23.3 1.5 %between_sweeps.1 = (f32[6,5,4,40,128]{4,3,2,1,0:T(8,128)S(1)}, f32[5,5,40,128]{3,2,1,0:T(8,128)S(1)}, f32[136,128]{1,0:T(8,128)S(1)}) custom-call(f32[152,128]{1,0:T(8,128)S(1)} %get-tuple-element.56.jac_ref, f32[11,4,40,128]{3,2,1,0:T(8,128)S(1)} %get-tuple-element.62.coef_ref, ...), custom_call_target="tpu_custom_call", output_to_operand_aliasing={{0}: (4, {}), {1}: (5, {})} | custom-call | tf_op jit(solution)/shard_map/between_sweeps/pallas_call | solution.py:638
  24.8 0.5 %collective-permute-done.6 = f32[136,128]{1,0:T(8,128)S(1)} collective-permute-done((f32[136,128]{1,0:T(8,128)S(1)}, f32[136,128]{1,0:T(8,128)S(1)}, u32[]{:S(2)}, u32[]{:S(2)}) %collective-permute-start.6) | collective-permute-done | bytes 69664 | tf_op jit(solution)/shard_map/ppermute | solution.py:608
  25.3 4.1 %collective-permute-start.8 = (f32[136,128]{1,0:T(8,128)S(1)}, f32[136,128]{1,0:T(8,128)S(1)}, u32[]{:S(2)}, u32[]{:S(2)}) collective-permute-start(f32[136,128]{1,0:T(8,128)S(1)} %add.11), channel_id=1, source_target_pairs={{8,2},{9,3},{10,0},{11,1},{12,6},{13,7},{14,4},{15,5},{16,10},{17,... | collective-permute-start | bytes 208904 | tf_op jit(solution)/shard_map/ppermute | solution.py:608
  29.4 1.9 %collective-permute-start.7 = (f32[136,128]{1,0:T(8,128)S(1)}, f32[136,128]{1,0:T(8,128)S(1)}, u32[]{:S(2)}, u32[]{:S(2)}) collective-permute-start(f32[136,128]{1,0:T(8,128)S(1)} %add.11), channel_id=1, source_target_pairs={{8,0},{9,1},{10,2},{11,3},{12,4},{13,5},{14,6},{15,7},{16,8},{17,9... | collective-permute-start | bytes 208904 | tf_op jit(solution)/shard_map/ppermute | solution.py:608
  31.3 0.7 %beside_sweeps.1 = (f32[6,5,4,40,128]{4,3,2,1,0:T(8,128)S(1)}, f32[5,5,40,128]{3,2,1,0:T(8,128)S(1)}) custom-call(f32[152,128]{1,0:T(8,128)S(1)} %get-tuple-element.56.jac_ref, f32[11,4,40,128]{3,2,1,0:T(8,128)S(1)} %get-tuple-element.62.coef_ref, f32[12,40,128]{2,1,0:T(8,128)S(1)} %get-tuple-element.65.edge_coef_ref, ...), custom_call_target="tpu_custom_call", output_to_operand_aliasing={{0}: (3, {}), {1}: (4, {})} | custom-call | tf_op jit(solution)/shard_map/beside_sweeps/pallas_call | solution.py:638
  32.1 3.3 %collective-permute-done.8.more_b_ref = f32[136,128]{1,0:T(8,128)S(1)} collective-permute-done((f32[136,128]{1,0:T(8,128)S(1)}, f32[136,128]{1,0:T(8,128)S(1)}, u32[]{:S(2)}, u32[]{:S(2)}) %collective-permute-start.8) | collective-permute-done | bytes 69664 | tf_op jit(solution)/shard_map/ppermute | solution.py:608
  35.3 0.0 collective-permute-done.7.more_a_ref
  35.3 3.2 %second_sweeps.1 = (f32[6,5,4,40,128]{4,3,2,1,0:T(8,128)S(1)}, f32[5,5,40,128]{3,2,1,0:T(8,128)S(1)}, f32[5,4,32,128]{3,2,1,0:T(8,128)}) custom-call(f32[152,128]{1,0:T(8,128)S(1)} %get-tuple-element.56.jac_ref, f32[11,4,40,128]{3,2,1,0:T(8,128)S(1)} %get-tuple-element.62.coef_ref, ...), custom_call_target="tpu_custom_call", output_to_operand_aliasing={{0}: (4, {}), {1}: (5, {})} | custom-call | tf_op jit(solution)/shard_map/second_sweeps/pallas_call | solution.py:638
  (5 shorter events, 0.0 us)
Async XLA Ops:
  1.7 3.7 %collective-permute-start = (f32[56,128]{1,0:T(8,128)S(1)}, f32[56,128]{1,0:T(8,128)S(1)}, u32[]{:S(2)}, u32[]{:S(2)}) collective-permute-start(f32[56,128]{1,0:T(8,128)S(1)} %get-tuple-element.43), channel_id=1, source_target_pairs={{0,4},{1,5},{2,6},{3,7},{4,0},{5,1},{6,2},{7,3},{8,12},{9,13},{10,... | collective-permute-start | bytes 86024 | tf_op jit(solution)/shard_map/ppermute | solution.py:608
  3.9 7.9 %collective-permute-start.1 = (f32[36,8,128]{2,1,0:T(8,128)S(1)}, f32[36,8,128]{2,1,0:T(8,128)S(1)}, u32[]{:S(2)}, u32[]{:S(2)}) collective-permute-start(f32[36,8,128]{2,1,0:T(8,128)S(1)} %get-tuple-element.58), channel_id=1, source_target_pairs={{0,4},{1,5},{2,6},{3,7},{4,0},{5,1},{6,2},{7,3},{8,12},{9,13},{10,... | collective-permute-start | bytes 442376 | tf_op jit(solution)/shard_map/ppermute | solution.py:608
  5.4 3.7 %collective-permute-start.2 = (f32[144,128]{1,0:T(8,128)S(1)}, f32[144,128]{1,0:T(8,128)S(1)}, u32[]{:S(2)}, u32[]{:S(2)}) collective-permute-start(f32[144,128]{1,0:T(8,128)S(1)} %slice_dynamic-update-slice_fusion), channel_id=1, source_target_pairs={{0,1},{1,0},{2,3},{3,2},{4,5},{5,4},{6,7},{7,6},{8,9},{9,8},{10,11... | collective-permute-start | bytes 221192 | tf_op jit(solution)/shard_map/ppermute | solution.py:608
  6.9 4.8 %collective-permute-start.3 = (f32[104,128]{1,0:T(8,128)S(1)}, f32[104,128]{1,0:T(8,128)S(1)}, u32[]{:S(2)}, u32[]{:S(2)}) collective-permute-start(f32[104,128]{1,0:T(8,128)S(1)} %slice_dynamic-update-slice_fusion.1), channel_id=1, source_target_pairs={{0,3},{1,2},{2,1},{3,0},{4,7},{5,6},{6,5},{7,4},{8,11},{9,10},{10,... | collective-permute-start | bytes 159752 | tf_op jit(solution)/shard_map/ppermute | solution.py:608
  9.1 4.3 %collective-permute-start.4 = (f32[40,128]{1,0:T(8,128)S(1)}, f32[40,128]{1,0:T(8,128)S(1)}, u32[]{:S(2)}, u32[]{:S(2)}) collective-permute-start(f32[40,128]{1,0:T(8,128)S(1)} %slice_add_fusion), channel_id=1, source_target_pairs={{0,2},{1,3},{2,0},{3,1},{4,6},{5,7},{6,4},{7,5},{8,10},{9,11},{10,... | collective-permute-start | bytes 61448 | tf_op jit(solution)/shard_map/ppermute | solution.py:608
  13.4 7.7 %collective-permute-start.5 = (f32[40,128]{1,0:T(8,128)S(1)}, f32[40,128]{1,0:T(8,128)S(1)}, u32[]{:S(2)}, u32[]{:S(2)}) collective-permute-start(f32[40,128]{1,0:T(8,128)S(1)} %add.10), channel_id=1, source_target_pairs={{8,0},{9,1},{10,2},{11,3},{12,4},{13,5},{14,6},{15,7},{16,8},{17,9... | collective-permute-start | bytes 61448 | tf_op jit(solution)/shard_map/ppermute | solution.py:608
  21.6 3.7 %collective-permute-start.6 = (f32[136,128]{1,0:T(8,128)S(1)}, f32[136,128]{1,0:T(8,128)S(1)}, u32[]{:S(2)}, u32[]{:S(2)}) collective-permute-start(f32[136,128]{1,0:T(8,128)S(1)} %late_modes.1.more_ref), channel_id=1, source_target_pairs={{0,1},{1,0},{2,3},{3,2},{4,5},{5,4},{6,7},{7,6},{8,9},{9,8},{10,11... | collective-permute-start | bytes 208904 | tf_op jit(solution)/shard_map/ppermute | solution.py:608
  25.3 10.0 %collective-permute-start.8 = (f32[136,128]{1,0:T(8,128)S(1)}, f32[136,128]{1,0:T(8,128)S(1)}, u32[]{:S(2)}, u32[]{:S(2)}) collective-permute-start(f32[136,128]{1,0:T(8,128)S(1)} %add.11), channel_id=1, source_target_pairs={{8,2},{9,3},{10,0},{11,1},{12,6},{13,7},{14,4},{15,5},{16,10},{17,... | collective-permute-start | bytes 208904 | tf_op jit(solution)/shard_map/ppermute | solution.py:608
  29.4 5.9 %collective-permute-start.7 = (f32[136,128]{1,0:T(8,128)S(1)}, f32[136,128]{1,0:T(8,128)S(1)}, u32[]{:S(2)}, u32[]{:S(2)}) collective-permute-start(f32[136,128]{1,0:T(8,128)S(1)} %add.11), channel_id=1, source_target_pairs={{8,0},{9,1},{10,2},{11,3},{12,4},{13,5},{14,6},{15,7},{16,8},{17,9... | collective-permute-start | bytes 208904 | tf_op jit(solution)/shard_map/ppermute | solution.py:608

commit v20 on v19

--- a/solution.py
+++ b/solution.py
@@ -543,7 +543,7 @@
 
 
 def second_kernel(
-    jac_ref, coef_ref, inv_ref, edge_coef_ref, state_in_ref, edge_in_ref, more_a_ref, more_b_ref, synth_ref,
+    jac_ref, coef_ref, inv_ref, edge_coef_ref, state_in_ref, edge_in_ref, more_b_ref, more_a_ref, synth_ref,
     state_ref, edge_ref, out_hbm, bound_ref, out_ref, sems,
 ):
     axial, components, span, pitch = out_ref.shape
@@ -749,7 +749,7 @@
     more_a = near(more)
     return call(
         second_kernel, "second_sweeps", (state_shape, edge_shape, struct(components, axial, span, pitch)),
-        [(vmem, x) for x in (jac, coef, inv, edge_coef, state, edge, more_a, more_b, synth)],
+        [(vmem, x) for x in (jac, coef, inv, edge_coef, state, edge, more_b, more_a, synth)],
         aliases={4: 0, 5: 1},
         scratch=[
             pltpu.VMEM((axial + 1, components, wide, pitch), jnp.float32),

time: 38.7 us -> 40.6 us (1.049)
  waiting for transfers between devices: 4.14 us -> 6.68 us
  starting transfers between devices: 21.1 us -> 20.4 us
    ppermute x9, waiting for transfers between devices: 4.14 us -> 6.68 us  [moved(): return lax.ppermute(x, AXES, pairs)]
    ppermute x9, starting transfers between devices: 21.1 us -> 20.4 us  [moved(): return lax.ppermute(x, AXES, pairs)]
  transfers between devices with their start and end apart: 9 -> 9, of which waited for: 4 -> 4; matrix products, arithmetic and copies ran while one was open for 0% -> 0% of each run, Pallas kernels for 20% -> 19%
where the time goes in v20:
time: 40.6 us; the launch traced here: 40.4 us
  starting transfers between devices  20.4 us (50%)
  Pallas kernels  13.2 us (33%)
  waiting for transfers between devices  6.68 us (16%)
    ppermute x9, starting transfers between devices, moved(): return lax.ppermute(x, AXES, pairs)  20.4 us
    pallas_call x9, Pallas kernels, call(): pl.pallas_call(functools.partial(kernel, **fixed), out_shape=outs, in_spe...  13.2 us
    ppermute x9, waiting for transfers between devices, moved(): return lax.ppermute(x, AXES, pairs)  6.68 us
  transfers between devices with their start and end apart: 9, of which 4 were waited for; matrix products, arithmetic and copies ran while one was open for 0% of the time, Pallas kernels for 19%

profile of v20, /device:TPU:1, one launch (start us, length us, event | category | flops | bytes accessed | tf_op | source)
XLA Modules:
  0.0 40.4 jit_solution(15680679649761164030)
XLA Ops:
  0.0 1.7 %start.1 = (f32[6,5,4,40,128]{4,3,2,1,0:T(8,128)S(1)}, f32[11,4,40,128]{3,2,1,0:T(8,128)S(1)}, f32[40,128]{1,0:T(8,128)S(1)}, f32[36,8,128]{2,1,0:T(8,128)S(1)},...) custom-call(f32[5,4,32,128]{3,2,1,0:T(8,128)} %adjoint_hbm.1, ...), custom_call_target="tpu_custom_call" | custom-call | tf_op jit(solution)/shard_map/start/pallas_call | solution.py:638
  1.7 2.1 %collective-permute-start = (f32[56,128]{1,0:T(8,128)S(1)}, f32[56,128]{1,0:T(8,128)S(1)}, u32[]{:S(2)}, u32[]{:S(2)}) collective-permute-start(f32[56,128]{1,0:T(8,128)S(1)} %get-tuple-element.43), channel_id=1, source_target_pairs={{0,4},{1,5},{2,6},{3,7},{4,0},{5,1},{6,2},{7,3},{8,12},{9,13},{10,... | collective-permute-start | bytes 86024 | tf_op jit(solution)/shard_map/ppermute | solution.py:608
  3.9 0.1 collective-permute-start.1
  3.9 0.8 %pack.1 = (f32[17,32,128]{2,1,0:T(8,128)S(1)}, f32[144,128]{1,0:T(8,128)S(1)}, f32[104,128]{1,0:T(8,128)S(1)}) custom-call(f32[6,5,4,40,128]{4,3,2,1,0:T(8,128)S(1)} %get-tuple-element.44.state_ref.state_in_ref, f32[11,4,40,128]{3,2,1,0:T(8,128)S(1)} %get-tuple-element.45.coef_ref.coef_in_ref, f32[40,128]{1,0:T(8,128)S(1)} %get-tuple-element.46.inv_ref.inv_in_ref, ...), custom_call_target="tpu_custom_call" | custom-call | tf_op jit(solution)/shard_map/pack/pallas_call | solution.py:638
  4.7 0.7 %synth.1 = (bf16[896,384]{1,0:T(8,128)(2,1)S(1)}, f32[152,128]{1,0:T(8,128)S(1)}) custom-call(s32[1,4]{1,0:T(1,128)S(1)} %get-tuple-element.49.blades_ref, f32[5,5,1,6]{3,2,1,0:T(1,128)S(1)} %get-tuple-element.50.jacobians_ref, f32[5,5,3,64]{3,2,1,0:T(4,128)S(1)} %get-tuple-element.51.giles_re_ref, f32[5,5,3,64]{3,2,1,0:T(4,128)S(1)} %get-tuple-element.52.giles_im_ref, ...), custom_call_target="tpu_custom_call" | custom-call | tf_op jit(solution)/shard_map/synth/pallas_call | solution.py:638
  5.4 0.0 collective-permute-done
  5.4 1.5 %collective-permute-start.2 = (f32[144,128]{1,0:T(8,128)S(1)}, f32[144,128]{1,0:T(8,128)S(1)}, u32[]{:S(2)}, u32[]{:S(2)}) collective-permute-start(f32[144,128]{1,0:T(8,128)S(1)} %slice_dynamic-update-slice_fusion), channel_id=1, source_target_pairs={{0,1},{1,0},{2,3},{3,2},{4,5},{5,4},{6,7},{7,6},{8,9},{9,8},{10,11... | collective-permute-start | bytes 221192 | tf_op jit(solution)/shard_map/ppermute | solution.py:608
  6.9 2.2 %collective-permute-start.3 = (f32[104,128]{1,0:T(8,128)S(1)}, f32[104,128]{1,0:T(8,128)S(1)}, u32[]{:S(2)}, u32[]{:S(2)}) collective-permute-start(f32[104,128]{1,0:T(8,128)S(1)} %slice_dynamic-update-slice_fusion.1), channel_id=1, source_target_pairs={{0,3},{1,2},{2,1},{3,0},{4,7},{5,6},{6,5},{7,4},{8,11},{9,10},{10,... | collective-permute-start | bytes 159752 | tf_op jit(solution)/shard_map/ppermute | solution.py:608
  9.1 0.0 collective-permute-done.2.inner_ref
  9.1 2.3 %collective-permute-start.4 = (f32[40,128]{1,0:T(8,128)S(1)}, f32[40,128]{1,0:T(8,128)S(1)}, u32[]{:S(2)}, u32[]{:S(2)}) collective-permute-start(f32[40,128]{1,0:T(8,128)S(1)} %slice_add_fusion), channel_id=1, source_target_pairs={{0,2},{1,3},{2,0},{3,1},{4,6},{5,7},{6,4},{7,5},{8,10},{9,11},{10,... | collective-permute-start | bytes 61448 | tf_op jit(solution)/shard_map/ppermute | solution.py:608
  11.5 0.3 collective-permute-done.3.outer_ref
  11.7 0.0 collective-permute-done.1.span_ref
  11.7 1.7 %first_sweep.1 = (f32[11,4,40,128]{3,2,1,0:T(8,128)S(1)}, f32[40,128]{1,0:T(8,128)S(1)}, f32[12,40,128]{2,1,0:T(8,128)S(1)}, f32[6,5,4,40,128]{4,3,2,1,0:T(8,128)S(1)}, f32[5,5,40,128]{3,2,1,0:T(8,128)S(1)}) custom-call(f32[152,128]{1,0:T(8,128)S(1)} %get-tuple-element.56.jac_ref, ...), custom_call_target="tpu_custom_call", output_to_operand_aliasing={{3}: (1, {}), {0}: (2, {}), {1}: (3, {})} | custom-call | tf_op jit(solution)/shard_map/first_sweep/pallas_call | solution.py:638
  13.4 0.0 collective-permute-done.4
  13.4 5.1 %collective-permute-start.5 = (f32[40,128]{1,0:T(8,128)S(1)}, f32[40,128]{1,0:T(8,128)S(1)}, u32[]{:S(2)}, u32[]{:S(2)}) collective-permute-start(f32[40,128]{1,0:T(8,128)S(1)} %add.10), channel_id=1, source_target_pairs={{8,0},{9,1},{10,2},{11,3},{12,4},{13,5},{14,6},{15,7},{16,8},{17,9... | collective-permute-start | bytes 61448 | tf_op jit(solution)/shard_map/ppermute | solution.py:608
  18.6 2.4 %more_sweeps.1 = (f32[6,5,4,40,128]{4,3,2,1,0:T(8,128)S(1)}, f32[5,5,40,128]{3,2,1,0:T(8,128)S(1)}, f32[104,128]{1,0:T(8,128)S(1)}, f32[32,128]{1,0:T(8,128)S(1)}) custom-call(f32[152,128]{1,0:T(8,128)S(1)} %get-tuple-element.56.jac_ref, f32[11,4,40,128]{3,2,1,0:T(8,128)S(1)} %get-tuple-element.62.coef_ref, ...), custom_call_target="tpu_custom_call", output_to_operand_aliasing={{0}: (3, {}), {1}: (4, {})} | custom-call | tf_op jit(solution)/shard_map/more_sweeps/pallas_call | solution.py:638
  21.0 0.1 collective-permute-done.5.first_ref.modes_ref
  21.1 0.5 %late_modes.1.more_ref = f32[136,128]{1,0:T(8,128)S(1)} custom-call(f32[152,128]{1,0:T(8,128)S(1)} %get-tuple-element.56.jac_ref, f32[11,4,40,128]{3,2,1,0:T(8,128)S(1)} %get-tuple-element.62.coef_ref, f32[40,128]{1,0:T(8,128)S(1)} %get-tuple-element.64.inv_ref, f32[32,128]{1,0:T(8,128)S(1)} %get-tuple-element.73.part_ref, ...), custom_call_target="tpu_custom_call" | custom-call | tf_op jit(solution)/shard_map/late_modes/pallas_call | solution.py:638
  21.6 1.7 %collective-permute-start.6 = (f32[136,128]{1,0:T(8,128)S(1)}, f32[136,128]{1,0:T(8,128)S(1)}, u32[]{:S(2)}, u32[]{:S(2)}) collective-permute-start(f32[136,128]{1,0:T(8,128)S(1)} %late_modes.1.more_ref), channel_id=1, source_target_pairs={{0,1},{1,0},{2,3},{3,2},{4,5},{5,4},{6,7},{7,6},{8,9},{9,8},{10,11... | collective-permute-start | bytes 208904 | tf_op jit(solution)/shard_map/ppermute | solution.py:608
  23.3 1.5 %between_sweeps.1 = (f32[6,5,4,40,128]{4,3,2,1,0:T(8,128)S(1)}, f32[5,5,40,128]{3,2,1,0:T(8,128)S(1)}, f32[136,128]{1,0:T(8,128)S(1)}) custom-call(f32[152,128]{1,0:T(8,128)S(1)} %get-tuple-element.56.jac_ref, f32[11,4,40,128]{3,2,1,0:T(8,128)S(1)} %get-tuple-element.62.coef_ref, ...), custom_call_target="tpu_custom_call", output_to_operand_aliasing={{0}: (4, {}), {1}: (5, {})} | custom-call | tf_op jit(solution)/shard_map/between_sweeps/pallas_call | solution.py:638
  24.8 0.5 %collective-permute-done.6 = f32[136,128]{1,0:T(8,128)S(1)} collective-permute-done((f32[136,128]{1,0:T(8,128)S(1)}, f32[136,128]{1,0:T(8,128)S(1)}, u32[]{:S(2)}, u32[]{:S(2)}) %collective-permute-start.6) | collective-permute-done | bytes 69664 | tf_op jit(solution)/shard_map/ppermute | solution.py:608
  25.3 2.2 %collective-permute-start.8 = (f32[136,128]{1,0:T(8,128)S(1)}, f32[136,128]{1,0:T(8,128)S(1)}, u32[]{:S(2)}, u32[]{:S(2)}) collective-permute-start(f32[136,128]{1,0:T(8,128)S(1)} %add.11), channel_id=1, source_target_pairs={{8,0},{9,1},{10,2},{11,3},{12,4},{13,5},{14,6},{15,7},{16,8},{17,9... | collective-permute-start | bytes 208904 | tf_op jit(solution)/shard_map/ppermute | solution.py:608
  27.5 3.1 %collective-permute-start.7 = (f32[136,128]{1,0:T(8,128)S(1)}, f32[136,128]{1,0:T(8,128)S(1)}, u32[]{:S(2)}, u32[]{:S(2)}) collective-permute-start(f32[136,128]{1,0:T(8,128)S(1)} %add.11), channel_id=1, source_target_pairs={{8,2},{9,3},{10,0},{11,1},{12,6},{13,7},{14,4},{15,5},{16,10},{17,... | collective-permute-start | bytes 208904 | tf_op jit(solution)/shard_map/ppermute | solution.py:608
  30.7 0.7 %beside_sweeps.1 = (f32[6,5,4,40,128]{4,3,2,1,0:T(8,128)S(1)}, f32[5,5,40,128]{3,2,1,0:T(8,128)S(1)}) custom-call(f32[152,128]{1,0:T(8,128)S(1)} %get-tuple-element.56.jac_ref, f32[11,4,40,128]{3,2,1,0:T(8,128)S(1)} %get-tuple-element.62.coef_ref, f32[12,40,128]{2,1,0:T(8,128)S(1)} %get-tuple-element.65.edge_coef_ref, ...), custom_call_target="tpu_custom_call", output_to_operand_aliasing={{0}: (3, {}), {1}: (4, {})} | custom-call | tf_op jit(solution)/shard_map/beside_sweeps/pallas_call | solution.py:638
  31.4 0.0 collective-permute-done.8.more_a_ref
  31.4 5.8 %collective-permute-done.7.more_b_ref = f32[136,128]{1,0:T(8,128)S(1)} collective-permute-done((f32[136,128]{1,0:T(8,128)S(1)}, f32[136,128]{1,0:T(8,128)S(1)}, u32[]{:S(2)}, u32[]{:S(2)}) %collective-permute-start.7) | collective-permute-done | bytes 69664 | tf_op jit(solution)/shard_map/ppermute | solution.py:608
  37.2 3.2 %second_sweeps.1 = (f32[6,5,4,40,128]{4,3,2,1,0:T(8,128)S(1)}, f32[5,5,40,128]{3,2,1,0:T(8,128)S(1)}, f32[5,4,32,128]{3,2,1,0:T(8,128)}) custom-call(f32[152,128]{1,0:T(8,128)S(1)} %get-tuple-element.56.jac_ref, f32[11,4,40,128]{3,2,1,0:T(8,128)S(1)} %get-tuple-element.62.coef_ref, ...), custom_call_target="tpu_custom_call", output_to_operand_aliasing={{0}: (4, {}), {1}: (5, {})} | custom-call | tf_op jit(solution)/shard_map/second_sweeps/pallas_call | solution.py:638
  (5 shorter events, 0.0 us)
Async XLA Ops:
  1.7 3.7 %collective-permute-start = (f32[56,128]{1,0:T(8,128)S(1)}, f32[56,128]{1,0:T(8,128)S(1)}, u32[]{:S(2)}, u32[]{:S(2)}) collective-permute-start(f32[56,128]{1,0:T(8,128)S(1)} %get-tuple-element.43), channel_id=1, source_target_pairs={{0,4},{1,5},{2,6},{3,7},{4,0},{5,1},{6,2},{7,3},{8,12},{9,13},{10,... | collective-permute-start | bytes 86024 | tf_op jit(solution)/shard_map/ppermute | solution.py:608
  3.9 7.9 %collective-permute-start.1 = (f32[36,8,128]{2,1,0:T(8,128)S(1)}, f32[36,8,128]{2,1,0:T(8,128)S(1)}, u32[]{:S(2)}, u32[]{:S(2)}) collective-permute-start(f32[36,8,128]{2,1,0:T(8,128)S(1)} %get-tuple-element.58), channel_id=1, source_target_pairs={{0,4},{1,5},{2,6},{3,7},{4,0},{5,1},{6,2},{7,3},{8,12},{9,13},{10,... | collective-permute-start | bytes 442376 | tf_op jit(solution)/shard_map/ppermute | solution.py:608
  5.4 3.7 %collective-permute-start.2 = (f32[144,128]{1,0:T(8,128)S(1)}, f32[144,128]{1,0:T(8,128)S(1)}, u32[]{:S(2)}, u32[]{:S(2)}) collective-permute-start(f32[144,128]{1,0:T(8,128)S(1)} %slice_dynamic-update-slice_fusion), channel_id=1, source_target_pairs={{0,1},{1,0},{2,3},{3,2},{4,5},{5,4},{6,7},{7,6},{8,9},{9,8},{10,11... | collective-permute-start | bytes 221192 | tf_op jit(solution)/shard_map/ppermute | solution.py:608
  6.9 4.8 %collective-permute-start.3 = (f32[104,128]{1,0:T(8,128)S(1)}, f32[104,128]{1,0:T(8,128)S(1)}, u32[]{:S(2)}, u32[]{:S(2)}) collective-permute-start(f32[104,128]{1,0:T(8,128)S(1)} %slice_dynamic-update-slice_fusion.1), channel_id=1, source_target_pairs={{0,3},{1,2},{2,1},{3,0},{4,7},{5,6},{6,5},{7,4},{8,11},{9,10},{10,... | collective-permute-start | bytes 159752 | tf_op jit(solution)/shard_map/ppermute | solution.py:608
  9.1 4.3 %collective-permute-start.4 = (f32[40,128]{1,0:T(8,128)S(1)}, f32[40,128]{1,0:T(8,128)S(1)}, u32[]{:S(2)}, u32[]{:S(2)}) collective-permute-start(f32[40,128]{1,0:T(8,128)S(1)} %slice_add_fusion), channel_id=1, source_target_pairs={{0,2},{1,3},{2,0},{3,1},{4,6},{5,7},{6,4},{7,5},{8,10},{9,11},{10,... | collective-permute-start | bytes 61448 | tf_op jit(solution)/shard_map/ppermute | solution.py:608
  13.4 7.7 %collective-permute-start.5 = (f32[40,128]{1,0:T(8,128)S(1)}, f32[40,128]{1,0:T(8,128)S(1)}, u32[]{:S(2)}, u32[]{:S(2)}) collective-permute-start(f32[40,128]{1,0:T(8,128)S(1)} %add.10), channel_id=1, source_target_pairs={{8,0},{9,1},{10,2},{11,3},{12,4},{13,5},{14,6},{15,7},{16,8},{17,9... | collective-permute-start | bytes 61448 | tf_op jit(solution)/shard_map/ppermute | solution.py:608
  21.6 3.7 %collective-permute-start.6 = (f32[136,128]{1,0:T(8,128)S(1)}, f32[136,128]{1,0:T(8,128)S(1)}, u32[]{:S(2)}, u32[]{:S(2)}) collective-permute-start(f32[136,128]{1,0:T(8,128)S(1)} %late_modes.1.more_ref), channel_id=1, source_target_pairs={{0,1},{1,0},{2,3},{3,2},{4,5},{5,4},{6,7},{7,6},{8,9},{9,8},{10,11... | collective-permute-start | bytes 208904 | tf_op jit(solution)/shard_map/ppermute | solution.py:608
  25.3 6.1 %collective-permute-start.8 = (f32[136,128]{1,0:T(8,128)S(1)}, f32[136,128]{1,0:T(8,128)S(1)}, u32[]{:S(2)}, u32[]{:S(2)}) collective-permute-start(f32[136,128]{1,0:T(8,128)S(1)} %add.11), channel_id=1, source_target_pairs={{8,0},{9,1},{10,2},{11,3},{12,4},{13,5},{14,6},{15,7},{16,8},{17,9... | collective-permute-start | bytes 208904 | tf_op jit(solution)/shard_map/ppermute | solution.py:608
  27.5 9.7 %collective-permute-start.7 = (f32[136,128]{1,0:T(8,128)S(1)}, f32[136,128]{1,0:T(8,128)S(1)}, u32[]{:S(2)}, u32[]{:S(2)}) collective-permute-start(f32[136,128]{1,0:T(8,128)S(1)} %add.11), channel_id=1, source_target_pairs={{8,2},{9,3},{10,0},{11,1},{12,6},{13,7},{14,4},{15,5},{16,10},{17,... | collective-permute-start | bytes 208904 | tf_op jit(solution)/shard_map/ppermute | solution.py:608
